TPU v7x, 128 devices: a whole 4x4x4 slice. The times are simulated.
128 devices in a mesh: band: 4 (over x_hi, core), wide: 32 (over y, z, x_lo).
Axes of the slice: x: 4 (x_hi: 2, x_lo: 2; x = x_hi * 2 + x_lo), y: 4, z: 4, core: 2. Of those that a mesh axis runs over, the one named last changes fastest.
Arguments:
- panels: bfloat16 [4096, 16512], P(('wide', 'band')), may hold values from -6 to 6
- void_mask: int32 [4096, 16384], P(('wide', 'band')), may hold values 0 or 1
- background: float32 [4096, 16384], P(('wide', 'band')), may hold values from -6 to 6
- row_offset: int32 [4096], P(('wide', 'band')), may hold values from 0 to 124
- row_frac: float32 [4096], P(('wide', 'band')), may hold values from 0 to 1
- tile_kind: int32 [128], replicated, may hold values from 0 to 1
- tile_shift: int32 [128], replicated, may hold values from 0 to 125
- tile_frac: float32 [128], replicated, may hold values from 0 to 1
- inverse_x: float32 [128, 128, 128], replicated, may hold values from -0.4 to 1.2, as said below
- couple_x: float32 [2, 128], replicated, may hold values from 0.2 to 0.8
- inverse_y: float32 [32, 128, 128], replicated, may hold values from -0.4 to 1.2, as said below
- couple_y: float32 [2, 32], replicated, may hold values from 0.2 to 0.8
Outputs:
- increment: float32 [4096, 16384], P(('wide', 'band'))
Inputs may be any that keep to these rules, and one draw needn't show every extreme that they name: `inverse_x`: each block has a diagonal of positive entries and small off-diagonal entries. `inverse_y`: each block has a diagonal of positive entries and small off-diagonal entries.
All inputs are finite; a program needn't handle non-finite values. No bound on the sum of `void_mask` on one device may be relied on, other than what follows from the above.
Results may differ from a plain program's by a relative error of at most 0.0027.
Values may be sent and summed in bfloat16 or wider, within the bound.
No kernel may reach another device: no remote copies, remote signals or barrier semaphores. Data moves between devices by JAX's collectives and lax.ppermute only.
A program may use at most 128 MiB of HBM per device.

v0:
```python
import jax
import jax.numpy as jnp
from jax import lax
from jax.sharding import PartitionSpec as P

BLK = 128
ITERS = 4


def cubic_terms(frac):
    f2 = frac * frac
    f3 = f2 * frac
    return [
        -0.5 * f3 + f2 - 0.5 * frac,
        1.5 * f3 - 2.5 * f2 + 1.0,
        -1.5 * f3 + 2.0 * f2 + 0.5 * frac,
        0.5 * f3 - 0.5 * f2,
    ]


def linear_terms(frac):
    zeros = jnp.zeros_like(frac)
    return [zeros, 1.0 - frac, frac, zeros]


def row_matrix(offsets, fracs, width, terms):
    columns = jnp.arange(width, dtype=jnp.int32)[None, :]
    total = jnp.zeros((offsets.shape[0], width), jnp.float32)
    for index, weight in enumerate(terms(fracs)):
        total = total + weight[:, None] * (columns == offsets[:, None] + index).astype(jnp.float32)
    return total.astype(jnp.bfloat16)


def column_tables(tile_kind, tile_frac):
    delta = (
        jnp.arange(BLK + 3, dtype=jnp.int32)[:, None] - jnp.arange(BLK, dtype=jnp.int32)[None, :]
    )
    cubic = jnp.zeros((tile_frac.shape[0], BLK + 3, BLK), jnp.float32)
    linear = jnp.zeros((tile_frac.shape[0], BLK + 3, BLK), jnp.float32)
    for index, (wc, wl) in enumerate(zip(cubic_terms(tile_frac), linear_terms(tile_frac))):
        hit = (delta == index).astype(jnp.float32)[None]
        cubic = cubic + wc[:, None, None] * hit
        linear = linear + wl[:, None, None] * hit
    return jnp.where(tile_kind[:, None, None] == 1, cubic, linear).astype(jnp.bfloat16)


def sweep_rows(source, inverse, couple):
    hp = lax.Precision.HIGHEST
    state = jnp.einsum("rbj,bij->rbi", source, inverse, precision=hp)
    for sweep in range(ITERS - 1):
        left = jnp.pad(state[:, :-1, -1], ((0, 0), (1, 0)))
        right = jnp.pad(state[:, 1:, 0], ((0, 0), (0, 1)))
        forced = source.at[:, :, 0].add(couple[0][None, :] * left)
        forced = forced.at[:, :, -1].add(couple[1][None, :] * right)
        state = jnp.einsum("rbj,bij->rbi", forced, inverse, precision=hp)
    return state


def sweep_columns(source, inverse, couple):
    hp = lax.Precision.HIGHEST
    state = jnp.einsum("bij,bjc->bic", inverse, source, precision=hp)
    for sweep in range(ITERS - 1):
        left = jnp.pad(state[:-1, -1, :], ((1, 0), (0, 0)))
        right = jnp.pad(state[1:, 0, :], ((0, 1), (0, 0)))
        forced = source.at[:, 0, :].add(couple[0][:, None] * left)
        forced = forced.at[:, -1, :].add(couple[1][:, None] * right)
        state = jnp.einsum("bij,bjc->bic", inverse, forced, precision=hp)
    return state


def body(
    panels,
    void_mask,
    background,
    row_offset,
    row_frac,
    tile_kind,
    tile_shift,
    tile_frac,
    inverse_x,
    couple_x,
    inverse_y,
    couple_y,
):
    rows = row_offset.shape[0]
    width = background.shape[1]
    tiles_count = width // BLK
    n_band = lax.axis_size("band")
    n_wide = lax.axis_size("wide")
    group = rows * n_band
    cubic = row_matrix(row_offset, row_frac, group, cubic_terms)
    linear = row_matrix(row_offset, row_frac, group, linear_terms)
    row_tiles = jnp.where(tile_kind[:, None, None] == 1, cubic[None], linear[None])
    starts = jnp.arange(tiles_count, dtype=jnp.int32) * BLK + tile_shift
    piece = lax.all_gather(panels, "band", axis=0, tiled=True)
    blocks = jax.vmap(lambda s: lax.dynamic_slice_in_dim(piece, s, BLK + 3, 1))(starts)
    section = jnp.einsum(
        "trs,tsc->trc", row_tiles, blocks, preferred_element_type=jnp.float32
    ).astype(jnp.bfloat16)
    col_weights = column_tables(tile_kind, tile_frac)
    estimate = jnp.einsum(
        "trc,tcj->rtj", section, col_weights, preferred_element_type=jnp.float32
    ).reshape(rows, width)
    misfit = void_mask.astype(jnp.float32) * (estimate - background)
    east_west = sweep_rows(misfit.reshape(rows, tiles_count, BLK), inverse_x, couple_x).reshape(
        rows, width
    )
    n_all = n_band * n_wide
    cols = width // n_all
    arrived = lax.all_to_all(
        east_west.reshape(rows, n_all, cols),
        ("band", "wide"),
        split_axis=1,
        concat_axis=0,
        tiled=True,
    )
    arrived = arrived.reshape(n_band, n_wide, rows, cols).transpose(1, 0, 2, 3)
    diffused = sweep_columns(arrived.reshape(-1, BLK, cols), inverse_y, couple_y)
    outgoing = (
        diffused.reshape(n_wide, n_band, rows, cols)
        .transpose(1, 0, 2, 3)
        .reshape(n_all, rows, cols)
    )
    returned = lax.all_to_all(outgoing, ("band", "wide"), split_axis=0, concat_axis=2, tiled=True)
    result = returned.reshape(rows, width)
    return result


def solution(mesh):
    placed = (
        P(("wide", "band"), None),
        P(("wide", "band"), None),
        P(("wide", "band"), None),
        P(("wide", "band")),
        P(("wide", "band")),
        P(),
        P(),
        P(),
        P(),
        P(),
        P(),
        P(),
    )
    return jax.shard_map(
        body, mesh=mesh, in_specs=placed, out_specs=P(("wide", "band"), None), check_vma=False
    )
```

profile of v0, /device:TPU:25, one launch (start us, length us, event | category | flops | bytes accessed | tf_op | source)
XLA Modules:
  0.0 717.3 jit_solution(2112297186666515963)
XLA Ops:
  12.2 38.1 %all-gather.2.cloned.1.call-done = bf16[128,16512]{1,0:T(8,128)(2,1)} async-done(((bf16[32,16512]{1,0:T(8,128)(2,1)}), bf16[128,16512]{1,0:T(8,128)(2,1)}) %all-gather.2.cloned.1.call-update) | async-done | bytes 4227088 | tf_op jit(solution)/shard_map/all_gather | solution.py:95
  50.3 378.8 %while.13 = (s32[]{:T(128)}, bf16[128,16512]{1,0:T(8,128)(2,1)}, s32[128,2]{0,1:T(2,128)S(1)}, bf16[128,128,131]{2,1,0:T(8,128)(2,1)}, s32[]{:T(128)}) while((s32[]{:T(128)}, bf16[128,16512]{1,0:T(8,128)(2,1)}, s32[128,2]{0,1:T(2,128)S(1)}, bf16[128,128,131]{2,1,0:T(8,128)(2,1)}, s32[]{:T(128)}) %tuple.86), condition=%wide.while_cond.12, body=%wide.while_body.12.sunk | while | flops 2 | bytes 131685 | solution.py:96
  429.1 8.6 %fusion.41 = f32[128,4,8,128]{3,2,1,0:T(8,128)} fusion(bf16[128,128,131]{2,1,0:T(8,128)(2,1)} %get-tuple-element.156, f32[128]{0:T(128)S(1)} %copy-done.8, f32[128]{0:T(128)S(1)} %get-tuple-element.197, f32[131,128]{1,0:T(8,128)S(1)} %get-tuple-element.201, f32[128]{0:T(128)S(1)} %get-tuple-element.195, f32[131,128]{1,0:T(8,128)S(1)} %get-tuple-element.200, ...), kind=kOutput, calls=%fused_computation.46 | convolution fusion | flops 301543424 | bytes 6677632 | tf_op jit(solution)/shard_map/trc,tcj->rtj/dot_general | solution.py:101
  445.4 13.1 %fusion.38 = f32[32,128,128]{2,0,1:T(8,128)S(1)} fusion(f32[128,128,128]{2,1,0:T(8,128)S(1)} %bitcast.135, f32[4,128,8,128]{3,2,1,0:T(8,128)S(1)} %get-tuple-element.165), kind=kOutput, calls=%fused_computation.45 | convolution fusion | flops 805306368 | bytes 12582912 | tf_op jit(solution)/shard_map/rbj,bij->rbi/dot_general | solution.py:49
  466.6 4.0 slice_add_fusion.5
  475.3 6.1 scatter-add.40
  481.4 4.2 slice_add_fusion.2
  485.6 7.7 %scatter-add.41 = f32[32,128,128]{2,1,0:T(8,128)} dynamic-update-slice(f32[32,128,128]{2,1,0:T(8,128)} %scatter-add.40, f32[32,128,1]{2,1,0:T(8,128)} %slice_add_fusion.2, s32[]{:T(128)} %constant.303.clone.1, s32[]{:T(128)} %constant.303.clone.1, s32[]{:T(128)} %constant.314.clone.1) | dynamic-update-slice | bytes 32772 | tf_op jit(solution)/shard_map/scatter-add | solution.py:54
  493.3 15.7 %fusion.29 = f32[32,128,128]{2,0,1:T(8,128)S(1)} fusion(f32[128,128,128]{2,1,0:T(8,128)} %param.44, f32[32,128,128]{2,1,0:T(8,128)} %scatter-add.41), kind=kOutput, calls=%fused_computation.42 | convolution fusion | flops 805306368 | bytes 12582912 | tf_op jit(solution)/shard_map/rbj,bij->rbi/dot_general | solution.py:55
  516.5 3.9 slice_add_fusion.4
  525.1 6.3 scatter-add.44
  531.4 4.2 slice_add_fusion.1
  535.6 7.7 %scatter-add.45 = f32[32,128,128]{2,1,0:T(8,128)} dynamic-update-slice(f32[32,128,128]{2,1,0:T(8,128)} %scatter-add.44, f32[32,128,1]{2,1,0:T(8,128)} %slice_add_fusion.1, s32[]{:T(128)} %constant.303.clone.1, s32[]{:T(128)} %constant.303.clone.1, s32[]{:T(128)} %constant.314.clone.1) | dynamic-update-slice | bytes 32772 | tf_op jit(solution)/shard_map/scatter-add | solution.py:54
  543.2 15.7 %fusion.32 = f32[32,128,128]{2,0,1:T(8,128)S(1)} fusion(f32[128,128,128]{2,1,0:T(8,128)} %param.44, f32[32,128,128]{2,1,0:T(8,128)} %scatter-add.45), kind=kOutput, calls=%fused_computation.43 | convolution fusion | flops 805306368 | bytes 12582912 | tf_op jit(solution)/shard_map/rbj,bij->rbi/dot_general | solution.py:55
  566.4 3.9 slice_add_fusion.3
  570.3 6.1 scatter-add.46
  581.2 4.2 slice_add_fusion
  585.4 7.7 %scatter-add.49 = f32[32,128,128]{2,1,0:T(8,128)} dynamic-update-slice(f32[32,128,128]{2,1,0:T(8,128)} %scatter-add.46, f32[32,128,1]{2,1,0:T(8,128)} %slice_add_fusion, s32[]{:T(128)} %constant.303.clone.1, s32[]{:T(128)} %constant.303.clone.1, s32[]{:T(128)} %constant.314.clone.1) | dynamic-update-slice | bytes 32772 | tf_op jit(solution)/shard_map/scatter-add | solution.py:54
  593.0 16.7 %fusion.35 = f32[32,128,128]{2,0,1:T(8,128)} fusion(f32[128,128,128]{2,1,0:T(8,128)} %param.44, f32[32,128,128]{2,1,0:T(8,128)} %scatter-add.49), kind=kOutput, calls=%fused_computation.44 | convolution fusion | flops 805306368 | bytes 12582912 | tf_op jit(solution)/shard_map/rbj,bij->rbi/dot_general | solution.py:55
  609.7 8.4 %all-to-all-start = ((f32[32,128,128]{2,0,1:T(8,128)}), f32[32,128,128]{2,0,1:T(8,128)}, u32[]{:S(2)}, u32[]{:S(2)}) async-start(f32[32,128,128]{2,0,1:T(8,128)} %fusion.35), calls=%async_computation | async-start | bytes 4194304 | tf_op jit(solution)/shard_map/all_to_all | solution.py:110
  618.1 27.1 %all-to-all-done = f32[32,128,128]{2,0,1:T(8,128)} async-done(((f32[32,128,128]{2,0,1:T(8,128)}), f32[32,128,128]{2,0,1:T(8,128)}, u32[]{:S(2)}, u32[]{:S(2)}) %all-to-all-start) | async-done | bytes 2097184 | tf_op jit(solution)/shard_map/all_to_all | solution.py:110
  658.6 3.6 fusion.16
  668.1 3.6 fusion.71
  672.0 34.6 %all_to_all.30 = f32[128,32,128]{2,1,0:T(8,128)S(1)} all-to-all(f32[128,32,128]{2,1,0:T(8,128)S(1)} %bitcast.146), channel_id=1, replica_groups=mesh['band'=4,'wide'=32] {'band','wide'}, dimensions={0} | all-to-all | bytes 4194304 | tf_op jit(solution)/shard_map/all_to_all | solution.py:124
  (468 shorter events, 452.2 us)
Async XLA Ops:
  6.5 643.0 %copy-start = (f32[32,128,128]{2,1,0:T(8,128)S(1)}, f32[32,128,128]{2,1,0:T(8,128)}, u32[]{:S(2)}) copy-start(f32[32,128,128]{2,1,0:T(8,128)} %param.46) | copy-start | bytes 6291460
  6.5 422.5 %copy-start.8 = (f32[128]{0:T(128)S(1)}, f32[128]{0:T(128)}, u32[]{:S(2)}) copy-start(f32[128]{0:T(128)} %param.43) | copy-start | bytes 1540
  6.5 43.7 %all-gather.2.cloned.1.call-start = ((), (), s32[]{:S(2)}) async-start(), calls=%async_computation.2 | async-start | bytes 5283840 | tf_op jit(solution)/shard_map/all_gather | solution.py:95
  437.7 7.2 %slice-start = ((s8[8388608]{0:T(1024)(128)(4,1)}), s8[4194304]{0:T(1024)(128)(4,1)S(1)}, s32[]{:S(2)}) async-start(s8[8388608]{0:T(1024)(128)(4,1)} %bitcast.134), calls=%async_computation.3 | async-start | bytes 8388608
  441.1 4.3 slice-start.1
  441.5 2.1 copy-start.1
  609.7 8.4 %copy-start.7 = (f32[2,32]{1,0:T(2,128)S(1)}, f32[2,32]{1,0:T(2,128)}, u32[]{:S(2)}) copy-start(f32[2,32]{1,0:T(2,128)} %param.47) | copy-start | bytes 772
  609.7 35.5 %all-to-all-start = ((f32[32,128,128]{2,0,1:T(8,128)}), f32[32,128,128]{2,0,1:T(8,128)}, u32[]{:S(2)}, u32[]{:S(2)}) async-start(f32[32,128,128]{2,0,1:T(8,128)} %fusion.35), calls=%async_computation | async-start | bytes 4194304 | tf_op jit(solution)/shard_map/all_to_all | solution.py:110
  646.9 2.6 copy-start.2
  648.2 1.4 copy-start.3
  651.6 1.6 copy-start.6
  656.8 1.6 copy-start.5
  662.2 1.6 copy-start.4
Sparse Core Ops, SparseCore 0:
  9.0 41.1 all-gather.1
where the time goes:
time: 731 us; the launch traced here: 717 us
  local copies, waits for them, and re-layouts  478 us (65%)
  matrix products  82.6 us (11%)
  waiting for transfers between devices  65.9 us (9%)
  blocking collectives  34.6 us (5%)
  other arithmetic  33.5 us (5%)
  between operations  13.9 us (2%)
  starting transfers between devices  8.38 us (1%)
    gather x384, local copies, waits for them, and re-layouts  379 us
    dot_general x3, matrix products, sweep_rows(): state = jnp.einsum('rbj,bij->rbi', forced, inverse, precision=hp)  48.1 us
    all_gather x1, waiting for transfers between devices, body(): piece = lax.all_gather(panels, 'band', axis=0, tiled=True)  38.1 us
    all_to_all x1, blocking collectives, body(): lax.all_to_all(outgoing, ('band', 'wide'), split_axis=0, concat_axis=2, t...  34.6 us
    all_to_all x1, waiting for transfers between devices, body(): lax.all_to_all(east_west.reshape(rows, n_all, cols), ('band', 'wide'), sp...  27.1 us
    scatter-add x3, local copies, waits for them, and re-layouts, sweep_rows(): forced = forced.at[:, :, -1].add(couple[1][None, :] * right)  23 us
    scatter-add x3, local copies, waits for them, and re-layouts, sweep_rows(): forced = source.at[:, :, 0].add(couple[0][None, :] * left)  18.5 us
    slice x6, local copies, waits for them, and re-layouts, sweep_rows(): right = jnp.pad(state[:, 1:, 0], ((0, 0), (0, 1)))  16.2 us
  transfers between devices with their start and end apart: 2, of which 2 were waited for; matrix products, arithmetic and copies ran while one was open for 1% of the time, Pallas kernels for 0%

commit v1 on v0

v1 whole, which is shorter than its diff:
```python
import functools

import jax
import jax.numpy as jnp
from jax import lax
from jax.experimental import pallas as pl
from jax.experimental.pallas import tpu as pltpu
from jax.sharding import PartitionSpec as P

BLK = 128
TG = 8
GW = TG * BLK
HALO = 3
PAD = 8
SPLITS = (0, 16)
VMEM_LIMIT = 48 * 1024 * 1024


def cubic_terms(frac):
    f2 = frac * frac
    f3 = f2 * frac
    return [
        -0.5 * f3 + f2 - 0.5 * frac,
        1.5 * f3 - 2.5 * f2 + 1.0,
        -1.5 * f3 + 2.0 * f2 + 0.5 * frac,
        0.5 * f3 - 0.5 * f2,
    ]


def linear_terms(frac):
    zeros = jnp.zeros_like(frac)
    return [zeros, 1.0 - frac, frac, zeros]


def row_matrix(offsets, fracs, columns, terms):
    total = jnp.zeros((offsets.shape[0], columns.shape[0]), jnp.float32)
    for index, weight in enumerate(terms(fracs)):
        hit = (columns[None, :] == offsets[:, None] + index).astype(jnp.float32)
        total = total + weight[:, None] * hit
    return total.astype(jnp.bfloat16)


def column_tables(kind, shift, frac):
    tiles = frac.shape[0]
    delta = (
        jnp.arange(2 * BLK, dtype=jnp.int32)[:, None] - jnp.arange(BLK, dtype=jnp.int32)[None, :]
    )
    tap = delta[None] - shift[:, None, None]
    total = jnp.zeros((tiles, 2 * BLK, BLK), jnp.float32)
    for index, (wc, wl) in enumerate(zip(cubic_terms(frac), linear_terms(frac))):
        weight = jnp.where(kind == 1, wc, wl)
        total = jnp.where(tap == index, weight[:, None, None], total)
    return total.astype(jnp.bfloat16)


def table_hi_lo(value):
    hi = lax.reduce_precision(value, 8, 7)
    return hi.astype(jnp.bfloat16), (value - hi).astype(jnp.bfloat16)


def split_hi_lo(value):
    hi = value.astype(jnp.bfloat16)
    lo = (value - hi.astype(jnp.float32)).astype(jnp.bfloat16)
    return hi, lo


def rows_kernel(first, groups, finals, carried, *refs):
    kind_ref, coef_ref = refs[:2]
    refs = refs[2:]
    (p0, p1, p2, p3, q0, q1, q2, q3, w_ref, t_ref, mask_ref, bg_ref, inv_ref) = refs[:13]
    refs = refs[13:]
    a_ref, b_ref, yw_ref = refs[:3]
    refs = refs[3:]
    if carried:
        u_in, f_in, l_in = refs[:3]
        refs = refs[3:]
    out_ref, part_ref, u_out, f_out, l_out, sec, u_st, f_st, l_st = refs
    step = pl.program_id(0)
    s = step + first

    @pl.when(step == 0)
    def _():
        if carried:
            u_st[0] = u_in[...]
            f_st[...] = f_in[...]
            l_st[...] = l_in[...]
        else:
            u_st[...] = jnp.zeros_like(u_st)
            f_st[...] = jnp.zeros_like(f_st)
            l_st[...] = jnp.zeros_like(l_st)

    @pl.when(step > 0)
    def _():
        u_st[0] = u_st[1]

    for st in (f_st, l_st):
        for i in range(HALO + TG):
            st[i] = st[i + TG]

    @pl.when(s < groups)
    def _():
        rows = jnp.concatenate([p0[...], p1[...], p2[...], p3[...]], axis=0)
        edge = jnp.concatenate([q0[...], q1[...], q2[...], q3[...]], axis=0)
        w = w_ref[...]
        both = jnp.dot(w, rows, preferred_element_type=jnp.float32).astype(jnp.bfloat16)
        tail = jnp.dot(w, edge, preferred_element_type=jnp.float32).astype(jnp.bfloat16)
        for k in range(2):
            sec[k, :, :GW] = both[k * 32 : (k + 1) * 32]
            sec[k, :, GW:] = tail[k * 32 : (k + 1) * 32]
        for i in range(TG):
            kind = kind_ref[s * TG + i]
            cols = slice(i * BLK, (i + 1) * BLK)
            taken = sec[kind, :, i * BLK : (i + 2) * BLK]
            est = jnp.dot(taken, t_ref[i], preferred_element_type=jnp.float32)
            misfit = mask_ref[:, cols].astype(jnp.float32) * (est - bg_ref[:, cols])
            hi, lo = split_hi_lo(misfit)
            u = jnp.dot(
                jnp.concatenate([hi, lo], axis=0), inv_ref[i], preferred_element_type=jnp.float32
            )
            u = u[:32, :BLK] + (u[32:, :BLK] + u[:32, BLK:])
            u_st[1, i] = u
            f_st[HALO + TG + i] = jnp.broadcast_to(u[:, :1], u.shape)
            l_st[HALO + TG + i] = jnp.broadcast_to(u[:, BLK - 1 :], u.shape)

    @pl.when(s >= groups)
    def _():
        for i in range(TG):
            f_st[HALO + TG + i] = jnp.zeros((32, BLK), jnp.float32)
            l_st[HALO + TG + i] = jnp.zeros((32, BLK), jnp.float32)

    @pl.when(s - 1 >= finals)
    def _():
        base = (s - 1) * TG + PAD - HALO

        def advance(which, j, west, east):
            st, r = (f_st, 0) if which == "f" else (l_st, 2)
            return st[j] + coef_ref[r, base + j] * west + coef_ref[r + 1, base + j] * east

        l1 = {j: advance("l", j, l_st[j - 1], f_st[j + 1]) for j in range(1, HALO + TG)}
        f1 = {j: advance("f", j, l_st[j - 1], f_st[j + 1]) for j in range(HALO, HALO + TG + 2)}
        outs = []
        for i in range(TG):
            j = HALO + i
            west = advance("l", j - 1, l1[j - 2], f1[j])
            east = advance("f", j + 1, l1[j], f1[j + 2])
            value = u_st[0, i] + a_ref[i : i + 1, :] * west + b_ref[i : i + 1, :] * east
            value = value.astype(jnp.bfloat16)
            out_ref[:, i * BLK : (i + 1) * BLK] = value
            outs.append(value)
        ends = jnp.dot(
            yw_ref[...], jnp.concatenate(outs, axis=1), preferred_element_type=jnp.float32
        )
        part_ref[...] = ends[0:2] + ends[8:10]

    @pl.when(step == pl.num_programs(0) - 1)
    def _():
        u_out[...] = u_st[1]
        f_out[...] = f_st[...]
        l_out[...] = l_st[...]


def run_rows(first, stop, groups, state, kinds, coefs, own, got, w, tables, mask, bg, inv, a, b, yw):
    ends_here = stop == groups
    steps = stop - first + (1 if ends_here else 0)
    finals = 0 if first == 0 else first - 1
    n_final = (stop if ends_here else stop - 1) - finals
    carried = state is not None
    count = stop - first
    here = lambda l: jnp.minimum(l, count - 1)
    done = lambda l: jnp.clip(l + first - 1, finals, finals + n_final - 1)
    full = lambda *shape: pl.BlockSpec(shape, lambda l, *_: (0,) * len(shape))
    wide = lambda off: pl.BlockSpec((32, GW), lambda l, *_: (0, here(l) + off))
    edge = lambda off: pl.BlockSpec((32, BLK), lambda l, *_: (0, (here(l) + off + 1) * TG))
    in_specs = [wide(first), wide(0), wide(0), wide(0), edge(first), edge(0), edge(0), edge(0)]
    in_specs += [
        full(64, BLK),
        pl.BlockSpec((TG, 2 * BLK, BLK), lambda l, *_: (here(l) + first, 0, 0)),
        wide(first),
        wide(first),
        pl.BlockSpec((TG, BLK, 2 * BLK), lambda l, *_: (here(l) + first, 0, 0)),
        pl.BlockSpec((TG, BLK), lambda l, *_: (done(l), 0)),
        pl.BlockSpec((TG, BLK), lambda l, *_: (done(l), 0)),
        full(16, 32),
    ]
    keep = [
        jax.ShapeDtypeStruct((TG, 32, BLK), jnp.float32),
        jax.ShapeDtypeStruct((HALO + 2 * TG, 32, BLK), jnp.float32),
        jax.ShapeDtypeStruct((HALO + 2 * TG, 32, BLK), jnp.float32),
    ]
    operands = [kinds, coefs, own, *got, own, *got, w, tables, mask, bg, inv, a, b, yw]
    if carried:
        in_specs += [full(*k.shape) for k in keep]
        operands += list(state)
    grid_spec = pltpu.PrefetchScalarGridSpec(
        num_scalar_prefetch=2,
        grid=(steps,),
        in_specs=in_specs,
        out_specs=[
            pl.BlockSpec((32, GW), lambda l, *_: (0, done(l) - finals)),
            pl.BlockSpec((2, GW), lambda l, *_: (0, done(l) - finals)),
            *[full(*k.shape) for k in keep],
        ],
        scratch_shapes=[
            pltpu.VMEM((2, 32, GW + BLK), jnp.bfloat16),
            pltpu.VMEM((2, TG, 32, BLK), jnp.float32),
            pltpu.VMEM((HALO + 2 * TG, 32, BLK), jnp.float32),
            pltpu.VMEM((HALO + 2 * TG, 32, BLK), jnp.float32),
        ],
    )
    outs = pl.pallas_call(
        functools.partial(rows_kernel, first, groups, finals, carried),
        grid_spec=grid_spec,
        out_shape=[
            jax.ShapeDtypeStruct((32, n_final * GW), jnp.bfloat16),
            jax.ShapeDtypeStruct((2, n_final * GW), jnp.float32),
            *keep,
        ],
        compiler_params=pltpu.CompilerParams(vmem_limit_bytes=VMEM_LIMIT),
    )(*operands)
    return outs[0], outs[1], tuple(outs[2:])


def columns_kernel(w_ref, ends_ref, e0, e1, e2, e3, n0, n1, *rest):
    out_ref = rest[-1]
    rows = jnp.concatenate([e0[...], e1[...], e2[...], e3[...]], axis=0)
    both = jnp.dot(w_ref[...], rows, preferred_element_type=jnp.float32)
    forced = n0[...] + n1[...]
    value = both[:32] + both[32:]
    value = value + ends_ref[:, 0:1] * forced[0:1, :] + ends_ref[:, 1:2] * forced[1:2, :]
    out_ref[...] = value


def run_columns(start, width, total, w, ends, pieces, near, far, so_far):
    cw = GW
    steps = width // cw
    full = lambda *shape: pl.BlockSpec(shape, lambda l: (0,) * len(shape))
    part = lambda rows: pl.BlockSpec((rows, cw), lambda l: (0, l))
    operands = [w, ends, *pieces, near, far]
    in_specs = [full(64, BLK), full(32, 2), *[part(32)] * 4, part(2), part(2)]
    aliases = {}
    if so_far is not None:
        operands.append(so_far)
        in_specs.append(pl.BlockSpec(memory_space=pl.ANY))
        aliases = {8: 0}
    return pl.pallas_call(
        columns_kernel,
        grid=(steps,),
        in_specs=in_specs,
        out_specs=pl.BlockSpec((32, cw), lambda l: (0, l + start // cw)),
        out_shape=jax.ShapeDtypeStruct((32, total), jnp.float32),
        input_output_aliases=aliases,
        compiler_params=pltpu.CompilerParams(vmem_limit_bytes=VMEM_LIMIT),
    )(*operands)


def body(
    panels,
    void_mask,
    background,
    row_offset,
    row_frac,
    tile_kind,
    tile_shift,
    tile_frac,
    inverse_x,
    couple_x,
    inverse_y,
    couple_y,
):
    rows = row_offset.shape[0]
    width = background.shape[1]
    groups = width // GW
    n_wide = lax.axis_size("wide")
    mine = lax.axis_index("band")
    block = lax.axis_index("wide")
    across = [(d, d ^ 2) for d in range(4)]
    sibling = [(d, d ^ 1) for d in range(4)]
    swap = lambda value, pairs: lax.ppermute(value, "band", pairs)

    near = swap(panels, sibling)
    bounds = [(SPLITS[i], SPLITS[i + 1]) for i in range(len(SPLITS) - 1)]
    gathered = []
    for first, stop in bounds:
        cols = slice(first * GW, stop * GW + BLK)
        far = swap(panels[:, cols], across)
        gathered.append((near[:, cols], far, swap(far, sibling)))

    order = ((jnp.arange(4, dtype=jnp.int32) ^ mine)[:, None] * rows + jnp.arange(rows)[None, :]).reshape(-1)
    w = jnp.concatenate(
        [
            row_matrix(row_offset, row_frac, order, linear_terms),
            row_matrix(row_offset, row_frac, order, cubic_terms),
        ],
        axis=0,
    )
    kinds = (tile_kind == 1).astype(jnp.int32)
    tables = column_tables(tile_kind, tile_shift, tile_frac)
    inv_xt = jnp.concatenate(table_hi_lo(jnp.swapaxes(inverse_x, 1, 2)), axis=2)
    a_x = couple_x[0][:, None] * inverse_x[:, :, 0]
    b_x = couple_x[1][:, None] * inverse_x[:, :, -1]
    coefs = jnp.stack([a_x[:, 0], b_x[:, 0], a_x[:, -1], b_x[:, -1]])
    coefs = jnp.pad(coefs, ((0, 0), (PAD, 2 * PAD)))

    a_y = couple_y[0][:, None] * inverse_y[:, :, 0]
    b_y = couple_y[1][:, None] * inverse_y[:, :, -1]
    corner = jnp.pad(
        jnp.stack([a_y[:, 0], b_y[:, 0], a_y[:, -1], b_y[:, -1]]), ((0, 0), (HALO, HALO))
    )
    corner = lax.dynamic_slice_in_dim(corner, block, 2 * HALO + 1, 1)
    own_inv = lax.dynamic_index_in_dim(inverse_y, block, 0, keepdims=False)
    at = mine * rows
    own_rows = lax.dynamic_slice_in_dim(own_inv, at, rows, 0)
    shuffled = jnp.concatenate(
        [lax.dynamic_slice_in_dim(own_rows, (q ^ mine) * rows, rows, 1) for q in range(4)], axis=1
    )
    w_y = jnp.concatenate(table_hi_lo(shuffled), axis=0)
    ends_y = jnp.stack(
        [
            couple_y[0, block] * own_rows[:, 0],
            couple_y[1, block] * own_rows[:, -1],
        ],
        axis=1,
    )
    end_rows = lax.dynamic_slice_in_dim(jnp.stack([own_inv[0], own_inv[-1]]), at, rows, 1)
    end_hi, end_lo = table_hi_lo(end_rows)
    gap = jnp.zeros((6, rows), jnp.bfloat16)
    yw = jnp.concatenate([end_hi, gap, end_lo, gap], axis=0)

    def neighbour(value, k):
        pairs = [(i + k, i) for i in range(n_wide) if 0 <= i + k < n_wide]
        return lax.ppermute(value, "wide", pairs)

    state = None
    result = None
    position = 0
    for (first, stop), got in zip(bounds, gathered):
        got = (got[0], got[1], got[2])
        east_west, part, state = run_rows(
            first, stop, groups, state, kinds, coefs, panels, got, w, tables,
            void_mask, background, inv_xt, a_x, b_x, yw,
        )
        far = swap(east_west, across)
        close = swap(east_west, sibling)
        f, l = {0: part[0:1]}, {0: part[1:2]}
        for k in (-1, 1):
            pair = neighbour(part, k)
            f[k], l[k] = pair[0:1], pair[1:2]
        for k in (2, 3):
            l[-k] = neighbour(part[1:2], -k)
            f[k] = neighbour(part[0:1], k)
        af, cf, al, cl = [{k: corner[r, HALO + k] for k in range(-HALO, HALO + 1)} for r in range(4)]
        l_m2 = l[-2] + al[-2] * l[-3] + cl[-2] * f[-1]
        f_0 = f[0] + af[0] * l[-1] + cf[0] * f[1]
        l_0 = l[0] + al[0] * l[-1] + cl[0] * f[1]
        f_p2 = f[2] + af[2] * l[1] + cf[2] * f[3]
        south = l[-1] + al[-1] * l_m2 + cl[-1] * f_0
        north = f[1] + af[1] * l_0 + cf[1] * f_p2
        forced = jnp.concatenate([south, north], axis=0)
        forced = forced + swap(forced, across)
        other = swap(forced, sibling)
        pieces = (east_west, close, far, swap(far, sibling))
        result = run_columns(
            position, east_west.shape[1], width, w_y, ends_y, pieces, forced, other, result
        )
        position += east_west.shape[1]
    return result


def solution(mesh):
    placed = (
        P(("wide", "band"), None),
        P(("wide", "band"), None),
        P(("wide", "band"), None),
        P(("wide", "band")),
        P(("wide", "band")),
        P(),
        P(),
        P(),
        P(),
        P(),
        P(),
        P(),
    )
    return jax.shard_map(
        body, mesh=mesh, in_specs=placed, out_specs=P(("wide", "band"), None), check_vma=False
    )
```

time: 731 us -> 175 us (0.24); the launches traced: 717 us -> 173 us
  local copies, waits for them, and re-layouts: 478 us -> 48 us
  matrix products: 82.6 us -> 0 us
  waiting for transfers between devices: 65.9 us -> 17.1 us
  blocking collectives: 34.6 us -> 0 us
  Pallas kernels: 0 us -> 32.8 us
  starting transfers between devices: 8.38 us -> 36.6 us
  between operations: 13.9 us -> 0.27 us
    gather x384 -> x0, local copies, waits for them, and re-layouts: 379 us -> none
    dot_general x9 -> x0, matrix products: 82.6 us -> none  [the longest x3 48.1 us: sweep_rows(): state = jnp.einsum('rbj,bij->rbi', forced, inverse, precision=hp)]
    scatter-add x8 -> x0, local copies, waits for them, and re-layouts: 44.8 us -> none  [the longest x3 23 us: sweep_rows(): forced = forced.at[:, :, -1].add(couple[1][None, :] * right)]
    all_gather x1 -> x0, waiting for transfers between devices: 38.1 us -> none  [body(): piece = lax.all_gather(panels, 'band', axis=0, tiled=True)]
    ppermute x0 -> x14, starting transfers between devices: none -> 36.6 us  [the longest x6 19.9 us: neighbour(): return lax.ppermute(value, 'wide', pairs)]
    all_to_all x1 -> x0, blocking collectives: 34.6 us -> none  [body(): lax.all_to_all(outgoing, ('band', 'wide'), split_axis=0, concat_axis=2, t...]
    pallas_call x0 -> x2, Pallas kernels: none -> 32.8 us  [the longest x1 22.7 us: run_rows(): pl.pallas_call(functools.partial(rows_kernel, first, groups, finals, carr...]
    all_to_all x1 -> x0, waiting for transfers between devices: 27.1 us -> none  [body(): lax.all_to_all(east_west.reshape(rows, n_all, cols), ('band', 'wide'), sp...]
  transfers between devices with their start and end apart: 2 -> 14, of which waited for: 2 -> 5; matrix products, arithmetic and copies ran while one was open for 1% -> 47% of each run, Pallas kernels for 0% -> 0%
where the time goes in v1:
time: 175 us; the launch traced here: 173 us
  local copies, waits for them, and re-layouts  48 us (27%)
  other arithmetic  38.7 us (22%)
  starting transfers between devices  36.6 us (21%)
  Pallas kernels  32.8 us (19%)
  waiting for transfers between devices  17.1 us (10%)
    unnamed x23, local copies, waits for them, and re-layouts  24.9 us
    pallas_call x1, Pallas kernels, run_rows(): pl.pallas_call(functools.partial(rows_kernel, first, groups, finals, carr...  22.7 us
    ppermute x6, starting transfers between devices, neighbour(): return lax.ppermute(value, 'wide', pairs)  19.9 us
    ppermute x8, starting transfers between devices, body(): swap = lambda value, pairs: lax.ppermute(value, 'band', pairs)  16.7 us
    slice x1, local copies, waits for them, and re-layouts, body(): a_x = couple_x[0][:, None] * inverse_x[:, :, 0]  13.3 us
    ppermute x8, waiting for transfers between devices, body(): swap = lambda value, pairs: lax.ppermute(value, 'band', pairs)  11.2 us
    pallas_call x1, Pallas kernels, run_columns(): pl.pallas_call(columns_kernel, grid=(steps,), in_specs=in_specs, out_spec...  10.2 us
    convert_element_type x1, other arithmetic, column_tables(): return total.astype(jnp.bfloat16)  9.28 us
  transfers between devices with their start and end apart: 14, of which 5 were waited for; matrix products, arithmetic and copies ran while one was open for 47% of the time, Pallas kernels for 0%

profile of v1, /device:TPU:25, one launch (start us, length us, event | category | flops | bytes accessed | tf_op | source)
XLA Modules:
  0.0 173.5 jit_solution(8137905972546639071)
XLA Ops:
  0.0 2.7 %collective-permute-start.1 = (bf16[32,16512]{1,0:T(8,128)(2,1)}, bf16[32,16512]{1,0:T(8,128)(2,1)S(1)}, u32[]{:S(2)}, u32[]{:S(2)}) collective-permute-start(bf16[32,16512]{1,0:T(8,128)(2,1)} %refs_6_.1), channel_id=1, source_target_pairs={{0,64},{32,96},{64,0},{96,32},{1,65},{33,97},{65,1},{97,33},{2,66}... | collective-permute-start | bytes 3170312 | tf_op jit(solution)/shard_map/ppermute | solution.py:278
  5.1 13.3 %fusion.18 = (f32[128,128,1]{2,1,0:T(8,128)}, f32[128,128,1]{2,1,0:T(8,128)}) fusion(f32[128,128,128]{2,1,0:T(8,128)} %param.20), kind=kLoop, calls=%fused_computation.102 | loop fusion | bytes 262144 | tf_op jit(solution)/shard_map/slice | solution.py:299
  18.4 5.2 %copy.28 = f32[128,128,1]{1,0,2:T(8,128)S(1)} copy(f32[128,128,1]{2,1,0:T(8,128)} %get-tuple-element.21) | data formatting | bytes 131072
  23.6 5.2 %copy.29 = f32[128,128,1]{1,0,2:T(8,128)S(1)} copy(f32[128,128,1]{2,1,0:T(8,128)} %get-tuple-element.22) | data formatting | bytes 131072
  29.4 4.9 %fusion.19 = (f32[32,128,1]{2,1,0:T(8,128)}, f32[32,128,1]{2,1,0:T(8,128)}) fusion(f32[32,128,128]{2,1,0:T(8,128)} %param.22), kind=kLoop, calls=%fused_computation.103 | loop fusion | bytes 65536 | tf_op jit(solution)/shard_map/slice | solution.py:304
  34.3 2.2 %copy.30 = f32[32,128,1]{1,0,2:T(8,128)S(1)} copy(f32[32,128,1]{2,1,0:T(8,128)} %get-tuple-element.23) | data formatting | bytes 32768
  36.5 2.2 %copy.31 = f32[32,128,1]{1,0,2:T(8,128)S(1)} copy(f32[32,128,1]{2,1,0:T(8,128)} %get-tuple-element.24) | data formatting | bytes 32768
  40.1 9.3 %select_convert_fusion.refs_11_ = bf16[128,256,128]{2,1,0:T(8,128)(2,1)} fusion(bf16[128]{0:T(256)(128)(2,1)S(1)} %get-tuple-element.54, bf16[128]{0:T(256)(128)(2,1)S(1)} %get-tuple-element.55, bf16[128]{0:T(256)(128)(2,1)S(1)} %get-tuple-element.56, bf16[128]{0:T(256)(128)(2,1)S(1)} %get-tuple-element.53, s32[128]{0:T(128)S(1)} %copy-done.6, ...), kind=kLoop, calls=%fused_computation.4 | loop fusion | flops 37748736 | bytes 8521216 | tf_op jit(solution)/shard_map/convert_element_type | solution.py:53
  49.5 9.0 %copy.24 = f32[128,128,128]{1,2,0:T(8,128)} copy(f32[128,128,128]{2,1,0:T(8,128)} %param.20) | data formatting | bytes 16777216 | tf_op args[8]
  59.9 9.1 %reduce-precision_convert_fusion = (bf16[128,128,128]{2,1,0:T(8,128)(2,1)}, bf16[128,128,128]{2,1,0:T(8,128)(2,1)}) fusion(f32[128,128,128]{1,2,0:T(8,128)} %copy.24), kind=kLoop, calls=%fused_computation.6 | loop fusion | flops 8388608 | bytes 16777216 | tf_op jit(solution)/shard_map/convert_element_type | solution.py:58
  69.0 8.6 %pad_maximum_fusion.refs_14_ = bf16[128,128,256]{2,1,0:T(8,128)(2,1)} fusion(bf16[128,128,128]{2,1,0:T(8,128)(2,1)} %get-tuple-element.20, bf16[128,128,128]{2,1,0:T(8,128)(2,1)} %get-tuple-element.19), kind=kLoop, calls=%fused_computation.8 | loop fusion | flops 16777216 | bytes 16777216 | tf_op jit(solution)/shard_map/concatenate | solution.py:298
  78.5 22.7 %shard_map.118 = (bf16[32,16384]{1,0:T(8,128)(2,1)S(1)}, f32[2,16384]{1,0:T(2,128)S(1)}, f32[8,32,128]{2,1,0:T(8,128)}, f32[19,32,128]{2,1,0:T(8,128)}, f32[19,32,128]{2,1,0:T(8,128)}) custom-call(s32[128]{0:T(128)S(1)} %fusion.16.refs_0_, f32[4,152]{1,0:T(4,128)S(1)} %select_maximum_fusion.refs_1_, bf16[32,16512]{1,0:T(8,128)(2,1)S(1)} %copy-done, ...), custom_call_target="tpu_custom_call" | custom-call | tf_op jit(solution)/shard_map/pallas_call | solution.py:210
  101.2 2.2 %collective-permute-start.6 = (f32[2,16384]{1,0:T(2,128)S(1)}, f32[2,16384]{1,0:T(2,128)S(1)}, u32[]{:S(2)}, u32[]{:S(2)}) collective-permute-start(f32[2,16384]{1,0:T(2,128)S(1)} %get-tuple-element.8), channel_id=1, source_target_pairs={{0,1},{1,2},{2,3},{3,4},{4,5},{5,6},{6,7},{7,8},{8,9},{9,10},{10,1... | collective-permute-start | bytes 393224 | tf_op jit(solution)/shard_map/ppermute | solution.py:331
  103.4 6.3 %collective-permute-start.9 = (f32[2,16384]{1,0:T(2,128)S(1)}, f32[2,16384]{1,0:T(2,128)S(1)}, u32[]{:S(2)}, u32[]{:S(2)}) collective-permute-start(f32[2,16384]{1,0:T(2,128)S(1)} %get-tuple-element.8), channel_id=1, source_target_pairs={{1,0},{2,1},{3,2},{4,3},{5,4},{6,5},{7,6},{8,7},{9,8},{10,9},{11,1... | collective-permute-start | bytes 393224 | tf_op jit(solution)/shard_map/ppermute | solution.py:331
  109.8 1.9 %collective-permute-start.7 = (f32[1,16384]{1,0:T(1,128)S(1)}, f32[1,16384]{1,0:T(1,128)S(1)}, u32[]{:S(2)}, u32[]{:S(2)}) collective-permute-start(f32[1,16384]{1,0:T(1,128)S(1)} %slice.148), channel_id=1, source_target_pairs={{0,2},{1,3},{2,4},{3,5},{4,6},{5,7},{6,8},{7,9},{8,10},{9,11},{10,... | collective-permute-start | bytes 196616 | tf_op jit(solution)/shard_map/ppermute | solution.py:331
  111.7 3.0 %collective-permute-start.8 = (f32[1,16384]{1,0:T(1,128)S(1)}, f32[1,16384]{1,0:T(1,128)S(1)}, u32[]{:S(2)}, u32[]{:S(2)}) collective-permute-start(f32[1,16384]{1,0:T(1,128)S(1)} %slice.148), channel_id=1, source_target_pairs={{0,3},{1,4},{2,5},{3,6},{4,7},{5,8},{6,9},{7,10},{8,11},{9,12},{10... | collective-permute-start | bytes 196616 | tf_op jit(solution)/shard_map/ppermute | solution.py:331
  116.9 3.1 %collective-permute-done.8 = f32[1,16384]{1,0:T(1,128)S(1)} collective-permute-done((f32[1,16384]{1,0:T(1,128)S(1)}, f32[1,16384]{1,0:T(1,128)S(1)}, u32[]{:S(2)}, u32[]{:S(2)}) %collective-permute-start.8) | collective-permute-done | bytes 65568 | tf_op jit(solution)/shard_map/ppermute | solution.py:331
  120.1 4.0 %multiply_add_fusion.1 = (f32[1,16384]{1,0:T(1,128)S(1)}, f32[1,16384]{1,0:T(1,128)S(1)}) fusion(f32[2,16384]{1,0:T(2,128)S(1)} %collective-permute-done.6, f32[1,16384]{1,0:T(1,128)S(1)} %collective-permute-done.7, f32[1,16384]{1,0:T(1,128)S(1)} %collective-permute-done.8, f32[2,16384]{1,0:T(2,128)S(1)} %collective-permute-done.9, f32[]{:T(128)} %bitcast.23, ...), kind=kLoop, calls=%fused_computation.23 | loop fusion | flops 196608 | bytes 524312 | tf_op jit(solution)/shard_map/add | solution.py:356
  124.1 4.6 %collective-permute-start.10 = (f32[1,16384]{1,0:T(1,128)S(1)}, f32[1,16384]{1,0:T(1,128)S(1)}, u32[]{:S(2)}, u32[]{:S(2)}) collective-permute-start(f32[1,16384]{1,0:T(1,128)S(1)} %get-tuple-element.32), channel_id=1, source_target_pairs={{2,0},{3,1},{4,2},{5,3},{6,4},{7,5},{8,6},{9,7},{10,8},{11,9},{12,... | collective-permute-start | bytes 196616 | tf_op jit(solution)/shard_map/ppermute | solution.py:331
  134.6 4.2 %multiply_add_fusion = f32[1,16384]{1,0:T(1,128)S(1)} fusion(f32[1,16384]{1,0:T(1,128)S(1)} %collective-permute-done.11, f32[1,16384]{1,0:T(1,128)S(1)} %collective-permute-done.10, f32[2,16384]{1,0:T(2,128)S(1)} %collective-permute-done.9, f32[2,16384]{1,0:T(2,128)S(1)} %collective-permute-done.6, f32[]{:T(128)} %bitcast.29, f32[]{:T(128)} %bitcast.28, ...), kind=kLoop, calls=%fused_computation.22 | loop fusion | flops 196608 | bytes 458776 | tf_op jit(solution)/shard_map/add | solution.py:357
  141.5 4.0 %collective-permute-start.3 = (bf16[32,16384]{1,0:T(8,128)(2,1)S(1)}, bf16[32,16384]{1,0:T(8,128)(2,1)S(1)}, u32[]{:S(2)}, u32[]{:S(2)}) collective-permute-start(bf16[32,16384]{1,0:T(8,128)(2,1)S(1)} %get-tuple-element.7.e0), channel_id=1, source_target_pairs={{0,32},{32,0},{64,96},{96,64},{1,33},{33,1},{65,97},{97,65},{2,34}... | collective-permute-start | bytes 3145736 | tf_op jit(solution)/shard_map/ppermute | solution.py:278
  145.5 10.3 %collective-permute-done.4.e2 = bf16[32,16384]{1,0:T(8,128)(2,1)S(1)} collective-permute-done((bf16[32,16384]{1,0:T(8,128)(2,1)S(1)}, bf16[32,16384]{1,0:T(8,128)(2,1)S(1)}, u32[]{:S(2)}, u32[]{:S(2)}) %collective-permute-start.4) | collective-permute-done | bytes 1048608 | tf_op jit(solution)/shard_map/ppermute | solution.py:278
  155.7 4.9 %collective-permute-start.5 = (bf16[32,16384]{1,0:T(8,128)(2,1)S(1)}, bf16[32,16384]{1,0:T(8,128)(2,1)}, u32[]{:S(2)}, u32[]{:S(2)}) collective-permute-start(bf16[32,16384]{1,0:T(8,128)(2,1)S(1)} %collective-permute-done.4.e2), channel_id=1, source_target_pairs={{0,32},{32,0},{64,96},{96,64},{1,33},{33,1},{65,97},{97,65},{2,34}... | collective-permute-start | bytes 3145736 | tf_op jit(solution)/shard_map/ppermute | solution.py:278
  163.3 10.2 %shard_map.119 = f32[32,16384]{1,0:T(8,128)} custom-call(bf16[64,128]{1,0:T(8,128)(2,1)S(1)} %pad_maximum_fusion.3.w_ref, f32[32,2]{1,0:T(8,128)S(1)} %copy.27.ends_ref, bf16[32,16384]{1,0:T(8,128)(2,1)S(1)} %get-tuple-element.7.e0, bf16[32,16384]{1,0:T(8,128)(2,1)S(1)} %collective-permute-done.3.e1, bf16[32,16384]{1,0:T(8,128)(2,1)S(1)} %collective-permute-done.4.e2, ...), custom_call_target="tpu_custom_call" | custom-call | tf_op jit(solution)/shard_map/pallas_call | solution.py:245
  (76 shorter events, 20.2 us)
Async XLA Ops:
  0.0 59.8 %collective-permute-start.1 = (bf16[32,16512]{1,0:T(8,128)(2,1)}, bf16[32,16512]{1,0:T(8,128)(2,1)S(1)}, u32[]{:S(2)}, u32[]{:S(2)}) collective-permute-start(bf16[32,16512]{1,0:T(8,128)(2,1)} %refs_6_.1), channel_id=1, source_target_pairs={{0,64},{32,96},{64,0},{96,32},{1,65},{33,97},{65,1},{97,33},{2,66}... | collective-permute-start | bytes 3170312 | tf_op jit(solution)/shard_map/ppermute | solution.py:278
  2.7 74.8 %collective-permute-start = (bf16[32,16512]{1,0:T(8,128)(2,1)}, bf16[32,16512]{1,0:T(8,128)(2,1)S(1)}, u32[]{:S(2)}, u32[]{:S(2)}) collective-permute-start(bf16[32,16512]{1,0:T(8,128)(2,1)} %refs_6_.1), channel_id=1, source_target_pairs={{0,32},{32,0},{64,96},{96,64},{1,33},{33,1},{65,97},{97,65},{2,34}... | collective-permute-start | bytes 3170312 | tf_op jit(solution)/shard_map/ppermute | solution.py:278
  18.4 10.4 %copy-start.5 = (f32[2,128]{1,0:T(2,128)S(1)}, f32[2,128]{1,0:T(2,128)}, u32[]{:S(2)}) copy-start(f32[2,128]{1,0:T(2,128)} %param.21) | copy-start | bytes 3076
  28.8 9.9 %copy-start.2 = (f32[2,32]{1,0:T(2,128)S(1)}, f32[2,32]{1,0:T(2,128)}, u32[]{:S(2)}) copy-start(f32[2,32]{1,0:T(2,128)} %param.23) | copy-start | bytes 772
  28.8 11.1 %copy-start.7 = (f32[128]{0:T(128)S(1)}, f32[128]{0:T(128)}, u32[]{:S(2)}) copy-start(f32[128]{0:T(128)} %param.19) | copy-start | bytes 1540
  28.9 11.1 %copy-start.8 = (s32[128]{0:T(128)S(1)}, s32[128]{0:T(128)}, u32[]{:S(2)}) copy-start(s32[128]{0:T(128)} %param.17) | copy-start | bytes 1540
  28.9 11.2 %copy-start.6 = (s32[128]{0:T(128)S(1)}, s32[128]{0:T(128)}, u32[]{:S(2)}) copy-start(s32[128]{0:T(128)} %param.18) | copy-start | bytes 1540
  49.5 9.1 %copy-start.3 = (f32[32]{0:T(128)S(1)}, f32[32]{0:T(128)}, u32[]{:S(2)}) copy-start(f32[32]{0:T(128)} %param.16) | copy-start | bytes 388
  49.5 9.1 %copy-start.4 = (s32[32]{0:T(128)S(1)}, s32[32]{0:T(128)}, u32[]{:S(2)}) copy-start(s32[32]{0:T(128)} %param.15) | copy-start | bytes 388
  59.8 17.7 %collective-permute-start.2 = (bf16[32,16512]{1,0:T(8,128)(2,1)S(1)}, bf16[32,16512]{1,0:T(8,128)(2,1)S(1)}, u32[]{:S(2)}, u32[]{:S(2)}) collective-permute-start(bf16[32,16512]{1,0:T(8,128)(2,1)S(1)} %collective-permute-done.1.refs_4_.refs_8_), channel_id=1, source_target_pairs={{0,32},{32,0},{64,96},{96,64},{1,33},{33,1},{65,97},{97,65},{2,34}... | collective-permute-start | bytes 3170312 | tf_op jit(solution)/shard_map/ppermute | solution.py:278
  69.0 9.6 %copy-start = (bf16[32,16512]{1,0:T(8,128)(2,1)S(1)}, bf16[32,16512]{1,0:T(8,128)(2,1)}, u32[]{:S(2)}) copy-start(bf16[32,16512]{1,0:T(8,128)(2,1)} %refs_6_.1) | copy-start | bytes 3170308
  77.5 1.0 copy-start.1
  101.2 18.9 %collective-permute-start.6 = (f32[2,16384]{1,0:T(2,128)S(1)}, f32[2,16384]{1,0:T(2,128)S(1)}, u32[]{:S(2)}, u32[]{:S(2)}) collective-permute-start(f32[2,16384]{1,0:T(2,128)S(1)} %get-tuple-element.8), channel_id=1, source_target_pairs={{0,1},{1,2},{2,3},{3,4},{4,5},{5,6},{6,7},{7,8},{8,9},{9,10},{10,1... | collective-permute-start | bytes 393224 | tf_op jit(solution)/shard_map/ppermute | solution.py:331
  103.4 16.7 %collective-permute-start.9 = (f32[2,16384]{1,0:T(2,128)S(1)}, f32[2,16384]{1,0:T(2,128)S(1)}, u32[]{:S(2)}, u32[]{:S(2)}) collective-permute-start(f32[2,16384]{1,0:T(2,128)S(1)} %get-tuple-element.8), channel_id=1, source_target_pairs={{1,0},{2,1},{3,2},{4,3},{5,4},{6,5},{7,6},{8,7},{9,8},{10,9},{11,1... | collective-permute-start | bytes 393224 | tf_op jit(solution)/shard_map/ppermute | solution.py:331
  109.8 7.1 %collective-permute-start.7 = (f32[1,16384]{1,0:T(1,128)S(1)}, f32[1,16384]{1,0:T(1,128)S(1)}, u32[]{:S(2)}, u32[]{:S(2)}) collective-permute-start(f32[1,16384]{1,0:T(1,128)S(1)} %slice.148), channel_id=1, source_target_pairs={{0,2},{1,3},{2,4},{3,5},{4,6},{5,7},{6,8},{7,9},{8,10},{9,11},{10,... | collective-permute-start | bytes 196616 | tf_op jit(solution)/shard_map/ppermute | solution.py:331
  111.7 8.3 %collective-permute-start.8 = (f32[1,16384]{1,0:T(1,128)S(1)}, f32[1,16384]{1,0:T(1,128)S(1)}, u32[]{:S(2)}, u32[]{:S(2)}) collective-permute-start(f32[1,16384]{1,0:T(1,128)S(1)} %slice.148), channel_id=1, source_target_pairs={{0,3},{1,4},{2,5},{3,6},{4,7},{5,8},{6,9},{7,10},{8,11},{9,12},{10... | collective-permute-start | bytes 196616 | tf_op jit(solution)/shard_map/ppermute | solution.py:331
  124.1 9.2 %collective-permute-start.10 = (f32[1,16384]{1,0:T(1,128)S(1)}, f32[1,16384]{1,0:T(1,128)S(1)}, u32[]{:S(2)}, u32[]{:S(2)}) collective-permute-start(f32[1,16384]{1,0:T(1,128)S(1)} %get-tuple-element.32), channel_id=1, source_target_pairs={{2,0},{3,1},{4,2},{5,3},{6,4},{7,5},{8,6},{9,7},{10,8},{11,9},{12,... | collective-permute-start | bytes 196616 | tf_op jit(solution)/shard_map/ppermute | solution.py:331
  128.7 5.9 %collective-permute-start.11 = (f32[1,16384]{1,0:T(1,128)S(1)}, f32[1,16384]{1,0:T(1,128)S(1)}, u32[]{:S(2)}, u32[]{:S(2)}) collective-permute-start(f32[1,16384]{1,0:T(1,128)S(1)} %get-tuple-element.32), channel_id=1, source_target_pairs={{3,0},{4,1},{5,2},{6,3},{7,4},{8,5},{9,6},{10,7},{11,8},{12,9},{13... | collective-permute-start | bytes 196616 | tf_op jit(solution)/shard_map/ppermute | solution.py:331
  132.1 23.7 %collective-permute-start.4 = (bf16[32,16384]{1,0:T(8,128)(2,1)S(1)}, bf16[32,16384]{1,0:T(8,128)(2,1)S(1)}, u32[]{:S(2)}, u32[]{:S(2)}) collective-permute-start(bf16[32,16384]{1,0:T(8,128)(2,1)S(1)} %get-tuple-element.7.e0), channel_id=1, source_target_pairs={{0,64},{32,96},{64,0},{96,32},{1,65},{33,97},{65,1},{97,33},{2,66}... | collective-permute-start | bytes 3145736 | tf_op jit(solution)/shard_map/ppermute | solution.py:278
  138.9 21.8 %collective-permute-start.12 = (f32[2,16384]{1,0:T(2,128)S(1)}, f32[2,16384]{1,0:T(2,128)S(1)}, u32[]{:S(2)}, u32[]{:S(2)}) collective-permute-start(f32[2,16384]{1,0:T(2,128)S(1)} %pad_maximum_fusion.1), channel_id=1, source_target_pairs={{0,64},{32,96},{64,0},{96,32},{1,65},{33,97},{65,1},{97,33},{2,66}... | collective-permute-start | bytes 393224 | tf_op jit(solution)/shard_map/ppermute | solution.py:278
  141.5 21.8 %collective-permute-start.3 = (bf16[32,16384]{1,0:T(8,128)(2,1)S(1)}, bf16[32,16384]{1,0:T(8,128)(2,1)S(1)}, u32[]{:S(2)}, u32[]{:S(2)}) collective-permute-start(bf16[32,16384]{1,0:T(8,128)(2,1)S(1)} %get-tuple-element.7.e0), channel_id=1, source_target_pairs={{0,32},{32,0},{64,96},{96,64},{1,33},{33,1},{65,97},{97,65},{2,34}... | collective-permute-start | bytes 3145736 | tf_op jit(solution)/shard_map/ppermute | solution.py:278
  155.7 7.6 %collective-permute-start.5 = (bf16[32,16384]{1,0:T(8,128)(2,1)S(1)}, bf16[32,16384]{1,0:T(8,128)(2,1)}, u32[]{:S(2)}, u32[]{:S(2)}) collective-permute-start(bf16[32,16384]{1,0:T(8,128)(2,1)S(1)} %collective-permute-done.4.e2), channel_id=1, source_target_pairs={{0,32},{32,0},{64,96},{96,64},{1,33},{33,1},{65,97},{97,65},{2,34}... | collective-permute-start | bytes 3145736 | tf_op jit(solution)/shard_map/ppermute | solution.py:278
  160.8 2.5 %collective-permute-start.13 = (f32[2,16384]{1,0:T(2,128)S(1)}, f32[2,16384]{1,0:T(2,128)S(1)}, u32[]{:S(2)}, u32[]{:S(2)}) collective-permute-start(f32[2,16384]{1,0:T(2,128)S(1)} %fusion.17.n0), channel_id=1, source_target_pairs={{0,32},{32,0},{64,96},{96,64},{1,33},{33,1},{65,97},{97,65},{2,34}... | collective-permute-start | bytes 393224 | tf_op jit(solution)/shard_map/ppermute | solution.py:278

commit v2 on v1

--- a/solution.py
+++ b/solution.py
@@ -12,6 +12,7 @@
 GW = TG * BLK
 HALO = 3
 PAD = 8
+CW = 2048
 SPLITS = (0, 16)
 VMEM_LIMIT = 48 * 1024 * 1024
 
@@ -40,17 +41,52 @@
     return total.astype(jnp.bfloat16)
 
 
-def column_tables(kind, shift, frac):
-    tiles = frac.shape[0]
-    delta = (
-        jnp.arange(2 * BLK, dtype=jnp.int32)[:, None] - jnp.arange(BLK, dtype=jnp.int32)[None, :]
-    )
-    tap = delta[None] - shift[:, None, None]
-    total = jnp.zeros((tiles, 2 * BLK, BLK), jnp.float32)
-    for index, (wc, wl) in enumerate(zip(cubic_terms(frac), linear_terms(frac))):
-        weight = jnp.where(kind == 1, wc, wl)
-        total = jnp.where(tap == index, weight[:, None, None], total)
-    return total.astype(jnp.bfloat16)
+def tap_weights(kind, frac):
+    taps = [
+        jnp.where(kind == 1, wc, wl)
+        for wc, wl in zip(cubic_terms(frac), linear_terms(frac))
+    ]
+    return lax.reduce_precision(jnp.stack(taps), 8, 7)
+
+
+def tables_kernel(shift_ref, tap_ref, couple_ref, inv_ref, t_ref, pair_ref, a_ref, b_ref):
+    step = pl.program_id(0)
+    shape = (2 * BLK, BLK)
+    delta = lax.broadcasted_iota(jnp.int32, shape, 0) - lax.broadcasted_iota(jnp.int32, shape, 1)
+    for i in range(TG):
+        tile = step * TG + i
+        tap = delta - shift_ref[tile]
+        total = jnp.zeros(shape, jnp.float32)
+        for k in range(4):
+            total = jnp.where(tap == k, tap_ref[k, tile], total)
+        t_ref[i] = total.astype(jnp.bfloat16)
+        turned = inv_ref[i].T
+        hi, lo = split_hi_lo(turned)
+        pair_ref[i, :, :BLK] = hi
+        pair_ref[i, :, BLK:] = lo
+        a_ref[i : i + 1, :] = couple_ref[0, tile] * turned[0:1, :]
+        b_ref[i : i + 1, :] = couple_ref[1, tile] * turned[BLK - 1 :, :]
+
+
+def run_tables(shift, taps, couple, inverse):
+    tiles = inverse.shape[0]
+    cube = lambda *shape: pl.BlockSpec((TG, *shape), lambda l, *_: (l,) + (0,) * len(shape))
+    return pl.pallas_call(
+        tables_kernel,
+        grid_spec=pltpu.PrefetchScalarGridSpec(
+            num_scalar_prefetch=3,
+            grid=(tiles // TG,),
+            in_specs=[cube(BLK, BLK)],
+            out_specs=[cube(2 * BLK, BLK), cube(BLK, 2 * BLK), cube(BLK), cube(BLK)],
+        ),
+        out_shape=[
+            jax.ShapeDtypeStruct((tiles, 2 * BLK, BLK), jnp.bfloat16),
+            jax.ShapeDtypeStruct((tiles, BLK, 2 * BLK), jnp.bfloat16),
+            jax.ShapeDtypeStruct((tiles, BLK), jnp.float32),
+            jax.ShapeDtypeStruct((tiles, BLK), jnp.float32),
+        ],
+        compiler_params=pltpu.CompilerParams(vmem_limit_bytes=VMEM_LIMIT),
+    )(shift, taps, couple, inverse)
 
 
 def table_hi_lo(value):
@@ -107,17 +143,21 @@
         for k in range(2):
             sec[k, :, :GW] = both[k * 32 : (k + 1) * 32]
             sec[k, :, GW:] = tail[k * 32 : (k + 1) * 32]
+        ests = []
         for i in range(TG):
             kind = kind_ref[s * TG + i]
+            taken = sec[kind, :, i * BLK : (i + 2) * BLK]
+            ests.append(jnp.dot(taken, t_ref[i], preferred_element_type=jnp.float32))
+        sides = []
+        for i in range(TG):
             cols = slice(i * BLK, (i + 1) * BLK)
-            taken = sec[kind, :, i * BLK : (i + 2) * BLK]
-            est = jnp.dot(taken, t_ref[i], preferred_element_type=jnp.float32)
-            misfit = mask_ref[:, cols].astype(jnp.float32) * (est - bg_ref[:, cols])
-            hi, lo = split_hi_lo(misfit)
-            u = jnp.dot(
-                jnp.concatenate([hi, lo], axis=0), inv_ref[i], preferred_element_type=jnp.float32
-            )
-            u = u[:32, :BLK] + (u[32:, :BLK] + u[:32, BLK:])
+            misfit = mask_ref[:, cols].astype(jnp.float32) * (ests[i] - bg_ref[:, cols])
+            sides.append(jnp.concatenate(split_hi_lo(misfit), axis=0))
+        solved = [
+            jnp.dot(sides[i], inv_ref[i], preferred_element_type=jnp.float32) for i in range(TG)
+        ]
+        for i in range(TG):
+            u = solved[i][:32, :BLK] + (solved[i][32:, :BLK] + solved[i][:32, BLK:])
             u_st[1, i] = u
             f_st[HALO + TG + i] = jnp.broadcast_to(u[:, :1], u.shape)
             l_st[HALO + TG + i] = jnp.broadcast_to(u[:, BLK - 1 :], u.shape)
@@ -150,7 +190,10 @@
         ends = jnp.dot(
             yw_ref[...], jnp.concatenate(outs, axis=1), preferred_element_type=jnp.float32
         )
-        part_ref[...] = ends[0:2] + ends[8:10]
+        ends = ends[0:8] + ends[8:16]
+        for i in range(TG):
+            for k in range(2):
+                part_ref[k, i : i + 1, :] = ends[k : k + 1, i * BLK : (i + 1) * BLK]
 
     @pl.when(step == pl.num_programs(0) - 1)
     def _():
@@ -197,7 +240,7 @@
         in_specs=in_specs,
         out_specs=[
             pl.BlockSpec((32, GW), lambda l, *_: (0, done(l) - finals)),
-            pl.BlockSpec((2, GW), lambda l, *_: (0, done(l) - finals)),
+            pl.BlockSpec((2, TG, BLK), lambda l, *_: (0, done(l) - finals, 0)),
             *[full(*k.shape) for k in keep],
         ],
         scratch_shapes=[
@@ -212,7 +255,7 @@
         grid_spec=grid_spec,
         out_shape=[
             jax.ShapeDtypeStruct((32, n_final * GW), jnp.bfloat16),
-            jax.ShapeDtypeStruct((2, n_final * GW), jnp.float32),
+            jax.ShapeDtypeStruct((2, n_final * TG, BLK), jnp.float32),
             *keep,
         ],
         compiler_params=pltpu.CompilerParams(vmem_limit_bytes=VMEM_LIMIT),
@@ -224,19 +267,22 @@
     out_ref = rest[-1]
     rows = jnp.concatenate([e0[...], e1[...], e2[...], e3[...]], axis=0)
     both = jnp.dot(w_ref[...], rows, preferred_element_type=jnp.float32)
-    forced = n0[...] + n1[...]
     value = both[:32] + both[32:]
-    value = value + ends_ref[:, 0:1] * forced[0:1, :] + ends_ref[:, 1:2] * forced[1:2, :]
-    out_ref[...] = value
+    south, north = ends_ref[:, 0:1], ends_ref[:, 1:2]
+    for i in range(CW // BLK):
+        cols = slice(i * BLK, (i + 1) * BLK)
+        row = [n0[k, i : i + 1, :] + n1[k, i : i + 1, :] for k in range(2)]
+        out_ref[:, cols] = value[:, cols] + south * row[0] + north * row[1]
 
 
 def run_columns(start, width, total, w, ends, pieces, near, far, so_far):
-    cw = GW
+    cw = CW
     steps = width // cw
     full = lambda *shape: pl.BlockSpec(shape, lambda l: (0,) * len(shape))
     part = lambda rows: pl.BlockSpec((rows, cw), lambda l: (0, l))
+    forced = pl.BlockSpec((2, cw // BLK, BLK), lambda l: (0, l + start // cw, 0))
     operands = [w, ends, *pieces, near, far]
-    in_specs = [full(64, BLK), full(32, 2), *[part(32)] * 4, part(2), part(2)]
+    in_specs = [full(64, BLK), full(32, 2), *[part(32)] * 4, forced, forced]
     aliases = {}
     if so_far is not None:
         operands.append(so_far)
@@ -294,18 +340,15 @@
         axis=0,
     )
     kinds = (tile_kind == 1).astype(jnp.int32)
-    tables = column_tables(tile_kind, tile_shift, tile_frac)
-    inv_xt = jnp.concatenate(table_hi_lo(jnp.swapaxes(inverse_x, 1, 2)), axis=2)
-    a_x = couple_x[0][:, None] * inverse_x[:, :, 0]
-    b_x = couple_x[1][:, None] * inverse_x[:, :, -1]
+    tables, inv_xt, a_x, b_x = run_tables(
+        tile_shift, tap_weights(tile_kind, tile_frac), couple_x, inverse_x
+    )
     coefs = jnp.stack([a_x[:, 0], b_x[:, 0], a_x[:, -1], b_x[:, -1]])
     coefs = jnp.pad(coefs, ((0, 0), (PAD, 2 * PAD)))
 
-    a_y = couple_y[0][:, None] * inverse_y[:, :, 0]
-    b_y = couple_y[1][:, None] * inverse_y[:, :, -1]
-    corner = jnp.pad(
-        jnp.stack([a_y[:, 0], b_y[:, 0], a_y[:, -1], b_y[:, -1]]), ((0, 0), (HALO, HALO))
-    )
+    tips = inverse_y[:, :: BLK - 1, :: BLK - 1] * couple_y.T[:, None, :]
+    corner = jnp.stack([tips[:, 0, 0], tips[:, 0, 1], tips[:, 1, 0], tips[:, 1, 1]])
+    corner = jnp.pad(corner, ((0, 0), (HALO, HALO)))
     corner = lax.dynamic_slice_in_dim(corner, block, 2 * HALO + 1, 1)
     own_inv = lax.dynamic_index_in_dim(inverse_y, block, 0, keepdims=False)
     at = mine * rows
@@ -326,43 +369,60 @@
     gap = jnp.zeros((6, rows), jnp.bfloat16)
     yw = jnp.concatenate([end_hi, gap, end_lo, gap], axis=0)
 
-    def neighbour(value, k):
-        pairs = [(i + k, i) for i in range(n_wide) if 0 <= i + k < n_wide]
-        return lax.ppermute(value, "wide", pairs)
-
     state = None
-    result = None
-    position = 0
+    sent = []
+    parts = []
     for (first, stop), got in zip(bounds, gathered):
-        got = (got[0], got[1], got[2])
         east_west, part, state = run_rows(
             first, stop, groups, state, kinds, coefs, panels, got, w, tables,
             void_mask, background, inv_xt, a_x, b_x, yw,
         )
         far = swap(east_west, across)
-        close = swap(east_west, sibling)
-        f, l = {0: part[0:1]}, {0: part[1:2]}
-        for k in (-1, 1):
-            pair = neighbour(part, k)
-            f[k], l[k] = pair[0:1], pair[1:2]
-        for k in (2, 3):
-            l[-k] = neighbour(part[1:2], -k)
-            f[k] = neighbour(part[0:1], k)
-        af, cf, al, cl = [{k: corner[r, HALO + k] for k in range(-HALO, HALO + 1)} for r in range(4)]
-        l_m2 = l[-2] + al[-2] * l[-3] + cl[-2] * f[-1]
-        f_0 = f[0] + af[0] * l[-1] + cf[0] * f[1]
-        l_0 = l[0] + al[0] * l[-1] + cl[0] * f[1]
-        f_p2 = f[2] + af[2] * l[1] + cf[2] * f[3]
-        south = l[-1] + al[-1] * l_m2 + cl[-1] * f_0
-        north = f[1] + af[1] * l_0 + cf[1] * f_p2
-        forced = jnp.concatenate([south, north], axis=0)
-        forced = forced + swap(forced, across)
-        other = swap(forced, sibling)
-        pieces = (east_west, close, far, swap(far, sibling))
-        result = run_columns(
-            position, east_west.shape[1], width, w_y, ends_y, pieces, forced, other, result
-        )
-        position += east_west.shape[1]
+        sent.append((east_west, swap(east_west, sibling), far, swap(far, sibling)))
+        parts.append(part)
+    part = jnp.concatenate(parts, axis=1) if len(parts) > 1 else parts[0]
+
+    every = [(d, k) for d in range(4) for k in range(n_wide)]
+    at = lambda d, k: d * n_wide + k
+    fetch = lambda db, dw: lax.ppermute(
+        part, ("band", "wide"), [(at(d ^ db, k ^ dw), at(d, k)) for d, k in every]
+    )
+    second = block % 2
+    own = part + fetch(2, 0)
+    other = fetch(0, 1) + fetch(2, 1)
+    even = jnp.where(second == 0, own, other)
+    odd = jnp.where(second == 0, other, own)
+    shifted = lambda value, k: lax.ppermute(
+        value, "wide", [(i, i + 2 * k) for i in range(n_wide) if 0 <= i + 2 * k < n_wide]
+    )
+    before = shifted(jnp.stack([even[1], odd[0], odd[1]]), 1)
+    after = shifted(jnp.stack([even[0], even[1], odd[0]]), -1)
+    beyond = lax.ppermute(
+        jnp.where(second == 0, odd[1], even[0]),
+        "wide",
+        [(i, j) for i in range(n_wide) for j in [i + 4 * (1 - 2 * (i % 2))] if 0 <= j < n_wide],
+    )
+    pick = lambda first, last: jnp.where(second == 0, first, last)
+    f = {0: own[0], -1: pick(before[1], other[0]), 1: pick(other[0], after[0])}
+    l = {0: own[1], -1: pick(before[2], other[1]), 1: pick(other[1], after[1])}
+    l[-2], l[-3] = pick(before[0], before[2]), pick(beyond, before[0])
+    f[2], f[3] = pick(after[0], after[2]), pick(after[2], beyond)
+    af, cf, al, cl = [{k: corner[r, HALO + k] for k in range(-HALO, HALO + 1)} for r in range(4)]
+    l_m2 = l[-2] + al[-2] * l[-3] + cl[-2] * f[-1]
+    f_0 = f[0] + af[0] * l[-1] + cf[0] * f[1]
+    l_0 = l[0] + al[0] * l[-1] + cl[0] * f[1]
+    f_p2 = f[2] + af[2] * l[1] + cf[2] * f[3]
+    south = l[-1] + al[-1] * l_m2 + cl[-1] * f_0
+    north = f[1] + af[1] * l_0 + cf[1] * f_p2
+    forced = jnp.stack([south, north])
+    rest = swap(forced, sibling)
+
+    result = None
+    position = 0
+    for pieces in sent:
+        size = pieces[0].shape[1]
+        result = run_columns(position, size, width, w_y, ends_y, pieces, forced, rest, result)
+        position += size
     return result
 
 

time: 175 us -> 120 us (0.69)
  local copies, waits for them, and re-layouts: 48 us -> 8.27 us
  other arithmetic: 38.7 us -> 10.8 us
  Pallas kernels: 32.8 us -> 46 us
  starting transfers between devices: 36.6 us -> 28.8 us
  waiting for transfers between devices: 17.1 us -> 24.5 us
    unnamed x23 -> x14, local copies, waits for them, and re-layouts: 24.9 us -> 1.36 us
    pallas_call x0 -> x1, Pallas kernels: none -> 17.4 us  [run_tables(): pl.pallas_call(tables_kernel, grid_spec=pltpu.PrefetchScalarGridSpec(num_...]
    slice x5 -> x2, local copies, waits for them, and re-layouts: 18.6 us -> 2.55 us  [the longest x1 1.65 us: body(): tips = inverse_y[:, ::BLK - 1, ::BLK - 1] * couple_y.T[:, None, :]]
    convert_element_type x1 -> x0, other arithmetic: 9.28 us -> none  [column_tables(): return total.astype(jnp.bfloat16)]
    convert_element_type x4 -> x3, other arithmetic: 9.22 us -> 0.16 us  [table_hi_lo(): return (hi.astype(jnp.bfloat16), (value - hi).astype(jnp.bfloat16))]
    concatenate x2 -> x0, other arithmetic: 8.71 us -> none  [the longest x1 8.59 us: body(): inv_xt = jnp.concatenate(table_hi_lo(jnp.swapaxes(inverse_x, 1, 2)), axis=2)]
    ppermute x8 -> x7, waiting for transfers between devices: 11.2 us -> 19.7 us  [body(): swap = lambda value, pairs: lax.ppermute(value, 'band', pairs)]
    add x3 -> x0, other arithmetic: 8.34 us -> none  [the longest x1 4.17 us: body(): north = f[1] + af[1] * l_0 + cf[1] * f_p2]
  transfers between devices with their start and end apart: 14 -> 13, of which waited for: 5 -> 4; matrix products, arithmetic and copies ran while one was open for 47% -> 15% of each run, Pallas kernels for 0% -> 15%
where the time goes in v2:
time: 120 us; the launch traced here: 119 us
  Pallas kernels  46 us (38%)
  starting transfers between devices  28.8 us (24%)
  waiting for transfers between devices  24.5 us (20%)
  other arithmetic  10.8 us (9%)
  local copies, waits for them, and re-layouts  8.27 us (7%)
    pallas_call x1, Pallas kernels, run_rows(): pl.pallas_call(functools.partial(rows_kernel, first, groups, finals, carr...  22.5 us
    ppermute x7, waiting for transfers between devices, body(): swap = lambda value, pairs: lax.ppermute(value, 'band', pairs)  19.7 us
    pallas_call x1, Pallas kernels, run_tables(): pl.pallas_call(tables_kernel, grid_spec=pltpu.PrefetchScalarGridSpec(num_...  17.4 us
    ppermute x7, starting transfers between devices, body(): swap = lambda value, pairs: lax.ppermute(value, 'band', pairs)  14.3 us
    another operation x3, other arithmetic, body(): forced = jnp.stack([south, north])  7.54 us
    ppermute x2, starting transfers between devices, body(): lax.ppermute(value, 'wide', [(i, i + 2 * k) for i in range(n_wide) if 0 <...  7.47 us
    pallas_call x1, Pallas kernels, run_columns(): pl.pallas_call(columns_kernel, grid=(steps,), in_specs=in_specs, out_spec...  6.18 us
    ppermute x3, starting transfers between devices, body(): lax.ppermute(part, ('band', 'wide'), [(at(d ^ db, k ^ dw), at(d, k)) for...  3.68 us
  transfers between devices with their start and end apart: 13, of which 4 were waited for; matrix products, arithmetic and copies ran while one was open for 15% of the time, Pallas kernels for 15%

profile of v2, /device:TPU:25, one launch (start us, length us, event | category | flops | bytes accessed | tf_op | source)
XLA Modules:
  0.0 118.5 jit_solution(10544614552084371133)
XLA Ops:
  0.0 2.7 %collective-permute-start.1 = (bf16[32,16512]{1,0:T(8,128)(2,1)}, bf16[32,16512]{1,0:T(8,128)(2,1)S(1)}, u32[]{:S(2)}, u32[]{:S(2)}) collective-permute-start(bf16[32,16512]{1,0:T(8,128)(2,1)} %refs_6_.1), channel_id=1, source_target_pairs={{0,64},{32,96},{64,0},{96,32},{1,65},{33,97},{65,1},{97,33},{2,66}... | collective-permute-start | bytes 3170312 | tf_op jit(solution)/shard_map/ppermute | solution.py:324
  2.7 1.0 collective-permute-start
  7.4 17.4 %shard_map.118 = (bf16[128,256,128]{2,1,0:T(8,128)(2,1)}, bf16[128,128,256]{2,1,0:T(8,128)(2,1)}, f32[128,128]{1,0:T(8,128)S(1)}, f32[128,128]{1,0:T(8,128)S(1)}) custom-call(s32[128]{0:T(128)S(1)} %copy-done.2, f32[4,128]{1,0:T(4,128)S(1)} %maximum_reduce-precision_fusion.tap_ref, f32[2,128]{1,0:T(2,128)S(1)} %copy-done.1, f32[128,128,128]{2,1,0:T(8,128)} %inv_ref.1), custom_call_target="tpu_custom_call" | custom-call | tf_op jit(solution)/shard_map/pallas_call | solution.py:74
  24.9 0.7 constant_dynamic-slice_fusion.4
  25.7 1.0 dynamic-slice_bitcast_fusion.3
  27.5 1.6 %slice.148 = f32[32,2,2]{2,1,0:T(2,128)S(1)} slice(f32[32,128,128]{2,1,0:T(8,128)} %param.22), slice={[0:32:1], [0:128:127], [0:128:127]} | slice | bytes 1024 | tf_op jit(solution)/shard_map/slice | solution.py:349
  30.1 1.2 %slice_multiply_fusion.1 = (f32[32,1]{0,1:T(1,128)S(1)}, f32[32,1]{0,1:T(1,128)S(1)}) fusion(f32[32,128]{0,1:T(8,128)S(1)} %bitcast.152, f32[]{:T(128)} %bitcast.4, f32[]{:T(128)} %bitcast.6), kind=kLoop, calls=%fused_computation.98 | loop fusion | flops 64 | bytes 520 | tf_op jit(solution)/shard_map/mul | solution.py:362
  31.4 22.5 %shard_map.119 = (bf16[32,16384]{1,0:T(8,128)(2,1)}, f32[2,128,128]{2,1,0:T(8,128)S(1)}, f32[8,32,128]{2,1,0:T(8,128)}, f32[19,32,128]{2,1,0:T(8,128)}, f32[19,32,128]{2,1,0:T(8,128)}) custom-call(s32[128]{0:T(128)S(1)} %fusion.36.refs_0_, f32[4,152]{1,0:T(4,128)S(1)} %select_maximum_fusion.refs_1_, bf16[32,16512]{1,0:T(8,128)(2,1)S(1)} %copy-done, ...), custom_call_target="tpu_custom_call" | custom-call | tf_op jit(solution)/shard_map/pallas_call | solution.py:253
  53.9 2.8 %collective-permute-start.6 = (f32[2,128,128]{2,1,0:T(8,128)S(1)}, f32[2,128,128]{2,1,0:T(8,128)S(1)}, u32[]{:S(2)}, u32[]{:S(2)}) collective-permute-start(f32[2,128,128]{2,1,0:T(8,128)S(1)} %get-tuple-element.16), channel_id=1, source_target_pairs={{64,0},{65,1},{66,2},{67,3},{68,4},{69,5},{70,6},{71,7},{72,8},{73... | collective-permute-start | bytes 393224 | tf_op jit(solution)/shard_map/ppermute | solution.py:387
  57.5 2.4 %collective-permute-start.4 = (bf16[32,16384]{1,0:T(8,128)(2,1)}, bf16[32,16384]{1,0:T(8,128)(2,1)S(1)}, u32[]{:S(2)}, u32[]{:S(2)}) collective-permute-start(bf16[32,16384]{1,0:T(8,128)(2,1)} %get-tuple-element.15.e0), channel_id=1, source_target_pairs={{0,64},{32,96},{64,0},{96,32},{1,65},{33,97},{65,1},{97,33},{2,66}... | collective-permute-start | bytes 3145736 | tf_op jit(solution)/shard_map/ppermute | solution.py:324
  59.9 0.9 slice_reduce_fusion.7
  60.9 1.1 collective-permute-start.3
  62.1 1.4 %collective-permute-done.7 = f32[2,128,128]{2,1,0:T(8,128)S(1)} collective-permute-done((f32[2,128,128]{2,1,0:T(8,128)S(1)}, f32[2,128,128]{2,1,0:T(8,128)S(1)}, u32[]{:S(2)}, u32[]{:S(2)}) %collective-permute-start.7) | collective-permute-done | bytes 131104 | tf_op jit(solution)/shard_map/ppermute | solution.py:387
  63.6 3.5 %collective-permute-start.9 = (f32[3,128,128]{2,1,0:T(8,128)S(1)}, f32[3,128,128]{2,1,0:T(8,128)S(1)}, u32[]{:S(2)}, u32[]{:S(2)}) collective-permute-start(f32[3,128,128]{2,1,0:T(8,128)S(1)} %pad_maximum_fusion), channel_id=1, source_target_pairs={{0,2},{1,3},{2,4},{3,5},{4,6},{5,7},{6,8},{7,9},{8,10},{9,11},{10,... | collective-permute-start | bytes 589832 | tf_op jit(solution)/shard_map/ppermute | solution.py:395
  67.1 18.8 %collective-permute-done.4.e2 = bf16[32,16384]{1,0:T(8,128)(2,1)S(1)} collective-permute-done((bf16[32,16384]{1,0:T(8,128)(2,1)}, bf16[32,16384]{1,0:T(8,128)(2,1)S(1)}, u32[]{:S(2)}, u32[]{:S(2)}) %collective-permute-start.4) | collective-permute-done | bytes 1048608 | tf_op jit(solution)/shard_map/ppermute | solution.py:324
  85.9 4.9 %collective-permute-start.5 = (bf16[32,16384]{1,0:T(8,128)(2,1)S(1)}, bf16[32,16384]{1,0:T(8,128)(2,1)S(1)}, u32[]{:S(2)}, u32[]{:S(2)}) collective-permute-start(bf16[32,16384]{1,0:T(8,128)(2,1)S(1)} %collective-permute-done.4.e2), channel_id=1, source_target_pairs={{0,32},{32,0},{64,96},{96,64},{1,33},{33,1},{65,97},{97,65},{2,34}... | collective-permute-start | bytes 3145736 | tf_op jit(solution)/shard_map/ppermute | solution.py:324
  90.9 3.9 %collective-permute-start.11 = (f32[3,128,128]{2,1,0:T(8,128)S(1)}, f32[3,128,128]{2,1,0:T(8,128)S(1)}, u32[]{:S(2)}, u32[]{:S(2)}) collective-permute-start(f32[3,128,128]{2,1,0:T(8,128)S(1)} %pad_maximum_fusion.1), channel_id=1, source_target_pairs={{2,0},{3,1},{4,2},{5,3},{6,4},{7,5},{8,6},{9,7},{10,8},{11,9},{12,... | collective-permute-start | bytes 589832 | tf_op jit(solution)/shard_map/ppermute | solution.py:395
  94.9 3.3 %collective-permute-start.10 = (f32[128,128]{1,0:T(8,128)S(1)}, f32[128,128]{1,0:T(8,128)S(1)}, u32[]{:S(2)}, u32[]{:S(2)}) collective-permute-start(f32[128,128]{1,0:T(8,128)S(1)} %get-tuple-element.37), channel_id=1, source_target_pairs={{0,4},{2,6},{4,8},{5,1},{6,10},{7,3},{8,12},{9,5},{10,14},{11,7},{... | collective-permute-start | bytes 196616 | tf_op jit(solution)/shard_map/ppermute | solution.py:400
  98.9 3.4 %collective-permute-done.10 = f32[128,128]{1,0:T(8,128)S(1)} collective-permute-done((f32[128,128]{1,0:T(8,128)S(1)}, f32[128,128]{1,0:T(8,128)S(1)}, u32[]{:S(2)}, u32[]{:S(2)}) %collective-permute-start.10) | collective-permute-done | bytes 65568 | tf_op jit(solution)/shard_map/ppermute | solution.py:400
  102.3 3.8 %fusion.15 = f32[1,128,128]{2,1,0:T(8,128)S(1)} fusion(f32[2,128,128]{2,1,0:T(8,128)S(1)} %get-tuple-element.26, f32[3,128,128]{2,1,0:T(8,128)S(1)} %collective-permute-done.9, f32[128,128]{1,0:T(8,128)S(1)} %collective-permute-done.10, f32[2,128,128]{2,1,0:T(8,128)S(1)} %get-tuple-element.27, f32[]{:T(128)} %bitcast.26, f32[]{:T(128)} %bitcast.25, ...), kind=kLoop, calls=%fused_computation.23 | loop fusion | flops 278528 | bytes 589849 | tf_op jit(solution)/shard_map/stack | solution.py:417
  106.1 3.7 %fusion.6 = f32[1,128,128]{2,1,0:T(8,128)S(1)} fusion(f32[3,128,128]{2,1,0:T(8,128)S(1)} %collective-permute-done.11, f32[2,128,128]{2,1,0:T(8,128)S(1)} %get-tuple-element.26, f32[128,128]{1,0:T(8,128)S(1)} %collective-permute-done.10, f32[2,128,128]{2,1,0:T(8,128)S(1)} %get-tuple-element.27, f32[]{:T(128)} %bitcast.37, f32[]{:T(128)} %bitcast.35, ...), kind=kLoop, calls=%fused_computation.10 | loop fusion | flops 278528 | bytes 589849 | tf_op jit(solution)/shard_map/stack | solution.py:417
  109.8 1.5 %collective-permute-start.12 = (f32[2,128,128]{2,1,0:T(8,128)S(1)}, f32[2,128,128]{2,1,0:T(8,128)S(1)}, u32[]{:S(2)}, u32[]{:S(2)}) collective-permute-start(f32[2,128,128]{2,1,0:T(8,128)S(1)} %pad_maximum_fusion.2.n0), channel_id=1, source_target_pairs={{0,32},{32,0},{64,96},{96,64},{1,33},{33,1},{65,97},{97,65},{2,34}... | collective-permute-start | bytes 393224 | tf_op jit(solution)/shard_map/ppermute | solution.py:324
  111.5 0.9 collective-permute-done.12.n1
  112.4 6.2 %shard_map.120 = f32[32,16384]{1,0:T(8,128)} custom-call(bf16[64,128]{1,0:T(8,128)(2,1)S(1)} %pad_maximum_fusion.4.w_ref, f32[32,2]{1,0:T(8,128)S(1)} %copy.17.ends_ref, bf16[32,16384]{1,0:T(8,128)(2,1)} %get-tuple-element.15.e0, bf16[32,16384]{1,0:T(8,128)(2,1)S(1)} %collective-permute-done.3.e1, bf16[32,16384]{1,0:T(8,128)(2,1)S(1)} %collective-permute-done.4.e2, ...), custom_call_target="tpu_custom_call" | custom-call | tf_op jit(solution)/shard_map/pallas_call | solution.py:291
  (61 shorter events, 7.6 us)
Async XLA Ops:
  0.0 26.8 %collective-permute-start.1 = (bf16[32,16512]{1,0:T(8,128)(2,1)}, bf16[32,16512]{1,0:T(8,128)(2,1)S(1)}, u32[]{:S(2)}, u32[]{:S(2)}) collective-permute-start(bf16[32,16512]{1,0:T(8,128)(2,1)} %refs_6_.1), channel_id=1, source_target_pairs={{0,64},{32,96},{64,0},{96,32},{1,65},{33,97},{65,1},{97,33},{2,66}... | collective-permute-start | bytes 3170312 | tf_op jit(solution)/shard_map/ppermute | solution.py:324
  2.7 28.6 %collective-permute-start = (bf16[32,16512]{1,0:T(8,128)(2,1)}, bf16[32,16512]{1,0:T(8,128)(2,1)S(1)}, u32[]{:S(2)}, u32[]{:S(2)}) collective-permute-start(bf16[32,16512]{1,0:T(8,128)(2,1)} %refs_6_.1), channel_id=1, source_target_pairs={{0,32},{32,0},{64,96},{96,64},{1,33},{33,1},{65,97},{97,65},{2,34}... | collective-permute-start | bytes 3170312 | tf_op jit(solution)/shard_map/ppermute | solution.py:324
  6.0 0.7 copy-start.1
  6.7 0.7 copy-start.2
  7.3 17.4 %copy-start.4 = (f32[32]{0:T(128)S(1)}, f32[32]{0:T(128)}, u32[]{:S(2)}) copy-start(f32[32]{0:T(128)} %param.16) | copy-start | bytes 388
  7.4 17.4 %copy-start.5 = (s32[32]{0:T(128)S(1)}, s32[32]{0:T(128)}, u32[]{:S(2)}) copy-start(s32[32]{0:T(128)} %param.15) | copy-start | bytes 388
  7.4 21.8 %copy-start.3 = (f32[2,32]{1,0:T(2,128)S(1)}, f32[2,32]{1,0:T(2,128)}, u32[]{:S(2)}) copy-start(f32[2,32]{1,0:T(2,128)} %param.23) | copy-start | bytes 772
  7.4 22.7 %copy-start.6 = (s32[128]{0:T(128)S(1)}, s32[128]{0:T(128)}, u32[]{:S(2)}) copy-start(s32[128]{0:T(128)} %param.17) | copy-start | bytes 1540
  7.4 24.0 %copy-start = (bf16[32,16512]{1,0:T(8,128)(2,1)S(1)}, bf16[32,16512]{1,0:T(8,128)(2,1)}, u32[]{:S(2)}) copy-start(bf16[32,16512]{1,0:T(8,128)(2,1)} %refs_6_.1) | copy-start | bytes 3170308
  26.9 4.5 %collective-permute-start.2 = (bf16[32,16512]{1,0:T(8,128)(2,1)S(1)}, bf16[32,16512]{1,0:T(8,128)(2,1)}, u32[]{:S(2)}, u32[]{:S(2)}) collective-permute-start(bf16[32,16512]{1,0:T(8,128)(2,1)S(1)} %collective-permute-done.1.refs_4_.refs_8_), channel_id=1, source_target_pairs={{0,32},{32,0},{64,96},{96,64},{1,33},{33,1},{65,97},{97,65},{2,34}... | collective-permute-start | bytes 3170312 | tf_op jit(solution)/shard_map/ppermute | solution.py:324
  53.9 8.2 %collective-permute-start.6 = (f32[2,128,128]{2,1,0:T(8,128)S(1)}, f32[2,128,128]{2,1,0:T(8,128)S(1)}, u32[]{:S(2)}, u32[]{:S(2)}) collective-permute-start(f32[2,128,128]{2,1,0:T(8,128)S(1)} %get-tuple-element.16), channel_id=1, source_target_pairs={{64,0},{65,1},{66,2},{67,3},{68,4},{69,5},{70,6},{71,7},{72,8},{73... | collective-permute-start | bytes 393224 | tf_op jit(solution)/shard_map/ppermute | solution.py:387
  56.7 6.8 %collective-permute-start.7 = (f32[2,128,128]{2,1,0:T(8,128)S(1)}, f32[2,128,128]{2,1,0:T(8,128)S(1)}, u32[]{:S(2)}, u32[]{:S(2)}) collective-permute-start(f32[2,128,128]{2,1,0:T(8,128)S(1)} %get-tuple-element.16), channel_id=1, source_target_pairs={{1,0},{0,1},{3,2},{2,3},{5,4},{4,5},{7,6},{6,7},{9,8},{8,9},{11,10... | collective-permute-start | bytes 393224 | tf_op jit(solution)/shard_map/ppermute | solution.py:387
  57.0 6.5 %collective-permute-start.8 = (f32[2,128,128]{2,1,0:T(8,128)S(1)}, f32[2,128,128]{2,1,0:T(8,128)S(1)}, u32[]{:S(2)}, u32[]{:S(2)}) collective-permute-start(f32[2,128,128]{2,1,0:T(8,128)S(1)} %get-tuple-element.16), channel_id=1, source_target_pairs={{65,0},{64,1},{67,2},{66,3},{69,4},{68,5},{71,6},{70,7},{73,8},{72... | collective-permute-start | bytes 393224 | tf_op jit(solution)/shard_map/ppermute | solution.py:387
  57.5 28.4 %collective-permute-start.4 = (bf16[32,16384]{1,0:T(8,128)(2,1)}, bf16[32,16384]{1,0:T(8,128)(2,1)S(1)}, u32[]{:S(2)}, u32[]{:S(2)}) collective-permute-start(bf16[32,16384]{1,0:T(8,128)(2,1)} %get-tuple-element.15.e0), channel_id=1, source_target_pairs={{0,64},{32,96},{64,0},{96,32},{1,65},{33,97},{65,1},{97,33},{2,66}... | collective-permute-start | bytes 3145736 | tf_op jit(solution)/shard_map/ppermute | solution.py:324
  60.9 51.5 %collective-permute-start.3 = (bf16[32,16384]{1,0:T(8,128)(2,1)}, bf16[32,16384]{1,0:T(8,128)(2,1)S(1)}, u32[]{:S(2)}, u32[]{:S(2)}) collective-permute-start(bf16[32,16384]{1,0:T(8,128)(2,1)} %get-tuple-element.15.e0), channel_id=1, source_target_pairs={{0,32},{32,0},{64,96},{96,64},{1,33},{33,1},{65,97},{97,65},{2,34}... | collective-permute-start | bytes 3145736 | tf_op jit(solution)/shard_map/ppermute | solution.py:324
  63.6 38.7 %collective-permute-start.9 = (f32[3,128,128]{2,1,0:T(8,128)S(1)}, f32[3,128,128]{2,1,0:T(8,128)S(1)}, u32[]{:S(2)}, u32[]{:S(2)}) collective-permute-start(f32[3,128,128]{2,1,0:T(8,128)S(1)} %pad_maximum_fusion), channel_id=1, source_target_pairs={{0,2},{1,3},{2,4},{3,5},{4,6},{5,7},{6,8},{7,9},{8,10},{9,11},{10,... | collective-permute-start | bytes 589832 | tf_op jit(solution)/shard_map/ppermute | solution.py:395
  85.9 26.5 %collective-permute-start.5 = (bf16[32,16384]{1,0:T(8,128)(2,1)S(1)}, bf16[32,16384]{1,0:T(8,128)(2,1)S(1)}, u32[]{:S(2)}, u32[]{:S(2)}) collective-permute-start(bf16[32,16384]{1,0:T(8,128)(2,1)S(1)} %collective-permute-done.4.e2), channel_id=1, source_target_pairs={{0,32},{32,0},{64,96},{96,64},{1,33},{33,1},{65,97},{97,65},{2,34}... | collective-permute-start | bytes 3145736 | tf_op jit(solution)/shard_map/ppermute | solution.py:324
  90.9 11.4 %collective-permute-start.11 = (f32[3,128,128]{2,1,0:T(8,128)S(1)}, f32[3,128,128]{2,1,0:T(8,128)S(1)}, u32[]{:S(2)}, u32[]{:S(2)}) collective-permute-start(f32[3,128,128]{2,1,0:T(8,128)S(1)} %pad_maximum_fusion.1), channel_id=1, source_target_pairs={{2,0},{3,1},{4,2},{5,3},{6,4},{7,5},{8,6},{9,7},{10,8},{11,9},{12,... | collective-permute-start | bytes 589832 | tf_op jit(solution)/shard_map/ppermute | solution.py:395
  94.9 7.4 %collective-permute-start.10 = (f32[128,128]{1,0:T(8,128)S(1)}, f32[128,128]{1,0:T(8,128)S(1)}, u32[]{:S(2)}, u32[]{:S(2)}) collective-permute-start(f32[128,128]{1,0:T(8,128)S(1)} %get-tuple-element.37), channel_id=1, source_target_pairs={{0,4},{2,6},{4,8},{5,1},{6,10},{7,3},{8,12},{9,5},{10,14},{11,7},{... | collective-permute-start | bytes 196616 | tf_op jit(solution)/shard_map/ppermute | solution.py:400
  109.8 2.5 %collective-permute-start.12 = (f32[2,128,128]{2,1,0:T(8,128)S(1)}, f32[2,128,128]{2,1,0:T(8,128)S(1)}, u32[]{:S(2)}, u32[]{:S(2)}) collective-permute-start(f32[2,128,128]{2,1,0:T(8,128)S(1)} %pad_maximum_fusion.2.n0), channel_id=1, source_target_pairs={{0,32},{32,0},{64,96},{96,64},{1,33},{33,1},{65,97},{97,65},{2,34}... | collective-permute-start | bytes 393224 | tf_op jit(solution)/shard_map/ppermute | solution.py:324

commit v3 on v2

--- a/solution.py
+++ b/solution.py
@@ -11,9 +11,8 @@
 TG = 8
 GW = TG * BLK
 HALO = 3
-PAD = 8
-CW = 2048
-SPLITS = (0, 16)
+CW = 1024
+SPLITS = (0, 8, 16)
 VMEM_LIMIT = 48 * 1024 * 1024
 
 
@@ -49,10 +48,16 @@
     return lax.reduce_precision(jnp.stack(taps), 8, 7)
 
 
-def tables_kernel(shift_ref, tap_ref, couple_ref, inv_ref, t_ref, pair_ref, a_ref, b_ref):
+NT = (((1,), (1,)), ((), ()))
+
+
+def tables_kernel(shift_ref, tap_ref, couple_ref, inv_ref, t_ref, corr_ref, a_ref, b_ref):
     step = pl.program_id(0)
     shape = (2 * BLK, BLK)
     delta = lax.broadcasted_iota(jnp.int32, shape, 0) - lax.broadcasted_iota(jnp.int32, shape, 1)
+    place = lax.broadcasted_iota(jnp.int32, (16, BLK), 0) * (BLK - 1)
+    units = (place == lax.broadcasted_iota(jnp.int32, (16, BLK), 1)).astype(jnp.bfloat16)
+    row = lax.broadcasted_iota(jnp.int32, (2 * TG, BLK), 0)
     for i in range(TG):
         tile = step * TG + i
         tap = delta - shift_ref[tile]
@@ -60,12 +65,15 @@
         for k in range(4):
             total = jnp.where(tap == k, tap_ref[k, tile], total)
         t_ref[i] = total.astype(jnp.bfloat16)
-        turned = inv_ref[i].T
-        hi, lo = split_hi_lo(turned)
-        pair_ref[i, :, :BLK] = hi
-        pair_ref[i, :, BLK:] = lo
-        a_ref[i : i + 1, :] = couple_ref[0, tile] * turned[0:1, :]
-        b_ref[i : i + 1, :] = couple_ref[1, tile] * turned[BLK - 1 :, :]
+        hi, lo = split_hi_lo(inv_ref[i])
+        ends = lax.dot_general(units, hi, NT, preferred_element_type=jnp.float32)
+        ends = ends + lax.dot_general(units, lo, NT, preferred_element_type=jnp.float32)
+        a = couple_ref[0, tile] * ends[0:1, :]
+        b = couple_ref[1, tile] * ends[1:2, :]
+        a_ref[i : i + 1, :] = a
+        b_ref[i : i + 1, :] = b
+        both = jnp.where(row == i, a, jnp.where(row == TG + i, b, 0.0))
+        corr_ref[0, :, i * BLK : (i + 1) * BLK] = both.astype(jnp.bfloat16)
 
 
 def run_tables(shift, taps, couple, inverse):
@@ -77,11 +85,16 @@
             num_scalar_prefetch=3,
             grid=(tiles // TG,),
             in_specs=[cube(BLK, BLK)],
-            out_specs=[cube(2 * BLK, BLK), cube(BLK, 2 * BLK), cube(BLK), cube(BLK)],
+            out_specs=[
+                cube(2 * BLK, BLK),
+                pl.BlockSpec((1, 2 * TG, GW), lambda l, *_: (l, 0, 0)),
+                cube(BLK),
+                cube(BLK),
+            ],
         ),
         out_shape=[
             jax.ShapeDtypeStruct((tiles, 2 * BLK, BLK), jnp.bfloat16),
-            jax.ShapeDtypeStruct((tiles, BLK, 2 * BLK), jnp.bfloat16),
+            jax.ShapeDtypeStruct((tiles // TG, 2 * TG, GW), jnp.bfloat16),
             jax.ShapeDtypeStruct((tiles, BLK), jnp.float32),
             jax.ShapeDtypeStruct((tiles, BLK), jnp.float32),
         ],
@@ -101,23 +114,22 @@
 
 
 def rows_kernel(first, groups, finals, carried, *refs):
-    kind_ref, coef_ref = refs[:2]
-    refs = refs[2:]
-    (p0, p1, p2, p3, q0, q1, q2, q3, w_ref, t_ref, mask_ref, bg_ref, inv_ref) = refs[:13]
-    refs = refs[13:]
-    a_ref, b_ref, yw_ref = refs[:3]
-    refs = refs[3:]
+    kind_ref, p0, p1, p2, p3, q0, q1, q2, q3, w_ref, t_ref, mask_ref, bg_ref, inv_ref = refs[:14]
+    coef_ref, corr_ref, yw_ref = refs[14:17]
+    refs = refs[17:]
     if carried:
         u_in, f_in, l_in = refs[:3]
         refs = refs[3:]
     out_ref, part_ref, u_out, f_out, l_out, sec, u_st, f_st, l_st = refs
     step = pl.program_id(0)
     s = step + first
+    lane = lax.broadcasted_iota(jnp.int32, (32, BLK), 1)
+    roll = lambda value, by: pltpu.roll(value, by % BLK, 1)
 
     @pl.when(step == 0)
     def _():
         if carried:
-            u_st[0] = u_in[...]
+            u_st[1] = u_in[...]
             f_st[...] = f_in[...]
             l_st[...] = l_in[...]
         else:
@@ -125,13 +137,9 @@
             f_st[...] = jnp.zeros_like(f_st)
             l_st[...] = jnp.zeros_like(l_st)
 
-    @pl.when(step > 0)
-    def _():
-        u_st[0] = u_st[1]
-
-    for st in (f_st, l_st):
-        for i in range(HALO + TG):
-            st[i] = st[i + TG]
+    u_st[0] = u_st[1]
+    f_st[...] = jnp.where(lane < HALO + TG, roll(f_st[...], -TG), 0.0)
+    l_st[...] = jnp.where(lane < HALO + TG, roll(l_st[...], -TG), 0.0)
 
     @pl.when(s < groups)
     def _():
@@ -153,47 +161,46 @@
             cols = slice(i * BLK, (i + 1) * BLK)
             misfit = mask_ref[:, cols].astype(jnp.float32) * (ests[i] - bg_ref[:, cols])
             sides.append(jnp.concatenate(split_hi_lo(misfit), axis=0))
-        solved = [
-            jnp.dot(sides[i], inv_ref[i], preferred_element_type=jnp.float32) for i in range(TG)
-        ]
+        solved = []
+        for i in range(TG):
+            pair = jnp.concatenate(split_hi_lo(inv_ref[i]), axis=0)
+            solved.append(lax.dot_general(sides[i], pair, NT, preferred_element_type=jnp.float32))
+        f, l = f_st[...], l_st[...]
         for i in range(TG):
             u = solved[i][:32, :BLK] + (solved[i][32:, :BLK] + solved[i][:32, BLK:])
             u_st[1, i] = u
-            f_st[HALO + TG + i] = jnp.broadcast_to(u[:, :1], u.shape)
-            l_st[HALO + TG + i] = jnp.broadcast_to(u[:, BLK - 1 :], u.shape)
-
-    @pl.when(s >= groups)
-    def _():
-        for i in range(TG):
-            f_st[HALO + TG + i] = jnp.zeros((32, BLK), jnp.float32)
-            l_st[HALO + TG + i] = jnp.zeros((32, BLK), jnp.float32)
+            here = lane == HALO + TG + i
+            f = jnp.where(here, u[:, :1], f)
+            l = jnp.where(here, u[:, BLK - 1 :], l)
+        f_st[...] = f
+        l_st[...] = l
 
     @pl.when(s - 1 >= finals)
     def _():
-        base = (s - 1) * TG + PAD - HALO
-
-        def advance(which, j, west, east):
-            st, r = (f_st, 0) if which == "f" else (l_st, 2)
-            return st[j] + coef_ref[r, base + j] * west + coef_ref[r + 1, base + j] * east
-
-        l1 = {j: advance("l", j, l_st[j - 1], f_st[j + 1]) for j in range(1, HALO + TG)}
-        f1 = {j: advance("f", j, l_st[j - 1], f_st[j + 1]) for j in range(HALO, HALO + TG + 2)}
+        af, cf, al, cl = [coef_ref[r, pl.ds(s - 1, 1), :] for r in range(4)]
+        f0, l0 = f_st[...], l_st[...]
+        west, east = roll(l0, 1), roll(f0, -1)
+        f1 = f0 + af * west + cf * east
+        l1 = l0 + al * west + cl * east
+        west, east = roll(l1, 1), roll(f1, -1)
+        f2 = f0 + af * west + cf * east
+        l2 = l0 + al * west + cl * east
+        ends = jnp.where(lane < TG, roll(l2, 1 - HALO), roll(f2, TG - 1 - HALO))
+        ends = ends[:, : 2 * TG].astype(jnp.bfloat16)
+        fix = jnp.dot(ends, corr_ref[0], preferred_element_type=jnp.float32)
         outs = []
         for i in range(TG):
-            j = HALO + i
-            west = advance("l", j - 1, l1[j - 2], f1[j])
-            east = advance("f", j + 1, l1[j], f1[j + 2])
-            value = u_st[0, i] + a_ref[i : i + 1, :] * west + b_ref[i : i + 1, :] * east
-            value = value.astype(jnp.bfloat16)
-            out_ref[:, i * BLK : (i + 1) * BLK] = value
+            cols = slice(i * BLK, (i + 1) * BLK)
+            value = (u_st[0, i] + fix[:, cols]).astype(jnp.bfloat16)
+            out_ref[:, cols] = value
             outs.append(value)
-        ends = jnp.dot(
+        tips = jnp.dot(
             yw_ref[...], jnp.concatenate(outs, axis=1), preferred_element_type=jnp.float32
         )
-        ends = ends[0:8] + ends[8:16]
+        tips = tips[0:8] + tips[8:16]
         for i in range(TG):
             for k in range(2):
-                part_ref[k, i : i + 1, :] = ends[k : k + 1, i * BLK : (i + 1) * BLK]
+                part_ref[k, i : i + 1, :] = tips[k : k + 1, i * BLK : (i + 1) * BLK]
 
     @pl.when(step == pl.num_programs(0) - 1)
     def _():
@@ -202,40 +209,44 @@
         l_out[...] = l_st[...]
 
 
-def run_rows(first, stop, groups, state, kinds, coefs, own, got, w, tables, mask, bg, inv, a, b, yw):
+def run_rows(first, stop, groups, state, kinds, own, got, w, tables, mask, bg, inv, coefs, corr, yw):
     ends_here = stop == groups
     steps = stop - first + (1 if ends_here else 0)
     finals = 0 if first == 0 else first - 1
     n_final = (stop if ends_here else stop - 1) - finals
     carried = state is not None
     count = stop - first
+    near, far, away = got
     here = lambda l: jnp.minimum(l, count - 1)
     done = lambda l: jnp.clip(l + first - 1, finals, finals + n_final - 1)
     full = lambda *shape: pl.BlockSpec(shape, lambda l, *_: (0,) * len(shape))
     wide = lambda off: pl.BlockSpec((32, GW), lambda l, *_: (0, here(l) + off))
     edge = lambda off: pl.BlockSpec((32, BLK), lambda l, *_: (0, (here(l) + off + 1) * TG))
-    in_specs = [wide(first), wide(0), wide(0), wide(0), edge(first), edge(0), edge(0), edge(0)]
+    cube = lambda *shape: pl.BlockSpec((TG, *shape), lambda l, *_: (here(l) + first, 0, 0))
+    in_specs = [wide(first), wide(first), wide(0), wide(0)]
+    in_specs += [edge(first), edge(first), edge(0), edge(0)]
     in_specs += [
         full(64, BLK),
-        pl.BlockSpec((TG, 2 * BLK, BLK), lambda l, *_: (here(l) + first, 0, 0)),
+        cube(2 * BLK, BLK),
         wide(first),
         wide(first),
-        pl.BlockSpec((TG, BLK, 2 * BLK), lambda l, *_: (here(l) + first, 0, 0)),
-        pl.BlockSpec((TG, BLK), lambda l, *_: (done(l), 0)),
-        pl.BlockSpec((TG, BLK), lambda l, *_: (done(l), 0)),
+        cube(BLK, BLK),
+        full(*coefs.shape),
+        pl.BlockSpec((1, 2 * TG, GW), lambda l, *_: (done(l), 0, 0)),
         full(16, 32),
     ]
     keep = [
         jax.ShapeDtypeStruct((TG, 32, BLK), jnp.float32),
-        jax.ShapeDtypeStruct((HALO + 2 * TG, 32, BLK), jnp.float32),
-        jax.ShapeDtypeStruct((HALO + 2 * TG, 32, BLK), jnp.float32),
+        jax.ShapeDtypeStruct((32, BLK), jnp.float32),
+        jax.ShapeDtypeStruct((32, BLK), jnp.float32),
     ]
-    operands = [kinds, coefs, own, *got, own, *got, w, tables, mask, bg, inv, a, b, yw]
+    operands = [kinds, own, near, far, away, own, near, far, away, w, tables, mask, bg, inv]
+    operands += [coefs, corr, yw]
     if carried:
         in_specs += [full(*k.shape) for k in keep]
         operands += list(state)
     grid_spec = pltpu.PrefetchScalarGridSpec(
-        num_scalar_prefetch=2,
+        num_scalar_prefetch=1,
         grid=(steps,),
         in_specs=in_specs,
         out_specs=[
@@ -246,8 +257,8 @@
         scratch_shapes=[
             pltpu.VMEM((2, 32, GW + BLK), jnp.bfloat16),
             pltpu.VMEM((2, TG, 32, BLK), jnp.float32),
-            pltpu.VMEM((HALO + 2 * TG, 32, BLK), jnp.float32),
-            pltpu.VMEM((HALO + 2 * TG, 32, BLK), jnp.float32),
+            pltpu.VMEM((32, BLK), jnp.float32),
+            pltpu.VMEM((32, BLK), jnp.float32),
         ],
     )
     outs = pl.pallas_call(
@@ -261,6 +272,33 @@
         compiler_params=pltpu.CompilerParams(vmem_limit_bytes=VMEM_LIMIT),
     )(*operands)
     return outs[0], outs[1], tuple(outs[2:])
+
+
+def ends_kernel(block_ref, corner_ref, own, other, before, after, beyond, out):
+    block = block_ref[0]
+    second = lax.rem(block, 2) == 1
+    pick = lambda even, odd: jnp.where(second, odd, even)
+    coef = lambda r, k: corner_ref[r, block + HALO + k]
+    f = {0: own[0], -1: pick(before[1], other[0]), 1: pick(other[0], after[0])}
+    l = {0: own[1], -1: pick(before[2], other[1]), 1: pick(other[1], after[1])}
+    l[-2], l[-3] = pick(before[0], before[2]), pick(beyond[...], before[0])
+    f[2], f[3] = pick(after[0], after[2]), pick(after[2], beyond[...])
+    last = lambda k, west, east: l[k] + coef(2, k) * west + coef(3, k) * east
+    head = lambda k, west, east: f[k] + coef(0, k) * west + coef(1, k) * east
+    out[0] = last(-1, last(-2, l[-3], f[-1]), head(0, l[-1], f[1]))
+    out[1] = head(1, last(0, l[-1], f[1]), head(2, l[1], f[3]))
+
+
+def run_ends(block, corner, own, *others):
+    smem = pl.BlockSpec(memory_space=pltpu.SMEM)
+    vmem = pl.BlockSpec(memory_space=pltpu.VMEM)
+    return pl.pallas_call(
+        ends_kernel,
+        in_specs=[smem, smem] + [vmem] * 5,
+        out_specs=vmem,
+        out_shape=jax.ShapeDtypeStruct(own.shape, own.dtype),
+        compiler_params=pltpu.CompilerParams(vmem_limit_bytes=VMEM_LIMIT),
+    )(block.reshape(1), corner, own, *others)
 
 
 def columns_kernel(w_ref, ends_ref, e0, e1, e2, e3, n0, n1, *rest):
@@ -327,9 +365,8 @@
     bounds = [(SPLITS[i], SPLITS[i + 1]) for i in range(len(SPLITS) - 1)]
     gathered = []
     for first, stop in bounds:
-        cols = slice(first * GW, stop * GW + BLK)
-        far = swap(panels[:, cols], across)
-        gathered.append((near[:, cols], far, swap(far, sibling)))
+        far = swap(panels[:, first * GW : stop * GW + BLK], across)
+        gathered.append((near, far, swap(far, sibling)))
 
     order = ((jnp.arange(4, dtype=jnp.int32) ^ mine)[:, None] * rows + jnp.arange(rows)[None, :]).reshape(-1)
     w = jnp.concatenate(
@@ -340,16 +377,17 @@
         axis=0,
     )
     kinds = (tile_kind == 1).astype(jnp.int32)
-    tables, inv_xt, a_x, b_x = run_tables(
+    tables, corr, a_x, b_x = run_tables(
         tile_shift, tap_weights(tile_kind, tile_frac), couple_x, inverse_x
     )
     coefs = jnp.stack([a_x[:, 0], b_x[:, 0], a_x[:, -1], b_x[:, -1]])
-    coefs = jnp.pad(coefs, ((0, 0), (PAD, 2 * PAD)))
+    coefs = jnp.pad(coefs, ((0, 0), (HALO, 2 * TG - HALO))).reshape(4, groups + 2, TG)
+    coefs = jnp.concatenate([coefs[:, k : k + groups] for k in range(3)], axis=2)
+    coefs = jnp.pad(coefs, ((0, 0), (0, 0), (0, BLK - 3 * TG)))
 
     tips = inverse_y[:, :: BLK - 1, :: BLK - 1] * couple_y.T[:, None, :]
     corner = jnp.stack([tips[:, 0, 0], tips[:, 0, 1], tips[:, 1, 0], tips[:, 1, 1]])
     corner = jnp.pad(corner, ((0, 0), (HALO, HALO)))
-    corner = lax.dynamic_slice_in_dim(corner, block, 2 * HALO + 1, 1)
     own_inv = lax.dynamic_index_in_dim(inverse_y, block, 0, keepdims=False)
     at = mine * rows
     own_rows = lax.dynamic_slice_in_dim(own_inv, at, rows, 0)
@@ -374,11 +412,11 @@
     parts = []
     for (first, stop), got in zip(bounds, gathered):
         east_west, part, state = run_rows(
-            first, stop, groups, state, kinds, coefs, panels, got, w, tables,
-            void_mask, background, inv_xt, a_x, b_x, yw,
+            first, stop, groups, state, kinds, panels, got, w, tables,
+            void_mask, background, inverse_x, coefs, corr, yw,
         )
         far = swap(east_west, across)
-        sent.append((east_west, swap(east_west, sibling), far, swap(far, sibling)))
+        sent.append([east_west, swap(east_west, sibling), far])
         parts.append(part)
     part = jnp.concatenate(parts, axis=1) if len(parts) > 1 else parts[0]
 
@@ -402,25 +440,15 @@
         "wide",
         [(i, j) for i in range(n_wide) for j in [i + 4 * (1 - 2 * (i % 2))] if 0 <= j < n_wide],
     )
-    pick = lambda first, last: jnp.where(second == 0, first, last)
-    f = {0: own[0], -1: pick(before[1], other[0]), 1: pick(other[0], after[0])}
-    l = {0: own[1], -1: pick(before[2], other[1]), 1: pick(other[1], after[1])}
-    l[-2], l[-3] = pick(before[0], before[2]), pick(beyond, before[0])
-    f[2], f[3] = pick(after[0], after[2]), pick(after[2], beyond)
-    af, cf, al, cl = [{k: corner[r, HALO + k] for k in range(-HALO, HALO + 1)} for r in range(4)]
-    l_m2 = l[-2] + al[-2] * l[-3] + cl[-2] * f[-1]
-    f_0 = f[0] + af[0] * l[-1] + cf[0] * f[1]
-    l_0 = l[0] + al[0] * l[-1] + cl[0] * f[1]
-    f_p2 = f[2] + af[2] * l[1] + cf[2] * f[3]
-    south = l[-1] + al[-1] * l_m2 + cl[-1] * f_0
-    north = f[1] + af[1] * l_0 + cf[1] * f_p2
-    forced = jnp.stack([south, north])
+    forced = run_ends(block, corner, own, other, before, after, beyond)
     rest = swap(forced, sibling)
+    sent[-1][2], rest = lax.optimization_barrier((sent[-1][2], rest))
 
     result = None
     position = 0
     for pieces in sent:
         size = pieces[0].shape[1]
+        pieces = (*pieces, swap(pieces[2], sibling))
         result = run_columns(position, size, width, w_y, ends_y, pieces, forced, rest, result)
         position += size
     return result

time: 120 us -> 129 us (1.075)
  starting transfers between devices: 28.8 us -> 48.7 us
  waiting for transfers between devices: 24.5 us -> 10.1 us
  Pallas kernels: 46 us -> 55.9 us
  other arithmetic: 10.8 us -> 2.03 us
  local copies, waits for them, and re-layouts: 8.27 us -> 10.5 us
    ppermute x7 -> x12, starting transfers between devices: 14.3 us -> 34.2 us  [body(): swap = lambda value, pairs: lax.ppermute(value, 'band', pairs)]
    ppermute x7 -> x12, waiting for transfers between devices: 19.7 us -> 3.82 us  [body(): swap = lambda value, pairs: lax.ppermute(value, 'band', pairs)]
    another operation x3 -> x0, other arithmetic: 7.54 us -> none  [body(): forced = jnp.stack([south, north])]
    pallas_call x1 -> x2, Pallas kernels: 22.5 us -> 28.2 us  [run_rows(): pl.pallas_call(functools.partial(rows_kernel, first, groups, finals, carr...]
    pallas_call x1 -> x2, Pallas kernels: 6.18 us -> 9.64 us  [run_columns(): pl.pallas_call(columns_kernel, grid=(steps,), in_specs=in_specs, out_spec...]
    slice x1 -> x2, local copies, waits for them, and re-layouts: 0.7 us -> 2.32 us  [the longest x1 2.31 us: body(): far = swap(panels[:, first * GW:stop * GW + BLK], across)]
  transfers between devices with their start and end apart: 13 -> 18, of which waited for: 4 -> 5; matrix products, arithmetic and copies ran while one was open for 15% -> 8% of each run, Pallas kernels for 15% -> 29%
where the time goes in v3:
time: 129 us; the launch traced here: 128 us
  Pallas kernels  55.9 us (43%)
  starting transfers between devices  48.7 us (38%)
  local copies, waits for them, and re-layouts  10.5 us (8%)
  waiting for transfers between devices  10.1 us (8%)
  other arithmetic  2.03 us (2%)
    ppermute x12, starting transfers between devices, body(): swap = lambda value, pairs: lax.ppermute(value, 'band', pairs)  34.2 us
    pallas_call x2, Pallas kernels, run_rows(): pl.pallas_call(functools.partial(rows_kernel, first, groups, finals, carr...  28.2 us
    pallas_call x1, Pallas kernels, run_tables(): pl.pallas_call(tables_kernel, grid_spec=pltpu.PrefetchScalarGridSpec(num_...  17.4 us
    pallas_call x2, Pallas kernels, run_columns(): pl.pallas_call(columns_kernel, grid=(steps,), in_specs=in_specs, out_spec...  9.64 us
    ppermute x2, starting transfers between devices, body(): lax.ppermute(value, 'wide', [(i, i + 2 * k) for i in range(n_wide) if 0 <...  7.78 us
    ppermute x1, waiting for transfers between devices, body(): lax.ppermute(jnp.where(second == 0, odd[1], even[0]), 'wide', [(i, j) for...  4.31 us
    ppermute x12, waiting for transfers between devices, body(): swap = lambda value, pairs: lax.ppermute(value, 'band', pairs)  3.82 us
    ppermute x3, starting transfers between devices, body(): lax.ppermute(part, ('band', 'wide'), [(at(d ^ db, k ^ dw), at(d, k)) for...  3.69 us
  transfers between devices with their start and end apart: 18, of which 5 were waited for; matrix products, arithmetic and copies ran while one was open for 8% of the time, Pallas kernels for 29%

profile of v3, /device:TPU:25, one launch (start us, length us, event | category | flops | bytes accessed | tf_op | source)
XLA Modules:
  0.0 127.6 jit_solution(14924429898712018960)
XLA Ops:
  0.8 2.3 %fusion.14 = (bf16[32,8320]{1,0:T(8,128)(2,1)}, bf16[32,8320]{1,0:T(8,128)(2,1)}) fusion(bf16[32,16512]{1,0:T(8,128)(2,1)} %refs_5_.3), kind=kLoop, calls=%fused_computation.87 | loop fusion | bytes 2129920 | tf_op jit(solution)/shard_map/slice | solution.py:368
  3.1 2.7 %collective-permute-start.3 = (bf16[32,8320]{1,0:T(8,128)(2,1)}, bf16[32,8320]{1,0:T(8,128)(2,1)S(1)}, u32[]{:S(2)}, u32[]{:S(2)}) collective-permute-start(bf16[32,8320]{1,0:T(8,128)(2,1)} %get-tuple-element.50), channel_id=1, source_target_pairs={{0,64},{32,96},{64,0},{96,32},{1,65},{33,97},{65,1},{97,33},{2,66}... | collective-permute-start | bytes 1597448 | tf_op jit(solution)/shard_map/ppermute | solution.py:362
  6.4 17.4 %shard_map.118 = (bf16[128,256,128]{2,1,0:T(8,128)(2,1)}, bf16[16,16,1024]{2,1,0:T(8,128)(2,1)S(1)}, f32[128,128]{1,0:T(8,128)S(1)}, f32[128,128]{1,0:T(8,128)S(1)}) custom-call(s32[128]{0:T(128)S(1)} %copy-done.6, f32[4,128]{1,0:T(4,128)S(1)} %maximum_reduce-precision_fusion.tap_ref, f32[2,128]{1,0:T(2,128)S(1)} %copy-done.5, f32[128,128,128]{2,1,0:T(8,128)} %refs_13_.3), custom_call_target="tpu_custom_call" | custom-call | tf_op jit(solution)/shard_map/pallas_call | solution.py:82
  23.8 0.8 copy-done.1
  25.7 1.6 %slice.93 = f32[32,2,2]{2,1,0:T(2,128)S(1)} slice(f32[32,128,128]{2,1,0:T(8,128)} %param.22), slice={[0:32:1], [0:128:127], [0:128:127]} | slice | bytes 1024 | tf_op jit(solution)/shard_map/slice | solution.py:388
  28.4 1.6 %collective-permute-done.1.refs_3_.refs_7_ = bf16[32,8320]{1,0:T(8,128)(2,1)S(1)} collective-permute-done((bf16[32,8320]{1,0:T(8,128)(2,1)}, bf16[32,8320]{1,0:T(8,128)(2,1)S(1)}, u32[]{:S(2)}, u32[]{:S(2)}) %collective-permute-start.1) | collective-permute-done | bytes 532512 | tf_op jit(solution)/shard_map/ppermute | solution.py:362
  29.9 0.8 collective-permute-start.2
  30.9 1.0 copy-done.2
  31.9 13.1 %shard_map.119 = (bf16[32,7168]{1,0:T(8,128)(2,1)S(1)}, f32[2,56,128]{2,1,0:T(8,128)S(1)}, f32[8,32,128]{2,1,0:T(8,128)S(1)}, f32[32,128]{1,0:T(8,128)S(1)}, f32[32,128]{1,0:T(8,128)S(1)}) custom-call(s32[128]{0:T(128)S(1)} %fusion.13.refs_0_, bf16[32,16512]{1,0:T(8,128)(2,1)S(1)} %copy-done, bf16[32,16512]{1,0:T(8,128)(2,1)S(1)} %collective-permute-done.refs_2_.refs_6_, ...), custom_call_target="tpu_custom_call" | custom-call | tf_op jit(solution)/shard_map/pallas_call | solution.py:264
  45.1 15.0 %shard_map.120 = (bf16[32,9216]{1,0:T(8,128)(2,1)S(1)}, f32[2,72,128]{2,1,0:T(8,128)S(1)}, f32[8,32,128]{2,1,0:T(8,128)}, f32[32,128]{1,0:T(8,128)}, f32[32,128]{1,0:T(8,128)}) custom-call(s32[128]{0:T(128)S(1)} %fusion.13.refs_0_, bf16[32,16512]{1,0:T(8,128)(2,1)S(1)} %copy-done, bf16[32,16512]{1,0:T(8,128)(2,1)S(1)} %collective-permute-done.refs_2_.refs_6_, ...), custom_call_target="tpu_custom_call" | custom-call | tf_op jit(solution)/shard_map/pallas_call | solution.py:264
  60.2 2.8 %collective-permute-start.7 = (f32[2,128,128]{2,1,0:T(8,128)S(1)}, f32[2,128,128]{2,1,0:T(8,128)S(1)}, u32[]{:S(2)}, u32[]{:S(2)}) collective-permute-start(f32[2,128,128]{2,1,0:T(8,128)S(1)} %constant_dynamic-update-slice_fusion), channel_id=1, source_target_pairs={{64,0},{65,1},{66,2},{67,3},{68,4},{69,5},{70,6},{71,7},{72,8},{73... | collective-permute-start | bytes 393224 | tf_op jit(solution)/shard_map/ppermute | solution.py:425
  63.9 0.9 slice_reduce_fusion.7
  64.8 2.5 %collective-permute-start.6 = (bf16[32,9216]{1,0:T(8,128)(2,1)S(1)}, bf16[32,9216]{1,0:T(8,128)(2,1)S(1)}, u32[]{:S(2)}, u32[]{:S(2)}) collective-permute-start(bf16[32,9216]{1,0:T(8,128)(2,1)S(1)} %get-tuple-element.25.e0), channel_id=1, source_target_pairs={{0,64},{32,96},{64,0},{96,32},{1,65},{33,97},{65,1},{97,33},{2,66}... | collective-permute-start | bytes 1769480 | tf_op jit(solution)/shard_map/ppermute | solution.py:362
  67.9 1.9 %collective-permute-done.8 = f32[2,128,128]{2,1,0:T(8,128)S(1)} collective-permute-done((f32[2,128,128]{2,1,0:T(8,128)S(1)}, f32[2,128,128]{2,1,0:T(8,128)S(1)}, u32[]{:S(2)}, u32[]{:S(2)}) %collective-permute-start.8) | collective-permute-done | bytes 131104 | tf_op jit(solution)/shard_map/ppermute | solution.py:425
  69.9 5.9 %collective-permute-start.11 = (f32[3,128,128]{2,1,0:T(8,128)S(1)}, f32[3,128,128]{2,1,0:T(8,128)S(1)}, u32[]{:S(2)}, u32[]{:S(2)}) collective-permute-start(f32[3,128,128]{2,1,0:T(8,128)S(1)} %pad_maximum_fusion.1), channel_id=1, source_target_pairs={{2,0},{3,1},{4,2},{5,3},{6,4},{7,5},{8,6},{9,7},{10,8},{11,9},{12,... | collective-permute-start | bytes 589832 | tf_op jit(solution)/shard_map/ppermute | solution.py:433
  75.8 1.9 %collective-permute-start.10 = (f32[3,128,128]{2,1,0:T(8,128)S(1)}, f32[3,128,128]{2,1,0:T(8,128)S(1)}, u32[]{:S(2)}, u32[]{:S(2)}) collective-permute-start(f32[3,128,128]{2,1,0:T(8,128)S(1)} %pad_maximum_fusion), channel_id=1, source_target_pairs={{0,2},{1,3},{2,4},{3,5},{4,6},{5,7},{6,8},{7,9},{8,10},{9,11},{10,... | collective-permute-start | bytes 589832 | tf_op jit(solution)/shard_map/ppermute | solution.py:433
  79.2 3.0 %collective-permute-start.12 = (f32[128,128]{1,0:T(8,128)S(1)}, f32[128,128]{1,0:T(8,128)S(1)}, u32[]{:S(2)}, u32[]{:S(2)}) collective-permute-start(f32[128,128]{1,0:T(8,128)S(1)} %get-tuple-element.52), channel_id=1, source_target_pairs={{0,4},{2,6},{4,8},{5,1},{6,10},{7,3},{8,12},{9,5},{10,14},{11,7},{... | collective-permute-start | bytes 196616 | tf_op jit(solution)/shard_map/ppermute | solution.py:438
  82.3 4.3 %collective-permute-done.12.beyond = f32[128,128]{1,0:T(8,128)S(1)} collective-permute-done((f32[128,128]{1,0:T(8,128)S(1)}, f32[128,128]{1,0:T(8,128)S(1)}, u32[]{:S(2)}, u32[]{:S(2)}) %collective-permute-start.12) | collective-permute-done | bytes 65568 | tf_op jit(solution)/shard_map/ppermute | solution.py:438
  87.3 24.8 %collective-permute-start.13 = (f32[2,128,128]{2,1,0:T(8,128)S(1)}, f32[2,128,128]{2,1,0:T(8,128)S(1)}, u32[]{:S(2)}, u32[]{:S(2)}) collective-permute-start(f32[2,128,128]{2,1,0:T(8,128)S(1)} %shard_map.121.n0), channel_id=1, source_target_pairs={{0,32},{32,0},{64,96},{96,64},{1,33},{33,1},{65,97},{97,65},{2,34}... | collective-permute-start | bytes 393224 | tf_op jit(solution)/shard_map/ppermute | solution.py:362
  112.1 1.2 slice_multiply_fusion.1
  114.0 1.0 dynamic-slice_bitcast_fusion.3
  115.7 2.0 %collective-permute-done.15.e1 = bf16[32,7168]{1,0:T(8,128)(2,1)} collective-permute-done((bf16[32,7168]{1,0:T(8,128)(2,1)S(1)}, bf16[32,7168]{1,0:T(8,128)(2,1)}, u32[]{:S(2)}, u32[]{:S(2)}) %collective-permute-start.15) | collective-permute-done | bytes 458784 | tf_op jit(solution)/shard_map/ppermute | solution.py:362
  117.9 5.3 %shard_map.122.rest_0_ = f32[32,16384]{1,0:T(8,128)} custom-call(bf16[64,128]{1,0:T(8,128)(2,1)S(1)} %pad_maximum_fusion.3.w_ref, f32[32,2]{1,0:T(8,128)S(1)} %copy.19.ends_ref, bf16[32,7168]{1,0:T(8,128)(2,1)S(1)} %copy-done.4, bf16[32,7168]{1,0:T(8,128)(2,1)} %collective-permute-done.15.e1, bf16[32,7168]{1,0:T(8,128)(2,1)} %collective-permute-done.16.e2, ...), custom_call_target="tpu_custom_call" | custom-call | tf_op jit(solution)/shard_map/pallas_call | solution.py:329
  123.2 4.4 %shard_map.123 = f32[32,16384]{1,0:T(8,128)} custom-call(bf16[64,128]{1,0:T(8,128)(2,1)S(1)} %pad_maximum_fusion.3.w_ref, f32[32,2]{1,0:T(8,128)S(1)} %copy.19.ends_ref, bf16[32,9216]{1,0:T(8,128)(2,1)S(1)} %get-tuple-element.25.e0, bf16[32,9216]{1,0:T(8,128)(2,1)S(1)} %collective-permute-done.5.e1, ...), custom_call_target="tpu_custom_call", output_to_operand_aliasing={{}: (8, {})} | custom-call | tf_op jit(solution)/shard_map/pallas_call | solution.py:329
  (85 shorter events, 8.8 us)
Async XLA Ops:
  0.0 6.3 %copy-start.6 = (s32[128]{0:T(128)S(1)}, s32[128]{0:T(128)}, u32[]{:S(2)}) copy-start(s32[128]{0:T(128)} %shift_ref.1) | copy-start | bytes 1540
  0.0 6.3 %copy-start.5 = (f32[2,128]{1,0:T(2,128)S(1)}, f32[2,128]{1,0:T(2,128)}, u32[]{:S(2)}) copy-start(f32[2,128]{1,0:T(2,128)} %couple_ref.1) | copy-start | bytes 3076
  0.0 30.8 %collective-permute-start = (bf16[32,16512]{1,0:T(8,128)(2,1)}, bf16[32,16512]{1,0:T(8,128)(2,1)S(1)}, u32[]{:S(2)}, u32[]{:S(2)}) collective-permute-start(bf16[32,16512]{1,0:T(8,128)(2,1)} %refs_5_.3), channel_id=1, source_target_pairs={{0,32},{32,0},{64,96},{96,64},{1,33},{33,1},{65,97},{97,65},{2,34}... | collective-permute-start | bytes 3170312 | tf_op jit(solution)/shard_map/ppermute | solution.py:362
  3.1 24.5 %collective-permute-start.3 = (bf16[32,8320]{1,0:T(8,128)(2,1)}, bf16[32,8320]{1,0:T(8,128)(2,1)S(1)}, u32[]{:S(2)}, u32[]{:S(2)}) collective-permute-start(bf16[32,8320]{1,0:T(8,128)(2,1)} %get-tuple-element.50), channel_id=1, source_target_pairs={{0,64},{32,96},{64,0},{96,32},{1,65},{33,97},{65,1},{97,33},{2,66}... | collective-permute-start | bytes 1597448 | tf_op jit(solution)/shard_map/ppermute | solution.py:362
  5.9 24.1 %collective-permute-start.1 = (bf16[32,8320]{1,0:T(8,128)(2,1)}, bf16[32,8320]{1,0:T(8,128)(2,1)S(1)}, u32[]{:S(2)}, u32[]{:S(2)}) collective-permute-start(bf16[32,8320]{1,0:T(8,128)(2,1)} %get-tuple-element.51), channel_id=1, source_target_pairs={{0,64},{32,96},{64,0},{96,32},{1,65},{33,97},{65,1},{97,33},{2,66}... | collective-permute-start | bytes 1597448 | tf_op jit(solution)/shard_map/ppermute | solution.py:362
  6.3 21.1 %copy-start.7 = (f32[2,32]{1,0:T(2,128)S(1)}, f32[2,32]{1,0:T(2,128)}, u32[]{:S(2)}) copy-start(f32[2,32]{1,0:T(2,128)} %param.23) | copy-start | bytes 772
  6.4 24.5 %copy-start = (bf16[32,16512]{1,0:T(8,128)(2,1)S(1)}, bf16[32,16512]{1,0:T(8,128)(2,1)}, u32[]{:S(2)}) copy-start(bf16[32,16512]{1,0:T(8,128)(2,1)} %refs_5_.3) | copy-start | bytes 3170308
  27.6 3.2 %collective-permute-start.4 = (bf16[32,8320]{1,0:T(8,128)(2,1)S(1)}, bf16[32,8320]{1,0:T(8,128)(2,1)S(1)}, u32[]{:S(2)}, u32[]{:S(2)}) collective-permute-start(bf16[32,8320]{1,0:T(8,128)(2,1)S(1)} %collective-permute-done.3.refs_3_.refs_7_), channel_id=1, source_target_pairs={{0,32},{32,0},{64,96},{96,64},{1,33},{33,1},{65,97},{97,65},{2,34}... | collective-permute-start | bytes 1597448 | tf_op jit(solution)/shard_map/ppermute | solution.py:362
  29.9 15.2 %collective-permute-start.2 = (bf16[32,8320]{1,0:T(8,128)(2,1)S(1)}, bf16[32,8320]{1,0:T(8,128)(2,1)S(1)}, u32[]{:S(2)}, u32[]{:S(2)}) collective-permute-start(bf16[32,8320]{1,0:T(8,128)(2,1)S(1)} %collective-permute-done.1.refs_3_.refs_7_), channel_id=1, source_target_pairs={{0,32},{32,0},{64,96},{96,64},{1,33},{33,1},{65,97},{97,65},{2,34}... | collective-permute-start | bytes 1597448 | tf_op jit(solution)/shard_map/ppermute | solution.py:362
  45.1 15.1 %copy-start.3 = (bf16[32,7168]{1,0:T(8,128)(2,1)}, bf16[32,7168]{1,0:T(8,128)(2,1)S(1)}, u32[]{:S(2)}) copy-start(bf16[32,7168]{1,0:T(8,128)(2,1)S(1)} %get-tuple-element.30.e0) | copy-start | bytes 1376260
  60.2 54.8 %copy-start.4 = (bf16[32,7168]{1,0:T(8,128)(2,1)S(1)}, bf16[32,7168]{1,0:T(8,128)(2,1)}, u32[]{:S(2)}) copy-start(bf16[32,7168]{1,0:T(8,128)(2,1)} %copy-done.3) | copy-start | bytes 1376260
  60.2 7.7 %collective-permute-start.7 = (f32[2,128,128]{2,1,0:T(8,128)S(1)}, f32[2,128,128]{2,1,0:T(8,128)S(1)}, u32[]{:S(2)}, u32[]{:S(2)}) collective-permute-start(f32[2,128,128]{2,1,0:T(8,128)S(1)} %constant_dynamic-update-slice_fusion), channel_id=1, source_target_pairs={{64,0},{65,1},{66,2},{67,3},{68,4},{69,5},{70,6},{71,7},{72,8},{73... | collective-permute-start | bytes 393224 | tf_op jit(solution)/shard_map/ppermute | solution.py:425
  63.0 6.8 %collective-permute-start.8 = (f32[2,128,128]{2,1,0:T(8,128)S(1)}, f32[2,128,128]{2,1,0:T(8,128)S(1)}, u32[]{:S(2)}, u32[]{:S(2)}) collective-permute-start(f32[2,128,128]{2,1,0:T(8,128)S(1)} %constant_dynamic-update-slice_fusion), channel_id=1, source_target_pairs={{1,0},{0,1},{3,2},{2,3},{5,4},{4,5},{7,6},{6,7},{9,8},{8,9},{11,10... | collective-permute-start | bytes 393224 | tf_op jit(solution)/shard_map/ppermute | solution.py:425
  63.3 6.5 %collective-permute-start.9 = (f32[2,128,128]{2,1,0:T(8,128)S(1)}, f32[2,128,128]{2,1,0:T(8,128)S(1)}, u32[]{:S(2)}, u32[]{:S(2)}) collective-permute-start(f32[2,128,128]{2,1,0:T(8,128)S(1)} %constant_dynamic-update-slice_fusion), channel_id=1, source_target_pairs={{65,0},{64,1},{67,2},{66,3},{69,4},{68,5},{71,6},{70,7},{73,8},{72... | collective-permute-start | bytes 393224 | tf_op jit(solution)/shard_map/ppermute | solution.py:425
  64.8 48.6 %collective-permute-start.6 = (bf16[32,9216]{1,0:T(8,128)(2,1)S(1)}, bf16[32,9216]{1,0:T(8,128)(2,1)S(1)}, u32[]{:S(2)}, u32[]{:S(2)}) collective-permute-start(bf16[32,9216]{1,0:T(8,128)(2,1)S(1)} %get-tuple-element.25.e0), channel_id=1, source_target_pairs={{0,64},{32,96},{64,0},{96,32},{1,65},{33,97},{65,1},{97,33},{2,66}... | collective-permute-start | bytes 1769480 | tf_op jit(solution)/shard_map/ppermute | solution.py:362
  67.3 47.8 %collective-permute-start.16 = (bf16[32,7168]{1,0:T(8,128)(2,1)}, bf16[32,7168]{1,0:T(8,128)(2,1)}, u32[]{:S(2)}, u32[]{:S(2)}) collective-permute-start(bf16[32,7168]{1,0:T(8,128)(2,1)} %copy-done.3), channel_id=1, source_target_pairs={{0,64},{32,96},{64,0},{96,32},{1,65},{33,97},{65,1},{97,33},{2,66}... | collective-permute-start | bytes 1376264 | tf_op jit(solution)/shard_map/ppermute | solution.py:362
  69.9 16.7 %collective-permute-start.11 = (f32[3,128,128]{2,1,0:T(8,128)S(1)}, f32[3,128,128]{2,1,0:T(8,128)S(1)}, u32[]{:S(2)}, u32[]{:S(2)}) collective-permute-start(f32[3,128,128]{2,1,0:T(8,128)S(1)} %pad_maximum_fusion.1), channel_id=1, source_target_pairs={{2,0},{3,1},{4,2},{5,3},{6,4},{7,5},{8,6},{9,7},{10,8},{11,9},{12,... | collective-permute-start | bytes 589832 | tf_op jit(solution)/shard_map/ppermute | solution.py:433
  75.8 10.8 %collective-permute-start.10 = (f32[3,128,128]{2,1,0:T(8,128)S(1)}, f32[3,128,128]{2,1,0:T(8,128)S(1)}, u32[]{:S(2)}, u32[]{:S(2)}) collective-permute-start(f32[3,128,128]{2,1,0:T(8,128)S(1)} %pad_maximum_fusion), channel_id=1, source_target_pairs={{0,2},{1,3},{2,4},{3,5},{4,6},{5,7},{6,8},{7,9},{8,10},{9,11},{10,... | collective-permute-start | bytes 589832 | tf_op jit(solution)/shard_map/ppermute | solution.py:433
  79.2 7.4 %collective-permute-start.12 = (f32[128,128]{1,0:T(8,128)S(1)}, f32[128,128]{1,0:T(8,128)S(1)}, u32[]{:S(2)}, u32[]{:S(2)}) collective-permute-start(f32[128,128]{1,0:T(8,128)S(1)} %get-tuple-element.52), channel_id=1, source_target_pairs={{0,4},{2,6},{4,8},{5,1},{6,10},{7,3},{8,12},{9,5},{10,14},{11,7},{... | collective-permute-start | bytes 196616 | tf_op jit(solution)/shard_map/ppermute | solution.py:438
  87.3 26.2 %collective-permute-start.13 = (f32[2,128,128]{2,1,0:T(8,128)S(1)}, f32[2,128,128]{2,1,0:T(8,128)S(1)}, u32[]{:S(2)}, u32[]{:S(2)}) collective-permute-start(f32[2,128,128]{2,1,0:T(8,128)S(1)} %shard_map.121.n0), channel_id=1, source_target_pairs={{0,32},{32,0},{64,96},{96,64},{1,33},{33,1},{65,97},{97,65},{2,34}... | collective-permute-start | bytes 393224 | tf_op jit(solution)/shard_map/ppermute | solution.py:362
  113.4 9.9 %collective-permute-start.5 = (bf16[32,9216]{1,0:T(8,128)(2,1)S(1)}, bf16[32,9216]{1,0:T(8,128)(2,1)S(1)}, u32[]{:S(2)}, u32[]{:S(2)}) collective-permute-start(bf16[32,9216]{1,0:T(8,128)(2,1)S(1)} %get-tuple-element.25.e0), channel_id=1, source_target_pairs={{0,32},{32,0},{64,96},{96,64},{1,33},{33,1},{65,97},{97,65},{2,34}... | collective-permute-start | bytes 1769480 | tf_op jit(solution)/shard_map/ppermute | solution.py:362
  113.5 9.7 %collective-permute-start.14 = (bf16[32,9216]{1,0:T(8,128)(2,1)S(1)}, bf16[32,9216]{1,0:T(8,128)(2,1)S(1)}, u32[]{:S(2)}, u32[]{:S(2)}) collective-permute-start(bf16[32,9216]{1,0:T(8,128)(2,1)S(1)} %collective-permute-done.6.e2), channel_id=1, source_target_pairs={{0,32},{32,0},{64,96},{96,64},{1,33},{33,1},{65,97},{97,65},{2,34}... | collective-permute-start | bytes 1769480 | tf_op jit(solution)/shard_map/ppermute | solution.py:362
  114.9 2.8 %collective-permute-start.15 = (bf16[32,7168]{1,0:T(8,128)(2,1)S(1)}, bf16[32,7168]{1,0:T(8,128)(2,1)}, u32[]{:S(2)}, u32[]{:S(2)}) collective-permute-start(bf16[32,7168]{1,0:T(8,128)(2,1)S(1)} %copy-done.4), channel_id=1, source_target_pairs={{0,32},{32,0},{64,96},{96,64},{1,33},{33,1},{65,97},{97,65},{2,34}... | collective-permute-start | bytes 1376264 | tf_op jit(solution)/shard_map/ppermute | solution.py:362
  115.1 2.8 %collective-permute-start.17 = (bf16[32,7168]{1,0:T(8,128)(2,1)}, bf16[32,7168]{1,0:T(8,128)(2,1)}, u32[]{:S(2)}, u32[]{:S(2)}) collective-permute-start(bf16[32,7168]{1,0:T(8,128)(2,1)} %collective-permute-done.16.e2), channel_id=1, source_target_pairs={{0,32},{32,0},{64,96},{96,64},{1,33},{33,1},{65,97},{97,65},{2,34}... | collective-permute-start | bytes 1376264 | tf_op jit(solution)/shard_map/ppermute | solution.py:362
  (6 other events, 26.9 us)

commit v4 on v3

v4 whole, which is shorter than its diff:
```python
import functools

import jax
import jax.numpy as jnp
from jax import lax
from jax.experimental import pallas as pl
from jax.experimental.pallas import tpu as pltpu
from jax.sharding import PartitionSpec as P

BLK = 128
TG = 32
GW = TG * BLK
SUB = 8
SW = SUB * BLK
HALO = 3
SPLITS = (0, 2, 4)
VMEM_LIMIT = 48 * 1024 * 1024


def cubic_terms(frac):
    f2 = frac * frac
    f3 = f2 * frac
    return [
        -0.5 * f3 + f2 - 0.5 * frac,
        1.5 * f3 - 2.5 * f2 + 1.0,
        -1.5 * f3 + 2.0 * f2 + 0.5 * frac,
        0.5 * f3 - 0.5 * f2,
    ]


def linear_terms(frac):
    zeros = jnp.zeros_like(frac)
    return [zeros, 1.0 - frac, frac, zeros]


def row_matrix(offsets, fracs, columns, terms):
    total = jnp.zeros((offsets.shape[0], columns.shape[0]), jnp.float32)
    for index, weight in enumerate(terms(fracs)):
        hit = (columns[None, :] == offsets[:, None] + index).astype(jnp.float32)
        total = total + weight[:, None] * hit
    return total.astype(jnp.bfloat16)


def tap_weights(kind, frac):
    taps = [
        jnp.where(kind == 1, wc, wl)
        for wc, wl in zip(cubic_terms(frac), linear_terms(frac))
    ]
    return lax.reduce_precision(jnp.stack(taps), 8, 7)


NT = (((1,), (1,)), ((), ()))


def tables_kernel(shift_ref, tap_ref, couple_ref, inv_ref, t_ref, corr_ref, a_ref, b_ref):
    step = pl.program_id(0)
    shape = (2 * BLK, BLK)
    delta = lax.broadcasted_iota(jnp.int32, shape, 0) - lax.broadcasted_iota(jnp.int32, shape, 1)
    place = lax.broadcasted_iota(jnp.int32, (16, BLK), 0) * (BLK - 1)
    units = (place == lax.broadcasted_iota(jnp.int32, (16, BLK), 1)).astype(jnp.bfloat16)
    row = lax.broadcasted_iota(jnp.int32, (2 * SUB, BLK), 0)
    for i in range(TG):
        tile = step * TG + i
        tap = delta - shift_ref[tile]
        total = jnp.zeros(shape, jnp.float32)
        for k in range(4):
            total = jnp.where(tap == k, tap_ref[k, tile], total)
        t_ref[i] = total.astype(jnp.bfloat16)
        hi, lo = split_hi_lo(inv_ref[i])
        ends = lax.dot_general(units, hi, NT, preferred_element_type=jnp.float32)
        ends = ends + lax.dot_general(units, lo, NT, preferred_element_type=jnp.float32)
        a = couple_ref[0, tile] * ends[0:1, :]
        b = couple_ref[1, tile] * ends[1:2, :]
        a_ref[i : i + 1, :] = a
        b_ref[i : i + 1, :] = b
        q, r = divmod(i, SUB)
        both = jnp.where(row == r, a, jnp.where(row == SUB + r, b, 0.0))
        corr_ref[q, :, r * BLK : (r + 1) * BLK] = both.astype(jnp.bfloat16)


def run_tables(shift, taps, couple, inverse):
    tiles = inverse.shape[0]
    cube = lambda *shape: pl.BlockSpec((TG, *shape), lambda l, *_: (l,) + (0,) * len(shape))
    return pl.pallas_call(
        tables_kernel,
        grid_spec=pltpu.PrefetchScalarGridSpec(
            num_scalar_prefetch=3,
            grid=(tiles // TG,),
            in_specs=[cube(BLK, BLK)],
            out_specs=[
                cube(2 * BLK, BLK),
                pl.BlockSpec((TG // SUB, 2 * SUB, SW), lambda l, *_: (l, 0, 0)),
                cube(BLK),
                cube(BLK),
            ],
        ),
        out_shape=[
            jax.ShapeDtypeStruct((tiles, 2 * BLK, BLK), jnp.bfloat16),
            jax.ShapeDtypeStruct((tiles // SUB, 2 * SUB, SW), jnp.bfloat16),
            jax.ShapeDtypeStruct((tiles, BLK), jnp.float32),
            jax.ShapeDtypeStruct((tiles, BLK), jnp.float32),
        ],
        compiler_params=pltpu.CompilerParams(vmem_limit_bytes=VMEM_LIMIT),
    )(shift, taps, couple, inverse)


def table_hi_lo(value):
    hi = lax.reduce_precision(value, 8, 7)
    return hi.astype(jnp.bfloat16), (value - hi).astype(jnp.bfloat16)


def split_hi_lo(value):
    hi = value.astype(jnp.bfloat16)
    lo = (value - hi.astype(jnp.float32)).astype(jnp.bfloat16)
    return hi, lo


def rows_kernel(first, groups, carried, *refs):
    kind_ref, p0, p1, p2, p3, q0, q1, q2, q3, w_ref, t_ref, mask_ref, bg_ref, inv_ref = refs[:14]
    coef_ref, corr_ref, yw_ref = refs[14:17]
    refs = refs[17:]
    if carried:
        u_in, f_in, l_in = refs[:3]
        refs = refs[3:]
    out_ref, part_ref, u_out, f_out, l_out, sec, u_st, f_st, l_st = refs
    step = pl.program_id(0)
    s = step + first
    lane = lax.broadcasted_iota(jnp.int32, (32, BLK), 1)
    roll = lambda value, by: pltpu.roll(value, by % BLK, 1)

    @pl.when(step == 0)
    def _():
        if carried:
            u_st[TG:] = u_in[...]
            f_st[...] = f_in[...]
            l_st[...] = l_in[...]
        else:
            u_st[...] = jnp.zeros_like(u_st)
            f_st[...] = jnp.zeros_like(f_st)
            l_st[...] = jnp.zeros_like(l_st)

    u_st[:SUB] = u_st[TG:]
    rows = jnp.concatenate([p0[...], p1[...], p2[...], p3[...]], axis=0)
    edge = jnp.concatenate([q0[...], q1[...], q2[...], q3[...]], axis=0)
    w = w_ref[...]
    both = jnp.dot(w, rows, preferred_element_type=jnp.float32).astype(jnp.bfloat16)
    tail = jnp.dot(w, edge, preferred_element_type=jnp.float32).astype(jnp.bfloat16)
    for k in range(2):
        sec[k, :, :GW] = both[k * 32 : (k + 1) * 32]
        sec[k, :, GW:] = tail[k * 32 : (k + 1) * 32]
    f = jnp.where(lane < HALO + SUB, roll(f_st[...], -TG), 0.0)
    l = jnp.where(lane < HALO + SUB, roll(l_st[...], -TG), 0.0)
    for at in range(0, TG, SUB):
        tiles = range(at, at + SUB)
        ests = []
        for i in tiles:
            kind = kind_ref[s * TG + i]
            taken = sec[kind, :, i * BLK : (i + 2) * BLK]
            ests.append(jnp.dot(taken, t_ref[i], preferred_element_type=jnp.float32))
        sides = []
        for i in tiles:
            cols = slice(i * BLK, (i + 1) * BLK)
            misfit = mask_ref[:, cols].astype(jnp.float32) * (ests[i - at] - bg_ref[:, cols])
            sides.append(jnp.concatenate(split_hi_lo(misfit), axis=0))
        solved = []
        for i in tiles:
            pair = jnp.concatenate(split_hi_lo(inv_ref[i]), axis=0)
            solved.append(
                lax.dot_general(sides[i - at], pair, NT, preferred_element_type=jnp.float32)
            )
        for i in tiles:
            u = solved[i - at]
            u = u[:32, :BLK] + (u[32:, :BLK] + u[:32, BLK:])
            u_st[SUB + i] = u
            here = lane == HALO + SUB + i
            f = jnp.where(here, u[:, :1], f)
            l = jnp.where(here, u[:, BLK - 1 :], l)
    f_st[...] = f
    l_st[...] = l

    af, cf, al, cl = [coef_ref[r, pl.ds(s, 1), :] for r in range(4)]

    def sweep(f, l):
        west, east = roll(l, 1), roll(f, -1)
        return f_st[...] + af * west + cf * east, l_st[...] + al * west + cl * east

    f2, l2 = sweep(*sweep(f, l))

    def finish(q):
        low = HALO + q * SUB
        ends = jnp.where(lane < SUB, roll(l2, 1 - low), roll(f2, SUB - 1 - low))
        ends = ends[:, : 2 * SUB].astype(jnp.bfloat16)
        sub = s * (TG // SUB) - 1 + q
        fix = jnp.dot(ends, corr_ref[sub], preferred_element_type=jnp.float32)
        spot = step * (TG // SUB) + q - (0 if carried else 1)
        outs = []
        for i in range(SUB):
            cols = slice(i * BLK, (i + 1) * BLK)
            outs.append((u_st[q * SUB + i] + fix[:, cols]).astype(jnp.bfloat16))
        value = jnp.concatenate(outs, axis=1)
        out_ref[:, pl.ds(pl.multiple_of(spot * SW, SW), SW)] = value
        tips = jnp.dot(yw_ref[...], value, preferred_element_type=jnp.float32)
        tips = tips[0:8] + tips[8:16]
        for k in range(2):
            lines = [tips[k : k + 1, i * BLK : (i + 1) * BLK] for i in range(SUB)]
            place = pl.ds(pl.multiple_of(spot * SUB, SUB), SUB)
            part_ref[k, place, :] = jnp.concatenate(lines, axis=0)

    if carried:
        finish(0)
    else:
        pl.when(step > 0)(lambda: finish(0))
    for q in range(1, TG // SUB):
        finish(q)
    pl.when(s == groups - 1)(lambda: finish(TG // SUB))

    @pl.when(step == pl.num_programs(0) - 1)
    def _():
        u_out[...] = u_st[TG:]
        f_out[...] = f_st[...]
        l_out[...] = l_st[...]


def run_rows(first, stop, groups, state, kinds, own, got, w, tables, mask, bg, inv, coefs, corr, yw):
    carried = state is not None
    steps = stop - first
    width = steps * GW - (0 if carried else SW) + (SW if stop == groups else 0)
    near, far, away = got
    full = lambda *shape: pl.BlockSpec(shape, lambda l, *_: (0,) * len(shape))
    wide = lambda off: pl.BlockSpec((32, GW), lambda l, *_: (0, l + off))
    edge = lambda off: pl.BlockSpec((32, BLK), lambda l, *_: (0, (l + off + 1) * TG))
    cube = lambda *shape: pl.BlockSpec((TG, *shape), lambda l, *_: (l + first, 0, 0))
    in_specs = [wide(first), wide(first), wide(0), wide(0)]
    in_specs += [edge(first), edge(first), edge(0), edge(0)]
    in_specs += [
        full(64, BLK),
        cube(2 * BLK, BLK),
        wide(first),
        wide(first),
        cube(BLK, BLK),
        full(*coefs.shape),
        full(*corr.shape),
        full(16, 32),
    ]
    keep = [
        jax.ShapeDtypeStruct((SUB, 32, BLK), jnp.float32),
        jax.ShapeDtypeStruct((32, BLK), jnp.float32),
        jax.ShapeDtypeStruct((32, BLK), jnp.float32),
    ]
    operands = [kinds, own, near, far, away, own, near, far, away, w, tables, mask, bg, inv]
    operands += [coefs, corr, yw]
    if carried:
        in_specs += [full(*k.shape) for k in keep]
        operands += list(state)
    grid_spec = pltpu.PrefetchScalarGridSpec(
        num_scalar_prefetch=1,
        grid=(steps,),
        in_specs=in_specs,
        out_specs=[full(32, width), full(2, width // BLK, BLK), *[full(*k.shape) for k in keep]],
        scratch_shapes=[
            pltpu.VMEM((2, 32, GW + BLK), jnp.bfloat16),
            pltpu.VMEM((SUB + TG, 32, BLK), jnp.float32),
            pltpu.VMEM((32, BLK), jnp.float32),
            pltpu.VMEM((32, BLK), jnp.float32),
        ],
    )
    outs = pl.pallas_call(
        functools.partial(rows_kernel, first, groups, carried),
        grid_spec=grid_spec,
        out_shape=[
            jax.ShapeDtypeStruct((32, width), jnp.bfloat16),
            jax.ShapeDtypeStruct((2, width // BLK, BLK), jnp.float32),
            *keep,
        ],
        compiler_params=pltpu.CompilerParams(vmem_limit_bytes=VMEM_LIMIT),
    )(*operands)
    return outs[0], outs[1], tuple(outs[2:])


def ends_kernel(blocks, block_ref, corner_ref, own, other, below, above, distant, out):
    block = block_ref[0]
    pair = block // 2
    before = jnp.where(pair > 0, below[...], 0.0)
    after = jnp.where(pair < blocks // 2 - 1, above[...], 0.0)
    inside = jnp.where(lax.rem(block, 2) == 1, pair < blocks // 2 - 2, pair > 1)
    beyond = jnp.where(inside, distant[...], 0.0)
    second = lax.rem(block, 2) == 1
    pick = lambda even, odd: jnp.where(second, odd, even)
    coef = lambda r, k: corner_ref[r, block + HALO + k]
    f = {0: own[0], -1: pick(before[1], other[0]), 1: pick(other[0], after[0])}
    l = {0: own[1], -1: pick(before[2], other[1]), 1: pick(other[1], after[1])}
    l[-2], l[-3] = pick(before[0], before[2]), pick(beyond, before[0])
    f[2], f[3] = pick(after[0], after[2]), pick(after[2], beyond)
    last = lambda k, west, east: l[k] + coef(2, k) * west + coef(3, k) * east
    head = lambda k, west, east: f[k] + coef(0, k) * west + coef(1, k) * east
    out[0] = last(-1, last(-2, l[-3], f[-1]), head(0, l[-1], f[1]))
    out[1] = head(1, last(0, l[-1], f[1]), head(2, l[1], f[3]))


def run_ends(blocks, block, corner, own, *others):
    smem = pl.BlockSpec(memory_space=pltpu.SMEM)
    vmem = pl.BlockSpec(memory_space=pltpu.VMEM)
    return pl.pallas_call(
        functools.partial(ends_kernel, blocks),
        in_specs=[smem, smem] + [vmem] * 5,
        out_specs=vmem,
        out_shape=jax.ShapeDtypeStruct(own.shape, own.dtype),
        compiler_params=pltpu.CompilerParams(vmem_limit_bytes=VMEM_LIMIT),
    )(block.reshape(1), corner, own, *others)


def columns_kernel(start, w_ref, ends_ref, e0, e1, e2, e3, n0, n1, *rest):
    out_ref, held, sems = rest[-3:]
    south, north = ends_ref[:, 0:1], ends_ref[:, 1:2]
    copies = []
    for at in range(0, held.shape[1], SW):
        cols = slice(at, at + SW)
        rows = jnp.concatenate([e[:, cols] for e in (e0, e1, e2, e3)], axis=0)
        both = jnp.dot(w_ref[...], rows, preferred_element_type=jnp.float32)
        value = both[:32] + both[32:]
        for i in range(SUB):
            line = (start + at) // BLK + i
            row = [n0[k, line : line + 1, :] + n1[k, line : line + 1, :] for k in range(2)]
            here = slice(i * BLK, (i + 1) * BLK)
            held[:, at + i * BLK : at + (i + 1) * BLK] = (
                value[:, here] + south * row[0] + north * row[1]
            )
        copy = pltpu.make_async_copy(
            held.at[:, cols], out_ref.at[:, start + at : start + at + SW], sems.at[at // SW]
        )
        copy.start()
        copies.append(copy)
    for copy in copies:
        copy.wait()


def run_columns(start, total, w, ends, pieces, near, far, so_far):
    width = pieces[0].shape[1]
    vmem = pl.BlockSpec(memory_space=pltpu.VMEM)
    operands = [w, ends, *pieces, near, far]
    in_specs = [vmem] * 8
    aliases = {}
    if so_far is not None:
        operands.append(so_far)
        in_specs.append(pl.BlockSpec(memory_space=pl.ANY))
        aliases = {8: 0}
    return pl.pallas_call(
        functools.partial(columns_kernel, start),
        in_specs=in_specs,
        out_specs=pl.BlockSpec(memory_space=pl.ANY),
        out_shape=jax.ShapeDtypeStruct((32, total), jnp.float32),
        scratch_shapes=[
            pltpu.VMEM((32, width), jnp.float32),
            pltpu.SemaphoreType.DMA((width // SW,)),
        ],
        input_output_aliases=aliases,
        compiler_params=pltpu.CompilerParams(vmem_limit_bytes=VMEM_LIMIT),
    )(*operands)


def body(
    panels,
    void_mask,
    background,
    row_offset,
    row_frac,
    tile_kind,
    tile_shift,
    tile_frac,
    inverse_x,
    couple_x,
    inverse_y,
    couple_y,
):
    rows = row_offset.shape[0]
    width = background.shape[1]
    groups = width // GW
    n_wide = lax.axis_size("wide")
    mine = lax.axis_index("band")
    block = lax.axis_index("wide")
    across = [(d, d ^ 2) for d in range(4)]
    sibling = [(d, d ^ 1) for d in range(4)]
    swap = lambda value, pairs: lax.ppermute(value, "band", pairs)

    near = swap(panels, sibling)
    bounds = [(SPLITS[i], SPLITS[i + 1]) for i in range(len(SPLITS) - 1)]
    gathered = []
    for first, stop in bounds:
        far = swap(panels[:, first * GW : stop * GW + BLK], across)
        gathered.append(far)

    order = ((jnp.arange(4, dtype=jnp.int32) ^ mine)[:, None] * rows + jnp.arange(rows)[None, :]).reshape(-1)
    w = jnp.concatenate(
        [
            row_matrix(row_offset, row_frac, order, linear_terms),
            row_matrix(row_offset, row_frac, order, cubic_terms),
        ],
        axis=0,
    )
    kinds = (tile_kind == 1).astype(jnp.int32)
    tables, corr, a_x, b_x = run_tables(
        tile_shift, tap_weights(tile_kind, tile_frac), couple_x, inverse_x
    )
    coefs = jnp.stack([a_x[:, 0], b_x[:, 0], a_x[:, -1], b_x[:, -1]])
    coefs = jnp.pad(coefs, ((0, 0), (SUB + HALO, TG - SUB - HALO))).reshape(4, groups + 1, TG)
    coefs = jnp.concatenate([coefs[:, :-1], coefs[:, 1:]], axis=2)
    coefs = jnp.pad(coefs, ((0, 0), (0, 0), (0, BLK - 2 * TG)))

    tips = inverse_y[:, :: BLK - 1, :: BLK - 1] * couple_y.T[:, None, :]
    corner = jnp.stack([tips[:, 0, 0], tips[:, 0, 1], tips[:, 1, 0], tips[:, 1, 1]])
    corner = jnp.pad(corner, ((0, 0), (HALO, HALO)))
    own_inv = lax.dynamic_index_in_dim(inverse_y, block, 0, keepdims=False)
    at = mine * rows
    own_rows = lax.dynamic_slice_in_dim(own_inv, at, rows, 0)
    shuffled = jnp.concatenate(
        [lax.dynamic_slice_in_dim(own_rows, (q ^ mine) * rows, rows, 1) for q in range(4)], axis=1
    )
    w_y = jnp.concatenate(table_hi_lo(shuffled), axis=0)
    ends_y = jnp.stack(
        [
            couple_y[0, block] * own_rows[:, 0],
            couple_y[1, block] * own_rows[:, -1],
        ],
        axis=1,
    )
    end_rows = lax.dynamic_slice_in_dim(jnp.stack([own_inv[0], own_inv[-1]]), at, rows, 1)
    end_hi, end_lo = table_hi_lo(end_rows)
    gap = jnp.zeros((6, rows), jnp.bfloat16)
    yw = jnp.concatenate([end_hi, gap, end_lo, gap], axis=0)

    state = None
    sent = []
    parts = []
    for (first, stop), far in zip(bounds, gathered):
        if state is not None:
            far, state = lax.optimization_barrier((far, state))
        got = (near, far, swap(far, sibling))
        east_west, part, state = run_rows(
            first, stop, groups, state, kinds, panels, got, w, tables,
            void_mask, background, inverse_x, coefs, corr, yw,
        )
        far = swap(east_west, across)
        sent.append([east_west, swap(east_west, sibling), far])
        parts.append(part)
    part = jnp.concatenate(parts, axis=1) if len(parts) > 1 else parts[0]
    if len(sent) > 1:
        part, sent[0][2] = lax.optimization_barrier((part, sent[0][2]))

    every = [(d, k) for d in range(4) for k in range(n_wide)]
    at = lambda d, k: d * n_wide + k
    fetch = lambda db, dw: lax.ppermute(
        part, ("band", "wide"), [(at(d ^ db, k ^ dw), at(d, k)) for d, k in every]
    )
    second = block % 2
    own = part + fetch(2, 0)
    other = fetch(0, 1) + fetch(2, 1)
    even = jnp.where(second == 0, own, other)
    odd = jnp.where(second == 0, other, own)
    shifted = lambda value, k: lax.ppermute(
        value, "wide", [(i, (i + 2 * k) % n_wide) for i in range(n_wide)]
    )
    before = shifted(jnp.stack([even[1], odd[0], odd[1]]), 1)
    after = shifted(jnp.stack([even[0], even[1], odd[0]]), -1)
    beyond = lax.ppermute(
        jnp.where(second == 0, odd[1], even[0]),
        "wide",
        [(i, (i + 4 * (1 - 2 * (i % 2))) % n_wide) for i in range(n_wide)],
    )
    forced = run_ends(n_wide, block, corner, own, other, before, after, beyond)
    rest = swap(forced, sibling)
    sent[-1][2], rest = lax.optimization_barrier((sent[-1][2], rest))

    result = None
    position = 0
    for pieces in sent:
        pieces = (*pieces, swap(pieces[2], sibling))
        result = run_columns(position, width, w_y, ends_y, pieces, forced, rest, result)
        position += pieces[0].shape[1]
    return result


def solution(mesh):
    placed = (
        P(("wide", "band"), None),
        P(("wide", "band"), None),
        P(("wide", "band"), None),
        P(("wide", "band")),
        P(("wide", "band")),
        P(),
        P(),
        P(),
        P(),
        P(),
        P(),
        P(),
    )
    return jax.shard_map(
        body, mesh=mesh, in_specs=placed, out_specs=P(("wide", "band"), None), check_vma=False
    )
```

time: 129 us -> 94 us (0.73)
  the two profiles are of different devices: /device:TPU:25 before, /device:TPU:1 now
where the time goes in v4:
time: 94 us; the launch traced here: 93.4 us
  Pallas kernels  38.2 us (41%)
  starting transfers between devices  24.2 us (26%)
  waiting for transfers between devices  15.9 us (17%)
  local copies, waits for them, and re-layouts  12.9 us (14%)
  other arithmetic  1.96 us (2%)
    pallas_call x2, Pallas kernels, run_rows(): pl.pallas_call(functools.partial(rows_kernel, first, groups, carried), gr...  19 us
    ppermute x12, starting transfers between devices, body(): swap = lambda value, pairs: lax.ppermute(value, 'band', pairs)  14.5 us
    pallas_call x1, Pallas kernels, run_tables(): pl.pallas_call(tables_kernel, grid_spec=pltpu.PrefetchScalarGridSpec(num_...  13.8 us
    ppermute x1, waiting for transfers between devices, body(): lax.ppermute(jnp.where(second == 0, odd[1], even[0]), 'wide', [(i, (i + 4...  7.34 us
    ppermute x2, starting transfers between devices, body(): lax.ppermute(value, 'wide', [(i, (i + 2 * k) % n_wide) for i in range(n_w...  6.34 us
    ppermute x3, waiting for transfers between devices, body(): lax.ppermute(part, ('band', 'wide'), [(at(d ^ db, k ^ dw), at(d, k)) for...  4.95 us
    pallas_call x2, Pallas kernels, run_columns(): pl.pallas_call(functools.partial(columns_kernel, start), in_specs=in_spec...  4.68 us
    ppermute x12, waiting for transfers between devices, body(): swap = lambda value, pairs: lax.ppermute(value, 'band', pairs)  3.46 us
  transfers between devices with their start and end apart: 18, of which 7 were waited for; matrix products, arithmetic and copies ran while one was open for 13% of the time, Pallas kernels for 38%

profile of v4, /device:TPU:1, one launch (start us, length us, event | category | flops | bytes accessed | tf_op | source)
XLA Modules:
  0.0 93.4 jit_solution(1030313691507823463)
XLA Ops:
  0.0 1.5 %collective-permute-start = (bf16[32,16512]{1,0:T(8,128)(2,1)}, bf16[32,16512]{1,0:T(8,128)(2,1)S(1)}, u32[]{:S(2)}, u32[]{:S(2)}) collective-permute-start(bf16[32,16512]{1,0:T(8,128)(2,1)} %refs_5_.3), channel_id=1, source_target_pairs={{0,32},{32,0},{64,96},{96,64},{1,33},{33,1},{65,97},{97,65},{2,34}... | collective-permute-start | bytes 3170312 | tf_op jit(solution)/shard_map/ppermute | solution.py:383
  1.5 2.3 %fusion.14 = (bf16[32,8320]{1,0:T(8,128)(2,1)}, bf16[32,8320]{1,0:T(8,128)(2,1)}) fusion(bf16[32,16512]{1,0:T(8,128)(2,1)} %refs_5_.3), kind=kLoop, calls=%fused_computation.85 | loop fusion | bytes 2129920 | tf_op jit(solution)/shard_map/slice | solution.py:389
  3.8 2.8 %collective-permute-start.2 = (bf16[32,8320]{1,0:T(8,128)(2,1)}, bf16[32,8320]{1,0:T(8,128)(2,1)S(1)}, u32[]{:S(2)}, u32[]{:S(2)}) collective-permute-start(bf16[32,8320]{1,0:T(8,128)(2,1)} %get-tuple-element.62), channel_id=1, source_target_pairs={{0,64},{32,96},{64,0},{96,32},{1,65},{33,97},{65,1},{97,33},{2,66}... | collective-permute-start | bytes 1597448 | tf_op jit(solution)/shard_map/ppermute | solution.py:383
  6.9 13.8 %shard_map.118 = (bf16[128,256,128]{2,1,0:T(8,128)(2,1)}, bf16[16,16,1024]{2,1,0:T(8,128)(2,1)S(1)}, f32[128,128]{1,0:T(8,128)S(1)}, f32[128,128]{1,0:T(8,128)S(1)}) custom-call(s32[128]{0:T(128)S(1)} %copy-done.5, f32[4,128]{1,0:T(4,128)S(1)} %maximum_reduce-precision_fusion.tap_ref, f32[2,128]{1,0:T(2,128)S(1)} %copy-done.4, f32[128,128,128]{2,1,0:T(8,128)} %refs_13_.3), custom_call_target="tpu_custom_call" | custom-call | tf_op jit(solution)/shard_map/pallas_call | solution.py:84
  23.8 1.4 %collective-permute-done.3.refs_4_.refs_8_ = bf16[32,8320]{1,0:T(8,128)(2,1)S(1)} collective-permute-done((bf16[32,8320]{1,0:T(8,128)(2,1)S(1)}, bf16[32,8320]{1,0:T(8,128)(2,1)S(1)}, u32[]{:S(2)}, u32[]{:S(2)}) %collective-permute-start.3) | collective-permute-done | bytes 532512 | tf_op jit(solution)/shard_map/ppermute | solution.py:383
  25.2 1.0 %copy-done.2 = bf16[16,16,1024]{2,1,0:T(8,128)(2,1)S(1)} copy-done((bf16[16,16,1024]{2,1,0:T(8,128)(2,1)S(1)}, bf16[16,16,1024]{2,1,0:T(8,128)(2,1)}, u32[]{:S(2)}) %copy-start.2) | copy-done | bytes 524312
  26.3 9.3 %shard_map.119 = (bf16[32,7168]{1,0:T(8,128)(2,1)}, f32[2,56,128]{2,1,0:T(8,128)S(1)}, f32[8,32,128]{2,1,0:T(8,128)S(1)}, f32[32,128]{1,0:T(8,128)S(1)}, f32[32,128]{1,0:T(8,128)S(1)}) custom-call(s32[128]{0:T(128)S(1)} %fusion.13.refs_0_, bf16[32,16512]{1,0:T(8,128)(2,1)S(1)} %copy-done, bf16[32,16512]{1,0:T(8,128)(2,1)S(1)} %collective-permute-done.refs_2_.refs_6_, ...), custom_call_target="tpu_custom_call" | custom-call | tf_op jit(solution)/shard_map/pallas_call | solution.py:267
  36.0 2.8 %collective-permute-start.7 = (bf16[32,7168]{1,0:T(8,128)(2,1)}, bf16[32,7168]{1,0:T(8,128)(2,1)}, u32[]{:S(2)}, u32[]{:S(2)}) collective-permute-start(bf16[32,7168]{1,0:T(8,128)(2,1)} %get-tuple-element.38.e0), channel_id=1, source_target_pairs={{0,64},{32,96},{64,0},{96,32},{1,65},{33,97},{65,1},{97,33},{2,66}... | collective-permute-start | bytes 1376264 | tf_op jit(solution)/shard_map/ppermute | solution.py:383
  38.8 1.6 %slice.89 = f32[32,2,2]{2,1,0:T(2,128)S(1)} slice(f32[32,128,128]{2,1,0:T(8,128)} %param.22), slice={[0:32:1], [0:128:127], [0:128:127]} | slice | bytes 1024 | tf_op jit(solution)/shard_map/slice | solution.py:409
  40.6 1.3 %constant_dynamic-slice_fusion.3 = f32[1,32,128]{2,1,0:T(8,128)} fusion(f32[32,128,128]{2,1,0:T(8,128)} %param.22, s32[]{:T(128)S(6)} %select_n.74, s32[]{:T(128)S(6)} %select_n.76), kind=kLoop, calls=%fused_computation.58 | loop fusion | bytes 32776 | tf_op jit(solution)/shard_map/dynamic_slice | solution.py:414
  43.4 1.0 %copy-done.3 = bf16[16,16,1024]{2,1,0:T(8,128)(2,1)S(1)} copy-done((bf16[16,16,1024]{2,1,0:T(8,128)(2,1)S(1)}, bf16[16,16,1024]{2,1,0:T(8,128)(2,1)}, u32[]{:S(2)}) %copy-start.3) | copy-done | bytes 524312
  44.4 9.7 %shard_map.120 = (bf16[32,9216]{1,0:T(8,128)(2,1)}, f32[2,72,128]{2,1,0:T(8,128)S(1)}, f32[8,32,128]{2,1,0:T(8,128)}, f32[32,128]{1,0:T(8,128)}, f32[32,128]{1,0:T(8,128)}) custom-call(s32[128]{0:T(128)S(1)} %fusion.13.refs_0_, bf16[32,16512]{1,0:T(8,128)(2,1)S(1)} %copy-done, bf16[32,16512]{1,0:T(8,128)(2,1)S(1)} %collective-permute-done.refs_2_.refs_6_, ...), custom_call_target="tpu_custom_call" | custom-call | tf_op jit(solution)/shard_map/pallas_call | solution.py:267
  54.1 0.9 collective-permute-start.10
  55.0 1.2 %collective-permute-start.8 = (f32[2,128,128]{2,1,0:T(8,128)S(1)}, f32[2,128,128]{2,1,0:T(8,128)S(1)}, u32[]{:S(2)}, u32[]{:S(2)}) collective-permute-start(f32[2,128,128]{2,1,0:T(8,128)S(1)} %pad_maximum_fusion.2), channel_id=1, source_target_pairs={{64,0},{65,1},{66,2},{67,3},{68,4},{69,5},{70,6},{71,7},{72,8},{73... | collective-permute-start | bytes 393224 | tf_op jit(solution)/shard_map/ppermute | solution.py:451
  56.3 1.2 %collective-permute-start.9 = (f32[2,128,128]{2,1,0:T(8,128)S(1)}, f32[2,128,128]{2,1,0:T(8,128)S(1)}, u32[]{:S(2)}, u32[]{:S(2)}) collective-permute-start(f32[2,128,128]{2,1,0:T(8,128)S(1)} %pad_maximum_fusion.2), channel_id=1, source_target_pairs={{1,0},{0,1},{3,2},{2,3},{5,4},{4,5},{7,6},{6,7},{9,8},{8,9},{11,10... | collective-permute-start | bytes 393224 | tf_op jit(solution)/shard_map/ppermute | solution.py:451
  58.3 4.2 %collective-permute-done.10 = f32[2,128,128]{2,1,0:T(8,128)S(1)} collective-permute-done((f32[2,128,128]{2,1,0:T(8,128)S(1)}, f32[2,128,128]{2,1,0:T(8,128)S(1)}, u32[]{:S(2)}, u32[]{:S(2)}) %collective-permute-start.10) | collective-permute-done | bytes 131104 | tf_op jit(solution)/shard_map/ppermute | solution.py:451
  63.3 6.3 %collective-permute-start.12 = (f32[3,128,128]{2,1,0:T(8,128)S(1)}, f32[3,128,128]{2,1,0:T(8,128)S(1)}, u32[]{:S(2)}, u32[]{:S(2)}) collective-permute-start(f32[3,128,128]{2,1,0:T(8,128)S(1)} %pad_maximum_fusion.1), channel_id=1, source_target_pairs={{0,30},{1,31},{2,0},{3,1},{4,2},{5,3},{6,4},{7,5},{8,6},{9,7},{10,... | collective-permute-start | bytes 589832 | tf_op jit(solution)/shard_map/ppermute | solution.py:459
  70.8 7.3 %collective-permute-done.13.distant = f32[128,128]{1,0:T(8,128)S(1)} collective-permute-done((f32[128,128]{1,0:T(8,128)S(1)}, f32[128,128]{1,0:T(8,128)S(1)}, u32[]{:S(2)}, u32[]{:S(2)}) %collective-permute-start.13) | collective-permute-done | bytes 65568 | tf_op jit(solution)/shard_map/ppermute | solution.py:464
  78.9 4.2 %collective-permute-start.14 = (f32[2,128,128]{2,1,0:T(8,128)S(1)}, f32[2,128,128]{2,1,0:T(8,128)S(1)}, u32[]{:S(2)}, u32[]{:S(2)}) collective-permute-start(f32[2,128,128]{2,1,0:T(8,128)S(1)} %shard_map.121.n0), channel_id=1, source_target_pairs={{0,32},{32,0},{64,96},{96,64},{1,33},{33,1},{65,97},{97,65},{2,34}... | collective-permute-start | bytes 393224 | tf_op jit(solution)/shard_map/ppermute | solution.py:383
  83.1 1.2 %slice_multiply_fusion.1 = (f32[32,1]{0,1:T(1,128)S(1)}, f32[32,1]{0,1:T(1,128)S(1)}) fusion(f32[32,128]{0,1:T(8,128)S(1)} %bitcast.35, f32[]{:T(128)} %bitcast.4, f32[]{:T(128)} %bitcast.6), kind=kLoop, calls=%fused_computation.66 | loop fusion | flops 64 | bytes 520 | tf_op jit(solution)/shard_map/mul | solution.py:421
  84.9 1.0 %dynamic-slice_bitcast_fusion.3 = (f32[32,32]{1,0:T(8,128)S(1)}, f32[32,32]{1,0:T(8,128)S(1)}, f32[32,32]{1,0:T(8,128)S(1)}, f32[32,32]{1,0:T(8,128)S(1)}) fusion(f32[32,128,128]{2,1,0:T(8,128)} %param.22, s32[]{:T(128)S(6)} %select_n.74, s32[]{:T(128)S(6)} %select_n.76, s32[]{:T(128)S(6)} %select_n.82, s32[]{:T(128)S(6)} %select_n.80, s32[]{:T(128)S(6)} %select_n.78), kind=kLoop, calls=%fused_computation.35 | loop fusion | bytes 32788 | tf_op jit(solution)/shard_map/dynamic_slice | solution.py:416
  86.7 1.4 %collective-permute-done.16.e1 = bf16[32,7168]{1,0:T(8,128)(2,1)S(1)} collective-permute-done((bf16[32,7168]{1,0:T(8,128)(2,1)}, bf16[32,7168]{1,0:T(8,128)(2,1)S(1)}, u32[]{:S(2)}, u32[]{:S(2)}) %collective-permute-start.16) | collective-permute-done | bytes 458784 | tf_op jit(solution)/shard_map/ppermute | solution.py:383
  88.7 2.3 %shard_map.122.rest_0_ = f32[32,16384]{1,0:T(8,128)} custom-call(bf16[64,128]{1,0:T(8,128)(2,1)S(1)} %pad_maximum_fusion.4.w_ref, f32[32,2]{1,0:T(8,128)S(1)} %copy.19.ends_ref, bf16[32,7168]{1,0:T(8,128)(2,1)} %get-tuple-element.38.e0, bf16[32,7168]{1,0:T(8,128)(2,1)S(1)} %collective-permute-done.16.e1, bf16[32,7168]{1,0:T(8,128)(2,1)} %collective-permute-done.7.e2, ...), custom_call_target="tpu_custom_call" | custom-call | tf_op jit(solution)/shard_map/pallas_call | solution.py:347
  91.1 2.3 %shard_map.123 = f32[32,16384]{1,0:T(8,128)} custom-call(bf16[64,128]{1,0:T(8,128)(2,1)S(1)} %pad_maximum_fusion.4.w_ref, f32[32,2]{1,0:T(8,128)S(1)} %copy.19.ends_ref, bf16[32,9216]{1,0:T(8,128)(2,1)} %get-tuple-element.35.e0, bf16[32,9216]{1,0:T(8,128)(2,1)S(1)} %collective-permute-done.5.e1, ...), custom_call_target="tpu_custom_call", output_to_operand_aliasing={{}: (8, {})} | custom-call | tf_op jit(solution)/shard_map/pallas_call | solution.py:347
  (82 shorter events, 10.8 us)
Async XLA Ops:
  0.0 6.8 %copy-start.5 = (s32[128]{0:T(128)S(1)}, s32[128]{0:T(128)}, u32[]{:S(2)}) copy-start(s32[128]{0:T(128)} %shift_ref.1) | copy-start | bytes 1540
  0.0 6.8 %copy-start.4 = (f32[2,128]{1,0:T(2,128)S(1)}, f32[2,128]{1,0:T(2,128)}, u32[]{:S(2)}) copy-start(f32[2,128]{1,0:T(2,128)} %couple_ref.1) | copy-start | bytes 3076
  0.0 23.8 %collective-permute-start = (bf16[32,16512]{1,0:T(8,128)(2,1)}, bf16[32,16512]{1,0:T(8,128)(2,1)S(1)}, u32[]{:S(2)}, u32[]{:S(2)}) collective-permute-start(bf16[32,16512]{1,0:T(8,128)(2,1)} %refs_5_.3), channel_id=1, source_target_pairs={{0,32},{32,0},{64,96},{96,64},{1,33},{33,1},{65,97},{97,65},{2,34}... | collective-permute-start | bytes 3170312 | tf_op jit(solution)/shard_map/ppermute | solution.py:383
  3.8 19.2 %collective-permute-start.2 = (bf16[32,8320]{1,0:T(8,128)(2,1)}, bf16[32,8320]{1,0:T(8,128)(2,1)S(1)}, u32[]{:S(2)}, u32[]{:S(2)}) collective-permute-start(bf16[32,8320]{1,0:T(8,128)(2,1)} %get-tuple-element.62), channel_id=1, source_target_pairs={{0,64},{32,96},{64,0},{96,32},{1,65},{33,97},{65,1},{97,33},{2,66}... | collective-permute-start | bytes 1597448 | tf_op jit(solution)/shard_map/ppermute | solution.py:383
  6.7 28.9 %collective-permute-start.1 = (bf16[32,8320]{1,0:T(8,128)(2,1)}, bf16[32,8320]{1,0:T(8,128)(2,1)S(1)}, u32[]{:S(2)}, u32[]{:S(2)}) collective-permute-start(bf16[32,8320]{1,0:T(8,128)(2,1)} %get-tuple-element.63), channel_id=1, source_target_pairs={{0,64},{32,96},{64,0},{96,32},{1,65},{33,97},{65,1},{97,33},{2,66}... | collective-permute-start | bytes 1597448 | tf_op jit(solution)/shard_map/ppermute | solution.py:383
  6.8 16.1 %copy-start.8 = (s32[32]{0:T(128)S(1)}, s32[32]{0:T(128)}, u32[]{:S(2)}) copy-start(s32[32]{0:T(128)} %param.15) | copy-start | bytes 388
  6.9 16.1 %copy-start.7 = (f32[32]{0:T(128)S(1)}, f32[32]{0:T(128)}, u32[]{:S(2)}) copy-start(f32[32]{0:T(128)} %param.16) | copy-start | bytes 388
  6.9 18.4 %copy-start = (bf16[32,16512]{1,0:T(8,128)(2,1)S(1)}, bf16[32,16512]{1,0:T(8,128)(2,1)}, u32[]{:S(2)}) copy-start(bf16[32,16512]{1,0:T(8,128)(2,1)} %refs_5_.3) | copy-start | bytes 3170308
  23.0 2.2 %collective-permute-start.3 = (bf16[32,8320]{1,0:T(8,128)(2,1)S(1)}, bf16[32,8320]{1,0:T(8,128)(2,1)S(1)}, u32[]{:S(2)}, u32[]{:S(2)}) collective-permute-start(bf16[32,8320]{1,0:T(8,128)(2,1)S(1)} %collective-permute-done.2.refs_3_.refs_7_), channel_id=1, source_target_pairs={{0,32},{32,0},{64,96},{96,64},{1,33},{33,1},{65,97},{97,65},{2,34}... | collective-permute-start | bytes 1597448 | tf_op jit(solution)/shard_map/ppermute | solution.py:383
  26.3 14.2 %copy-start.6 = (f32[2,32]{1,0:T(2,128)S(1)}, f32[2,32]{1,0:T(2,128)}, u32[]{:S(2)}) copy-start(f32[2,32]{1,0:T(2,128)} %param.23) | copy-start | bytes 772
  35.6 7.8 %collective-permute-start.4 = (bf16[32,8320]{1,0:T(8,128)(2,1)S(1)}, bf16[32,8320]{1,0:T(8,128)(2,1)S(1)}, u32[]{:S(2)}, u32[]{:S(2)}) collective-permute-start(bf16[32,8320]{1,0:T(8,128)(2,1)S(1)} %collective-permute-done.1.refs_3_.refs_7_), channel_id=1, source_target_pairs={{0,32},{32,0},{64,96},{96,64},{1,33},{33,1},{65,97},{97,65},{2,34}... | collective-permute-start | bytes 1597448 | tf_op jit(solution)/shard_map/ppermute | solution.py:383
  36.0 18.2 %collective-permute-start.7 = (bf16[32,7168]{1,0:T(8,128)(2,1)}, bf16[32,7168]{1,0:T(8,128)(2,1)}, u32[]{:S(2)}, u32[]{:S(2)}) collective-permute-start(bf16[32,7168]{1,0:T(8,128)(2,1)} %get-tuple-element.38.e0), channel_id=1, source_target_pairs={{0,64},{32,96},{64,0},{96,32},{1,65},{33,97},{65,1},{97,33},{2,66}... | collective-permute-start | bytes 1376264 | tf_op jit(solution)/shard_map/ppermute | solution.py:383
  54.1 8.3 %collective-permute-start.10 = (f32[2,128,128]{2,1,0:T(8,128)S(1)}, f32[2,128,128]{2,1,0:T(8,128)S(1)}, u32[]{:S(2)}, u32[]{:S(2)}) collective-permute-start(f32[2,128,128]{2,1,0:T(8,128)S(1)} %pad_maximum_fusion.2), channel_id=1, source_target_pairs={{65,0},{64,1},{67,2},{66,3},{69,4},{68,5},{71,6},{70,7},{73,8},{72... | collective-permute-start | bytes 393224 | tf_op jit(solution)/shard_map/ppermute | solution.py:451
  55.0 7.4 %collective-permute-start.8 = (f32[2,128,128]{2,1,0:T(8,128)S(1)}, f32[2,128,128]{2,1,0:T(8,128)S(1)}, u32[]{:S(2)}, u32[]{:S(2)}) collective-permute-start(f32[2,128,128]{2,1,0:T(8,128)S(1)} %pad_maximum_fusion.2), channel_id=1, source_target_pairs={{64,0},{65,1},{66,2},{67,3},{68,4},{69,5},{70,6},{71,7},{72,8},{73... | collective-permute-start | bytes 393224 | tf_op jit(solution)/shard_map/ppermute | solution.py:451
  56.3 6.9 %collective-permute-start.9 = (f32[2,128,128]{2,1,0:T(8,128)S(1)}, f32[2,128,128]{2,1,0:T(8,128)S(1)}, u32[]{:S(2)}, u32[]{:S(2)}) collective-permute-start(f32[2,128,128]{2,1,0:T(8,128)S(1)} %pad_maximum_fusion.2), channel_id=1, source_target_pairs={{1,0},{0,1},{3,2},{2,3},{5,4},{4,5},{7,6},{6,7},{9,8},{8,9},{11,10... | collective-permute-start | bytes 393224 | tf_op jit(solution)/shard_map/ppermute | solution.py:451
  57.5 26.9 %collective-permute-start.6 = (bf16[32,9216]{1,0:T(8,128)(2,1)}, bf16[32,9216]{1,0:T(8,128)(2,1)S(1)}, u32[]{:S(2)}, u32[]{:S(2)}) collective-permute-start(bf16[32,9216]{1,0:T(8,128)(2,1)} %get-tuple-element.35.e0), channel_id=1, source_target_pairs={{0,64},{32,96},{64,0},{96,32},{1,65},{33,97},{65,1},{97,33},{2,66}... | collective-permute-start | bytes 1769480 | tf_op jit(solution)/shard_map/ppermute | solution.py:383
  63.3 14.8 %collective-permute-start.12 = (f32[3,128,128]{2,1,0:T(8,128)S(1)}, f32[3,128,128]{2,1,0:T(8,128)S(1)}, u32[]{:S(2)}, u32[]{:S(2)}) collective-permute-start(f32[3,128,128]{2,1,0:T(8,128)S(1)} %pad_maximum_fusion.1), channel_id=1, source_target_pairs={{0,30},{1,31},{2,0},{3,1},{4,2},{5,3},{6,4},{7,5},{8,6},{9,7},{10,... | collective-permute-start | bytes 589832 | tf_op jit(solution)/shard_map/ppermute | solution.py:459
  69.6 8.6 %collective-permute-start.11 = (f32[3,128,128]{2,1,0:T(8,128)S(1)}, f32[3,128,128]{2,1,0:T(8,128)S(1)}, u32[]{:S(2)}, u32[]{:S(2)}) collective-permute-start(f32[3,128,128]{2,1,0:T(8,128)S(1)} %pad_maximum_fusion), channel_id=1, source_target_pairs={{0,2},{1,3},{2,4},{3,5},{4,6},{5,7},{6,8},{7,9},{8,10},{9,11},{10,... | collective-permute-start | bytes 589832 | tf_op jit(solution)/shard_map/ppermute | solution.py:459
  70.6 7.5 %collective-permute-start.13 = (f32[128,128]{1,0:T(8,128)S(1)}, f32[128,128]{1,0:T(8,128)S(1)}, u32[]{:S(2)}, u32[]{:S(2)}) collective-permute-start(f32[128,128]{1,0:T(8,128)S(1)} %get-tuple-element.64), channel_id=1, source_target_pairs={{0,4},{1,29},{2,6},{3,31},{4,8},{5,1},{6,10},{7,3},{8,12},{9,5},{1... | collective-permute-start | bytes 196616 | tf_op jit(solution)/shard_map/ppermute | solution.py:464
  78.9 5.5 %collective-permute-start.14 = (f32[2,128,128]{2,1,0:T(8,128)S(1)}, f32[2,128,128]{2,1,0:T(8,128)S(1)}, u32[]{:S(2)}, u32[]{:S(2)}) collective-permute-start(f32[2,128,128]{2,1,0:T(8,128)S(1)} %shard_map.121.n0), channel_id=1, source_target_pairs={{0,32},{32,0},{64,96},{96,64},{1,33},{33,1},{65,97},{97,65},{2,34}... | collective-permute-start | bytes 393224 | tf_op jit(solution)/shard_map/ppermute | solution.py:383
  84.3 6.8 %collective-permute-start.5 = (bf16[32,9216]{1,0:T(8,128)(2,1)}, bf16[32,9216]{1,0:T(8,128)(2,1)S(1)}, u32[]{:S(2)}, u32[]{:S(2)}) collective-permute-start(bf16[32,9216]{1,0:T(8,128)(2,1)} %get-tuple-element.35.e0), channel_id=1, source_target_pairs={{0,32},{32,0},{64,96},{96,64},{1,33},{33,1},{65,97},{97,65},{2,34}... | collective-permute-start | bytes 1769480 | tf_op jit(solution)/shard_map/ppermute | solution.py:383
  84.4 6.7 %collective-permute-start.15 = (bf16[32,9216]{1,0:T(8,128)(2,1)S(1)}, bf16[32,9216]{1,0:T(8,128)(2,1)S(1)}, u32[]{:S(2)}, u32[]{:S(2)}) collective-permute-start(bf16[32,9216]{1,0:T(8,128)(2,1)S(1)} %collective-permute-done.6.e2), channel_id=1, source_target_pairs={{0,32},{32,0},{64,96},{96,64},{1,33},{33,1},{65,97},{97,65},{2,34}... | collective-permute-start | bytes 1769480 | tf_op jit(solution)/shard_map/ppermute | solution.py:383
  85.9 2.2 %collective-permute-start.16 = (bf16[32,7168]{1,0:T(8,128)(2,1)}, bf16[32,7168]{1,0:T(8,128)(2,1)S(1)}, u32[]{:S(2)}, u32[]{:S(2)}) collective-permute-start(bf16[32,7168]{1,0:T(8,128)(2,1)} %get-tuple-element.38.e0), channel_id=1, source_target_pairs={{0,32},{32,0},{64,96},{96,64},{1,33},{33,1},{65,97},{97,65},{2,34}... | collective-permute-start | bytes 1376264 | tf_op jit(solution)/shard_map/ppermute | solution.py:383
  86.0 2.7 %collective-permute-start.17 = (bf16[32,7168]{1,0:T(8,128)(2,1)}, bf16[32,7168]{1,0:T(8,128)(2,1)S(1)}, u32[]{:S(2)}, u32[]{:S(2)}) collective-permute-start(bf16[32,7168]{1,0:T(8,128)(2,1)} %collective-permute-done.7.e2), channel_id=1, source_target_pairs={{0,32},{32,0},{64,96},{96,64},{1,33},{33,1},{65,97},{97,65},{2,34}... | collective-permute-start | bytes 1376264 | tf_op jit(solution)/shard_map/ppermute | solution.py:383
  (5 other events, 16.5 us)

commit v5 on v4

--- a/solution.py
+++ b/solution.py
@@ -52,13 +52,12 @@
 NT = (((1,), (1,)), ((), ()))
 
 
-def tables_kernel(shift_ref, tap_ref, couple_ref, inv_ref, t_ref, corr_ref, a_ref, b_ref):
+def tables_kernel(here_ref, shift_ref, tap_ref, inv_ref, couple_ref, *outs):
+    t_ref, w_ref, ends_ref, yw_ref, corner_ref = outs
     step = pl.program_id(0)
+    block, mine = here_ref[0], here_ref[1]
     shape = (2 * BLK, BLK)
     delta = lax.broadcasted_iota(jnp.int32, shape, 0) - lax.broadcasted_iota(jnp.int32, shape, 1)
-    place = lax.broadcasted_iota(jnp.int32, (16, BLK), 0) * (BLK - 1)
-    units = (place == lax.broadcasted_iota(jnp.int32, (16, BLK), 1)).astype(jnp.bfloat16)
-    row = lax.broadcasted_iota(jnp.int32, (2 * SUB, BLK), 0)
     for i in range(TG):
         tile = step * TG + i
         tap = delta - shift_ref[tile]
@@ -66,47 +65,60 @@
         for k in range(4):
             total = jnp.where(tap == k, tap_ref[k, tile], total)
         t_ref[i] = total.astype(jnp.bfloat16)
-        hi, lo = split_hi_lo(inv_ref[i])
-        ends = lax.dot_general(units, hi, NT, preferred_element_type=jnp.float32)
-        ends = ends + lax.dot_general(units, lo, NT, preferred_element_type=jnp.float32)
-        a = couple_ref[0, tile] * ends[0:1, :]
-        b = couple_ref[1, tile] * ends[1:2, :]
-        a_ref[i : i + 1, :] = a
-        b_ref[i : i + 1, :] = b
-        q, r = divmod(i, SUB)
-        both = jnp.where(row == r, a, jnp.where(row == SUB + r, b, 0.0))
-        corr_ref[q, :, r * BLK : (r + 1) * BLK] = both.astype(jnp.bfloat16)
-
-
-def run_tables(shift, taps, couple, inverse):
-    tiles = inverse.shape[0]
-    cube = lambda *shape: pl.BlockSpec((TG, *shape), lambda l, *_: (l,) + (0,) * len(shape))
+
+    @pl.when(step == 0)
+    def _():
+        lane = lax.broadcasted_iota(jnp.int32, (32, BLK), 1)
+        odd, high = lax.rem(mine, 2) == 1, mine > 1
+        own = inv_ref[block, pl.ds(pl.multiple_of(mine * 32, 32), 32), :]
+        swapped = jnp.where(lax.rem(lane // 32, 2) == 0, pltpu.roll(own, 96, 1), pltpu.roll(own, 32, 1))
+        turned = jnp.where(odd, swapped, own)
+        turned = jnp.where(high, pltpu.roll(turned, 64, 1), turned)
+        w_ref[...] = jnp.concatenate(split_hi_lo(turned), axis=0)
+        pair = jnp.where(lane == 0, own[:, :1], own[:, BLK - 1 :])
+        couple = couple_ref[pl.ds(block, 1), :]
+        ends_ref[...] = pair * jnp.where(lane == 0, couple[:, :1], couple[:, 1:2])
+        row = lax.broadcasted_iota(jnp.int32, (8, BLK), 0)
+        tips = jnp.where(row == 0, inv_ref[block, 0:1, :], inv_ref[block, BLK - 1 :, :])
+        tips = jnp.where(row < 2, tips, 0.0)
+        tips = jnp.where(odd, pltpu.roll(tips, 96, 1), tips)
+        tips = jnp.where(high, pltpu.roll(tips, 64, 1), tips)
+        yw_ref[...] = jnp.concatenate(split_hi_lo(tips), axis=0)[:, :32]
+        top, bottom = inv_ref[:, 0, :], inv_ref[:, BLK - 1, :]
+        west, east = couple_ref[:, 0:1], couple_ref[:, 1:2]
+        values = (top[:, :1] * west, top[:, BLK - 1 :] * east, bottom[:, :1] * west, bottom[:, BLK - 1 :] * east)
+        total = jnp.zeros((32, BLK), jnp.float32)
+        for k, value in enumerate(values):
+            total = jnp.where(lane == k, value, total)
+        corner_ref[...] = total
+
+
+def run_tables(here, shift, taps, inverse_y, couple_y):
+    tiles = shift.shape[0]
+    full = lambda *shape: pl.BlockSpec(shape, lambda l, *_: (0,) * len(shape))
     return pl.pallas_call(
         tables_kernel,
         grid_spec=pltpu.PrefetchScalarGridSpec(
             num_scalar_prefetch=3,
             grid=(tiles // TG,),
-            in_specs=[cube(BLK, BLK)],
+            in_specs=[full(*inverse_y.shape), full(*couple_y.shape)],
             out_specs=[
-                cube(2 * BLK, BLK),
-                pl.BlockSpec((TG // SUB, 2 * SUB, SW), lambda l, *_: (l, 0, 0)),
-                cube(BLK),
-                cube(BLK),
+                pl.BlockSpec((TG, 2 * BLK, BLK), lambda l, *_: (l, 0, 0)),
+                full(64, BLK),
+                full(32, BLK),
+                full(16, 32),
+                full(32, BLK),
             ],
         ),
         out_shape=[
             jax.ShapeDtypeStruct((tiles, 2 * BLK, BLK), jnp.bfloat16),
-            jax.ShapeDtypeStruct((tiles // SUB, 2 * SUB, SW), jnp.bfloat16),
-            jax.ShapeDtypeStruct((tiles, BLK), jnp.float32),
-            jax.ShapeDtypeStruct((tiles, BLK), jnp.float32),
+            jax.ShapeDtypeStruct((64, BLK), jnp.bfloat16),
+            jax.ShapeDtypeStruct((32, BLK), jnp.float32),
+            jax.ShapeDtypeStruct((16, 32), jnp.bfloat16),
+            jax.ShapeDtypeStruct((32, BLK), jnp.float32),
         ],
         compiler_params=pltpu.CompilerParams(vmem_limit_bytes=VMEM_LIMIT),
-    )(shift, taps, couple, inverse)
-
-
-def table_hi_lo(value):
-    hi = lax.reduce_precision(value, 8, 7)
-    return hi.astype(jnp.bfloat16), (value - hi).astype(jnp.bfloat16)
+    )(here, shift, taps, inverse_y, couple_y)
 
 
 def split_hi_lo(value):
@@ -116,16 +128,21 @@
 
 
 def rows_kernel(first, groups, carried, *refs):
-    kind_ref, p0, p1, p2, p3, q0, q1, q2, q3, w_ref, t_ref, mask_ref, bg_ref, inv_ref = refs[:14]
-    coef_ref, corr_ref, yw_ref = refs[14:17]
+    kind_ref, couple_ref, p0, p1, p2, p3, q0, q1, q2, q3, w_ref, t_ref = refs[:12]
+    mask_ref, bg_ref, inv_ref, lanes_ref, yw_ref = refs[12:17]
     refs = refs[17:]
     if carried:
-        u_in, f_in, l_in = refs[:3]
-        refs = refs[3:]
-    out_ref, part_ref, u_out, f_out, l_out, sec, u_st, f_st, l_st = refs
+        u_in, f_in, l_in, c_in = refs[:4]
+        refs = refs[4:]
+    out_ref, part_ref, u_out, f_out, l_out, c_out, sec, u_st, f_st, l_st, c_st = refs
     step = pl.program_id(0)
     s = step + first
+    tall = (40, BLK)
+    tall_lane = lax.broadcasted_iota(jnp.int32, tall, 1)
     lane = lax.broadcasted_iota(jnp.int32, (32, BLK), 1)
+    row = lax.broadcasted_iota(jnp.int32, (2 * SUB, BLK), 0)
+    units = row * (BLK - 1) == lax.broadcasted_iota(jnp.int32, (2 * SUB, BLK), 1)
+    units = units.astype(jnp.float32).astype(jnp.bfloat16)
     roll = lambda value, by: pltpu.roll(value, by % BLK, 1)
 
     @pl.when(step == 0)
@@ -134,12 +151,15 @@
             u_st[TG:] = u_in[...]
             f_st[...] = f_in[...]
             l_st[...] = l_in[...]
+            c_st[TG // SUB] = c_in[...]
         else:
+            c_st[...] = jnp.zeros_like(c_st)
             u_st[...] = jnp.zeros_like(u_st)
             f_st[...] = jnp.zeros_like(f_st)
             l_st[...] = jnp.zeros_like(l_st)
 
     u_st[:SUB] = u_st[TG:]
+    c_st[0] = c_st[TG // SUB]
     rows = jnp.concatenate([p0[...], p1[...], p2[...], p3[...]], axis=0)
     edge = jnp.concatenate([q0[...], q1[...], q2[...], q3[...]], axis=0)
     w = w_ref[...]
@@ -148,8 +168,8 @@
     for k in range(2):
         sec[k, :, :GW] = both[k * 32 : (k + 1) * 32]
         sec[k, :, GW:] = tail[k * 32 : (k + 1) * 32]
-    f = jnp.where(lane < HALO + SUB, roll(f_st[...], -TG), 0.0)
-    l = jnp.where(lane < HALO + SUB, roll(l_st[...], -TG), 0.0)
+    f = jnp.where(tall_lane < HALO + SUB, roll(f_st[...], -TG), 0.0)
+    l = jnp.where(tall_lane < HALO + SUB, roll(l_st[...], -TG), 0.0)
     for at in range(0, TG, SUB):
         tiles = range(at, at + SUB)
         ests = []
@@ -161,7 +181,7 @@
         for i in tiles:
             cols = slice(i * BLK, (i + 1) * BLK)
             misfit = mask_ref[:, cols].astype(jnp.float32) * (ests[i - at] - bg_ref[:, cols])
-            sides.append(jnp.concatenate(split_hi_lo(misfit), axis=0))
+            sides.append(jnp.concatenate([*split_hi_lo(misfit), units], axis=0))
         solved = []
         for i in tiles:
             pair = jnp.concatenate(split_hi_lo(inv_ref[i]), axis=0)
@@ -170,28 +190,36 @@
             )
         for i in tiles:
             u = solved[i - at]
-            u = u[:32, :BLK] + (u[32:, :BLK] + u[:32, BLK:])
+            tips = u[64:72, :BLK] + u[64:72, BLK:]
+            u = u[:32, :BLK] + (u[32:64, :BLK] + u[:32, BLK:])
             u_st[SUB + i] = u
-            here = lane == HALO + SUB + i
+            tile = s * TG + i
+            west, east = couple_ref[0, tile] * tips[0:1], couple_ref[1, tile] * tips[1:2]
+            both = jnp.where(row == i - at, west, jnp.where(row == SUB + i - at, east, 0.0))
+            spot = (i - at) * BLK
+            c_st[at // SUB + 1, :, spot : spot + BLK] = both.astype(jnp.bfloat16)
+            u = jnp.concatenate([u, tips], axis=0)
+            here = tall_lane == HALO + SUB + i
             f = jnp.where(here, u[:, :1], f)
             l = jnp.where(here, u[:, BLK - 1 :], l)
     f_st[...] = f
     l_st[...] = l
 
-    af, cf, al, cl = [coef_ref[r, pl.ds(s, 1), :] for r in range(4)]
+    west, east = lanes_ref[0, pl.ds(s, 1), :], lanes_ref[1, pl.ds(s, 1), :]
+    af, cf, al, cl = f[32:33] * west, f[33:34] * east, l[32:33] * west, l[33:34] * east
+    f0, l0 = f[:32], l[:32]
 
     def sweep(f, l):
         west, east = roll(l, 1), roll(f, -1)
-        return f_st[...] + af * west + cf * east, l_st[...] + al * west + cl * east
-
-    f2, l2 = sweep(*sweep(f, l))
+        return f0 + af * west + cf * east, l0 + al * west + cl * east
+
+    f2, l2 = sweep(*sweep(f0, l0))
 
     def finish(q):
         low = HALO + q * SUB
         ends = jnp.where(lane < SUB, roll(l2, 1 - low), roll(f2, SUB - 1 - low))
         ends = ends[:, : 2 * SUB].astype(jnp.bfloat16)
-        sub = s * (TG // SUB) - 1 + q
-        fix = jnp.dot(ends, corr_ref[sub], preferred_element_type=jnp.float32)
+        fix = jnp.dot(ends, c_st[q], preferred_element_type=jnp.float32)
         spot = step * (TG // SUB) + q - (0 if carried else 1)
         outs = []
         for i in range(SUB):
@@ -219,9 +247,10 @@
         u_out[...] = u_st[TG:]
         f_out[...] = f_st[...]
         l_out[...] = l_st[...]
-
-
-def run_rows(first, stop, groups, state, kinds, own, got, w, tables, mask, bg, inv, coefs, corr, yw):
+        c_out[...] = c_st[TG // SUB]
+
+
+def run_rows(first, stop, groups, state, kinds, couple, own, got, w, tables, mask, bg, inv, lanes, yw):
     carried = state is not None
     steps = stop - first
     width = steps * GW - (0 if carried else SW) + (SW if stop == groups else 0)
@@ -238,30 +267,31 @@
         wide(first),
         wide(first),
         cube(BLK, BLK),
-        full(*coefs.shape),
-        full(*corr.shape),
+        full(*lanes.shape),
         full(16, 32),
     ]
     keep = [
         jax.ShapeDtypeStruct((SUB, 32, BLK), jnp.float32),
-        jax.ShapeDtypeStruct((32, BLK), jnp.float32),
-        jax.ShapeDtypeStruct((32, BLK), jnp.float32),
+        jax.ShapeDtypeStruct((40, BLK), jnp.float32),
+        jax.ShapeDtypeStruct((40, BLK), jnp.float32),
+        jax.ShapeDtypeStruct((2 * SUB, SW), jnp.bfloat16),
     ]
-    operands = [kinds, own, near, far, away, own, near, far, away, w, tables, mask, bg, inv]
-    operands += [coefs, corr, yw]
+    operands = [kinds, couple, own, near, far, away, own, near, far, away, w, tables, mask, bg]
+    operands += [inv, lanes, yw]
     if carried:
         in_specs += [full(*k.shape) for k in keep]
         operands += list(state)
     grid_spec = pltpu.PrefetchScalarGridSpec(
-        num_scalar_prefetch=1,
+        num_scalar_prefetch=2,
         grid=(steps,),
         in_specs=in_specs,
         out_specs=[full(32, width), full(2, width // BLK, BLK), *[full(*k.shape) for k in keep]],
         scratch_shapes=[
             pltpu.VMEM((2, 32, GW + BLK), jnp.bfloat16),
             pltpu.VMEM((SUB + TG, 32, BLK), jnp.float32),
-            pltpu.VMEM((32, BLK), jnp.float32),
-            pltpu.VMEM((32, BLK), jnp.float32),
+            pltpu.VMEM((40, BLK), jnp.float32),
+            pltpu.VMEM((40, BLK), jnp.float32),
+            pltpu.VMEM((TG // SUB + 1, 2 * SUB, SW), jnp.bfloat16),
         ],
     )
     outs = pl.pallas_call(
@@ -280,13 +310,18 @@
 def ends_kernel(blocks, block_ref, corner_ref, own, other, below, above, distant, out):
     block = block_ref[0]
     pair = block // 2
-    before = jnp.where(pair > 0, below[...], 0.0)
-    after = jnp.where(pair < blocks // 2 - 1, above[...], 0.0)
+    value = lambda ref: ref[...].astype(jnp.float32)
+    before = jnp.where(pair > 0, value(below), 0.0)
+    after = jnp.where(pair < blocks // 2 - 1, value(above), 0.0)
     inside = jnp.where(lax.rem(block, 2) == 1, pair < blocks // 2 - 2, pair > 1)
-    beyond = jnp.where(inside, distant[...], 0.0)
+    beyond = jnp.where(inside, value(distant), 0.0)
     second = lax.rem(block, 2) == 1
     pick = lambda even, odd: jnp.where(second, odd, even)
-    coef = lambda r, k: corner_ref[r, block + HALO + k]
+
+    def coef(r, k):
+        at = block + k
+        return jnp.where((at >= 0) & (at < blocks), corner_ref[jnp.clip(at, 0, blocks - 1), r], 0.0)
+
     f = {0: own[0], -1: pick(before[1], other[0]), 1: pick(other[0], after[0])}
     l = {0: own[1], -1: pick(before[2], other[1]), 1: pick(other[1], after[1])}
     l[-2], l[-3] = pick(before[0], before[2]), pick(beyond, before[0])
@@ -398,35 +433,12 @@
         axis=0,
     )
     kinds = (tile_kind == 1).astype(jnp.int32)
-    tables, corr, a_x, b_x = run_tables(
-        tile_shift, tap_weights(tile_kind, tile_frac), couple_x, inverse_x
-    )
-    coefs = jnp.stack([a_x[:, 0], b_x[:, 0], a_x[:, -1], b_x[:, -1]])
-    coefs = jnp.pad(coefs, ((0, 0), (SUB + HALO, TG - SUB - HALO))).reshape(4, groups + 1, TG)
-    coefs = jnp.concatenate([coefs[:, :-1], coefs[:, 1:]], axis=2)
-    coefs = jnp.pad(coefs, ((0, 0), (0, 0), (0, BLK - 2 * TG)))
-
-    tips = inverse_y[:, :: BLK - 1, :: BLK - 1] * couple_y.T[:, None, :]
-    corner = jnp.stack([tips[:, 0, 0], tips[:, 0, 1], tips[:, 1, 0], tips[:, 1, 1]])
-    corner = jnp.pad(corner, ((0, 0), (HALO, HALO)))
-    own_inv = lax.dynamic_index_in_dim(inverse_y, block, 0, keepdims=False)
-    at = mine * rows
-    own_rows = lax.dynamic_slice_in_dim(own_inv, at, rows, 0)
-    shuffled = jnp.concatenate(
-        [lax.dynamic_slice_in_dim(own_rows, (q ^ mine) * rows, rows, 1) for q in range(4)], axis=1
-    )
-    w_y = jnp.concatenate(table_hi_lo(shuffled), axis=0)
-    ends_y = jnp.stack(
-        [
-            couple_y[0, block] * own_rows[:, 0],
-            couple_y[1, block] * own_rows[:, -1],
-        ],
-        axis=1,
-    )
-    end_rows = lax.dynamic_slice_in_dim(jnp.stack([own_inv[0], own_inv[-1]]), at, rows, 1)
-    end_hi, end_lo = table_hi_lo(end_rows)
-    gap = jnp.zeros((6, rows), jnp.bfloat16)
-    yw = jnp.concatenate([end_hi, gap, end_lo, gap], axis=0)
+    tables, w_y, ends_y, yw, corner = run_tables(
+        jnp.stack([block, mine]), tile_shift, tap_weights(tile_kind, tile_frac), inverse_y, couple_y.T
+    )
+    lanes = jnp.pad(couple_x, ((0, 0), (SUB + HALO, TG - SUB - HALO))).reshape(2, groups + 1, TG)
+    lanes = jnp.concatenate([lanes[:, :-1], lanes[:, 1:]], axis=2)
+    lanes = jnp.pad(lanes, ((0, 0), (0, 0), (0, BLK - 2 * TG)))
 
     state = None
     sent = []
@@ -436,26 +448,31 @@
             far, state = lax.optimization_barrier((far, state))
         got = (near, far, swap(far, sibling))
         east_west, part, state = run_rows(
-            first, stop, groups, state, kinds, panels, got, w, tables,
-            void_mask, background, inverse_x, coefs, corr, yw,
+            first, stop, groups, state, kinds, couple_x, panels, got, w, tables,
+            void_mask, background, inverse_x, lanes, yw,
         )
         far = swap(east_west, across)
         sent.append([east_west, swap(east_west, sibling), far])
         parts.append(part)
+    together = lax.optimization_barrier
     part = jnp.concatenate(parts, axis=1) if len(parts) > 1 else parts[0]
-    if len(sent) > 1:
-        part, sent[0][2] = lax.optimization_barrier((part, sent[0][2]))
+    for pieces in sent[:-1]:
+        part, pieces[1], pieces[2] = together((part, pieces[1], pieces[2]))
 
     every = [(d, k) for d in range(4) for k in range(n_wide)]
     at = lambda d, k: d * n_wide + k
+    half = part.astype(jnp.bfloat16)
     fetch = lambda db, dw: lax.ppermute(
-        part, ("band", "wide"), [(at(d ^ db, k ^ dw), at(d, k)) for d, k in every]
-    )
+        half, ("band", "wide"), [(at(d ^ db, k ^ dw), at(d, k)) for d, k in every]
+    ).astype(jnp.float32)
     second = block % 2
     own = part + fetch(2, 0)
     other = fetch(0, 1) + fetch(2, 1)
-    even = jnp.where(second == 0, own, other)
-    odd = jnp.where(second == 0, other, own)
+    for pieces in sent[:-1]:
+        pieces.append(swap(pieces[2], sibling))
+        own, pieces[3] = together((own, pieces[3]))
+    even = jnp.where(second == 0, own, other).astype(jnp.bfloat16)
+    odd = jnp.where(second == 0, other, own).astype(jnp.bfloat16)
     shifted = lambda value, k: lax.ppermute(
         value, "wide", [(i, (i + 2 * k) % n_wide) for i in range(n_wide)]
     )
@@ -466,14 +483,19 @@
         "wide",
         [(i, (i + 4 * (1 - 2 * (i % 2))) % n_wide) for i in range(n_wide)],
     )
+    before, sent[-1][1] = together((before, sent[-1][1]))
     forced = run_ends(n_wide, block, corner, own, other, before, after, beyond)
     rest = swap(forced, sibling)
-    sent[-1][2], rest = lax.optimization_barrier((sent[-1][2], rest))
 
     result = None
     position = 0
     for pieces in sent:
-        pieces = (*pieces, swap(pieces[2], sibling))
+        if len(pieces) == 3:
+            if result is None:
+                pieces[2], rest = together((pieces[2], rest))
+            else:
+                pieces[2], result = together((pieces[2], result))
+            pieces.append(swap(pieces[2], sibling))
         result = run_columns(position, width, w_y, ends_y, pieces, forced, rest, result)
         position += pieces[0].shape[1]
     return result

time: 94 us -> 78.6 us (0.84)
  Pallas kernels: 38.2 us -> 29.9 us
  local copies, waits for them, and re-layouts: 12.9 us -> 5.24 us
  starting transfers between devices: 24.2 us -> 27.9 us
  other arithmetic: 1.96 us -> 0.5 us
  waiting for transfers between devices: 15.9 us -> 14.6 us
    ppermute x1, waiting for transfers between devices: 7.34 us -> 0.01 us  [body(): lax.ppermute(jnp.where(second == 0, odd[1], even[0]), 'wide', [(i, (i + 4...]
    ppermute x2, waiting for transfers between devices: 0.12 us -> 7.02 us  [body(): lax.ppermute(value, 'wide', [(i, (i + 2 * k) % n_wide) for i in range(n_w...]
    pallas_call x1, Pallas kernels: 13.8 us -> 7.48 us  [run_tables(): pl.pallas_call(tables_kernel, grid_spec=pltpu.PrefetchScalarGridSpec(num_...]
    ppermute x3, waiting for transfers between devices: 4.95 us -> 0.96 us  [body(): lax.ppermute(half, ('band', 'wide'), [(at(d ^ db, k ^ dw), at(d, k)) for...]
    dynamic_slice x4 -> x0, local copies, waits for them, and re-layouts: 3.81 us -> none  [the longest x2 2.15 us: body(): own_rows = lax.dynamic_slice_in_dim(own_inv, at, rows, 0)]
    slice x5 -> x1, local copies, waits for them, and re-layouts: 3.5 us -> 0.01 us  [body(): lanes = jnp.concatenate([lanes[:, :-1], lanes[:, 1:]], axis=2)]
    ppermute x12, starting transfers between devices: 14.5 us -> 17.7 us  [body(): swap = lambda value, pairs: lax.ppermute(value, 'band', pairs)]
    ppermute x12, waiting for transfers between devices: 3.46 us -> 6.64 us  [body(): swap = lambda value, pairs: lax.ppermute(value, 'band', pairs)]
  transfers between devices with their start and end apart: 18 -> 18, of which waited for: 7 -> 7; matrix products, arithmetic and copies ran while one was open for 13% -> 4% of each run, Pallas kernels for 38% -> 36%
where the time goes in v5:
time: 78.6 us; the launch traced here: 78.4 us
  Pallas kernels  29.9 us (38%)
  starting transfers between devices  27.9 us (35%)
  waiting for transfers between devices  14.6 us (19%)
  local copies, waits for them, and re-layouts  5.24 us (7%)
    pallas_call x2, Pallas kernels, run_rows(): pl.pallas_call(functools.partial(rows_kernel, first, groups, carried), gr...  17.9 us
    ppermute x12, starting transfers between devices, body(): swap = lambda value, pairs: lax.ppermute(value, 'band', pairs)  17.7 us
    pallas_call x1, Pallas kernels, run_tables(): pl.pallas_call(tables_kernel, grid_spec=pltpu.PrefetchScalarGridSpec(num_...  7.48 us
    ppermute x2, waiting for transfers between devices, body(): lax.ppermute(value, 'wide', [(i, (i + 2 * k) % n_wide) for i in range(n_w...  7.02 us
    ppermute x12, waiting for transfers between devices, body(): swap = lambda value, pairs: lax.ppermute(value, 'band', pairs)  6.64 us
    ppermute x2, starting transfers between devices, body(): lax.ppermute(value, 'wide', [(i, (i + 2 * k) % n_wide) for i in range(n_w...  6.35 us
    ppermute x3, starting transfers between devices, body(): lax.ppermute(half, ('band', 'wide'), [(at(d ^ db, k ^ dw), at(d, k)) for...  3.78 us
    pallas_call x2, Pallas kernels, run_columns(): pl.pallas_call(functools.partial(columns_kernel, start), in_specs=in_spec...  3.54 us
  transfers between devices with their start and end apart: 18, of which 7 were waited for; matrix products, arithmetic and copies ran while one was open for 4% of the time, Pallas kernels for 36%

profile of v5, /device:TPU:1, one launch (start us, length us, event | category | flops | bytes accessed | tf_op | source)
XLA Modules:
  0.0 78.4 jit_solution(12935264868734728217)
XLA Ops:
  0.1 1.5 %collective-permute-start = (bf16[32,16512]{1,0:T(8,128)(2,1)}, bf16[32,16512]{1,0:T(8,128)(2,1)S(1)}, u32[]{:S(2)}, u32[]{:S(2)}) collective-permute-start(bf16[32,16512]{1,0:T(8,128)(2,1)} %refs_6_.3), channel_id=1, source_target_pairs={{0,32},{32,0},{64,96},{96,64},{1,33},{33,1},{65,97},{97,65},{2,34}... | collective-permute-start | bytes 3170312 | tf_op jit(solution)/shard_map/ppermute | solution.py:418
  1.5 2.3 %fusion.8 = (bf16[32,8320]{1,0:T(8,128)(2,1)}, bf16[32,8320]{1,0:T(8,128)(2,1)}) fusion(bf16[32,16512]{1,0:T(8,128)(2,1)} %refs_6_.3), kind=kLoop, calls=%fused_computation.42 | loop fusion | bytes 2129920 | tf_op jit(solution)/shard_map/slice | solution.py:424
  3.8 2.9 %collective-permute-start.2 = (bf16[32,8320]{1,0:T(8,128)(2,1)}, bf16[32,8320]{1,0:T(8,128)(2,1)S(1)}, u32[]{:S(2)}, u32[]{:S(2)}) collective-permute-start(bf16[32,8320]{1,0:T(8,128)(2,1)} %get-tuple-element.59), channel_id=1, source_target_pairs={{0,64},{32,96},{64,0},{96,32},{1,65},{33,97},{65,1},{97,33},{2,66}... | collective-permute-start | bytes 1597448 | tf_op jit(solution)/shard_map/ppermute | solution.py:418
  7.4 1.7 %copy-done.2 = f32[32,128,128]{2,1,0:T(8,128)S(1)} copy-done((f32[32,128,128]{2,1,0:T(8,128)S(1)}, f32[32,128,128]{2,1,0:T(8,128)}, u32[]{:S(2)}) %copy-start.2) | copy-done | bytes 2097176
  9.2 7.5 %shard_map.118 = (bf16[128,256,128]{2,1,0:T(8,128)(2,1)}, bf16[64,128]{1,0:T(8,128)(2,1)S(1)}, f32[32,128]{1,0:T(8,128)S(1)}, bf16[16,32]{1,0:T(8,128)(2,1)S(1)}, f32[32,128]{1,0:T(8,128)S(1)}) custom-call(s32[2]{0:T(128)S(1)} %pad_add_fusion.here_ref, s32[128]{0:T(128)S(1)} %copy-done.8, f32[4,128]{1,0:T(4,128)S(1)} %maximum_reduce-precision_fusion.tap_ref, ...), custom_call_target="tpu_custom_call" | custom-call | tf_op jit(solution)/shard_map/pallas_call | solution.py:99
  16.7 2.5 %collective-permute-done.2.refs_4_.refs_8_ = bf16[32,8320]{1,0:T(8,128)(2,1)S(1)} collective-permute-done((bf16[32,8320]{1,0:T(8,128)(2,1)}, bf16[32,8320]{1,0:T(8,128)(2,1)S(1)}, u32[]{:S(2)}, u32[]{:S(2)}) %collective-permute-start.2) | collective-permute-done | bytes 532512 | tf_op jit(solution)/shard_map/ppermute | solution.py:418
  19.2 1.3 %collective-permute-start.3 = (bf16[32,8320]{1,0:T(8,128)(2,1)S(1)}, bf16[32,8320]{1,0:T(8,128)(2,1)S(1)}, u32[]{:S(2)}, u32[]{:S(2)}) collective-permute-start(bf16[32,8320]{1,0:T(8,128)(2,1)S(1)} %collective-permute-done.2.refs_4_.refs_8_), channel_id=1, source_target_pairs={{0,32},{32,0},{64,96},{96,64},{1,33},{33,1},{65,97},{97,65},{2,34}... | collective-permute-start | bytes 1597448 | tf_op jit(solution)/shard_map/ppermute | solution.py:418
  20.7 1.4 %collective-permute-done.3.refs_5_.refs_9_ = bf16[32,8320]{1,0:T(8,128)(2,1)S(1)} collective-permute-done((bf16[32,8320]{1,0:T(8,128)(2,1)S(1)}, bf16[32,8320]{1,0:T(8,128)(2,1)S(1)}, u32[]{:S(2)}, u32[]{:S(2)}) %collective-permute-start.3) | collective-permute-done | bytes 532512 | tf_op jit(solution)/shard_map/ppermute | solution.py:418
  22.1 8.4 %shard_map.119 = (bf16[32,7168]{1,0:T(8,128)(2,1)S(1)}, f32[2,56,128]{2,1,0:T(8,128)S(1)}, f32[8,32,128]{2,1,0:T(8,128)S(1)}, f32[40,128]{1,0:T(8,128)S(1)}, f32...) custom-call(s32[128]{0:T(128)S(1)} %fusion.7.refs_0_, f32[2,128]{1,0:T(2,128)S(1)} %copy-done.7, ...), custom_call_target="tpu_custom_call" | custom-call | tf_op jit(solution)/shard_map/pallas_call | solution.py:297
  30.6 0.9 %collective-permute-start.4 = (bf16[32,8320]{1,0:T(8,128)(2,1)S(1)}, bf16[32,8320]{1,0:T(8,128)(2,1)S(1)}, u32[]{:S(2)}, u32[]{:S(2)}) collective-permute-start(bf16[32,8320]{1,0:T(8,128)(2,1)S(1)} %collective-permute-done.1.refs_4_.refs_8_), channel_id=1, source_target_pairs={{0,32},{32,0},{64,96},{96,64},{1,33},{33,1},{65,97},{97,65},{2,34}... | collective-permute-start | bytes 1597448 | tf_op jit(solution)/shard_map/ppermute | solution.py:418
  31.5 2.8 %collective-permute-start.6 = (bf16[32,7168]{1,0:T(8,128)(2,1)S(1)}, bf16[32,7168]{1,0:T(8,128)(2,1)}, u32[]{:S(2)}, u32[]{:S(2)}) collective-permute-start(bf16[32,7168]{1,0:T(8,128)(2,1)S(1)} %get-tuple-element.48.e0), channel_id=1, source_target_pairs={{0,64},{32,96},{64,0},{96,32},{1,65},{33,97},{65,1},{97,33},{2,66}... | collective-permute-start | bytes 1376264 | tf_op jit(solution)/shard_map/ppermute | solution.py:418
  34.4 9.5 %shard_map.120 = (bf16[32,9216]{1,0:T(8,128)(2,1)S(1)}, f32[2,72,128]{2,1,0:T(8,128)S(1)}, f32[8,32,128]{2,1,0:T(8,128)}, f32[40,128]{1,0:T(8,128)}, f32[40,128]{1,0:T(8,128)}, /*index=5*/bf16[16,1024]{1,0:T(8,128)(2,1)}) custom-call(s32[128]{0:T(128)S(1)} %fusion.7.refs_0_, f32[2,128]{1,0:T(2,128)S(1)} %copy-done.7, bf16[32,16512]{1,0:T(8,128)(2,1)S(1)} %copy-done, ...), custom_call_target="tpu_custom_call" | custom-call | tf_op jit(solution)/shard_map/pallas_call | solution.py:297
  44.7 1.3 %collective-permute-start.8 = (bf16[32,7168]{1,0:T(8,128)(2,1)}, bf16[32,7168]{1,0:T(8,128)(2,1)S(1)}, u32[]{:S(2)}, u32[]{:S(2)}) collective-permute-start(bf16[32,7168]{1,0:T(8,128)(2,1)} %collective-permute-done.6.e2), channel_id=1, source_target_pairs={{0,32},{32,0},{64,96},{96,64},{1,33},{33,1},{65,97},{97,65},{2,34}... | collective-permute-start | bytes 1376264 | tf_op jit(solution)/shard_map/ppermute | solution.py:418
  46.1 2.9 %collective-permute-start.7 = (bf16[2,128,128]{2,1,0:T(8,128)(2,1)S(1)}, bf16[2,128,128]{2,1,0:T(8,128)(2,1)S(1)}, u32[]{:S(2)}, u32[]{:S(2)}) collective-permute-start(bf16[2,128,128]{2,1,0:T(8,128)(2,1)S(1)} %convert_element_type.42), channel_id=1, source_target_pairs={{64,0},{65,1},{66,2},{67,3},{68,4},{69,5},{70,6},{71,7},{72,8},{73... | collective-permute-start | bytes 196616 | tf_op jit(solution)/shard_map/ppermute | solution.py:465
  50.4 1.0 %collective-permute-done.7 = bf16[2,128,128]{2,1,0:T(8,128)(2,1)S(1)} collective-permute-done((bf16[2,128,128]{2,1,0:T(8,128)(2,1)S(1)}, bf16[2,128,128]{2,1,0:T(8,128)(2,1)S(1)}, u32[]{:S(2)}, u32[]{:S(2)}) %collective-permute-start.7) | collective-permute-done | bytes 65568 | tf_op jit(solution)/shard_map/ppermute | solution.py:465
  51.4 2.9 %collective-permute-start.13 = (bf16[32,9216]{1,0:T(8,128)(2,1)}, bf16[32,9216]{1,0:T(8,128)(2,1)S(1)}, u32[]{:S(2)}, u32[]{:S(2)}) collective-permute-start(bf16[32,9216]{1,0:T(8,128)(2,1)} %copy-done.3), channel_id=1, source_target_pairs={{0,64},{32,96},{64,0},{96,32},{1,65},{33,97},{65,1},{97,33},{2,66}... | collective-permute-start | bytes 1769480 | tf_op jit(solution)/shard_map/ppermute | solution.py:418
  54.4 6.3 %collective-permute-start.14 = (bf16[3,128,128]{2,1,0:T(8,128)(2,1)S(1)}, bf16[3,128,128]{2,1,0:T(8,128)(2,1)S(1)}, u32[]{:S(2)}, u32[]{:S(2)}) collective-permute-start(bf16[3,128,128]{2,1,0:T(8,128)(2,1)S(1)} %pad_maximum_fusion.2), channel_id=1, source_target_pairs={{0,30},{1,31},{2,0},{3,1},{4,2},{5,3},{6,4},{7,5},{8,6},{9,7},{10,... | collective-permute-start | bytes 294920 | tf_op jit(solution)/shard_map/ppermute | solution.py:476
  60.9 7.0 %collective-permute-done.11.below = bf16[3,128,128]{2,1,0:T(8,128)(2,1)S(1)} collective-permute-done((bf16[3,128,128]{2,1,0:T(8,128)(2,1)S(1)}, bf16[3,128,128]{2,1,0:T(8,128)(2,1)S(1)}, u32[]{:S(2)}, u32[]{:S(2)}) %collective-permute-start.11) | collective-permute-done | bytes 98336 | tf_op jit(solution)/shard_map/ppermute | solution.py:476
  67.9 0.9 %shard_map.121.n0 = f32[2,128,128]{2,1,0:T(8,128)S(1)} custom-call(s32[1]{0:T(128)} %bitcast.block_ref, f32[32,128]{1,0:T(8,128)S(1)} %get-tuple-element.55.corner_ref, f32[2,128,128]{2,1,0:T(8,128)S(1)} %convert_add_fusion.1.own, f32[2,128,128]{2,1,0:T(8,128)S(1)} %convert_add_fusion.other, bf16[3,128,128]{2,1,0:T(8,128)(2,1)S(1)} %collective-permute-done.11.below, ...), custom_call_target="tpu_custom_call" | custom-call | tf_op jit(solution)/shard_map/pallas_call | solution.py:338
  68.8 3.0 %collective-permute-start.16 = (f32[2,128,128]{2,1,0:T(8,128)S(1)}, f32[2,128,128]{2,1,0:T(8,128)S(1)}, u32[]{:S(2)}, u32[]{:S(2)}) collective-permute-start(f32[2,128,128]{2,1,0:T(8,128)S(1)} %shard_map.121.n0), channel_id=1, source_target_pairs={{0,32},{32,0},{64,96},{96,64},{1,33},{33,1},{65,97},{97,65},{2,34}... | collective-permute-start | bytes 393224 | tf_op jit(solution)/shard_map/ppermute | solution.py:418
  71.8 1.0 %collective-permute-done.16.n1 = f32[2,128,128]{2,1,0:T(8,128)S(1)} collective-permute-done((f32[2,128,128]{2,1,0:T(8,128)S(1)}, f32[2,128,128]{2,1,0:T(8,128)S(1)}, u32[]{:S(2)}, u32[]{:S(2)}) %collective-permute-start.16) | collective-permute-done | bytes 131104 | tf_op jit(solution)/shard_map/ppermute | solution.py:418
  72.8 2.3 %shard_map.122.rest_0_ = f32[32,16384]{1,0:T(8,128)} custom-call(bf16[64,128]{1,0:T(8,128)(2,1)S(1)} %get-tuple-element.32.w_ref, f32[32,128]{1,0:T(8,128)S(1)} %get-tuple-element.33.ends_ref, bf16[32,7168]{1,0:T(8,128)(2,1)S(1)} %copy-done.6, bf16[32,7168]{1,0:T(8,128)(2,1)S(1)} %collective-permute-done.5.e1, bf16[32,7168]{1,0:T(8,128)(2,1)} %collective-permute-done.6.e2, ...), custom_call_target="tpu_custom_call" | custom-call | tf_op jit(solution)/shard_map/pallas_call | solution.py:382
  75.5 1.6 %collective-permute-done.17.e3 = bf16[32,9216]{1,0:T(8,128)(2,1)S(1)} collective-permute-done((bf16[32,9216]{1,0:T(8,128)(2,1)S(1)}, bf16[32,9216]{1,0:T(8,128)(2,1)S(1)}, u32[]{:S(2)}, u32[]{:S(2)}) %collective-permute-start.17) | collective-permute-done | bytes 589856 | tf_op jit(solution)/shard_map/ppermute | solution.py:418
  77.1 1.3 %shard_map.123 = f32[32,16384]{1,0:T(8,128)} custom-call(bf16[64,128]{1,0:T(8,128)(2,1)S(1)} %get-tuple-element.32.w_ref, f32[32,128]{1,0:T(8,128)S(1)} %get-tuple-element.33.ends_ref, bf16[32,9216]{1,0:T(8,128)(2,1)S(1)} %copy-done.4, bf16[32,9216]{1,0:T(8,128)(2,1)S(1)} %collective-permute-done.12.e1, ...), custom_call_target="tpu_custom_call", output_to_operand_aliasing={{}: (8, {})} | custom-call | tf_op jit(solution)/shard_map/pallas_call | solution.py:382
  (71 shorter events, 4.0 us)
Async XLA Ops:
  0.0 22.1 %copy-start = (bf16[32,16512]{1,0:T(8,128)(2,1)S(1)}, bf16[32,16512]{1,0:T(8,128)(2,1)}, u32[]{:S(2)}) copy-start(bf16[32,16512]{1,0:T(8,128)(2,1)} %refs_6_.3) | copy-start | bytes 3170308
  0.0 16.6 %copy-start.10 = (s32[32]{0:T(128)S(1)}, s32[32]{0:T(128)}, u32[]{:S(2)}) copy-start(s32[32]{0:T(128)} %param.15) | copy-start | bytes 388
  0.0 16.6 %copy-start.9 = (f32[32]{0:T(128)S(1)}, f32[32]{0:T(128)}, u32[]{:S(2)}) copy-start(f32[32]{0:T(128)} %param.16) | copy-start | bytes 388
  0.1 20.6 %collective-permute-start = (bf16[32,16512]{1,0:T(8,128)(2,1)}, bf16[32,16512]{1,0:T(8,128)(2,1)S(1)}, u32[]{:S(2)}, u32[]{:S(2)}) collective-permute-start(bf16[32,16512]{1,0:T(8,128)(2,1)} %refs_6_.3), channel_id=1, source_target_pairs={{0,32},{32,0},{64,96},{96,64},{1,33},{33,1},{65,97},{97,65},{2,34}... | collective-permute-start | bytes 3170312 | tf_op jit(solution)/shard_map/ppermute | solution.py:418
  3.8 15.4 %collective-permute-start.2 = (bf16[32,8320]{1,0:T(8,128)(2,1)}, bf16[32,8320]{1,0:T(8,128)(2,1)S(1)}, u32[]{:S(2)}, u32[]{:S(2)}) collective-permute-start(bf16[32,8320]{1,0:T(8,128)(2,1)} %get-tuple-element.59), channel_id=1, source_target_pairs={{0,64},{32,96},{64,0},{96,32},{1,65},{33,97},{65,1},{97,33},{2,66}... | collective-permute-start | bytes 1597448 | tf_op jit(solution)/shard_map/ppermute | solution.py:418
  6.7 23.9 %collective-permute-start.1 = (bf16[32,8320]{1,0:T(8,128)(2,1)}, bf16[32,8320]{1,0:T(8,128)(2,1)S(1)}, u32[]{:S(2)}, u32[]{:S(2)}) collective-permute-start(bf16[32,8320]{1,0:T(8,128)(2,1)} %get-tuple-element.60), channel_id=1, source_target_pairs={{0,64},{32,96},{64,0},{96,32},{1,65},{33,97},{65,1},{97,33},{2,66}... | collective-permute-start | bytes 1597448 | tf_op jit(solution)/shard_map/ppermute | solution.py:418
  7.4 14.7 %copy-start.1 = (s32[32,16384]{1,0:T(8,128)S(1)}, s32[32,16384]{1,0:T(8,128)}, u32[]{:S(2)}) copy-start(s32[32,16384]{1,0:T(8,128)} %refs_12_.3) | copy-start | bytes 6291460
  19.2 2.9 %collective-permute-start.3 = (bf16[32,8320]{1,0:T(8,128)(2,1)S(1)}, bf16[32,8320]{1,0:T(8,128)(2,1)S(1)}, u32[]{:S(2)}, u32[]{:S(2)}) collective-permute-start(bf16[32,8320]{1,0:T(8,128)(2,1)S(1)} %collective-permute-done.2.refs_4_.refs_8_), channel_id=1, source_target_pairs={{0,32},{32,0},{64,96},{96,64},{1,33},{33,1},{65,97},{97,65},{2,34}... | collective-permute-start | bytes 1597448 | tf_op jit(solution)/shard_map/ppermute | solution.py:418
  30.6 13.3 %copy-start.5 = (bf16[32,7168]{1,0:T(8,128)(2,1)}, bf16[32,7168]{1,0:T(8,128)(2,1)S(1)}, u32[]{:S(2)}) copy-start(bf16[32,7168]{1,0:T(8,128)(2,1)S(1)} %get-tuple-element.48.e0) | copy-start | bytes 1376260
  30.6 3.7 %collective-permute-start.4 = (bf16[32,8320]{1,0:T(8,128)(2,1)S(1)}, bf16[32,8320]{1,0:T(8,128)(2,1)S(1)}, u32[]{:S(2)}, u32[]{:S(2)}) collective-permute-start(bf16[32,8320]{1,0:T(8,128)(2,1)S(1)} %collective-permute-done.1.refs_4_.refs_8_), channel_id=1, source_target_pairs={{0,32},{32,0},{64,96},{96,64},{1,33},{33,1},{65,97},{97,65},{2,34}... | collective-permute-start | bytes 1597448 | tf_op jit(solution)/shard_map/ppermute | solution.py:418
  31.5 13.2 %collective-permute-start.5 = (bf16[32,7168]{1,0:T(8,128)(2,1)S(1)}, bf16[32,7168]{1,0:T(8,128)(2,1)S(1)}, u32[]{:S(2)}, u32[]{:S(2)}) collective-permute-start(bf16[32,7168]{1,0:T(8,128)(2,1)S(1)} %get-tuple-element.48.e0), channel_id=1, source_target_pairs={{0,32},{32,0},{64,96},{96,64},{1,33},{33,1},{65,97},{97,65},{2,34}... | collective-permute-start | bytes 1376264 | tf_op jit(solution)/shard_map/ppermute | solution.py:418
  31.5 13.2 %collective-permute-start.6 = (bf16[32,7168]{1,0:T(8,128)(2,1)S(1)}, bf16[32,7168]{1,0:T(8,128)(2,1)}, u32[]{:S(2)}, u32[]{:S(2)}) collective-permute-start(bf16[32,7168]{1,0:T(8,128)(2,1)S(1)} %get-tuple-element.48.e0), channel_id=1, source_target_pairs={{0,64},{32,96},{64,0},{96,32},{1,65},{33,97},{65,1},{97,33},{2,66}... | collective-permute-start | bytes 1376264 | tf_op jit(solution)/shard_map/ppermute | solution.py:418
  44.7 28.1 %copy-start.6 = (bf16[32,7168]{1,0:T(8,128)(2,1)S(1)}, bf16[32,7168]{1,0:T(8,128)(2,1)}, u32[]{:S(2)}) copy-start(bf16[32,7168]{1,0:T(8,128)(2,1)} %copy-done.5) | copy-start | bytes 1376260
  44.7 9.6 %collective-permute-start.8 = (bf16[32,7168]{1,0:T(8,128)(2,1)}, bf16[32,7168]{1,0:T(8,128)(2,1)S(1)}, u32[]{:S(2)}, u32[]{:S(2)}) collective-permute-start(bf16[32,7168]{1,0:T(8,128)(2,1)} %collective-permute-done.6.e2), channel_id=1, source_target_pairs={{0,32},{32,0},{64,96},{96,64},{1,33},{33,1},{65,97},{97,65},{2,34}... | collective-permute-start | bytes 1376264 | tf_op jit(solution)/shard_map/ppermute | solution.py:418
  46.1 5.3 %collective-permute-start.7 = (bf16[2,128,128]{2,1,0:T(8,128)(2,1)S(1)}, bf16[2,128,128]{2,1,0:T(8,128)(2,1)S(1)}, u32[]{:S(2)}, u32[]{:S(2)}) collective-permute-start(bf16[2,128,128]{2,1,0:T(8,128)(2,1)S(1)} %convert_element_type.42), channel_id=1, source_target_pairs={{64,0},{65,1},{66,2},{67,3},{68,4},{69,5},{70,6},{71,7},{72,8},{73... | collective-permute-start | bytes 196616 | tf_op jit(solution)/shard_map/ppermute | solution.py:465
  49.0 5.3 %collective-permute-start.10 = (bf16[2,128,128]{2,1,0:T(8,128)(2,1)S(1)}, bf16[2,128,128]{2,1,0:T(8,128)(2,1)S(1)}, u32[]{:S(2)}, u32[]{:S(2)}) collective-permute-start(bf16[2,128,128]{2,1,0:T(8,128)(2,1)S(1)} %convert_element_type.42), channel_id=1, source_target_pairs={{65,0},{64,1},{67,2},{66,3},{69,4},{68,5},{71,6},{70,7},{73,8},{72... | collective-permute-start | bytes 196616 | tf_op jit(solution)/shard_map/ppermute | solution.py:465
  49.8 4.5 %collective-permute-start.9 = (bf16[2,128,128]{2,1,0:T(8,128)(2,1)S(1)}, bf16[2,128,128]{2,1,0:T(8,128)(2,1)S(1)}, u32[]{:S(2)}, u32[]{:S(2)}) collective-permute-start(bf16[2,128,128]{2,1,0:T(8,128)(2,1)S(1)} %convert_element_type.42), channel_id=1, source_target_pairs={{1,0},{0,1},{3,2},{2,3},{5,4},{4,5},{7,6},{6,7},{9,8},{8,9},{11,10... | collective-permute-start | bytes 196616 | tf_op jit(solution)/shard_map/ppermute | solution.py:465
  49.9 18.0 %collective-permute-start.12 = (bf16[32,9216]{1,0:T(8,128)(2,1)}, bf16[32,9216]{1,0:T(8,128)(2,1)S(1)}, u32[]{:S(2)}, u32[]{:S(2)}) collective-permute-start(bf16[32,9216]{1,0:T(8,128)(2,1)} %copy-done.3), channel_id=1, source_target_pairs={{0,32},{32,0},{64,96},{96,64},{1,33},{33,1},{65,97},{97,65},{2,34}... | collective-permute-start | bytes 1769480 | tf_op jit(solution)/shard_map/ppermute | solution.py:418
  51.4 23.7 %collective-permute-start.13 = (bf16[32,9216]{1,0:T(8,128)(2,1)}, bf16[32,9216]{1,0:T(8,128)(2,1)S(1)}, u32[]{:S(2)}, u32[]{:S(2)}) collective-permute-start(bf16[32,9216]{1,0:T(8,128)(2,1)} %copy-done.3), channel_id=1, source_target_pairs={{0,64},{32,96},{64,0},{96,32},{1,65},{33,97},{65,1},{97,33},{2,66}... | collective-permute-start | bytes 1769480 | tf_op jit(solution)/shard_map/ppermute | solution.py:418
  54.4 13.5 %collective-permute-start.14 = (bf16[3,128,128]{2,1,0:T(8,128)(2,1)S(1)}, bf16[3,128,128]{2,1,0:T(8,128)(2,1)S(1)}, u32[]{:S(2)}, u32[]{:S(2)}) collective-permute-start(bf16[3,128,128]{2,1,0:T(8,128)(2,1)S(1)} %pad_maximum_fusion.2), channel_id=1, source_target_pairs={{0,30},{1,31},{2,0},{3,1},{4,2},{5,3},{6,4},{7,5},{8,6},{9,7},{10,... | collective-permute-start | bytes 294920 | tf_op jit(solution)/shard_map/ppermute | solution.py:476
  60.7 7.2 %collective-permute-start.11 = (bf16[3,128,128]{2,1,0:T(8,128)(2,1)S(1)}, bf16[3,128,128]{2,1,0:T(8,128)(2,1)S(1)}, u32[]{:S(2)}, u32[]{:S(2)}) collective-permute-start(bf16[3,128,128]{2,1,0:T(8,128)(2,1)S(1)} %pad_maximum_fusion.1), channel_id=1, source_target_pairs={{0,2},{1,3},{2,4},{3,5},{4,6},{5,7},{6,8},{7,9},{8,10},{9,11},{10,... | collective-permute-start | bytes 294920 | tf_op jit(solution)/shard_map/ppermute | solution.py:476
  60.8 7.1 %collective-permute-start.15 = (bf16[128,128]{1,0:T(8,128)(2,1)S(1)}, bf16[128,128]{1,0:T(8,128)(2,1)S(1)}, u32[]{:S(2)}, u32[]{:S(2)}) collective-permute-start(bf16[128,128]{1,0:T(8,128)(2,1)S(1)} %get-tuple-element.63), channel_id=1, source_target_pairs={{0,4},{1,29},{2,6},{3,31},{4,8},{5,1},{6,10},{7,3},{8,12},{9,5},{1... | collective-permute-start | bytes 98312 | tf_op jit(solution)/shard_map/ppermute | solution.py:481
  68.8 3.9 %collective-permute-start.16 = (f32[2,128,128]{2,1,0:T(8,128)S(1)}, f32[2,128,128]{2,1,0:T(8,128)S(1)}, u32[]{:S(2)}, u32[]{:S(2)}) collective-permute-start(f32[2,128,128]{2,1,0:T(8,128)S(1)} %shard_map.121.n0), channel_id=1, source_target_pairs={{0,32},{32,0},{64,96},{96,64},{1,33},{33,1},{65,97},{97,65},{2,34}... | collective-permute-start | bytes 393224 | tf_op jit(solution)/shard_map/ppermute | solution.py:418
  75.0 2.1 %collective-permute-start.17 = (bf16[32,9216]{1,0:T(8,128)(2,1)S(1)}, bf16[32,9216]{1,0:T(8,128)(2,1)S(1)}, u32[]{:S(2)}, u32[]{:S(2)}) collective-permute-start(bf16[32,9216]{1,0:T(8,128)(2,1)S(1)} %collective-permute-done.13.e2), channel_id=1, source_target_pairs={{0,32},{32,0},{64,96},{96,64},{1,33},{33,1},{65,97},{97,65},{2,34}... | collective-permute-start | bytes 1769480 | tf_op jit(solution)/shard_map/ppermute | solution.py:418
  (8 other events, 42.7 us)

commit v6 on v5

--- a/solution.py
+++ b/solution.py
@@ -14,7 +14,8 @@
 SW = SUB * BLK
 HALO = 3
 SPLITS = (0, 2, 4)
-VMEM_LIMIT = 48 * 1024 * 1024
+LATE = 1
+VMEM_LIMIT = 32 * 1024 * 1024
 
 
 def cubic_terms(frac):
@@ -52,7 +53,7 @@
 NT = (((1,), (1,)), ((), ()))
 
 
-def tables_kernel(here_ref, shift_ref, tap_ref, inv_ref, couple_ref, *outs):
+def tables_kernel(here_ref, shift_ref, tap_ref, inv_ref, first_ref, last_ref, couple_ref, *outs):
     t_ref, w_ref, ends_ref, yw_ref, corner_ref = outs
     step = pl.program_id(0)
     block, mine = here_ref[0], here_ref[1]
@@ -70,7 +71,7 @@
     def _():
         lane = lax.broadcasted_iota(jnp.int32, (32, BLK), 1)
         odd, high = lax.rem(mine, 2) == 1, mine > 1
-        own = inv_ref[block, pl.ds(pl.multiple_of(mine * 32, 32), 32), :]
+        own = inv_ref[0, pl.ds(pl.multiple_of(mine * 32, 32), 32), :]
         swapped = jnp.where(lax.rem(lane // 32, 2) == 0, pltpu.roll(own, 96, 1), pltpu.roll(own, 32, 1))
         turned = jnp.where(odd, swapped, own)
         turned = jnp.where(high, pltpu.roll(turned, 64, 1), turned)
@@ -79,12 +80,12 @@
         couple = couple_ref[pl.ds(block, 1), :]
         ends_ref[...] = pair * jnp.where(lane == 0, couple[:, :1], couple[:, 1:2])
         row = lax.broadcasted_iota(jnp.int32, (8, BLK), 0)
-        tips = jnp.where(row == 0, inv_ref[block, 0:1, :], inv_ref[block, BLK - 1 :, :])
+        tips = jnp.where(row == 0, inv_ref[0, 0:1, :], inv_ref[0, BLK - 1 :, :])
         tips = jnp.where(row < 2, tips, 0.0)
         tips = jnp.where(odd, pltpu.roll(tips, 96, 1), tips)
         tips = jnp.where(high, pltpu.roll(tips, 64, 1), tips)
         yw_ref[...] = jnp.concatenate(split_hi_lo(tips), axis=0)[:, :32]
-        top, bottom = inv_ref[:, 0, :], inv_ref[:, BLK - 1, :]
+        top, bottom = first_ref[:, 0, :], last_ref[:, 7, :]
         west, east = couple_ref[:, 0:1], couple_ref[:, 1:2]
         values = (top[:, :1] * west, top[:, BLK - 1 :] * east, bottom[:, :1] * west, bottom[:, BLK - 1 :] * east)
         total = jnp.zeros((32, BLK), jnp.float32)
@@ -101,7 +102,12 @@
         grid_spec=pltpu.PrefetchScalarGridSpec(
             num_scalar_prefetch=3,
             grid=(tiles // TG,),
-            in_specs=[full(*inverse_y.shape), full(*couple_y.shape)],
+            in_specs=[
+                pl.BlockSpec((1, BLK, BLK), lambda l, here, *_: (here[0], 0, 0)),
+                pl.BlockSpec((inverse_y.shape[0], 8, BLK), lambda l, *_: (0, 0, 0)),
+                pl.BlockSpec((inverse_y.shape[0], 8, BLK), lambda l, *_: (0, BLK // 8 - 1, 0)),
+                full(*couple_y.shape),
+            ],
             out_specs=[
                 pl.BlockSpec((TG, 2 * BLK, BLK), lambda l, *_: (l, 0, 0)),
                 full(64, BLK),
@@ -118,7 +124,7 @@
             jax.ShapeDtypeStruct((32, BLK), jnp.float32),
         ],
         compiler_params=pltpu.CompilerParams(vmem_limit_bytes=VMEM_LIMIT),
-    )(here, shift, taps, inverse_y, couple_y)
+    )(here, shift, taps, inverse_y, inverse_y, inverse_y, couple_y)
 
 
 def split_hi_lo(value):
@@ -344,41 +350,46 @@
     )(block.reshape(1), corner, own, *others)
 
 
-def columns_kernel(start, w_ref, ends_ref, e0, e1, e2, e3, n0, n1, *rest):
+def columns_kernel(start, w_ref, ends_ref, n0, n1, *rest):
     out_ref, held, sems = rest[-3:]
     south, north = ends_ref[:, 0:1], ends_ref[:, 1:2]
     copies = []
-    for at in range(0, held.shape[1], SW):
-        cols = slice(at, at + SW)
-        rows = jnp.concatenate([e[:, cols] for e in (e0, e1, e2, e3)], axis=0)
-        both = jnp.dot(w_ref[...], rows, preferred_element_type=jnp.float32)
-        value = both[:32] + both[32:]
-        for i in range(SUB):
-            line = (start + at) // BLK + i
-            row = [n0[k, line : line + 1, :] + n1[k, line : line + 1, :] for k in range(2)]
-            here = slice(i * BLK, (i + 1) * BLK)
-            held[:, at + i * BLK : at + (i + 1) * BLK] = (
-                value[:, here] + south * row[0] + north * row[1]
+    at = 0
+    for chunk in range(0, (len(rest) - 3) // 4 * 4, 4):
+        pieces = rest[chunk : chunk + 4]
+        for within in range(0, pieces[0].shape[1], SW):
+            rows = jnp.concatenate([e[:, within : within + SW] for e in pieces], axis=0)
+            both = jnp.dot(w_ref[...], rows, preferred_element_type=jnp.float32)
+            value = both[:32] + both[32:]
+            for i in range(SUB):
+                line = (start + at) // BLK + i
+                row = [n0[k, line : line + 1, :] + n1[k, line : line + 1, :] for k in range(2)]
+                here = slice(i * BLK, (i + 1) * BLK)
+                held[:, at + i * BLK : at + (i + 1) * BLK] = (
+                    value[:, here] + south * row[0] + north * row[1]
+                )
+            copy = pltpu.make_async_copy(
+                held.at[:, at : at + SW],
+                out_ref.at[:, start + at : start + at + SW],
+                sems.at[at // SW],
             )
-        copy = pltpu.make_async_copy(
-            held.at[:, cols], out_ref.at[:, start + at : start + at + SW], sems.at[at // SW]
-        )
-        copy.start()
-        copies.append(copy)
+            copy.start()
+            copies.append(copy)
+            at += SW
     for copy in copies:
         copy.wait()
 
 
-def run_columns(start, total, w, ends, pieces, near, far, so_far):
-    width = pieces[0].shape[1]
+def run_columns(start, total, w, ends, chunks, near, far, so_far):
+    width = sum(pieces[0].shape[1] for pieces in chunks)
     vmem = pl.BlockSpec(memory_space=pltpu.VMEM)
-    operands = [w, ends, *pieces, near, far]
-    in_specs = [vmem] * 8
+    operands = [w, ends, near, far] + [piece for pieces in chunks for piece in pieces]
+    in_specs = [vmem] * len(operands)
     aliases = {}
     if so_far is not None:
+        aliases = {len(operands): 0}
         operands.append(so_far)
         in_specs.append(pl.BlockSpec(memory_space=pl.ANY))
-        aliases = {8: 0}
     return pl.pallas_call(
         functools.partial(columns_kernel, start),
         in_specs=in_specs,
@@ -417,12 +428,11 @@
     sibling = [(d, d ^ 1) for d in range(4)]
     swap = lambda value, pairs: lax.ppermute(value, "band", pairs)
 
-    near = swap(panels, sibling)
     bounds = [(SPLITS[i], SPLITS[i + 1]) for i in range(len(SPLITS) - 1)]
     gathered = []
+    near = swap(panels, sibling)
     for first, stop in bounds:
-        far = swap(panels[:, first * GW : stop * GW + BLK], across)
-        gathered.append(far)
+        gathered.append(swap(panels[:, first * GW : stop * GW + BLK], across))
 
     order = ((jnp.arange(4, dtype=jnp.int32) ^ mine)[:, None] * rows + jnp.arange(rows)[None, :]).reshape(-1)
     w = jnp.concatenate(
@@ -443,6 +453,7 @@
     state = None
     sent = []
     parts = []
+    early = len(bounds) - LATE
     for (first, stop), far in zip(bounds, gathered):
         if state is not None:
             far, state = lax.optimization_barrier((far, state))
@@ -451,12 +462,12 @@
             first, stop, groups, state, kinds, couple_x, panels, got, w, tables,
             void_mask, background, inverse_x, lanes, yw,
         )
-        far = swap(east_west, across)
+        far = swap(east_west, across) if len(sent) < early else None
         sent.append([east_west, swap(east_west, sibling), far])
         parts.append(part)
     together = lax.optimization_barrier
     part = jnp.concatenate(parts, axis=1) if len(parts) > 1 else parts[0]
-    for pieces in sent[:-1]:
+    for pieces in sent[:early]:
         part, pieces[1], pieces[2] = together((part, pieces[1], pieces[2]))
 
     every = [(d, k) for d in range(4) for k in range(n_wide)]
@@ -468,9 +479,9 @@
     second = block % 2
     own = part + fetch(2, 0)
     other = fetch(0, 1) + fetch(2, 1)
-    for pieces in sent[:-1]:
-        pieces.append(swap(pieces[2], sibling))
-        own, pieces[3] = together((own, pieces[3]))
+    for pieces in sent[early:]:
+        last, own, other = together((pieces[0], own, other))
+        pieces[2] = swap(last, across)
     even = jnp.where(second == 0, own, other).astype(jnp.bfloat16)
     odd = jnp.where(second == 0, other, own).astype(jnp.bfloat16)
     shifted = lambda value, k: lax.ppermute(
@@ -481,24 +492,21 @@
     beyond = lax.ppermute(
         jnp.where(second == 0, odd[1], even[0]),
         "wide",
-        [(i, (i + 4 * (1 - 2 * (i % 2))) % n_wide) for i in range(n_wide)],
-    )
-    before, sent[-1][1] = together((before, sent[-1][1]))
+        [(i, j) for i in range(n_wide) for j in [i + 4 * (1 - 2 * (i % 2))] if 0 <= j < n_wide],
+    )
+    for pieces in sent[early:]:
+        before, pieces[1] = together((before, pieces[1]))
+    for pieces in sent[:early]:
+        pieces.append(swap(pieces[2], sibling))
+        before, pieces[3] = together((before, pieces[3]))
     forced = run_ends(n_wide, block, corner, own, other, before, after, beyond)
+    for pieces in sent[early:]:
+        pieces[2], forced = together((pieces[2], forced))
     rest = swap(forced, sibling)
-
-    result = None
-    position = 0
-    for pieces in sent:
-        if len(pieces) == 3:
-            if result is None:
-                pieces[2], rest = together((pieces[2], rest))
-            else:
-                pieces[2], result = together((pieces[2], result))
-            pieces.append(swap(pieces[2], sibling))
-        result = run_columns(position, width, w_y, ends_y, pieces, forced, rest, result)
-        position += pieces[0].shape[1]
-    return result
+    for pieces in sent[early:]:
+        pieces.append(swap(pieces[2], sibling))
+
+    return run_columns(0, width, w_y, ends_y, sent, forced, rest, None)
 
 
 def solution(mesh):

time: 78.6 us -> 75.8 us (0.964)
  the two profiles are of different devices: /device:TPU:1 before, /device:TPU:25 now
where the time goes in v6:
time: 75.8 us; the launch traced here: 75 us
  starting transfers between devices  27.6 us (36%)
  Pallas kernels  24.9 us (33%)
  waiting for transfers between devices  19.1 us (25%)
  local copies, waits for them, and re-layouts  2.64 us (3%)
    ppermute x12, starting transfers between devices, body(): swap = lambda value, pairs: lax.ppermute(value, 'band', pairs)  16.8 us
    pallas_call x2, Pallas kernels, run_rows(): pl.pallas_call(functools.partial(rows_kernel, first, groups, carried), gr...  16.3 us
    ppermute x12, waiting for transfers between devices, body(): swap = lambda value, pairs: lax.ppermute(value, 'band', pairs)  11.1 us
    pallas_call x1, Pallas kernels, run_tables(): pl.pallas_call(tables_kernel, grid_spec=pltpu.PrefetchScalarGridSpec(num_...  6.11 us
    ppermute x2, starting transfers between devices, body(): lax.ppermute(value, 'wide', [(i, (i + 2 * k) % n_wide) for i in range(n_w...  4.09 us
    ppermute x1, waiting for transfers between devices, body(): lax.ppermute(jnp.where(second == 0, odd[1], even[0]), 'wide', [(i, j) for...  4 us
    ppermute x3, starting transfers between devices, body(): lax.ppermute(half, ('band', 'wide'), [(at(d ^ db, k ^ dw), at(d, k)) for...  3.69 us
    ppermute x1, starting transfers between devices, body(): lax.ppermute(jnp.where(second == 0, odd[1], even[0]), 'wide', [(i, j) for...  3.02 us
  transfers between devices with their start and end apart: 18, of which 9 were waited for; matrix products, arithmetic and copies ran while one was open for 4% of the time, Pallas kernels for 31%

profile of v6, /device:TPU:25, one launch (start us, length us, event | category | flops | bytes accessed | tf_op | source)
XLA Modules:
  0.0 75.0 jit_solution(6704087736896857640)
XLA Ops:
  0.0 0.8 %collective-permute-start = (bf16[32,16512]{1,0:T(8,128)(2,1)}, bf16[32,16512]{1,0:T(8,128)(2,1)S(1)}, u32[]{:S(2)}, u32[]{:S(2)}) collective-permute-start(bf16[32,16512]{1,0:T(8,128)(2,1)} %refs_6_.3), channel_id=1, source_target_pairs={{0,32},{32,0},{64,96},{96,64},{1,33},{33,1},{65,97},{97,65},{2,34}... | collective-permute-start | bytes 3170312 | tf_op jit(solution)/shard_map/ppermute | solution.py:429
  0.8 2.3 %fusion.8 = (bf16[32,8320]{1,0:T(8,128)(2,1)}, bf16[32,8320]{1,0:T(8,128)(2,1)}) fusion(bf16[32,16512]{1,0:T(8,128)(2,1)} %refs_6_.3), kind=kLoop, calls=%fused_computation.42 | loop fusion | bytes 2129920 | tf_op jit(solution)/shard_map/slice | solution.py:435
  3.1 2.7 %collective-permute-start.2 = (bf16[32,8320]{1,0:T(8,128)(2,1)}, bf16[32,8320]{1,0:T(8,128)(2,1)}, u32[]{:S(2)}, u32[]{:S(2)}) collective-permute-start(bf16[32,8320]{1,0:T(8,128)(2,1)} %get-tuple-element.65), channel_id=1, source_target_pairs={{0,64},{32,96},{64,0},{96,32},{1,65},{33,97},{65,1},{97,33},{2,66}... | collective-permute-start | bytes 1597448 | tf_op jit(solution)/shard_map/ppermute | solution.py:429
  6.7 6.1 %shard_map.118 = (bf16[128,256,128]{2,1,0:T(8,128)(2,1)S(1)}, bf16[64,128]{1,0:T(8,128)(2,1)S(1)}, f32[32,128]{1,0:T(8,128)S(1)}, bf16[16,32]{1,0:T(8,128)(2,1)S(1)}, f32[32,128]{1,0:T(8,128)S(1)}) custom-call(s32[2]{0:T(128)S(1)} %pad_add_fusion.here_ref, s32[128]{0:T(128)S(1)} %copy-done.5, f32[4,128]{1,0:T(4,128)S(1)} %maximum_reduce-precision_fusion.tap_ref, ...), custom_call_target="tpu_custom_call" | custom-call | tf_op jit(solution)/shard_map/pallas_call | solution.py:100
  12.9 5.6 %collective-permute-done.2.refs_4_.refs_8_ = bf16[32,8320]{1,0:T(8,128)(2,1)} collective-permute-done((bf16[32,8320]{1,0:T(8,128)(2,1)}, bf16[32,8320]{1,0:T(8,128)(2,1)}, u32[]{:S(2)}, u32[]{:S(2)}) %collective-permute-start.2) | collective-permute-done | bytes 532512 | tf_op jit(solution)/shard_map/ppermute | solution.py:429
  18.4 1.5 %collective-permute-start.3 = (bf16[32,8320]{1,0:T(8,128)(2,1)}, bf16[32,8320]{1,0:T(8,128)(2,1)S(1)}, u32[]{:S(2)}, u32[]{:S(2)}) collective-permute-start(bf16[32,8320]{1,0:T(8,128)(2,1)} %collective-permute-done.2.refs_4_.refs_8_), channel_id=1, source_target_pairs={{0,32},{32,0},{64,96},{96,64},{1,33},{33,1},{65,97},{97,65},{2,34}... | collective-permute-start | bytes 1597448 | tf_op jit(solution)/shard_map/ppermute | solution.py:429
  20.1 1.6 %collective-permute-done.3.refs_5_.refs_9_ = bf16[32,8320]{1,0:T(8,128)(2,1)S(1)} collective-permute-done((bf16[32,8320]{1,0:T(8,128)(2,1)}, bf16[32,8320]{1,0:T(8,128)(2,1)S(1)}, u32[]{:S(2)}, u32[]{:S(2)}) %collective-permute-start.3) | collective-permute-done | bytes 532512 | tf_op jit(solution)/shard_map/ppermute | solution.py:429
  21.7 7.7 %shard_map.119 = (bf16[32,7168]{1,0:T(8,128)(2,1)S(1)}, f32[2,56,128]{2,1,0:T(8,128)S(1)}, f32[8,32,128]{2,1,0:T(8,128)S(1)}, f32[40,128]{1,0:T(8,128)S(1)}, f32...) custom-call(s32[128]{0:T(128)S(1)} %fusion.7.refs_0_, f32[2,128]{1,0:T(2,128)S(1)} %copy-done.4, ...), custom_call_target="tpu_custom_call" | custom-call | tf_op jit(solution)/shard_map/pallas_call | solution.py:303
  29.8 1.0 %collective-permute-start.4 = (bf16[32,8320]{1,0:T(8,128)(2,1)}, bf16[32,8320]{1,0:T(8,128)(2,1)S(1)}, u32[]{:S(2)}, u32[]{:S(2)}) collective-permute-start(bf16[32,8320]{1,0:T(8,128)(2,1)} %collective-permute-done.1.refs_4_.refs_8_), channel_id=1, source_target_pairs={{0,32},{32,0},{64,96},{96,64},{1,33},{33,1},{65,97},{97,65},{2,34}... | collective-permute-start | bytes 1597448 | tf_op jit(solution)/shard_map/ppermute | solution.py:429
  30.8 2.7 %collective-permute-start.6 = (bf16[32,7168]{1,0:T(8,128)(2,1)S(1)}, bf16[32,7168]{1,0:T(8,128)(2,1)S(1)}, u32[]{:S(2)}, u32[]{:S(2)}) collective-permute-start(bf16[32,7168]{1,0:T(8,128)(2,1)S(1)} %get-tuple-element.51.rest_0_), channel_id=1, source_target_pairs={{0,64},{32,96},{64,0},{96,32},{1,65},{33,97},{65,1},{97,33},{2,66}... | collective-permute-start | bytes 1376264 | tf_op jit(solution)/shard_map/ppermute | solution.py:429
  33.6 8.6 %shard_map.120 = (bf16[32,9216]{1,0:T(8,128)(2,1)S(1)}, f32[2,72,128]{2,1,0:T(8,128)S(1)}, f32[8,32,128]{2,1,0:T(8,128)}, f32[40,128]{1,0:T(8,128)}, f32[40,128]{1,0:T(8,128)}, /*index=5*/bf16[16,1024]{1,0:T(8,128)(2,1)}) custom-call(s32[128]{0:T(128)S(1)} %fusion.7.refs_0_, f32[2,128]{1,0:T(2,128)S(1)} %copy-done.4, bf16[32,16512]{1,0:T(8,128)(2,1)S(1)} %copy-done, ...), custom_call_target="tpu_custom_call" | custom-call | tf_op jit(solution)/shard_map/pallas_call | solution.py:303
  42.1 1.7 %collective-permute-done.6.rest_2_ = bf16[32,7168]{1,0:T(8,128)(2,1)S(1)} collective-permute-done((bf16[32,7168]{1,0:T(8,128)(2,1)S(1)}, bf16[32,7168]{1,0:T(8,128)(2,1)S(1)}, u32[]{:S(2)}, u32[]{:S(2)}) %collective-permute-start.6) | collective-permute-done | bytes 458784 | tf_op jit(solution)/shard_map/ppermute | solution.py:429
  43.9 2.8 %collective-permute-start.7 = (bf16[2,128,128]{2,1,0:T(8,128)(2,1)S(1)}, bf16[2,128,128]{2,1,0:T(8,128)(2,1)S(1)}, u32[]{:S(2)}, u32[]{:S(2)}) collective-permute-start(bf16[2,128,128]{2,1,0:T(8,128)(2,1)S(1)} %convert_element_type.42), channel_id=1, source_target_pairs={{64,0},{65,1},{66,2},{67,3},{68,4},{69,5},{70,6},{71,7},{72,8},{73... | collective-permute-start | bytes 196616 | tf_op jit(solution)/shard_map/ppermute | solution.py:476
  47.6 1.9 %collective-permute-start.12 = (bf16[32,9216]{1,0:T(8,128)(2,1)S(1)}, bf16[32,9216]{1,0:T(8,128)(2,1)S(1)}, u32[]{:S(2)}, u32[]{:S(2)}) collective-permute-start(bf16[32,9216]{1,0:T(8,128)(2,1)S(1)} %get-tuple-element.53.rest_4_), channel_id=1, source_target_pairs={{0,32},{32,0},{64,96},{96,64},{1,33},{33,1},{65,97},{97,65},{2,34}... | collective-permute-start | bytes 1769480 | tf_op jit(solution)/shard_map/ppermute | solution.py:429
  50.2 1.4 %collective-permute-done.9 = bf16[2,128,128]{2,1,0:T(8,128)(2,1)S(1)} collective-permute-done((bf16[2,128,128]{2,1,0:T(8,128)(2,1)S(1)}, bf16[2,128,128]{2,1,0:T(8,128)(2,1)S(1)}, u32[]{:S(2)}, u32[]{:S(2)}) %collective-permute-start.9) | collective-permute-done | bytes 65568 | tf_op jit(solution)/shard_map/ppermute | solution.py:476
  52.4 1.7 %collective-permute-start.11 = (bf16[3,128,128]{2,1,0:T(8,128)(2,1)S(1)}, bf16[3,128,128]{2,1,0:T(8,128)(2,1)S(1)}, u32[]{:S(2)}, u32[]{:S(2)}) collective-permute-start(bf16[3,128,128]{2,1,0:T(8,128)(2,1)S(1)} %pad_maximum_fusion.1), channel_id=1, source_target_pairs={{0,2},{1,3},{2,4},{3,5},{4,6},{5,7},{6,8},{7,9},{8,10},{9,11},{10,... | collective-permute-start | bytes 294920 | tf_op jit(solution)/shard_map/ppermute | solution.py:487
  54.1 2.4 %collective-permute-start.14 = (bf16[3,128,128]{2,1,0:T(8,128)(2,1)S(1)}, bf16[3,128,128]{2,1,0:T(8,128)(2,1)S(1)}, u32[]{:S(2)}, u32[]{:S(2)}) collective-permute-start(bf16[3,128,128]{2,1,0:T(8,128)(2,1)S(1)} %pad_maximum_fusion.2), channel_id=1, source_target_pairs={{0,30},{1,31},{2,0},{3,1},{4,2},{5,3},{6,4},{7,5},{8,6},{9,7},{10,... | collective-permute-start | bytes 294920 | tf_op jit(solution)/shard_map/ppermute | solution.py:487
  56.5 1.9 %collective-permute-done.11.below = bf16[3,128,128]{2,1,0:T(8,128)(2,1)S(1)} collective-permute-done((bf16[3,128,128]{2,1,0:T(8,128)(2,1)S(1)}, bf16[3,128,128]{2,1,0:T(8,128)(2,1)S(1)}, u32[]{:S(2)}, u32[]{:S(2)}) %collective-permute-start.11) | collective-permute-done | bytes 98336 | tf_op jit(solution)/shard_map/ppermute | solution.py:487
  58.4 3.0 %collective-permute-start.15 = (bf16[128,128]{1,0:T(8,128)(2,1)S(1)}, bf16[128,128]{1,0:T(8,128)(2,1)S(1)}, u32[]{:S(2)}, u32[]{:S(2)}) collective-permute-start(bf16[128,128]{1,0:T(8,128)(2,1)S(1)} %get-tuple-element.69), channel_id=1, source_target_pairs={{0,4},{2,6},{4,8},{5,1},{6,10},{7,3},{8,12},{9,5},{10,14},{11,7},{... | collective-permute-start | bytes 98312 | tf_op jit(solution)/shard_map/ppermute | solution.py:492
  61.5 4.0 %collective-permute-done.15.distant = bf16[128,128]{1,0:T(8,128)(2,1)S(1)} collective-permute-done((bf16[128,128]{1,0:T(8,128)(2,1)S(1)}, bf16[128,128]{1,0:T(8,128)(2,1)S(1)}, u32[]{:S(2)}, u32[]{:S(2)}) %collective-permute-start.15) | collective-permute-done | bytes 32800 | tf_op jit(solution)/shard_map/ppermute | solution.py:492
  65.5 0.9 %shard_map.121.n0 = f32[2,128,128]{2,1,0:T(8,128)S(1)} custom-call(s32[1]{0:T(128)} %bitcast.block_ref, f32[32,128]{1,0:T(8,128)S(1)} %get-tuple-element.54.corner_ref, f32[2,128,128]{2,1,0:T(8,128)S(1)} %convert_add_fusion.1.own, f32[2,128,128]{2,1,0:T(8,128)S(1)} %convert_add_fusion.other, bf16[3,128,128]{2,1,0:T(8,128)(2,1)S(1)} %collective-permute-done.11.below, ...), custom_call_target="tpu_custom_call" | custom-call | tf_op jit(solution)/shard_map/pallas_call | solution.py:344
  66.4 5.1 %collective-permute-start.17 = (bf16[32,9216]{1,0:T(8,128)(2,1)S(1)}, bf16[32,9216]{1,0:T(8,128)(2,1)S(1)}, u32[]{:S(2)}, u32[]{:S(2)}) collective-permute-start(bf16[32,9216]{1,0:T(8,128)(2,1)S(1)} %collective-permute-done.10.rest_6_), channel_id=1, source_target_pairs={{0,32},{32,0},{64,96},{96,64},{1,33},{33,1},{65,97},{97,65},{2,34}... | collective-permute-start | bytes 1769480 | tf_op jit(solution)/shard_map/ppermute | solution.py:429
  71.6 1.7 %collective-permute-done.16.n1 = f32[2,128,128]{2,1,0:T(8,128)S(1)} collective-permute-done((f32[2,128,128]{2,1,0:T(8,128)S(1)}, f32[2,128,128]{2,1,0:T(8,128)S(1)}, u32[]{:S(2)}, u32[]{:S(2)}) %collective-permute-start.16) | collective-permute-done | bytes 131104 | tf_op jit(solution)/shard_map/ppermute | solution.py:429
  73.3 1.6 %shard_map.122 = f32[32,16384]{1,0:T(8,128)} custom-call(bf16[64,128]{1,0:T(8,128)(2,1)S(1)} %get-tuple-element.35.w_ref, f32[32,128]{1,0:T(8,128)S(1)} %get-tuple-element.36.ends_ref, f32[2,128,128]{2,1,0:T(8,128)S(1)} %shard_map.121.n0, f32[2,128,128]{2,1,0:T(8,128)S(1)} %collective-permute-done.16.n1, bf16[32,7168]{1,0:T(8,128)(2,1)S(1)} %get-tuple-element.51.rest_0_, ...), custom_call_target="tpu_custom_call" | custom-call | tf_op jit(solution)/shard_map/pallas_call | solution.py:393
  (64 shorter events, 3.9 us)
Async XLA Ops:
  0.0 6.5 %copy-start.8 = (f32[2,32]{1,0:T(2,128)S(1)}, f32[2,32]{1,0:T(2,128)}, u32[]{:S(2)}) copy-start(f32[2,32]{1,0:T(2,128)} %param.23) | copy-start | bytes 772
  0.0 6.6 %copy-start.5 = (s32[128]{0:T(128)S(1)}, s32[128]{0:T(128)}, u32[]{:S(2)}) copy-start(s32[128]{0:T(128)} %shift_ref.1) | copy-start | bytes 1540
  0.0 6.6 %copy-start.1 = (f32[32,128,128]{2,1,0:T(8,128)S(1)}, f32[32,128,128]{2,1,0:T(8,128)}, u32[]{:S(2)}) copy-start(f32[32,128,128]{2,1,0:T(8,128)} %last_ref.1) | copy-start | bytes 6291460
  0.0 20.1 %collective-permute-start = (bf16[32,16512]{1,0:T(8,128)(2,1)}, bf16[32,16512]{1,0:T(8,128)(2,1)S(1)}, u32[]{:S(2)}, u32[]{:S(2)}) collective-permute-start(bf16[32,16512]{1,0:T(8,128)(2,1)} %refs_6_.3), channel_id=1, source_target_pairs={{0,32},{32,0},{64,96},{96,64},{1,33},{33,1},{65,97},{97,65},{2,34}... | collective-permute-start | bytes 3170312 | tf_op jit(solution)/shard_map/ppermute | solution.py:429
  3.1 15.4 %collective-permute-start.2 = (bf16[32,8320]{1,0:T(8,128)(2,1)}, bf16[32,8320]{1,0:T(8,128)(2,1)}, u32[]{:S(2)}, u32[]{:S(2)}) collective-permute-start(bf16[32,8320]{1,0:T(8,128)(2,1)} %get-tuple-element.65), channel_id=1, source_target_pairs={{0,64},{32,96},{64,0},{96,32},{1,65},{33,97},{65,1},{97,33},{2,66}... | collective-permute-start | bytes 1597448 | tf_op jit(solution)/shard_map/ppermute | solution.py:429
  5.8 24.0 %collective-permute-start.1 = (bf16[32,8320]{1,0:T(8,128)(2,1)}, bf16[32,8320]{1,0:T(8,128)(2,1)}, u32[]{:S(2)}, u32[]{:S(2)}) collective-permute-start(bf16[32,8320]{1,0:T(8,128)(2,1)} %get-tuple-element.66), channel_id=1, source_target_pairs={{0,64},{32,96},{64,0},{96,32},{1,65},{33,97},{65,1},{97,33},{2,66}... | collective-permute-start | bytes 1597448 | tf_op jit(solution)/shard_map/ppermute | solution.py:429
  6.7 15.1 %copy-start = (bf16[32,16512]{1,0:T(8,128)(2,1)S(1)}, bf16[32,16512]{1,0:T(8,128)(2,1)}, u32[]{:S(2)}) copy-start(bf16[32,16512]{1,0:T(8,128)(2,1)} %refs_6_.3) | copy-start | bytes 3170308
  6.7 15.0 %copy-start.2 = (s32[32,16384]{1,0:T(8,128)S(1)}, s32[32,16384]{1,0:T(8,128)}, u32[]{:S(2)}) copy-start(s32[32,16384]{1,0:T(8,128)} %refs_12_.3) | copy-start | bytes 6291460
  6.7 15.0 %copy-start.3 = (f32[32,16384]{1,0:T(8,128)S(1)}, f32[32,16384]{1,0:T(8,128)}, u32[]{:S(2)}) copy-start(f32[32,16384]{1,0:T(8,128)} %refs_13_.3) | copy-start | bytes 6291460
  18.4 3.3 %collective-permute-start.3 = (bf16[32,8320]{1,0:T(8,128)(2,1)}, bf16[32,8320]{1,0:T(8,128)(2,1)S(1)}, u32[]{:S(2)}, u32[]{:S(2)}) collective-permute-start(bf16[32,8320]{1,0:T(8,128)(2,1)} %collective-permute-done.2.refs_4_.refs_8_), channel_id=1, source_target_pairs={{0,32},{32,0},{64,96},{96,64},{1,33},{33,1},{65,97},{97,65},{2,34}... | collective-permute-start | bytes 1597448 | tf_op jit(solution)/shard_map/ppermute | solution.py:429
  29.8 3.7 %collective-permute-start.4 = (bf16[32,8320]{1,0:T(8,128)(2,1)}, bf16[32,8320]{1,0:T(8,128)(2,1)S(1)}, u32[]{:S(2)}, u32[]{:S(2)}) collective-permute-start(bf16[32,8320]{1,0:T(8,128)(2,1)} %collective-permute-done.1.refs_4_.refs_8_), channel_id=1, source_target_pairs={{0,32},{32,0},{64,96},{96,64},{1,33},{33,1},{65,97},{97,65},{2,34}... | collective-permute-start | bytes 1597448 | tf_op jit(solution)/shard_map/ppermute | solution.py:429
  30.8 11.3 %collective-permute-start.5 = (bf16[32,7168]{1,0:T(8,128)(2,1)S(1)}, bf16[32,7168]{1,0:T(8,128)(2,1)S(1)}, u32[]{:S(2)}, u32[]{:S(2)}) collective-permute-start(bf16[32,7168]{1,0:T(8,128)(2,1)S(1)} %get-tuple-element.51.rest_0_), channel_id=1, source_target_pairs={{0,32},{32,0},{64,96},{96,64},{1,33},{33,1},{65,97},{97,65},{2,34}... | collective-permute-start | bytes 1376264 | tf_op jit(solution)/shard_map/ppermute | solution.py:429
  30.8 13.1 %collective-permute-start.6 = (bf16[32,7168]{1,0:T(8,128)(2,1)S(1)}, bf16[32,7168]{1,0:T(8,128)(2,1)S(1)}, u32[]{:S(2)}, u32[]{:S(2)}) collective-permute-start(bf16[32,7168]{1,0:T(8,128)(2,1)S(1)} %get-tuple-element.51.rest_0_), channel_id=1, source_target_pairs={{0,64},{32,96},{64,0},{96,32},{1,65},{33,97},{65,1},{97,33},{2,66}... | collective-permute-start | bytes 1376264 | tf_op jit(solution)/shard_map/ppermute | solution.py:429
  43.9 5.6 %collective-permute-start.7 = (bf16[2,128,128]{2,1,0:T(8,128)(2,1)S(1)}, bf16[2,128,128]{2,1,0:T(8,128)(2,1)S(1)}, u32[]{:S(2)}, u32[]{:S(2)}) collective-permute-start(bf16[2,128,128]{2,1,0:T(8,128)(2,1)S(1)} %convert_element_type.42), channel_id=1, source_target_pairs={{64,0},{65,1},{66,2},{67,3},{68,4},{69,5},{70,6},{71,7},{72,8},{73... | collective-permute-start | bytes 196616 | tf_op jit(solution)/shard_map/ppermute | solution.py:476
  46.7 3.5 %collective-permute-start.8 = (bf16[2,128,128]{2,1,0:T(8,128)(2,1)S(1)}, bf16[2,128,128]{2,1,0:T(8,128)(2,1)S(1)}, u32[]{:S(2)}, u32[]{:S(2)}) collective-permute-start(bf16[2,128,128]{2,1,0:T(8,128)(2,1)S(1)} %convert_element_type.42), channel_id=1, source_target_pairs={{1,0},{0,1},{3,2},{2,3},{5,4},{4,5},{7,6},{6,7},{9,8},{8,9},{11,10... | collective-permute-start | bytes 196616 | tf_op jit(solution)/shard_map/ppermute | solution.py:476
  47.0 4.6 %collective-permute-start.9 = (bf16[2,128,128]{2,1,0:T(8,128)(2,1)S(1)}, bf16[2,128,128]{2,1,0:T(8,128)(2,1)S(1)}, u32[]{:S(2)}, u32[]{:S(2)}) collective-permute-start(bf16[2,128,128]{2,1,0:T(8,128)(2,1)S(1)} %convert_element_type.42), channel_id=1, source_target_pairs={{65,0},{64,1},{67,2},{66,3},{69,4},{68,5},{71,6},{70,7},{73,8},{72... | collective-permute-start | bytes 196616 | tf_op jit(solution)/shard_map/ppermute | solution.py:476
  47.6 13.9 %collective-permute-start.12 = (bf16[32,9216]{1,0:T(8,128)(2,1)S(1)}, bf16[32,9216]{1,0:T(8,128)(2,1)S(1)}, u32[]{:S(2)}, u32[]{:S(2)}) collective-permute-start(bf16[32,9216]{1,0:T(8,128)(2,1)S(1)} %get-tuple-element.53.rest_4_), channel_id=1, source_target_pairs={{0,32},{32,0},{64,96},{96,64},{1,33},{33,1},{65,97},{97,65},{2,34}... | collective-permute-start | bytes 1769480 | tf_op jit(solution)/shard_map/ppermute | solution.py:429
  49.5 11.9 %collective-permute-start.13 = (bf16[32,7168]{1,0:T(8,128)(2,1)S(1)}, bf16[32,7168]{1,0:T(8,128)(2,1)S(1)}, u32[]{:S(2)}, u32[]{:S(2)}) collective-permute-start(bf16[32,7168]{1,0:T(8,128)(2,1)S(1)} %collective-permute-done.6.rest_2_), channel_id=1, source_target_pairs={{0,32},{32,0},{64,96},{96,64},{1,33},{33,1},{65,97},{97,65},{2,34}... | collective-permute-start | bytes 1376264 | tf_op jit(solution)/shard_map/ppermute | solution.py:429
  51.6 14.8 %collective-permute-start.10 = (bf16[32,9216]{1,0:T(8,128)(2,1)S(1)}, bf16[32,9216]{1,0:T(8,128)(2,1)S(1)}, u32[]{:S(2)}, u32[]{:S(2)}) collective-permute-start(bf16[32,9216]{1,0:T(8,128)(2,1)S(1)} %get-tuple-element.53.rest_4_), channel_id=1, source_target_pairs={{0,64},{32,96},{64,0},{96,32},{1,65},{33,97},{65,1},{97,33},{2,66}... | collective-permute-start | bytes 1769480 | tf_op jit(solution)/shard_map/ppermute | solution.py:429
  52.4 6.0 %collective-permute-start.11 = (bf16[3,128,128]{2,1,0:T(8,128)(2,1)S(1)}, bf16[3,128,128]{2,1,0:T(8,128)(2,1)S(1)}, u32[]{:S(2)}, u32[]{:S(2)}) collective-permute-start(bf16[3,128,128]{2,1,0:T(8,128)(2,1)S(1)} %pad_maximum_fusion.1), channel_id=1, source_target_pairs={{0,2},{1,3},{2,4},{3,5},{4,6},{5,7},{6,8},{7,9},{8,10},{9,11},{10,... | collective-permute-start | bytes 294920 | tf_op jit(solution)/shard_map/ppermute | solution.py:487
  54.1 11.3 %collective-permute-start.14 = (bf16[3,128,128]{2,1,0:T(8,128)(2,1)S(1)}, bf16[3,128,128]{2,1,0:T(8,128)(2,1)S(1)}, u32[]{:S(2)}, u32[]{:S(2)}) collective-permute-start(bf16[3,128,128]{2,1,0:T(8,128)(2,1)S(1)} %pad_maximum_fusion.2), channel_id=1, source_target_pairs={{0,30},{1,31},{2,0},{3,1},{4,2},{5,3},{6,4},{7,5},{8,6},{9,7},{10,... | collective-permute-start | bytes 294920 | tf_op jit(solution)/shard_map/ppermute | solution.py:487
  58.4 7.1 %collective-permute-start.15 = (bf16[128,128]{1,0:T(8,128)(2,1)S(1)}, bf16[128,128]{1,0:T(8,128)(2,1)S(1)}, u32[]{:S(2)}, u32[]{:S(2)}) collective-permute-start(bf16[128,128]{1,0:T(8,128)(2,1)S(1)} %get-tuple-element.69), channel_id=1, source_target_pairs={{0,4},{2,6},{4,8},{5,1},{6,10},{7,3},{8,12},{9,5},{10,14},{11,7},{... | collective-permute-start | bytes 98312 | tf_op jit(solution)/shard_map/ppermute | solution.py:492
  66.4 6.9 %collective-permute-start.17 = (bf16[32,9216]{1,0:T(8,128)(2,1)S(1)}, bf16[32,9216]{1,0:T(8,128)(2,1)S(1)}, u32[]{:S(2)}, u32[]{:S(2)}) collective-permute-start(bf16[32,9216]{1,0:T(8,128)(2,1)S(1)} %collective-permute-done.10.rest_6_), channel_id=1, source_target_pairs={{0,32},{32,0},{64,96},{96,64},{1,33},{33,1},{65,97},{97,65},{2,34}... | collective-permute-start | bytes 1769480 | tf_op jit(solution)/shard_map/ppermute | solution.py:429
  71.5 1.8 %collective-permute-start.16 = (f32[2,128,128]{2,1,0:T(8,128)S(1)}, f32[2,128,128]{2,1,0:T(8,128)S(1)}, u32[]{:S(2)}, u32[]{:S(2)}) collective-permute-start(f32[2,128,128]{2,1,0:T(8,128)S(1)} %shard_map.121.n0), channel_id=1, source_target_pairs={{0,32},{32,0},{64,96},{96,64},{1,33},{33,1},{65,97},{97,65},{2,34}... | collective-permute-start | bytes 393224 | tf_op jit(solution)/shard_map/ppermute | solution.py:429
  (5 other events, 31.0 us)

commit v7 on v6

--- a/solution.py
+++ b/solution.py
@@ -456,7 +456,7 @@
     early = len(bounds) - LATE
     for (first, stop), far in zip(bounds, gathered):
         if state is not None:
-            far, state = lax.optimization_barrier((far, state))
+            far, state, sent[-1][1] = lax.optimization_barrier((far, state, sent[-1][1]))
         got = (near, far, swap(far, sibling))
         east_west, part, state = run_rows(
             first, stop, groups, state, kinds, couple_x, panels, got, w, tables,
@@ -467,8 +467,6 @@
         parts.append(part)
     together = lax.optimization_barrier
     part = jnp.concatenate(parts, axis=1) if len(parts) > 1 else parts[0]
-    for pieces in sent[:early]:
-        part, pieces[1], pieces[2] = together((part, pieces[1], pieces[2]))
 
     every = [(d, k) for d in range(4) for k in range(n_wide)]
     at = lambda d, k: d * n_wide + k
@@ -479,6 +477,9 @@
     second = block % 2
     own = part + fetch(2, 0)
     other = fetch(0, 1) + fetch(2, 1)
+    for pieces in sent[:early]:
+        own, pieces[2] = together((own, pieces[2]))
+        pieces.append(swap(pieces[2], sibling))
     for pieces in sent[early:]:
         last, own, other = together((pieces[0], own, other))
         pieces[2] = swap(last, across)
@@ -496,9 +497,6 @@
     )
     for pieces in sent[early:]:
         before, pieces[1] = together((before, pieces[1]))
-    for pieces in sent[:early]:
-        pieces.append(swap(pieces[2], sibling))
-        before, pieces[3] = together((before, pieces[3]))
     forced = run_ends(n_wide, block, corner, own, other, before, after, beyond)
     for pieces in sent[early:]:
         pieces[2], forced = together((pieces[2], forced))

time: 75.8 us -> 72.3 us (0.954)
  starting transfers between devices: 27.6 us -> 25.2 us
  waiting for transfers between devices: 19.1 us -> 17.8 us
    ppermute x12, starting transfers between devices: 16.8 us -> 14.8 us  [body(): swap = lambda value, pairs: lax.ppermute(value, 'band', pairs)]
    ppermute x2, waiting for transfers between devices: 1.91 us -> 0.01 us  [body(): lax.ppermute(value, 'wide', [(i, (i + 2 * k) % n_wide) for i in range(n_w...]
  transfers between devices with their start and end apart: 18 -> 18, of which waited for: 9 -> 10; matrix products, arithmetic and copies ran while one was open for 4% -> 4% of each run, Pallas kernels for 31% -> 33%
where the time goes in v7:
time: 72.3 us; the launch traced here: 71.3 us
  starting transfers between devices  25.2 us (35%)
  Pallas kernels  25 us (35%)
  waiting for transfers between devices  17.8 us (25%)
  local copies, waits for them, and re-layouts  2.65 us (4%)
    pallas_call x2, Pallas kernels, run_rows(): pl.pallas_call(functools.partial(rows_kernel, first, groups, carried), gr...  16.3 us
    ppermute x12, starting transfers between devices, body(): swap = lambda value, pairs: lax.ppermute(value, 'band', pairs)  14.8 us
    ppermute x12, waiting for transfers between devices, body(): swap = lambda value, pairs: lax.ppermute(value, 'band', pairs)  11.7 us
    pallas_call x1, Pallas kernels, run_tables(): pl.pallas_call(tables_kernel, grid_spec=pltpu.PrefetchScalarGridSpec(num_...  6.11 us
    ppermute x2, starting transfers between devices, body(): lax.ppermute(value, 'wide', [(i, (i + 2 * k) % n_wide) for i in range(n_w...  4.09 us
    ppermute x1, waiting for transfers between devices, body(): lax.ppermute(jnp.where(second == 0, odd[1], even[0]), 'wide', [(i, j) for...  4.02 us
    ppermute x3, starting transfers between devices, body(): lax.ppermute(half, ('band', 'wide'), [(at(d ^ db, k ^ dw), at(d, k)) for...  3.33 us
    ppermute x1, starting transfers between devices, body(): lax.ppermute(jnp.where(second == 0, odd[1], even[0]), 'wide', [(i, j) for...  3 us
  transfers between devices with their start and end apart: 18, of which 10 were waited for; matrix products, arithmetic and copies ran while one was open for 4% of the time, Pallas kernels for 33%

profile of v7, /device:TPU:25, one launch (start us, length us, event | category | flops | bytes accessed | tf_op | source)
XLA Modules:
  0.0 71.3 jit_solution(10887838294132729544)
XLA Ops:
  0.8 2.3 %fusion.8 = (bf16[32,8320]{1,0:T(8,128)(2,1)}, bf16[32,8320]{1,0:T(8,128)(2,1)}) fusion(bf16[32,16512]{1,0:T(8,128)(2,1)} %refs_6_.3), kind=kLoop, calls=%fused_computation.43 | loop fusion | bytes 2129920 | tf_op jit(solution)/shard_map/slice | solution.py:435
  3.1 2.7 %collective-permute-start.2 = (bf16[32,8320]{1,0:T(8,128)(2,1)}, bf16[32,8320]{1,0:T(8,128)(2,1)}, u32[]{:S(2)}, u32[]{:S(2)}) collective-permute-start(bf16[32,8320]{1,0:T(8,128)(2,1)} %get-tuple-element.61), channel_id=1, source_target_pairs={{0,64},{32,96},{64,0},{96,32},{1,65},{33,97},{65,1},{97,33},{2,66}... | collective-permute-start | bytes 1597448 | tf_op jit(solution)/shard_map/ppermute | solution.py:429
  6.6 6.1 %shard_map.118 = (bf16[128,256,128]{2,1,0:T(8,128)(2,1)S(1)}, bf16[64,128]{1,0:T(8,128)(2,1)S(1)}, f32[32,128]{1,0:T(8,128)S(1)}, bf16[16,32]{1,0:T(8,128)(2,1)S(1)}, f32[32,128]{1,0:T(8,128)S(1)}) custom-call(s32[2]{0:T(128)S(1)} %pad_add_fusion.here_ref, s32[128]{0:T(128)S(1)} %copy-done.5, f32[4,128]{1,0:T(4,128)S(1)} %maximum_reduce-precision_fusion.tap_ref, ...), custom_call_target="tpu_custom_call" | custom-call | tf_op jit(solution)/shard_map/pallas_call | solution.py:100
  12.9 5.5 %collective-permute-done.2.refs_4_.refs_8_ = bf16[32,8320]{1,0:T(8,128)(2,1)} collective-permute-done((bf16[32,8320]{1,0:T(8,128)(2,1)}, bf16[32,8320]{1,0:T(8,128)(2,1)}, u32[]{:S(2)}, u32[]{:S(2)}) %collective-permute-start.2) | collective-permute-done | bytes 532512 | tf_op jit(solution)/shard_map/ppermute | solution.py:429
  18.4 1.5 %collective-permute-start.3 = (bf16[32,8320]{1,0:T(8,128)(2,1)}, bf16[32,8320]{1,0:T(8,128)(2,1)S(1)}, u32[]{:S(2)}, u32[]{:S(2)}) collective-permute-start(bf16[32,8320]{1,0:T(8,128)(2,1)} %collective-permute-done.2.refs_4_.refs_8_), channel_id=1, source_target_pairs={{0,32},{32,0},{64,96},{96,64},{1,33},{33,1},{65,97},{97,65},{2,34}... | collective-permute-start | bytes 1597448 | tf_op jit(solution)/shard_map/ppermute | solution.py:429
  20.0 1.7 %collective-permute-done.3.refs_5_.refs_9_ = bf16[32,8320]{1,0:T(8,128)(2,1)S(1)} collective-permute-done((bf16[32,8320]{1,0:T(8,128)(2,1)}, bf16[32,8320]{1,0:T(8,128)(2,1)S(1)}, u32[]{:S(2)}, u32[]{:S(2)}) %collective-permute-start.3) | collective-permute-done | bytes 532512 | tf_op jit(solution)/shard_map/ppermute | solution.py:429
  21.7 7.7 %shard_map.119 = (bf16[32,7168]{1,0:T(8,128)(2,1)S(1)}, f32[2,56,128]{2,1,0:T(8,128)S(1)}, f32[8,32,128]{2,1,0:T(8,128)S(1)}, f32[40,128]{1,0:T(8,128)S(1)}, f32...) custom-call(s32[128]{0:T(128)S(1)} %fusion.7.refs_0_, f32[2,128]{1,0:T(2,128)S(1)} %copy-done.4, ...), custom_call_target="tpu_custom_call" | custom-call | tf_op jit(solution)/shard_map/pallas_call | solution.py:303
  29.9 1.4 %collective-permute-done.4.rest_1_ = bf16[32,7168]{1,0:T(8,128)(2,1)S(1)} collective-permute-done((bf16[32,7168]{1,0:T(8,128)(2,1)S(1)}, bf16[32,7168]{1,0:T(8,128)(2,1)S(1)}, u32[]{:S(2)}, u32[]{:S(2)}) %collective-permute-start.4) | collective-permute-done | bytes 458784 | tf_op jit(solution)/shard_map/ppermute | solution.py:429
  31.7 2.7 %collective-permute-start.7 = (bf16[32,7168]{1,0:T(8,128)(2,1)S(1)}, bf16[32,7168]{1,0:T(8,128)(2,1)S(1)}, u32[]{:S(2)}, u32[]{:S(2)}) collective-permute-start(bf16[32,7168]{1,0:T(8,128)(2,1)S(1)} %get-tuple-element.41.rest_0_), channel_id=1, source_target_pairs={{0,64},{32,96},{64,0},{96,32},{1,65},{33,97},{65,1},{97,33},{2,66}... | collective-permute-start | bytes 1376264 | tf_op jit(solution)/shard_map/ppermute | solution.py:429
  34.5 8.6 %shard_map.120 = (bf16[32,9216]{1,0:T(8,128)(2,1)S(1)}, f32[2,72,128]{2,1,0:T(8,128)S(1)}, f32[8,32,128]{2,1,0:T(8,128)}, f32[40,128]{1,0:T(8,128)}, f32[40,128]{1,0:T(8,128)}, /*index=5*/bf16[16,1024]{1,0:T(8,128)(2,1)}) custom-call(s32[128]{0:T(128)S(1)} %fusion.7.refs_0_, f32[2,128]{1,0:T(2,128)S(1)} %copy-done.4, bf16[32,16512]{1,0:T(8,128)(2,1)S(1)} %copy-done, ...), custom_call_target="tpu_custom_call" | custom-call | tf_op jit(solution)/shard_map/pallas_call | solution.py:303
  43.1 1.8 %collective-permute-start.6 = (bf16[2,128,128]{2,1,0:T(8,128)(2,1)S(1)}, bf16[2,128,128]{2,1,0:T(8,128)(2,1)S(1)}, u32[]{:S(2)}, u32[]{:S(2)}) collective-permute-start(bf16[2,128,128]{2,1,0:T(8,128)(2,1)S(1)} %convert_element_type.42), channel_id=1, source_target_pairs={{64,0},{65,1},{66,2},{67,3},{68,4},{69,5},{70,6},{71,7},{72,8},{73... | collective-permute-start | bytes 196616 | tf_op jit(solution)/shard_map/ppermute | solution.py:474
  45.2 1.2 %collective-permute-start.9 = (bf16[2,128,128]{2,1,0:T(8,128)(2,1)S(1)}, bf16[2,128,128]{2,1,0:T(8,128)(2,1)S(1)}, u32[]{:S(2)}, u32[]{:S(2)}) collective-permute-start(bf16[2,128,128]{2,1,0:T(8,128)(2,1)S(1)} %convert_element_type.42), channel_id=1, source_target_pairs={{65,0},{64,1},{67,2},{66,3},{69,4},{68,5},{71,6},{70,7},{73,8},{72... | collective-permute-start | bytes 196616 | tf_op jit(solution)/shard_map/ppermute | solution.py:474
  46.4 1.3 %collective-permute-start.12 = (bf16[32,9216]{1,0:T(8,128)(2,1)S(1)}, bf16[32,9216]{1,0:T(8,128)(2,1)S(1)}, u32[]{:S(2)}, u32[]{:S(2)}) collective-permute-start(bf16[32,9216]{1,0:T(8,128)(2,1)S(1)} %get-tuple-element.51.rest_4_), channel_id=1, source_target_pairs={{0,32},{32,0},{64,96},{96,64},{1,33},{33,1},{65,97},{97,65},{2,34}... | collective-permute-start | bytes 1769480 | tf_op jit(solution)/shard_map/ppermute | solution.py:429
  48.7 1.1 %collective-permute-done.9 = bf16[2,128,128]{2,1,0:T(8,128)(2,1)S(1)} collective-permute-done((bf16[2,128,128]{2,1,0:T(8,128)(2,1)S(1)}, bf16[2,128,128]{2,1,0:T(8,128)(2,1)S(1)}, u32[]{:S(2)}, u32[]{:S(2)}) %collective-permute-start.9) | collective-permute-done | bytes 65568 | tf_op jit(solution)/shard_map/ppermute | solution.py:474
  49.8 1.4 %collective-permute-start.10 = (bf16[32,9216]{1,0:T(8,128)(2,1)S(1)}, bf16[32,9216]{1,0:T(8,128)(2,1)S(1)}, u32[]{:S(2)}, u32[]{:S(2)}) collective-permute-start(bf16[32,9216]{1,0:T(8,128)(2,1)S(1)} %get-tuple-element.51.rest_4_), channel_id=1, source_target_pairs={{0,64},{32,96},{64,0},{96,32},{1,65},{33,97},{65,1},{97,33},{2,66}... | collective-permute-start | bytes 1769480 | tf_op jit(solution)/shard_map/ppermute | solution.py:429
  51.3 1.7 %collective-permute-start.11 = (bf16[3,128,128]{2,1,0:T(8,128)(2,1)S(1)}, bf16[3,128,128]{2,1,0:T(8,128)(2,1)S(1)}, u32[]{:S(2)}, u32[]{:S(2)}) collective-permute-start(bf16[3,128,128]{2,1,0:T(8,128)(2,1)S(1)} %pad_maximum_fusion), channel_id=1, source_target_pairs={{0,2},{1,3},{2,4},{3,5},{4,6},{5,7},{6,8},{7,9},{8,10},{9,11},{10,... | collective-permute-start | bytes 294920 | tf_op jit(solution)/shard_map/ppermute | solution.py:488
  53.0 2.4 %collective-permute-start.13 = (bf16[3,128,128]{2,1,0:T(8,128)(2,1)S(1)}, bf16[3,128,128]{2,1,0:T(8,128)(2,1)S(1)}, u32[]{:S(2)}, u32[]{:S(2)}) collective-permute-start(bf16[3,128,128]{2,1,0:T(8,128)(2,1)S(1)} %pad_maximum_fusion.1), channel_id=1, source_target_pairs={{0,30},{1,31},{2,0},{3,1},{4,2},{5,3},{6,4},{7,5},{8,6},{9,7},{10,... | collective-permute-start | bytes 294920 | tf_op jit(solution)/shard_map/ppermute | solution.py:488
  55.4 3.0 %collective-permute-start.14 = (bf16[128,128]{1,0:T(8,128)(2,1)S(1)}, bf16[128,128]{1,0:T(8,128)(2,1)S(1)}, u32[]{:S(2)}, u32[]{:S(2)}) collective-permute-start(bf16[128,128]{1,0:T(8,128)(2,1)S(1)} %get-tuple-element.65), channel_id=1, source_target_pairs={{0,4},{2,6},{4,8},{5,1},{6,10},{7,3},{8,12},{9,5},{10,14},{11,7},{... | collective-permute-start | bytes 98312 | tf_op jit(solution)/shard_map/ppermute | solution.py:493
  58.4 4.0 %collective-permute-done.14.distant = bf16[128,128]{1,0:T(8,128)(2,1)S(1)} collective-permute-done((bf16[128,128]{1,0:T(8,128)(2,1)S(1)}, bf16[128,128]{1,0:T(8,128)(2,1)S(1)}, u32[]{:S(2)}, u32[]{:S(2)}) %collective-permute-start.14) | collective-permute-done | bytes 32800 | tf_op jit(solution)/shard_map/ppermute | solution.py:493
  62.5 0.9 %shard_map.121.n0 = f32[2,128,128]{2,1,0:T(8,128)S(1)} custom-call(s32[1]{0:T(128)} %bitcast.block_ref, f32[32,128]{1,0:T(8,128)S(1)} %get-tuple-element.52.corner_ref, f32[2,128,128]{2,1,0:T(8,128)S(1)} %convert_add_fusion.1.own, f32[2,128,128]{2,1,0:T(8,128)S(1)} %convert_add_fusion.other, bf16[3,128,128]{2,1,0:T(8,128)(2,1)S(1)} %collective-permute-done.11.below, ...), custom_call_target="tpu_custom_call" | custom-call | tf_op jit(solution)/shard_map/pallas_call | solution.py:344
  63.4 1.0 %collective-permute-done.10.rest_6_ = bf16[32,9216]{1,0:T(8,128)(2,1)S(1)} collective-permute-done((bf16[32,9216]{1,0:T(8,128)(2,1)S(1)}, bf16[32,9216]{1,0:T(8,128)(2,1)S(1)}, u32[]{:S(2)}, u32[]{:S(2)}) %collective-permute-start.10) | collective-permute-done | bytes 589856 | tf_op jit(solution)/shard_map/ppermute | solution.py:429
  64.4 2.7 %collective-permute-start.17 = (bf16[32,9216]{1,0:T(8,128)(2,1)S(1)}, bf16[32,9216]{1,0:T(8,128)(2,1)S(1)}, u32[]{:S(2)}, u32[]{:S(2)}) collective-permute-start(bf16[32,9216]{1,0:T(8,128)(2,1)S(1)} %collective-permute-done.10.rest_6_), channel_id=1, source_target_pairs={{0,32},{32,0},{64,96},{96,64},{1,33},{33,1},{65,97},{97,65},{2,34}... | collective-permute-start | bytes 1769480 | tf_op jit(solution)/shard_map/ppermute | solution.py:429
  67.7 1.8 %collective-permute-done.16.rest_3_ = bf16[32,7168]{1,0:T(8,128)(2,1)S(1)} collective-permute-done((bf16[32,7168]{1,0:T(8,128)(2,1)S(1)}, bf16[32,7168]{1,0:T(8,128)(2,1)S(1)}, u32[]{:S(2)}, u32[]{:S(2)}) %collective-permute-start.16) | collective-permute-done | bytes 458784 | tf_op jit(solution)/shard_map/ppermute | solution.py:429
  69.6 1.6 %shard_map.122 = f32[32,16384]{1,0:T(8,128)} custom-call(bf16[64,128]{1,0:T(8,128)(2,1)S(1)} %get-tuple-element.33.w_ref, f32[32,128]{1,0:T(8,128)S(1)} %get-tuple-element.34.ends_ref, f32[2,128,128]{2,1,0:T(8,128)S(1)} %shard_map.121.n0, f32[2,128,128]{2,1,0:T(8,128)S(1)} %collective-permute-done.15.n1, bf16[32,7168]{1,0:T(8,128)(2,1)S(1)} %get-tuple-element.41.rest_0_, ...), custom_call_target="tpu_custom_call" | custom-call | tf_op jit(solution)/shard_map/pallas_call | solution.py:393
  (65 shorter events, 4.7 us)
Async XLA Ops:
  0.0 6.4 %copy-start.10 = (s32[128]{0:T(128)S(1)}, s32[128]{0:T(128)}, u32[]{:S(2)}) copy-start(s32[128]{0:T(128)} %param.17) | copy-start | bytes 1540
  0.0 6.5 %copy-start.5 = (s32[128]{0:T(128)S(1)}, s32[128]{0:T(128)}, u32[]{:S(2)}) copy-start(s32[128]{0:T(128)} %shift_ref.1) | copy-start | bytes 1540
  0.0 6.5 %copy-start.1 = (f32[32,128,128]{2,1,0:T(8,128)S(1)}, f32[32,128,128]{2,1,0:T(8,128)}, u32[]{:S(2)}) copy-start(f32[32,128,128]{2,1,0:T(8,128)} %last_ref.1) | copy-start | bytes 6291460
  0.0 20.0 %collective-permute-start = (bf16[32,16512]{1,0:T(8,128)(2,1)}, bf16[32,16512]{1,0:T(8,128)(2,1)S(1)}, u32[]{:S(2)}, u32[]{:S(2)}) collective-permute-start(bf16[32,16512]{1,0:T(8,128)(2,1)} %refs_6_.3), channel_id=1, source_target_pairs={{0,32},{32,0},{64,96},{96,64},{1,33},{33,1},{65,97},{97,65},{2,34}... | collective-permute-start | bytes 3170312 | tf_op jit(solution)/shard_map/ppermute | solution.py:429
  3.1 15.4 %collective-permute-start.2 = (bf16[32,8320]{1,0:T(8,128)(2,1)}, bf16[32,8320]{1,0:T(8,128)(2,1)}, u32[]{:S(2)}, u32[]{:S(2)}) collective-permute-start(bf16[32,8320]{1,0:T(8,128)(2,1)} %get-tuple-element.61), channel_id=1, source_target_pairs={{0,64},{32,96},{64,0},{96,32},{1,65},{33,97},{65,1},{97,33},{2,66}... | collective-permute-start | bytes 1597448 | tf_op jit(solution)/shard_map/ppermute | solution.py:429
  5.8 24.1 %collective-permute-start.1 = (bf16[32,8320]{1,0:T(8,128)(2,1)}, bf16[32,8320]{1,0:T(8,128)(2,1)}, u32[]{:S(2)}, u32[]{:S(2)}) collective-permute-start(bf16[32,8320]{1,0:T(8,128)(2,1)} %get-tuple-element.62), channel_id=1, source_target_pairs={{0,64},{32,96},{64,0},{96,32},{1,65},{33,97},{65,1},{97,33},{2,66}... | collective-permute-start | bytes 1597448 | tf_op jit(solution)/shard_map/ppermute | solution.py:429
  6.6 15.1 %copy-start = (bf16[32,16512]{1,0:T(8,128)(2,1)S(1)}, bf16[32,16512]{1,0:T(8,128)(2,1)}, u32[]{:S(2)}) copy-start(bf16[32,16512]{1,0:T(8,128)(2,1)} %refs_6_.3) | copy-start | bytes 3170308
  6.6 15.1 %copy-start.2 = (s32[32,16384]{1,0:T(8,128)S(1)}, s32[32,16384]{1,0:T(8,128)}, u32[]{:S(2)}) copy-start(s32[32,16384]{1,0:T(8,128)} %refs_12_.3) | copy-start | bytes 6291460
  6.6 15.1 %copy-start.3 = (f32[32,16384]{1,0:T(8,128)S(1)}, f32[32,16384]{1,0:T(8,128)}, u32[]{:S(2)}) copy-start(f32[32,16384]{1,0:T(8,128)} %refs_13_.3) | copy-start | bytes 6291460
  18.4 3.3 %collective-permute-start.3 = (bf16[32,8320]{1,0:T(8,128)(2,1)}, bf16[32,8320]{1,0:T(8,128)(2,1)S(1)}, u32[]{:S(2)}, u32[]{:S(2)}) collective-permute-start(bf16[32,8320]{1,0:T(8,128)(2,1)} %collective-permute-done.2.refs_4_.refs_8_), channel_id=1, source_target_pairs={{0,32},{32,0},{64,96},{96,64},{1,33},{33,1},{65,97},{97,65},{2,34}... | collective-permute-start | bytes 1597448 | tf_op jit(solution)/shard_map/ppermute | solution.py:429
  29.4 1.9 %collective-permute-start.4 = (bf16[32,7168]{1,0:T(8,128)(2,1)S(1)}, bf16[32,7168]{1,0:T(8,128)(2,1)S(1)}, u32[]{:S(2)}, u32[]{:S(2)}) collective-permute-start(bf16[32,7168]{1,0:T(8,128)(2,1)S(1)} %get-tuple-element.41.rest_0_), channel_id=1, source_target_pairs={{0,32},{32,0},{64,96},{96,64},{1,33},{33,1},{65,97},{97,65},{2,34}... | collective-permute-start | bytes 1376264 | tf_op jit(solution)/shard_map/ppermute | solution.py:429
  31.4 3.1 %collective-permute-start.5 = (bf16[32,8320]{1,0:T(8,128)(2,1)}, bf16[32,8320]{1,0:T(8,128)(2,1)S(1)}, u32[]{:S(2)}, u32[]{:S(2)}) collective-permute-start(bf16[32,8320]{1,0:T(8,128)(2,1)} %collective-permute-done.1.refs_4_.refs_8_), channel_id=1, source_target_pairs={{0,32},{32,0},{64,96},{96,64},{1,33},{33,1},{65,97},{97,65},{2,34}... | collective-permute-start | bytes 1597448 | tf_op jit(solution)/shard_map/ppermute | solution.py:429
  31.7 16.1 %collective-permute-start.7 = (bf16[32,7168]{1,0:T(8,128)(2,1)S(1)}, bf16[32,7168]{1,0:T(8,128)(2,1)S(1)}, u32[]{:S(2)}, u32[]{:S(2)}) collective-permute-start(bf16[32,7168]{1,0:T(8,128)(2,1)S(1)} %get-tuple-element.41.rest_0_), channel_id=1, source_target_pairs={{0,64},{32,96},{64,0},{96,32},{1,65},{33,97},{65,1},{97,33},{2,66}... | collective-permute-start | bytes 1376264 | tf_op jit(solution)/shard_map/ppermute | solution.py:429
  43.1 4.7 %collective-permute-start.6 = (bf16[2,128,128]{2,1,0:T(8,128)(2,1)S(1)}, bf16[2,128,128]{2,1,0:T(8,128)(2,1)S(1)}, u32[]{:S(2)}, u32[]{:S(2)}) collective-permute-start(bf16[2,128,128]{2,1,0:T(8,128)(2,1)S(1)} %convert_element_type.42), channel_id=1, source_target_pairs={{64,0},{65,1},{66,2},{67,3},{68,4},{69,5},{70,6},{71,7},{72,8},{73... | collective-permute-start | bytes 196616 | tf_op jit(solution)/shard_map/ppermute | solution.py:474
  44.9 3.8 %collective-permute-start.8 = (bf16[2,128,128]{2,1,0:T(8,128)(2,1)S(1)}, bf16[2,128,128]{2,1,0:T(8,128)(2,1)S(1)}, u32[]{:S(2)}, u32[]{:S(2)}) collective-permute-start(bf16[2,128,128]{2,1,0:T(8,128)(2,1)S(1)} %convert_element_type.42), channel_id=1, source_target_pairs={{1,0},{0,1},{3,2},{2,3},{5,4},{4,5},{7,6},{6,7},{9,8},{8,9},{11,10... | collective-permute-start | bytes 196616 | tf_op jit(solution)/shard_map/ppermute | solution.py:474
  45.2 4.6 %collective-permute-start.9 = (bf16[2,128,128]{2,1,0:T(8,128)(2,1)S(1)}, bf16[2,128,128]{2,1,0:T(8,128)(2,1)S(1)}, u32[]{:S(2)}, u32[]{:S(2)}) collective-permute-start(bf16[2,128,128]{2,1,0:T(8,128)(2,1)S(1)} %convert_element_type.42), channel_id=1, source_target_pairs={{65,0},{64,1},{67,2},{66,3},{69,4},{68,5},{71,6},{70,7},{73,8},{72... | collective-permute-start | bytes 196616 | tf_op jit(solution)/shard_map/ppermute | solution.py:474
  46.4 12.0 %collective-permute-start.12 = (bf16[32,9216]{1,0:T(8,128)(2,1)S(1)}, bf16[32,9216]{1,0:T(8,128)(2,1)S(1)}, u32[]{:S(2)}, u32[]{:S(2)}) collective-permute-start(bf16[32,9216]{1,0:T(8,128)(2,1)S(1)} %get-tuple-element.51.rest_4_), channel_id=1, source_target_pairs={{0,32},{32,0},{64,96},{96,64},{1,33},{33,1},{65,97},{97,65},{2,34}... | collective-permute-start | bytes 1769480 | tf_op jit(solution)/shard_map/ppermute | solution.py:429
  49.8 14.6 %collective-permute-start.10 = (bf16[32,9216]{1,0:T(8,128)(2,1)S(1)}, bf16[32,9216]{1,0:T(8,128)(2,1)S(1)}, u32[]{:S(2)}, u32[]{:S(2)}) collective-permute-start(bf16[32,9216]{1,0:T(8,128)(2,1)S(1)} %get-tuple-element.51.rest_4_), channel_id=1, source_target_pairs={{0,64},{32,96},{64,0},{96,32},{1,65},{33,97},{65,1},{97,33},{2,66}... | collective-permute-start | bytes 1769480 | tf_op jit(solution)/shard_map/ppermute | solution.py:429
  51.3 7.1 %collective-permute-start.11 = (bf16[3,128,128]{2,1,0:T(8,128)(2,1)S(1)}, bf16[3,128,128]{2,1,0:T(8,128)(2,1)S(1)}, u32[]{:S(2)}, u32[]{:S(2)}) collective-permute-start(bf16[3,128,128]{2,1,0:T(8,128)(2,1)S(1)} %pad_maximum_fusion), channel_id=1, source_target_pairs={{0,2},{1,3},{2,4},{3,5},{4,6},{5,7},{6,8},{7,9},{8,10},{9,11},{10,... | collective-permute-start | bytes 294920 | tf_op jit(solution)/shard_map/ppermute | solution.py:488
  53.0 9.4 %collective-permute-start.13 = (bf16[3,128,128]{2,1,0:T(8,128)(2,1)S(1)}, bf16[3,128,128]{2,1,0:T(8,128)(2,1)S(1)}, u32[]{:S(2)}, u32[]{:S(2)}) collective-permute-start(bf16[3,128,128]{2,1,0:T(8,128)(2,1)S(1)} %pad_maximum_fusion.1), channel_id=1, source_target_pairs={{0,30},{1,31},{2,0},{3,1},{4,2},{5,3},{6,4},{7,5},{8,6},{9,7},{10,... | collective-permute-start | bytes 294920 | tf_op jit(solution)/shard_map/ppermute | solution.py:488
  55.4 7.0 %collective-permute-start.14 = (bf16[128,128]{1,0:T(8,128)(2,1)S(1)}, bf16[128,128]{1,0:T(8,128)(2,1)S(1)}, u32[]{:S(2)}, u32[]{:S(2)}) collective-permute-start(bf16[128,128]{1,0:T(8,128)(2,1)S(1)} %get-tuple-element.65), channel_id=1, source_target_pairs={{0,4},{2,6},{4,8},{5,1},{6,10},{7,3},{8,12},{9,5},{10,14},{11,7},{... | collective-permute-start | bytes 98312 | tf_op jit(solution)/shard_map/ppermute | solution.py:493
  64.4 5.2 %collective-permute-start.17 = (bf16[32,9216]{1,0:T(8,128)(2,1)S(1)}, bf16[32,9216]{1,0:T(8,128)(2,1)S(1)}, u32[]{:S(2)}, u32[]{:S(2)}) collective-permute-start(bf16[32,9216]{1,0:T(8,128)(2,1)S(1)} %collective-permute-done.10.rest_6_), channel_id=1, source_target_pairs={{0,32},{32,0},{64,96},{96,64},{1,33},{33,1},{65,97},{97,65},{2,34}... | collective-permute-start | bytes 1769480 | tf_op jit(solution)/shard_map/ppermute | solution.py:429
  67.2 2.3 %collective-permute-start.16 = (bf16[32,7168]{1,0:T(8,128)(2,1)S(1)}, bf16[32,7168]{1,0:T(8,128)(2,1)S(1)}, u32[]{:S(2)}, u32[]{:S(2)}) collective-permute-start(bf16[32,7168]{1,0:T(8,128)(2,1)S(1)} %collective-permute-done.7.rest_2_), channel_id=1, source_target_pairs={{0,32},{32,0},{64,96},{96,64},{1,33},{33,1},{65,97},{97,65},{2,34}... | collective-permute-start | bytes 1376264 | tf_op jit(solution)/shard_map/ppermute | solution.py:429
  67.2 2.5 %collective-permute-start.15 = (f32[2,128,128]{2,1,0:T(8,128)S(1)}, f32[2,128,128]{2,1,0:T(8,128)S(1)}, u32[]{:S(2)}, u32[]{:S(2)}) collective-permute-start(f32[2,128,128]{2,1,0:T(8,128)S(1)} %shard_map.121.n0), channel_id=1, source_target_pairs={{0,32},{32,0},{64,96},{96,64},{1,33},{33,1},{65,97},{97,65},{2,34}... | collective-permute-start | bytes 393224 | tf_op jit(solution)/shard_map/ppermute | solution.py:429
  (5 other events, 31.1 us)

commit v8 on v7

--- a/solution.py
+++ b/solution.py
@@ -92,6 +92,28 @@
         for k, value in enumerate(values):
             total = jnp.where(lane == k, value, total)
         corner_ref[...] = total
+
+
+def cut_kernel(bounds, source, *rest):
+    outs, sems = rest[:-1], rest[-1]
+    copies = []
+    for k, (start, stop) in enumerate(bounds):
+        copies.append(pltpu.make_async_copy(source.at[:, start:stop], outs[k], sems.at[k]))
+        copies[-1].start()
+    for copy in copies:
+        copy.wait()
+
+
+def run_cut(source, bounds):
+    anywhere = pl.BlockSpec(memory_space=pl.ANY)
+    return pl.pallas_call(
+        functools.partial(cut_kernel, bounds),
+        in_specs=[pl.BlockSpec(memory_space=pltpu.HBM)],
+        out_specs=[anywhere] * len(bounds),
+        out_shape=[jax.ShapeDtypeStruct((32, stop - start), source.dtype) for start, stop in bounds],
+        scratch_shapes=[pltpu.SemaphoreType.DMA((len(bounds),))],
+        compiler_params=pltpu.CompilerParams(vmem_limit_bytes=VMEM_LIMIT),
+    )(source)
 
 
 def run_tables(here, shift, taps, inverse_y, couple_y):
@@ -432,7 +454,8 @@
     gathered = []
     near = swap(panels, sibling)
     for first, stop in bounds:
-        gathered.append(swap(panels[:, first * GW : stop * GW + BLK], across))
+        (piece,) = run_cut(panels, [(first * GW, stop * GW + BLK)])
+        gathered.append(swap(piece, across))
 
     order = ((jnp.arange(4, dtype=jnp.int32) ^ mine)[:, None] * rows + jnp.arange(rows)[None, :]).reshape(-1)
     w = jnp.concatenate(
@@ -456,7 +479,7 @@
     early = len(bounds) - LATE
     for (first, stop), far in zip(bounds, gathered):
         if state is not None:
-            far, state, sent[-1][1] = lax.optimization_barrier((far, state, sent[-1][1]))
+            far, state = lax.optimization_barrier((far, state))
         got = (near, far, swap(far, sibling))
         east_west, part, state = run_rows(
             first, stop, groups, state, kinds, couple_x, panels, got, w, tables,
@@ -467,6 +490,9 @@
         parts.append(part)
     together = lax.optimization_barrier
     part = jnp.concatenate(parts, axis=1) if len(parts) > 1 else parts[0]
+
+    for pieces in sent[:early]:
+        part, pieces[1] = together((part, pieces[1]))
 
     every = [(d, k) for d in range(4) for k in range(n_wide)]
     at = lambda d, k: d * n_wide + k

time: 72.3 us -> 71.5 us (0.989)
  waiting for transfers between devices: 17.8 us -> 15.9 us
  Pallas kernels: 25 us -> 26.5 us
  local copies, waits for them, and re-layouts: 2.65 us -> 1.61 us
    slice x1 -> x0, local copies, waits for them, and re-layouts: 2.26 us -> none  [body(): gathered.append(swap(panels[:, first * GW:stop * GW + BLK], across))]
    ppermute x12, waiting for transfers between devices: 11.7 us -> 9.74 us  [body(): swap = lambda value, pairs: lax.ppermute(value, 'band', pairs)]
    pallas_call x0 -> x2, Pallas kernels: none -> 1.62 us  [run_cut(): pl.pallas_call(functools.partial(cut_kernel, bounds), in_specs=[pl.BlockS...]
    unnamed x24 -> x25, local copies, waits for them, and re-layouts: 0.14 us -> 1.37 us
  transfers between devices with their start and end apart: 18 -> 18, of which waited for: 10 -> 9; matrix products, arithmetic and copies ran while one was open for 4% -> 1% of each run, Pallas kernels for 33% -> 35%
where the time goes in v8:
time: 71.5 us; the launch traced here: 70.5 us
  Pallas kernels  26.5 us (37%)
  starting transfers between devices  25.7 us (36%)
  waiting for transfers between devices  15.9 us (22%)
  local copies, waits for them, and re-layouts  1.61 us (2%)
    pallas_call x2, Pallas kernels, run_rows(): pl.pallas_call(functools.partial(rows_kernel, first, groups, carried), gr...  16.2 us
    ppermute x12, starting transfers between devices, body(): swap = lambda value, pairs: lax.ppermute(value, 'band', pairs)  15.3 us
    ppermute x12, waiting for transfers between devices, body(): swap = lambda value, pairs: lax.ppermute(value, 'band', pairs)  9.74 us
    pallas_call x1, Pallas kernels, run_tables(): pl.pallas_call(tables_kernel, grid_spec=pltpu.PrefetchScalarGridSpec(num_...  6.11 us
    ppermute x2, starting transfers between devices, body(): lax.ppermute(value, 'wide', [(i, (i + 2 * k) % n_wide) for i in range(n_w...  4.09 us
    ppermute x1, waiting for transfers between devices, body(): lax.ppermute(jnp.where(second == 0, odd[1], even[0]), 'wide', [(i, j) for...  4.01 us
    ppermute x3, starting transfers between devices, body(): lax.ppermute(half, ('band', 'wide'), [(at(d ^ db, k ^ dw), at(d, k)) for...  3.36 us
    ppermute x1, starting transfers between devices, body(): lax.ppermute(jnp.where(second == 0, odd[1], even[0]), 'wide', [(i, j) for...  3.01 us
  transfers between devices with their start and end apart: 18, of which 9 were waited for; matrix products, arithmetic and copies ran while one was open for 1% of the time, Pallas kernels for 35%

profile of v8, /device:TPU:25, one launch (start us, length us, event | category | flops | bytes accessed | tf_op | source)
XLA Modules:
  0.0 70.5 jit_solution(14034156944957880181)
XLA Ops:
  0.7 1.2 %copy-done = bf16[32,16512]{1,0:T(8,128)(2,1)S(1)} copy-done((bf16[32,16512]{1,0:T(8,128)(2,1)S(1)}, bf16[32,16512]{1,0:T(8,128)(2,1)}, u32[]{:S(2)}) %copy-start) | copy-done | bytes 1056792
  1.9 0.8 %shard_map.120 = bf16[32,8320]{1,0:T(8,128)(2,1)} custom-call(bf16[32,16512]{1,0:T(8,128)(2,1)S(1)} %copy-done), custom_call_target="tpu_custom_call" | custom-call | tf_op jit(solution)/shard_map/pallas_call | solution.py:109
  2.8 2.8 %collective-permute-start.2 = (bf16[32,8320]{1,0:T(8,128)(2,1)}, bf16[32,8320]{1,0:T(8,128)(2,1)}, u32[]{:S(2)}, u32[]{:S(2)}) collective-permute-start(bf16[32,8320]{1,0:T(8,128)(2,1)} %shard_map.120), channel_id=1, source_target_pairs={{0,64},{32,96},{64,0},{96,32},{1,65},{33,97},{65,1},{97,33},{2,66}... | collective-permute-start | bytes 1597448 | tf_op jit(solution)/shard_map/ppermute | solution.py:451
  5.6 0.8 %shard_map.119 = bf16[32,8320]{1,0:T(8,128)(2,1)} custom-call(bf16[32,16512]{1,0:T(8,128)(2,1)S(1)} %copy-done), custom_call_target="tpu_custom_call" | custom-call | tf_op jit(solution)/shard_map/pallas_call | solution.py:109
  7.4 6.1 %shard_map.118 = (bf16[128,256,128]{2,1,0:T(8,128)(2,1)S(1)}, bf16[64,128]{1,0:T(8,128)(2,1)S(1)}, f32[32,128]{1,0:T(8,128)S(1)}, bf16[16,32]{1,0:T(8,128)(2,1)S(1)}, f32[32,128]{1,0:T(8,128)S(1)}) custom-call(s32[2]{0:T(128)S(1)} %pad_add_fusion.here_ref, s32[128]{0:T(128)S(1)} %copy-done.6, f32[4,128]{1,0:T(4,128)S(1)} %maximum_reduce-precision_fusion.tap_ref, ...), custom_call_target="tpu_custom_call" | custom-call | tf_op jit(solution)/shard_map/pallas_call | solution.py:122
  13.5 4.9 %collective-permute-done.2.refs_4_.refs_8_ = bf16[32,8320]{1,0:T(8,128)(2,1)} collective-permute-done((bf16[32,8320]{1,0:T(8,128)(2,1)}, bf16[32,8320]{1,0:T(8,128)(2,1)}, u32[]{:S(2)}, u32[]{:S(2)}) %collective-permute-start.2) | collective-permute-done | bytes 532512 | tf_op jit(solution)/shard_map/ppermute | solution.py:451
  18.4 1.2 %collective-permute-start.3 = (bf16[32,8320]{1,0:T(8,128)(2,1)}, bf16[32,8320]{1,0:T(8,128)(2,1)S(1)}, u32[]{:S(2)}, u32[]{:S(2)}) collective-permute-start(bf16[32,8320]{1,0:T(8,128)(2,1)} %collective-permute-done.2.refs_4_.refs_8_), channel_id=1, source_target_pairs={{0,32},{32,0},{64,96},{96,64},{1,33},{33,1},{65,97},{97,65},{2,34}... | collective-permute-start | bytes 1597448 | tf_op jit(solution)/shard_map/ppermute | solution.py:451
  19.7 1.6 %collective-permute-done.3.refs_5_.refs_9_ = bf16[32,8320]{1,0:T(8,128)(2,1)S(1)} collective-permute-done((bf16[32,8320]{1,0:T(8,128)(2,1)}, bf16[32,8320]{1,0:T(8,128)(2,1)S(1)}, u32[]{:S(2)}, u32[]{:S(2)}) %collective-permute-start.3) | collective-permute-done | bytes 532512 | tf_op jit(solution)/shard_map/ppermute | solution.py:451
  21.3 7.7 %shard_map.121 = (bf16[32,7168]{1,0:T(8,128)(2,1)S(1)}, f32[2,56,128]{2,1,0:T(8,128)S(1)}, f32[8,32,128]{2,1,0:T(8,128)S(1)}, f32[40,128]{1,0:T(8,128)S(1)}, f32...) custom-call(s32[128]{0:T(128)S(1)} %fusion.7.refs_0_, f32[2,128]{1,0:T(2,128)S(1)} %copy-done.5, ...), custom_call_target="tpu_custom_call" | custom-call | tf_op jit(solution)/shard_map/pallas_call | solution.py:325
  30.6 2.7 %collective-permute-start.7 = (bf16[32,7168]{1,0:T(8,128)(2,1)S(1)}, bf16[32,7168]{1,0:T(8,128)(2,1)S(1)}, u32[]{:S(2)}, u32[]{:S(2)}) collective-permute-start(bf16[32,7168]{1,0:T(8,128)(2,1)S(1)} %get-tuple-element.50.rest_0_), channel_id=1, source_target_pairs={{0,64},{32,96},{64,0},{96,32},{1,65},{33,97},{65,1},{97,33},{2,66}... | collective-permute-start | bytes 1376264 | tf_op jit(solution)/shard_map/ppermute | solution.py:451
  33.3 8.6 %shard_map.122 = (bf16[32,9216]{1,0:T(8,128)(2,1)S(1)}, f32[2,72,128]{2,1,0:T(8,128)S(1)}, f32[8,32,128]{2,1,0:T(8,128)}, f32[40,128]{1,0:T(8,128)}, f32[40,128]{1,0:T(8,128)}, /*index=5*/bf16[16,1024]{1,0:T(8,128)(2,1)}) custom-call(s32[128]{0:T(128)S(1)} %fusion.7.refs_0_, f32[2,128]{1,0:T(2,128)S(1)} %copy-done.5, bf16[32,16512]{1,0:T(8,128)(2,1)S(1)} %copy-done.1, ...), custom_call_target="tpu_custom_call" | custom-call | tf_op jit(solution)/shard_map/pallas_call | solution.py:325
  41.9 2.5 %collective-permute-start.6 = (bf16[2,128,128]{2,1,0:T(8,128)(2,1)S(1)}, bf16[2,128,128]{2,1,0:T(8,128)(2,1)S(1)}, u32[]{:S(2)}, u32[]{:S(2)}) collective-permute-start(bf16[2,128,128]{2,1,0:T(8,128)(2,1)S(1)} %convert_element_type.42), channel_id=1, source_target_pairs={{64,0},{65,1},{66,2},{67,3},{68,4},{69,5},{70,6},{71,7},{72,8},{73... | collective-permute-start | bytes 196616 | tf_op jit(solution)/shard_map/ppermute | solution.py:500
  45.3 1.6 %collective-permute-start.12 = (bf16[32,9216]{1,0:T(8,128)(2,1)S(1)}, bf16[32,9216]{1,0:T(8,128)(2,1)S(1)}, u32[]{:S(2)}, u32[]{:S(2)}) collective-permute-start(bf16[32,9216]{1,0:T(8,128)(2,1)S(1)} %get-tuple-element.53.rest_4_), channel_id=1, source_target_pairs={{0,32},{32,0},{64,96},{96,64},{1,33},{33,1},{65,97},{97,65},{2,34}... | collective-permute-start | bytes 1769480 | tf_op jit(solution)/shard_map/ppermute | solution.py:451
  46.9 1.3 %collective-permute-done.8 = bf16[2,128,128]{2,1,0:T(8,128)(2,1)S(1)} collective-permute-done((bf16[2,128,128]{2,1,0:T(8,128)(2,1)S(1)}, bf16[2,128,128]{2,1,0:T(8,128)(2,1)S(1)}, u32[]{:S(2)}, u32[]{:S(2)}) %collective-permute-start.8) | collective-permute-done | bytes 65568 | tf_op jit(solution)/shard_map/ppermute | solution.py:500
  48.2 0.8 %collective-permute-done.9 = bf16[2,128,128]{2,1,0:T(8,128)(2,1)S(1)} collective-permute-done((bf16[2,128,128]{2,1,0:T(8,128)(2,1)S(1)}, bf16[2,128,128]{2,1,0:T(8,128)(2,1)S(1)}, u32[]{:S(2)}, u32[]{:S(2)}) %collective-permute-start.9) | collective-permute-done | bytes 65568 | tf_op jit(solution)/shard_map/ppermute | solution.py:500
  49.1 1.7 %collective-permute-start.10 = (bf16[32,9216]{1,0:T(8,128)(2,1)S(1)}, bf16[32,9216]{1,0:T(8,128)(2,1)S(1)}, u32[]{:S(2)}, u32[]{:S(2)}) collective-permute-start(bf16[32,9216]{1,0:T(8,128)(2,1)S(1)} %get-tuple-element.53.rest_4_), channel_id=1, source_target_pairs={{0,64},{32,96},{64,0},{96,32},{1,65},{33,97},{65,1},{97,33},{2,66}... | collective-permute-start | bytes 1769480 | tf_op jit(solution)/shard_map/ppermute | solution.py:451
  50.8 1.7 %collective-permute-start.11 = (bf16[3,128,128]{2,1,0:T(8,128)(2,1)S(1)}, bf16[3,128,128]{2,1,0:T(8,128)(2,1)S(1)}, u32[]{:S(2)}, u32[]{:S(2)}) collective-permute-start(bf16[3,128,128]{2,1,0:T(8,128)(2,1)S(1)} %pad_maximum_fusion.1), channel_id=1, source_target_pairs={{0,2},{1,3},{2,4},{3,5},{4,6},{5,7},{6,8},{7,9},{8,10},{9,11},{10,... | collective-permute-start | bytes 294920 | tf_op jit(solution)/shard_map/ppermute | solution.py:514
  52.5 2.4 %collective-permute-start.13 = (bf16[3,128,128]{2,1,0:T(8,128)(2,1)S(1)}, bf16[3,128,128]{2,1,0:T(8,128)(2,1)S(1)}, u32[]{:S(2)}, u32[]{:S(2)}) collective-permute-start(bf16[3,128,128]{2,1,0:T(8,128)(2,1)S(1)} %pad_maximum_fusion.2), channel_id=1, source_target_pairs={{0,30},{1,31},{2,0},{3,1},{4,2},{5,3},{6,4},{7,5},{8,6},{9,7},{10,... | collective-permute-start | bytes 294920 | tf_op jit(solution)/shard_map/ppermute | solution.py:514
  54.9 3.0 %collective-permute-start.14 = (bf16[128,128]{1,0:T(8,128)(2,1)S(1)}, bf16[128,128]{1,0:T(8,128)(2,1)S(1)}, u32[]{:S(2)}, u32[]{:S(2)}) collective-permute-start(bf16[128,128]{1,0:T(8,128)(2,1)S(1)} %get-tuple-element.65), channel_id=1, source_target_pairs={{0,4},{2,6},{4,8},{5,1},{6,10},{7,3},{8,12},{9,5},{10,14},{11,7},{... | collective-permute-start | bytes 98312 | tf_op jit(solution)/shard_map/ppermute | solution.py:519
  57.9 4.0 %collective-permute-done.14.distant = bf16[128,128]{1,0:T(8,128)(2,1)S(1)} collective-permute-done((bf16[128,128]{1,0:T(8,128)(2,1)S(1)}, bf16[128,128]{1,0:T(8,128)(2,1)S(1)}, u32[]{:S(2)}, u32[]{:S(2)}) %collective-permute-start.14) | collective-permute-done | bytes 32800 | tf_op jit(solution)/shard_map/ppermute | solution.py:519
  62.0 0.9 %shard_map.123.n0 = f32[2,128,128]{2,1,0:T(8,128)S(1)} custom-call(s32[1]{0:T(128)} %bitcast.block_ref, f32[32,128]{1,0:T(8,128)S(1)} %get-tuple-element.54.corner_ref, f32[2,128,128]{2,1,0:T(8,128)S(1)} %convert_add_fusion.1.own, f32[2,128,128]{2,1,0:T(8,128)S(1)} %convert_add_fusion.other, bf16[3,128,128]{2,1,0:T(8,128)(2,1)S(1)} %collective-permute-done.11.below, ...), custom_call_target="tpu_custom_call" | custom-call | tf_op jit(solution)/shard_map/pallas_call | solution.py:366
  63.4 3.0 %collective-permute-start.17 = (bf16[32,9216]{1,0:T(8,128)(2,1)S(1)}, bf16[32,9216]{1,0:T(8,128)(2,1)S(1)}, u32[]{:S(2)}, u32[]{:S(2)}) collective-permute-start(bf16[32,9216]{1,0:T(8,128)(2,1)S(1)} %collective-permute-done.10.rest_6_), channel_id=1, source_target_pairs={{0,32},{32,0},{64,96},{96,64},{1,33},{33,1},{65,97},{97,65},{2,34}... | collective-permute-start | bytes 1769480 | tf_op jit(solution)/shard_map/ppermute | solution.py:451
  66.9 1.8 %collective-permute-done.16.rest_3_ = bf16[32,7168]{1,0:T(8,128)(2,1)S(1)} collective-permute-done((bf16[32,7168]{1,0:T(8,128)(2,1)S(1)}, bf16[32,7168]{1,0:T(8,128)(2,1)S(1)}, u32[]{:S(2)}, u32[]{:S(2)}) %collective-permute-start.16) | collective-permute-done | bytes 458784 | tf_op jit(solution)/shard_map/ppermute | solution.py:451
  68.9 1.6 %shard_map.124 = f32[32,16384]{1,0:T(8,128)} custom-call(bf16[64,128]{1,0:T(8,128)(2,1)S(1)} %get-tuple-element.34.w_ref, f32[32,128]{1,0:T(8,128)S(1)} %get-tuple-element.35.ends_ref, f32[2,128,128]{2,1,0:T(8,128)S(1)} %shard_map.123.n0, f32[2,128,128]{2,1,0:T(8,128)S(1)} %collective-permute-done.15.n1, bf16[32,7168]{1,0:T(8,128)(2,1)S(1)} %get-tuple-element.50.rest_0_, ...), custom_call_target="tpu_custom_call" | custom-call | tf_op jit(solution)/shard_map/pallas_call | solution.py:415
  (67 shorter events, 5.5 us)
Async XLA Ops:
  0.0 19.7 %collective-permute-start = (bf16[32,16512]{1,0:T(8,128)(2,1)}, bf16[32,16512]{1,0:T(8,128)(2,1)S(1)}, u32[]{:S(2)}, u32[]{:S(2)}) collective-permute-start(bf16[32,16512]{1,0:T(8,128)(2,1)} %refs_6_.3), channel_id=1, source_target_pairs={{0,32},{32,0},{64,96},{96,64},{1,33},{33,1},{65,97},{97,65},{2,34}... | collective-permute-start | bytes 3170312 | tf_op jit(solution)/shard_map/ppermute | solution.py:451
  1.9 5.4 %copy-start.2 = (f32[32,128,128]{2,1,0:T(8,128)S(1)}, f32[32,128,128]{2,1,0:T(8,128)}, u32[]{:S(2)}) copy-start(f32[32,128,128]{2,1,0:T(8,128)} %last_ref.1) | copy-start | bytes 6291460
  2.8 15.6 %collective-permute-start.2 = (bf16[32,8320]{1,0:T(8,128)(2,1)}, bf16[32,8320]{1,0:T(8,128)(2,1)}, u32[]{:S(2)}, u32[]{:S(2)}) collective-permute-start(bf16[32,8320]{1,0:T(8,128)(2,1)} %shard_map.120), channel_id=1, source_target_pairs={{0,64},{32,96},{64,0},{96,32},{1,65},{33,97},{65,1},{97,33},{2,66}... | collective-permute-start | bytes 1597448 | tf_op jit(solution)/shard_map/ppermute | solution.py:451
  6.4 23.4 %collective-permute-start.1 = (bf16[32,8320]{1,0:T(8,128)(2,1)}, bf16[32,8320]{1,0:T(8,128)(2,1)}, u32[]{:S(2)}, u32[]{:S(2)}) collective-permute-start(bf16[32,8320]{1,0:T(8,128)(2,1)} %shard_map.119), channel_id=1, source_target_pairs={{0,64},{32,96},{64,0},{96,32},{1,65},{33,97},{65,1},{97,33},{2,66}... | collective-permute-start | bytes 1597448 | tf_op jit(solution)/shard_map/ppermute | solution.py:451
  7.3 6.2 %copy-start.8 = (s32[32]{0:T(128)S(1)}, s32[32]{0:T(128)}, u32[]{:S(2)}) copy-start(s32[32]{0:T(128)} %param.15) | copy-start | bytes 388
  7.3 6.2 %copy-start.7 = (f32[32]{0:T(128)S(1)}, f32[32]{0:T(128)}, u32[]{:S(2)}) copy-start(f32[32]{0:T(128)} %param.16) | copy-start | bytes 388
  7.3 14.0 %copy-start.1 = (bf16[32,16512]{1,0:T(8,128)(2,1)S(1)}, bf16[32,16512]{1,0:T(8,128)(2,1)}, u32[]{:S(2)}) copy-start(bf16[32,16512]{1,0:T(8,128)(2,1)} %refs_6_.3) | copy-start | bytes 3170308
  7.3 14.0 %copy-start.3 = (s32[32,16384]{1,0:T(8,128)S(1)}, s32[32,16384]{1,0:T(8,128)}, u32[]{:S(2)}) copy-start(s32[32,16384]{1,0:T(8,128)} %refs_12_.3) | copy-start | bytes 6291460
  7.4 14.0 %copy-start.4 = (f32[32,16384]{1,0:T(8,128)S(1)}, f32[32,16384]{1,0:T(8,128)}, u32[]{:S(2)}) copy-start(f32[32,16384]{1,0:T(8,128)} %refs_13_.3) | copy-start | bytes 6291460
  18.4 2.9 %collective-permute-start.3 = (bf16[32,8320]{1,0:T(8,128)(2,1)}, bf16[32,8320]{1,0:T(8,128)(2,1)S(1)}, u32[]{:S(2)}, u32[]{:S(2)}) collective-permute-start(bf16[32,8320]{1,0:T(8,128)(2,1)} %collective-permute-done.2.refs_4_.refs_8_), channel_id=1, source_target_pairs={{0,32},{32,0},{64,96},{96,64},{1,33},{33,1},{65,97},{97,65},{2,34}... | collective-permute-start | bytes 1597448 | tf_op jit(solution)/shard_map/ppermute | solution.py:451
  29.8 3.5 %collective-permute-start.4 = (bf16[32,8320]{1,0:T(8,128)(2,1)}, bf16[32,8320]{1,0:T(8,128)(2,1)S(1)}, u32[]{:S(2)}, u32[]{:S(2)}) collective-permute-start(bf16[32,8320]{1,0:T(8,128)(2,1)} %collective-permute-done.1.refs_4_.refs_8_), channel_id=1, source_target_pairs={{0,32},{32,0},{64,96},{96,64},{1,33},{33,1},{65,97},{97,65},{2,34}... | collective-permute-start | bytes 1597448 | tf_op jit(solution)/shard_map/ppermute | solution.py:451
  30.6 11.3 %collective-permute-start.5 = (bf16[32,7168]{1,0:T(8,128)(2,1)S(1)}, bf16[32,7168]{1,0:T(8,128)(2,1)S(1)}, u32[]{:S(2)}, u32[]{:S(2)}) collective-permute-start(bf16[32,7168]{1,0:T(8,128)(2,1)S(1)} %get-tuple-element.50.rest_0_), channel_id=1, source_target_pairs={{0,32},{32,0},{64,96},{96,64},{1,33},{33,1},{65,97},{97,65},{2,34}... | collective-permute-start | bytes 1376264 | tf_op jit(solution)/shard_map/ppermute | solution.py:451
  30.6 16.3 %collective-permute-start.7 = (bf16[32,7168]{1,0:T(8,128)(2,1)S(1)}, bf16[32,7168]{1,0:T(8,128)(2,1)S(1)}, u32[]{:S(2)}, u32[]{:S(2)}) collective-permute-start(bf16[32,7168]{1,0:T(8,128)(2,1)S(1)} %get-tuple-element.50.rest_0_), channel_id=1, source_target_pairs={{0,64},{32,96},{64,0},{96,32},{1,65},{33,97},{65,1},{97,33},{2,66}... | collective-permute-start | bytes 1376264 | tf_op jit(solution)/shard_map/ppermute | solution.py:451
  41.9 5.0 %collective-permute-start.6 = (bf16[2,128,128]{2,1,0:T(8,128)(2,1)S(1)}, bf16[2,128,128]{2,1,0:T(8,128)(2,1)S(1)}, u32[]{:S(2)}, u32[]{:S(2)}) collective-permute-start(bf16[2,128,128]{2,1,0:T(8,128)(2,1)S(1)} %convert_element_type.42), channel_id=1, source_target_pairs={{64,0},{65,1},{66,2},{67,3},{68,4},{69,5},{70,6},{71,7},{72,8},{73... | collective-permute-start | bytes 196616 | tf_op jit(solution)/shard_map/ppermute | solution.py:500
  44.4 3.8 %collective-permute-start.8 = (bf16[2,128,128]{2,1,0:T(8,128)(2,1)S(1)}, bf16[2,128,128]{2,1,0:T(8,128)(2,1)S(1)}, u32[]{:S(2)}, u32[]{:S(2)}) collective-permute-start(bf16[2,128,128]{2,1,0:T(8,128)(2,1)S(1)} %convert_element_type.42), channel_id=1, source_target_pairs={{1,0},{0,1},{3,2},{2,3},{5,4},{4,5},{7,6},{6,7},{9,8},{8,9},{11,10... | collective-permute-start | bytes 196616 | tf_op jit(solution)/shard_map/ppermute | solution.py:500
  44.7 4.3 %collective-permute-start.9 = (bf16[2,128,128]{2,1,0:T(8,128)(2,1)S(1)}, bf16[2,128,128]{2,1,0:T(8,128)(2,1)S(1)}, u32[]{:S(2)}, u32[]{:S(2)}) collective-permute-start(bf16[2,128,128]{2,1,0:T(8,128)(2,1)S(1)} %convert_element_type.42), channel_id=1, source_target_pairs={{65,0},{64,1},{67,2},{66,3},{69,4},{68,5},{71,6},{70,7},{73,8},{72... | collective-permute-start | bytes 196616 | tf_op jit(solution)/shard_map/ppermute | solution.py:500
  45.3 12.7 %collective-permute-start.12 = (bf16[32,9216]{1,0:T(8,128)(2,1)S(1)}, bf16[32,9216]{1,0:T(8,128)(2,1)S(1)}, u32[]{:S(2)}, u32[]{:S(2)}) collective-permute-start(bf16[32,9216]{1,0:T(8,128)(2,1)S(1)} %get-tuple-element.53.rest_4_), channel_id=1, source_target_pairs={{0,32},{32,0},{64,96},{96,64},{1,33},{33,1},{65,97},{97,65},{2,34}... | collective-permute-start | bytes 1769480 | tf_op jit(solution)/shard_map/ppermute | solution.py:451
  49.1 14.3 %collective-permute-start.10 = (bf16[32,9216]{1,0:T(8,128)(2,1)S(1)}, bf16[32,9216]{1,0:T(8,128)(2,1)S(1)}, u32[]{:S(2)}, u32[]{:S(2)}) collective-permute-start(bf16[32,9216]{1,0:T(8,128)(2,1)S(1)} %get-tuple-element.53.rest_4_), channel_id=1, source_target_pairs={{0,64},{32,96},{64,0},{96,32},{1,65},{33,97},{65,1},{97,33},{2,66}... | collective-permute-start | bytes 1769480 | tf_op jit(solution)/shard_map/ppermute | solution.py:451
  50.8 7.1 %collective-permute-start.11 = (bf16[3,128,128]{2,1,0:T(8,128)(2,1)S(1)}, bf16[3,128,128]{2,1,0:T(8,128)(2,1)S(1)}, u32[]{:S(2)}, u32[]{:S(2)}) collective-permute-start(bf16[3,128,128]{2,1,0:T(8,128)(2,1)S(1)} %pad_maximum_fusion.1), channel_id=1, source_target_pairs={{0,2},{1,3},{2,4},{3,5},{4,6},{5,7},{6,8},{7,9},{8,10},{9,11},{10,... | collective-permute-start | bytes 294920 | tf_op jit(solution)/shard_map/ppermute | solution.py:514
  52.5 9.4 %collective-permute-start.13 = (bf16[3,128,128]{2,1,0:T(8,128)(2,1)S(1)}, bf16[3,128,128]{2,1,0:T(8,128)(2,1)S(1)}, u32[]{:S(2)}, u32[]{:S(2)}) collective-permute-start(bf16[3,128,128]{2,1,0:T(8,128)(2,1)S(1)} %pad_maximum_fusion.2), channel_id=1, source_target_pairs={{0,30},{1,31},{2,0},{3,1},{4,2},{5,3},{6,4},{7,5},{8,6},{9,7},{10,... | collective-permute-start | bytes 294920 | tf_op jit(solution)/shard_map/ppermute | solution.py:514
  54.9 7.0 %collective-permute-start.14 = (bf16[128,128]{1,0:T(8,128)(2,1)S(1)}, bf16[128,128]{1,0:T(8,128)(2,1)S(1)}, u32[]{:S(2)}, u32[]{:S(2)}) collective-permute-start(bf16[128,128]{1,0:T(8,128)(2,1)S(1)} %get-tuple-element.65), channel_id=1, source_target_pairs={{0,4},{2,6},{4,8},{5,1},{6,10},{7,3},{8,12},{9,5},{10,14},{11,7},{... | collective-permute-start | bytes 98312 | tf_op jit(solution)/shard_map/ppermute | solution.py:519
  63.4 5.5 %collective-permute-start.17 = (bf16[32,9216]{1,0:T(8,128)(2,1)S(1)}, bf16[32,9216]{1,0:T(8,128)(2,1)S(1)}, u32[]{:S(2)}, u32[]{:S(2)}) collective-permute-start(bf16[32,9216]{1,0:T(8,128)(2,1)S(1)} %collective-permute-done.10.rest_6_), channel_id=1, source_target_pairs={{0,32},{32,0},{64,96},{96,64},{1,33},{33,1},{65,97},{97,65},{2,34}... | collective-permute-start | bytes 1769480 | tf_op jit(solution)/shard_map/ppermute | solution.py:451
  66.4 2.3 %collective-permute-start.16 = (bf16[32,7168]{1,0:T(8,128)(2,1)S(1)}, bf16[32,7168]{1,0:T(8,128)(2,1)S(1)}, u32[]{:S(2)}, u32[]{:S(2)}) collective-permute-start(bf16[32,7168]{1,0:T(8,128)(2,1)S(1)} %collective-permute-done.7.rest_2_), channel_id=1, source_target_pairs={{0,32},{32,0},{64,96},{96,64},{1,33},{33,1},{65,97},{97,65},{2,34}... | collective-permute-start | bytes 1376264 | tf_op jit(solution)/shard_map/ppermute | solution.py:451
  66.4 2.5 %collective-permute-start.15 = (f32[2,128,128]{2,1,0:T(8,128)S(1)}, f32[2,128,128]{2,1,0:T(8,128)S(1)}, u32[]{:S(2)}, u32[]{:S(2)}) collective-permute-start(f32[2,128,128]{2,1,0:T(8,128)S(1)} %shard_map.123.n0), channel_id=1, source_target_pairs={{0,32},{32,0},{64,96},{96,64},{1,33},{33,1},{65,97},{97,65},{2,34}... | collective-permute-start | bytes 393224 | tf_op jit(solution)/shard_map/ppermute | solution.py:451
  (6 other events, 26.9 us)

commit v9 on v8

--- a/solution.py
+++ b/solution.py
@@ -94,24 +94,31 @@
         corner_ref[...] = total
 
 
-def cut_kernel(bounds, source, *rest):
-    outs, sems = rest[:-1], rest[-1]
+CUTS = 5
+
+
+def cut_kernel(start, source, out, sems):
+    size = out.shape[1] // CUTS
     copies = []
-    for k, (start, stop) in enumerate(bounds):
-        copies.append(pltpu.make_async_copy(source.at[:, start:stop], outs[k], sems.at[k]))
+    for k in range(CUTS):
+        at = k * size
+        copies.append(
+            pltpu.make_async_copy(
+                source.at[:, start + at : start + at + size], out.at[:, at : at + size], sems.at[k]
+            )
+        )
         copies[-1].start()
     for copy in copies:
         copy.wait()
 
 
-def run_cut(source, bounds):
-    anywhere = pl.BlockSpec(memory_space=pl.ANY)
+def run_cut(source, start, stop):
     return pl.pallas_call(
-        functools.partial(cut_kernel, bounds),
+        functools.partial(cut_kernel, start),
         in_specs=[pl.BlockSpec(memory_space=pltpu.HBM)],
-        out_specs=[anywhere] * len(bounds),
-        out_shape=[jax.ShapeDtypeStruct((32, stop - start), source.dtype) for start, stop in bounds],
-        scratch_shapes=[pltpu.SemaphoreType.DMA((len(bounds),))],
+        out_specs=pl.BlockSpec(memory_space=pltpu.VMEM),
+        out_shape=jax.ShapeDtypeStruct((32, stop - start), source.dtype),
+        scratch_shapes=[pltpu.SemaphoreType.DMA((CUTS,))],
         compiler_params=pltpu.CompilerParams(vmem_limit_bytes=VMEM_LIMIT),
     )(source)
 
@@ -452,10 +459,10 @@
 
     bounds = [(SPLITS[i], SPLITS[i + 1]) for i in range(len(SPLITS) - 1)]
     gathered = []
-    near = swap(panels, sibling)
-    for first, stop in bounds:
-        (piece,) = run_cut(panels, [(first * GW, stop * GW + BLK)])
-        gathered.append(swap(piece, across))
+    pieces = [run_cut(panels, first * GW, stop * GW + BLK) for first, stop in bounds]
+    pieces[0], source = lax.optimization_barrier((pieces[0], panels))
+    gathered = [swap(piece, across) for piece in pieces]
+    near = swap(source, sibling)
 
     order = ((jnp.arange(4, dtype=jnp.int32) ^ mine)[:, None] * rows + jnp.arange(rows)[None, :]).reshape(-1)
     w = jnp.concatenate(

time: 71.5 us -> 70.9 us (level)
  waiting for transfers between devices: 15.9 us -> 12.3 us
  Pallas kernels: 26.5 us -> 28.9 us
  starting transfers between devices: 25.7 us -> 27.5 us
  local copies, waits for them, and re-layouts: 1.61 us -> 0.37 us
    ppermute x12, waiting for transfers between devices: 9.74 us -> 6.11 us  [body(): swap = lambda value, pairs: lax.ppermute(value, 'band', pairs)]
    pallas_call x2, Pallas kernels: 1.62 us -> 4.03 us  [run_cut(): pl.pallas_call(functools.partial(cut_kernel, start), in_specs=[pl.BlockSp...]
    ppermute x12, starting transfers between devices: 15.3 us -> 17.1 us  [body(): swap = lambda value, pairs: lax.ppermute(value, 'band', pairs)]
    unnamed x25 -> x21, local copies, waits for them, and re-layouts: 1.37 us -> 0.13 us
  transfers between devices with their start and end apart: 18 -> 18, of which waited for: 9 -> 8; matrix products, arithmetic and copies ran while one was open for 1% -> 1% of each run, Pallas kernels for 35% -> 36%
where the time goes in v9:
time: 70.9 us; the launch traced here: 69.9 us
  Pallas kernels  28.9 us (41%)
  starting transfers between devices  27.5 us (39%)
  waiting for transfers between devices  12.3 us (17%)
    ppermute x12, starting transfers between devices, body(): swap = lambda value, pairs: lax.ppermute(value, 'band', pairs)  17.1 us
    pallas_call x2, Pallas kernels, run_rows(): pl.pallas_call(functools.partial(rows_kernel, first, groups, carried), gr...  16.2 us
    ppermute x12, waiting for transfers between devices, body(): swap = lambda value, pairs: lax.ppermute(value, 'band', pairs)  6.11 us
    pallas_call x1, Pallas kernels, run_tables(): pl.pallas_call(tables_kernel, grid_spec=pltpu.PrefetchScalarGridSpec(num_...  6.11 us
    ppermute x2, starting transfers between devices, body(): lax.ppermute(value, 'wide', [(i, (i + 2 * k) % n_wide) for i in range(n_w...  4.11 us
    ppermute x1, waiting for transfers between devices, body(): lax.ppermute(jnp.where(second == 0, odd[1], even[0]), 'wide', [(i, j) for...  4.05 us
    pallas_call x2, Pallas kernels, run_cut(): pl.pallas_call(functools.partial(cut_kernel, start), in_specs=[pl.BlockSp...  4.03 us
    ppermute x3, starting transfers between devices, body(): lax.ppermute(half, ('band', 'wide'), [(at(d ^ db, k ^ dw), at(d, k)) for...  3.35 us
  transfers between devices with their start and end apart: 18, of which 8 were waited for; matrix products, arithmetic and copies ran while one was open for 1% of the time, Pallas kernels for 36%

profile of v9, /device:TPU:25, one launch (start us, length us, event | category | flops | bytes accessed | tf_op | source)
XLA Modules:
  0.0 69.9 jit_solution(16571161452432816606)
XLA Ops:
  0.0 2.1 %shard_map.119 = bf16[32,8320]{1,0:T(8,128)(2,1)} custom-call(bf16[32,16512]{1,0:T(8,128)(2,1)} %refs_6_.3), custom_call_target="tpu_custom_call" | custom-call | tf_op jit(solution)/shard_map/pallas_call | solution.py:116
  2.1 2.8 %collective-permute-start.2 = (bf16[32,8320]{1,0:T(8,128)(2,1)}, bf16[32,8320]{1,0:T(8,128)(2,1)}, u32[]{:S(2)}, u32[]{:S(2)}) collective-permute-start(bf16[32,8320]{1,0:T(8,128)(2,1)} %shard_map.119), channel_id=1, source_target_pairs={{0,64},{32,96},{64,0},{96,32},{1,65},{33,97},{65,1},{97,33},{2,66}... | collective-permute-start | bytes 1597448 | tf_op jit(solution)/shard_map/ppermute | solution.py:458
  5.0 1.0 %collective-permute-start = (bf16[32,16512]{1,0:T(8,128)(2,1)}, bf16[32,16512]{1,0:T(8,128)(2,1)S(1)}, u32[]{:S(2)}, u32[]{:S(2)}) collective-permute-start(bf16[32,16512]{1,0:T(8,128)(2,1)} %refs_6_.3), channel_id=1, source_target_pairs={{0,32},{32,0},{64,96},{96,64},{1,33},{33,1},{65,97},{97,65},{2,34}... | collective-permute-start | bytes 3170312 | tf_op jit(solution)/shard_map/ppermute | solution.py:458
  5.9 1.9 %shard_map.120 = bf16[32,8320]{1,0:T(8,128)(2,1)} custom-call(bf16[32,16512]{1,0:T(8,128)(2,1)} %refs_6_.3), custom_call_target="tpu_custom_call" | custom-call | tf_op jit(solution)/shard_map/pallas_call | solution.py:116
  8.8 6.1 %shard_map.118 = (bf16[128,256,128]{2,1,0:T(8,128)(2,1)S(1)}, bf16[64,128]{1,0:T(8,128)(2,1)S(1)}, f32[32,128]{1,0:T(8,128)S(1)}, bf16[16,32]{1,0:T(8,128)(2,1)S(1)}, f32[32,128]{1,0:T(8,128)S(1)}) custom-call(s32[2]{0:T(128)S(1)} %pad_add_fusion.here_ref, s32[128]{0:T(128)S(1)} %copy-done.4, f32[4,128]{1,0:T(4,128)S(1)} %maximum_reduce-precision_fusion.tap_ref, ...), custom_call_target="tpu_custom_call" | custom-call | tf_op jit(solution)/shard_map/pallas_call | solution.py:129
  15.0 2.0 %collective-permute-done.2.refs_4_.refs_8_ = bf16[32,8320]{1,0:T(8,128)(2,1)} collective-permute-done((bf16[32,8320]{1,0:T(8,128)(2,1)}, bf16[32,8320]{1,0:T(8,128)(2,1)}, u32[]{:S(2)}, u32[]{:S(2)}) %collective-permute-start.2) | collective-permute-done | bytes 532512 | tf_op jit(solution)/shard_map/ppermute | solution.py:458
  17.0 2.7 %collective-permute-start.3 = (bf16[32,8320]{1,0:T(8,128)(2,1)}, bf16[32,8320]{1,0:T(8,128)(2,1)S(1)}, u32[]{:S(2)}, u32[]{:S(2)}) collective-permute-start(bf16[32,8320]{1,0:T(8,128)(2,1)} %collective-permute-done.2.refs_4_.refs_8_), channel_id=1, source_target_pairs={{0,32},{32,0},{64,96},{96,64},{1,33},{33,1},{65,97},{97,65},{2,34}... | collective-permute-start | bytes 1597448 | tf_op jit(solution)/shard_map/ppermute | solution.py:458
  19.9 1.6 %collective-permute-done.3.refs_5_.refs_9_ = bf16[32,8320]{1,0:T(8,128)(2,1)S(1)} collective-permute-done((bf16[32,8320]{1,0:T(8,128)(2,1)}, bf16[32,8320]{1,0:T(8,128)(2,1)S(1)}, u32[]{:S(2)}, u32[]{:S(2)}) %collective-permute-start.3) | collective-permute-done | bytes 532512 | tf_op jit(solution)/shard_map/ppermute | solution.py:458
  21.5 7.7 %shard_map.121 = (bf16[32,7168]{1,0:T(8,128)(2,1)S(1)}, f32[2,56,128]{2,1,0:T(8,128)S(1)}, f32[8,32,128]{2,1,0:T(8,128)S(1)}, f32[40,128]{1,0:T(8,128)S(1)}, f32...) custom-call(s32[128]{0:T(128)S(1)} %fusion.7.refs_0_, f32[2,128]{1,0:T(2,128)S(1)} %copy-done.3, ...), custom_call_target="tpu_custom_call" | custom-call | tf_op jit(solution)/shard_map/pallas_call | solution.py:332
  30.0 2.7 %collective-permute-start.7 = (bf16[32,7168]{1,0:T(8,128)(2,1)S(1)}, bf16[32,7168]{1,0:T(8,128)(2,1)S(1)}, u32[]{:S(2)}, u32[]{:S(2)}) collective-permute-start(bf16[32,7168]{1,0:T(8,128)(2,1)S(1)} %get-tuple-element.54.rest_0_), channel_id=1, source_target_pairs={{0,64},{32,96},{64,0},{96,32},{1,65},{33,97},{65,1},{97,33},{2,66}... | collective-permute-start | bytes 1376264 | tf_op jit(solution)/shard_map/ppermute | solution.py:458
  32.7 8.6 %shard_map.122 = (bf16[32,9216]{1,0:T(8,128)(2,1)S(1)}, f32[2,72,128]{2,1,0:T(8,128)S(1)}, f32[8,32,128]{2,1,0:T(8,128)}, f32[40,128]{1,0:T(8,128)}, f32[40,128]{1,0:T(8,128)}, /*index=5*/bf16[16,1024]{1,0:T(8,128)(2,1)}) custom-call(s32[128]{0:T(128)S(1)} %fusion.7.refs_0_, f32[2,128]{1,0:T(2,128)S(1)} %copy-done.3, bf16[32,16512]{1,0:T(8,128)(2,1)} %refs_6_.3, ...), custom_call_target="tpu_custom_call" | custom-call | tf_op jit(solution)/shard_map/pallas_call | solution.py:332
  41.3 2.5 %collective-permute-start.6 = (bf16[2,128,128]{2,1,0:T(8,128)(2,1)S(1)}, bf16[2,128,128]{2,1,0:T(8,128)(2,1)S(1)}, u32[]{:S(2)}, u32[]{:S(2)}) collective-permute-start(bf16[2,128,128]{2,1,0:T(8,128)(2,1)S(1)} %convert_element_type.42), channel_id=1, source_target_pairs={{64,0},{65,1},{66,2},{67,3},{68,4},{69,5},{70,6},{71,7},{72,8},{73... | collective-permute-start | bytes 196616 | tf_op jit(solution)/shard_map/ppermute | solution.py:507
  44.7 1.6 %collective-permute-start.12 = (bf16[32,9216]{1,0:T(8,128)(2,1)S(1)}, bf16[32,9216]{1,0:T(8,128)(2,1)S(1)}, u32[]{:S(2)}, u32[]{:S(2)}) collective-permute-start(bf16[32,9216]{1,0:T(8,128)(2,1)S(1)} %get-tuple-element.57.rest_4_), channel_id=1, source_target_pairs={{0,32},{32,0},{64,96},{96,64},{1,33},{33,1},{65,97},{97,65},{2,34}... | collective-permute-start | bytes 1769480 | tf_op jit(solution)/shard_map/ppermute | solution.py:458
  46.3 1.3 %collective-permute-done.8 = bf16[2,128,128]{2,1,0:T(8,128)(2,1)S(1)} collective-permute-done((bf16[2,128,128]{2,1,0:T(8,128)(2,1)S(1)}, bf16[2,128,128]{2,1,0:T(8,128)(2,1)S(1)}, u32[]{:S(2)}, u32[]{:S(2)}) %collective-permute-start.8) | collective-permute-done | bytes 65568 | tf_op jit(solution)/shard_map/ppermute | solution.py:507
  47.6 0.8 %collective-permute-done.9 = bf16[2,128,128]{2,1,0:T(8,128)(2,1)S(1)} collective-permute-done((bf16[2,128,128]{2,1,0:T(8,128)(2,1)S(1)}, bf16[2,128,128]{2,1,0:T(8,128)(2,1)S(1)}, u32[]{:S(2)}, u32[]{:S(2)}) %collective-permute-start.9) | collective-permute-done | bytes 65568 | tf_op jit(solution)/shard_map/ppermute | solution.py:507
  48.5 1.7 %collective-permute-start.10 = (bf16[32,9216]{1,0:T(8,128)(2,1)S(1)}, bf16[32,9216]{1,0:T(8,128)(2,1)S(1)}, u32[]{:S(2)}, u32[]{:S(2)}) collective-permute-start(bf16[32,9216]{1,0:T(8,128)(2,1)S(1)} %get-tuple-element.57.rest_4_), channel_id=1, source_target_pairs={{0,64},{32,96},{64,0},{96,32},{1,65},{33,97},{65,1},{97,33},{2,66}... | collective-permute-start | bytes 1769480 | tf_op jit(solution)/shard_map/ppermute | solution.py:458
  50.2 1.7 %collective-permute-start.11 = (bf16[3,128,128]{2,1,0:T(8,128)(2,1)S(1)}, bf16[3,128,128]{2,1,0:T(8,128)(2,1)S(1)}, u32[]{:S(2)}, u32[]{:S(2)}) collective-permute-start(bf16[3,128,128]{2,1,0:T(8,128)(2,1)S(1)} %pad_maximum_fusion.1), channel_id=1, source_target_pairs={{0,2},{1,3},{2,4},{3,5},{4,6},{5,7},{6,8},{7,9},{8,10},{9,11},{10,... | collective-permute-start | bytes 294920 | tf_op jit(solution)/shard_map/ppermute | solution.py:521
  51.9 2.4 %collective-permute-start.13 = (bf16[3,128,128]{2,1,0:T(8,128)(2,1)S(1)}, bf16[3,128,128]{2,1,0:T(8,128)(2,1)S(1)}, u32[]{:S(2)}, u32[]{:S(2)}) collective-permute-start(bf16[3,128,128]{2,1,0:T(8,128)(2,1)S(1)} %pad_maximum_fusion.2), channel_id=1, source_target_pairs={{0,30},{1,31},{2,0},{3,1},{4,2},{5,3},{6,4},{7,5},{8,6},{9,7},{10,... | collective-permute-start | bytes 294920 | tf_op jit(solution)/shard_map/ppermute | solution.py:521
  54.3 3.0 %collective-permute-start.14 = (bf16[128,128]{1,0:T(8,128)(2,1)S(1)}, bf16[128,128]{1,0:T(8,128)(2,1)S(1)}, u32[]{:S(2)}, u32[]{:S(2)}) collective-permute-start(bf16[128,128]{1,0:T(8,128)(2,1)S(1)} %get-tuple-element.69), channel_id=1, source_target_pairs={{0,4},{2,6},{4,8},{5,1},{6,10},{7,3},{8,12},{9,5},{10,14},{11,7},{... | collective-permute-start | bytes 98312 | tf_op jit(solution)/shard_map/ppermute | solution.py:526
  57.3 4.0 %collective-permute-done.14.distant = bf16[128,128]{1,0:T(8,128)(2,1)S(1)} collective-permute-done((bf16[128,128]{1,0:T(8,128)(2,1)S(1)}, bf16[128,128]{1,0:T(8,128)(2,1)S(1)}, u32[]{:S(2)}, u32[]{:S(2)}) %collective-permute-start.14) | collective-permute-done | bytes 32800 | tf_op jit(solution)/shard_map/ppermute | solution.py:526
  61.4 0.9 %shard_map.123.n0 = f32[2,128,128]{2,1,0:T(8,128)S(1)} custom-call(s32[1]{0:T(128)} %bitcast.block_ref, f32[32,128]{1,0:T(8,128)S(1)} %get-tuple-element.58.corner_ref, f32[2,128,128]{2,1,0:T(8,128)S(1)} %convert_add_fusion.1.own, f32[2,128,128]{2,1,0:T(8,128)S(1)} %convert_add_fusion.other, bf16[3,128,128]{2,1,0:T(8,128)(2,1)S(1)} %collective-permute-done.11.below, ...), custom_call_target="tpu_custom_call" | custom-call | tf_op jit(solution)/shard_map/pallas_call | solution.py:373
  62.8 3.0 %collective-permute-start.17 = (bf16[32,9216]{1,0:T(8,128)(2,1)S(1)}, bf16[32,9216]{1,0:T(8,128)(2,1)S(1)}, u32[]{:S(2)}, u32[]{:S(2)}) collective-permute-start(bf16[32,9216]{1,0:T(8,128)(2,1)S(1)} %collective-permute-done.10.rest_6_), channel_id=1, source_target_pairs={{0,32},{32,0},{64,96},{96,64},{1,33},{33,1},{65,97},{97,65},{2,34}... | collective-permute-start | bytes 1769480 | tf_op jit(solution)/shard_map/ppermute | solution.py:458
  66.3 1.8 %collective-permute-done.16.rest_3_ = bf16[32,7168]{1,0:T(8,128)(2,1)S(1)} collective-permute-done((bf16[32,7168]{1,0:T(8,128)(2,1)S(1)}, bf16[32,7168]{1,0:T(8,128)(2,1)S(1)}, u32[]{:S(2)}, u32[]{:S(2)}) %collective-permute-start.16) | collective-permute-done | bytes 458784 | tf_op jit(solution)/shard_map/ppermute | solution.py:458
  68.3 1.6 %shard_map.124 = f32[32,16384]{1,0:T(8,128)} custom-call(bf16[64,128]{1,0:T(8,128)(2,1)S(1)} %get-tuple-element.36.w_ref, f32[32,128]{1,0:T(8,128)S(1)} %get-tuple-element.37.ends_ref, f32[2,128,128]{2,1,0:T(8,128)S(1)} %shard_map.123.n0, f32[2,128,128]{2,1,0:T(8,128)S(1)} %collective-permute-done.15.n1, bf16[32,7168]{1,0:T(8,128)(2,1)S(1)} %get-tuple-element.54.rest_0_, ...), custom_call_target="tpu_custom_call" | custom-call | tf_op jit(solution)/shard_map/pallas_call | solution.py:422
  (63 shorter events, 4.1 us)
Async XLA Ops:
  0.0 8.4 %copy-start.8 = (f32[128]{0:T(128)S(1)}, f32[128]{0:T(128)}, u32[]{:S(2)}) copy-start(f32[128]{0:T(128)} %param.19) | copy-start | bytes 1540
  0.0 8.7 %copy-start.7 = (f32[2,32]{1,0:T(2,128)S(1)}, f32[2,32]{1,0:T(2,128)}, u32[]{:S(2)}) copy-start(f32[2,32]{1,0:T(2,128)} %param.23) | copy-start | bytes 772
  0.0 8.8 %copy-start.4 = (s32[128]{0:T(128)S(1)}, s32[128]{0:T(128)}, u32[]{:S(2)}) copy-start(s32[128]{0:T(128)} %shift_ref.1) | copy-start | bytes 1540
  0.0 8.8 %copy-start = (f32[32,128,128]{2,1,0:T(8,128)S(1)}, f32[32,128,128]{2,1,0:T(8,128)}, u32[]{:S(2)}) copy-start(f32[32,128,128]{2,1,0:T(8,128)} %last_ref.1) | copy-start | bytes 6291460
  2.1 14.9 %collective-permute-start.2 = (bf16[32,8320]{1,0:T(8,128)(2,1)}, bf16[32,8320]{1,0:T(8,128)(2,1)}, u32[]{:S(2)}, u32[]{:S(2)}) collective-permute-start(bf16[32,8320]{1,0:T(8,128)(2,1)} %shard_map.119), channel_id=1, source_target_pairs={{0,64},{32,96},{64,0},{96,32},{1,65},{33,97},{65,1},{97,33},{2,66}... | collective-permute-start | bytes 1597448 | tf_op jit(solution)/shard_map/ppermute | solution.py:458
  5.0 14.9 %collective-permute-start = (bf16[32,16512]{1,0:T(8,128)(2,1)}, bf16[32,16512]{1,0:T(8,128)(2,1)S(1)}, u32[]{:S(2)}, u32[]{:S(2)}) collective-permute-start(bf16[32,16512]{1,0:T(8,128)(2,1)} %refs_6_.3), channel_id=1, source_target_pairs={{0,32},{32,0},{64,96},{96,64},{1,33},{33,1},{65,97},{97,65},{2,34}... | collective-permute-start | bytes 3170312 | tf_op jit(solution)/shard_map/ppermute | solution.py:458
  7.9 21.3 %collective-permute-start.1 = (bf16[32,8320]{1,0:T(8,128)(2,1)}, bf16[32,8320]{1,0:T(8,128)(2,1)}, u32[]{:S(2)}, u32[]{:S(2)}) collective-permute-start(bf16[32,8320]{1,0:T(8,128)(2,1)} %shard_map.120), channel_id=1, source_target_pairs={{0,64},{32,96},{64,0},{96,32},{1,65},{33,97},{65,1},{97,33},{2,66}... | collective-permute-start | bytes 1597448 | tf_op jit(solution)/shard_map/ppermute | solution.py:458
  8.8 12.7 %copy-start.1 = (s32[32,16384]{1,0:T(8,128)S(1)}, s32[32,16384]{1,0:T(8,128)}, u32[]{:S(2)}) copy-start(s32[32,16384]{1,0:T(8,128)} %refs_12_.3) | copy-start | bytes 6291460
  8.8 12.7 %copy-start.2 = (f32[32,16384]{1,0:T(8,128)S(1)}, f32[32,16384]{1,0:T(8,128)}, u32[]{:S(2)}) copy-start(f32[32,16384]{1,0:T(8,128)} %refs_13_.3) | copy-start | bytes 6291460
  17.0 4.5 %collective-permute-start.3 = (bf16[32,8320]{1,0:T(8,128)(2,1)}, bf16[32,8320]{1,0:T(8,128)(2,1)S(1)}, u32[]{:S(2)}, u32[]{:S(2)}) collective-permute-start(bf16[32,8320]{1,0:T(8,128)(2,1)} %collective-permute-done.2.refs_4_.refs_8_), channel_id=1, source_target_pairs={{0,32},{32,0},{64,96},{96,64},{1,33},{33,1},{65,97},{97,65},{2,34}... | collective-permute-start | bytes 1597448 | tf_op jit(solution)/shard_map/ppermute | solution.py:458
  29.2 3.6 %collective-permute-start.4 = (bf16[32,8320]{1,0:T(8,128)(2,1)}, bf16[32,8320]{1,0:T(8,128)(2,1)S(1)}, u32[]{:S(2)}, u32[]{:S(2)}) collective-permute-start(bf16[32,8320]{1,0:T(8,128)(2,1)} %collective-permute-done.1.refs_4_.refs_8_), channel_id=1, source_target_pairs={{0,32},{32,0},{64,96},{96,64},{1,33},{33,1},{65,97},{97,65},{2,34}... | collective-permute-start | bytes 1597448 | tf_op jit(solution)/shard_map/ppermute | solution.py:458
  30.0 11.3 %collective-permute-start.5 = (bf16[32,7168]{1,0:T(8,128)(2,1)S(1)}, bf16[32,7168]{1,0:T(8,128)(2,1)S(1)}, u32[]{:S(2)}, u32[]{:S(2)}) collective-permute-start(bf16[32,7168]{1,0:T(8,128)(2,1)S(1)} %get-tuple-element.54.rest_0_), channel_id=1, source_target_pairs={{0,32},{32,0},{64,96},{96,64},{1,33},{33,1},{65,97},{97,65},{2,34}... | collective-permute-start | bytes 1376264 | tf_op jit(solution)/shard_map/ppermute | solution.py:458
  30.0 16.3 %collective-permute-start.7 = (bf16[32,7168]{1,0:T(8,128)(2,1)S(1)}, bf16[32,7168]{1,0:T(8,128)(2,1)S(1)}, u32[]{:S(2)}, u32[]{:S(2)}) collective-permute-start(bf16[32,7168]{1,0:T(8,128)(2,1)S(1)} %get-tuple-element.54.rest_0_), channel_id=1, source_target_pairs={{0,64},{32,96},{64,0},{96,32},{1,65},{33,97},{65,1},{97,33},{2,66}... | collective-permute-start | bytes 1376264 | tf_op jit(solution)/shard_map/ppermute | solution.py:458
  41.3 5.0 %collective-permute-start.6 = (bf16[2,128,128]{2,1,0:T(8,128)(2,1)S(1)}, bf16[2,128,128]{2,1,0:T(8,128)(2,1)S(1)}, u32[]{:S(2)}, u32[]{:S(2)}) collective-permute-start(bf16[2,128,128]{2,1,0:T(8,128)(2,1)S(1)} %convert_element_type.42), channel_id=1, source_target_pairs={{64,0},{65,1},{66,2},{67,3},{68,4},{69,5},{70,6},{71,7},{72,8},{73... | collective-permute-start | bytes 196616 | tf_op jit(solution)/shard_map/ppermute | solution.py:507
  43.8 3.8 %collective-permute-start.8 = (bf16[2,128,128]{2,1,0:T(8,128)(2,1)S(1)}, bf16[2,128,128]{2,1,0:T(8,128)(2,1)S(1)}, u32[]{:S(2)}, u32[]{:S(2)}) collective-permute-start(bf16[2,128,128]{2,1,0:T(8,128)(2,1)S(1)} %convert_element_type.42), channel_id=1, source_target_pairs={{1,0},{0,1},{3,2},{2,3},{5,4},{4,5},{7,6},{6,7},{9,8},{8,9},{11,10... | collective-permute-start | bytes 196616 | tf_op jit(solution)/shard_map/ppermute | solution.py:507
  44.1 4.3 %collective-permute-start.9 = (bf16[2,128,128]{2,1,0:T(8,128)(2,1)S(1)}, bf16[2,128,128]{2,1,0:T(8,128)(2,1)S(1)}, u32[]{:S(2)}, u32[]{:S(2)}) collective-permute-start(bf16[2,128,128]{2,1,0:T(8,128)(2,1)S(1)} %convert_element_type.42), channel_id=1, source_target_pairs={{65,0},{64,1},{67,2},{66,3},{69,4},{68,5},{71,6},{70,7},{73,8},{72... | collective-permute-start | bytes 196616 | tf_op jit(solution)/shard_map/ppermute | solution.py:507
  44.7 12.6 %collective-permute-start.12 = (bf16[32,9216]{1,0:T(8,128)(2,1)S(1)}, bf16[32,9216]{1,0:T(8,128)(2,1)S(1)}, u32[]{:S(2)}, u32[]{:S(2)}) collective-permute-start(bf16[32,9216]{1,0:T(8,128)(2,1)S(1)} %get-tuple-element.57.rest_4_), channel_id=1, source_target_pairs={{0,32},{32,0},{64,96},{96,64},{1,33},{33,1},{65,97},{97,65},{2,34}... | collective-permute-start | bytes 1769480 | tf_op jit(solution)/shard_map/ppermute | solution.py:458
  48.5 14.3 %collective-permute-start.10 = (bf16[32,9216]{1,0:T(8,128)(2,1)S(1)}, bf16[32,9216]{1,0:T(8,128)(2,1)S(1)}, u32[]{:S(2)}, u32[]{:S(2)}) collective-permute-start(bf16[32,9216]{1,0:T(8,128)(2,1)S(1)} %get-tuple-element.57.rest_4_), channel_id=1, source_target_pairs={{0,64},{32,96},{64,0},{96,32},{1,65},{33,97},{65,1},{97,33},{2,66}... | collective-permute-start | bytes 1769480 | tf_op jit(solution)/shard_map/ppermute | solution.py:458
  50.2 7.1 %collective-permute-start.11 = (bf16[3,128,128]{2,1,0:T(8,128)(2,1)S(1)}, bf16[3,128,128]{2,1,0:T(8,128)(2,1)S(1)}, u32[]{:S(2)}, u32[]{:S(2)}) collective-permute-start(bf16[3,128,128]{2,1,0:T(8,128)(2,1)S(1)} %pad_maximum_fusion.1), channel_id=1, source_target_pairs={{0,2},{1,3},{2,4},{3,5},{4,6},{5,7},{6,8},{7,9},{8,10},{9,11},{10,... | collective-permute-start | bytes 294920 | tf_op jit(solution)/shard_map/ppermute | solution.py:521
  51.9 9.5 %collective-permute-start.13 = (bf16[3,128,128]{2,1,0:T(8,128)(2,1)S(1)}, bf16[3,128,128]{2,1,0:T(8,128)(2,1)S(1)}, u32[]{:S(2)}, u32[]{:S(2)}) collective-permute-start(bf16[3,128,128]{2,1,0:T(8,128)(2,1)S(1)} %pad_maximum_fusion.2), channel_id=1, source_target_pairs={{0,30},{1,31},{2,0},{3,1},{4,2},{5,3},{6,4},{7,5},{8,6},{9,7},{10,... | collective-permute-start | bytes 294920 | tf_op jit(solution)/shard_map/ppermute | solution.py:521
  54.3 7.0 %collective-permute-start.14 = (bf16[128,128]{1,0:T(8,128)(2,1)S(1)}, bf16[128,128]{1,0:T(8,128)(2,1)S(1)}, u32[]{:S(2)}, u32[]{:S(2)}) collective-permute-start(bf16[128,128]{1,0:T(8,128)(2,1)S(1)} %get-tuple-element.69), channel_id=1, source_target_pairs={{0,4},{2,6},{4,8},{5,1},{6,10},{7,3},{8,12},{9,5},{10,14},{11,7},{... | collective-permute-start | bytes 98312 | tf_op jit(solution)/shard_map/ppermute | solution.py:526
  62.8 5.5 %collective-permute-start.17 = (bf16[32,9216]{1,0:T(8,128)(2,1)S(1)}, bf16[32,9216]{1,0:T(8,128)(2,1)S(1)}, u32[]{:S(2)}, u32[]{:S(2)}) collective-permute-start(bf16[32,9216]{1,0:T(8,128)(2,1)S(1)} %collective-permute-done.10.rest_6_), channel_id=1, source_target_pairs={{0,32},{32,0},{64,96},{96,64},{1,33},{33,1},{65,97},{97,65},{2,34}... | collective-permute-start | bytes 1769480 | tf_op jit(solution)/shard_map/ppermute | solution.py:458
  65.8 2.3 %collective-permute-start.16 = (bf16[32,7168]{1,0:T(8,128)(2,1)S(1)}, bf16[32,7168]{1,0:T(8,128)(2,1)S(1)}, u32[]{:S(2)}, u32[]{:S(2)}) collective-permute-start(bf16[32,7168]{1,0:T(8,128)(2,1)S(1)} %collective-permute-done.7.rest_2_), channel_id=1, source_target_pairs={{0,32},{32,0},{64,96},{96,64},{1,33},{33,1},{65,97},{97,65},{2,34}... | collective-permute-start | bytes 1376264 | tf_op jit(solution)/shard_map/ppermute | solution.py:458
  65.8 2.5 %collective-permute-start.15 = (f32[2,128,128]{2,1,0:T(8,128)S(1)}, f32[2,128,128]{2,1,0:T(8,128)S(1)}, u32[]{:S(2)}, u32[]{:S(2)}) collective-permute-start(f32[2,128,128]{2,1,0:T(8,128)S(1)} %shard_map.123.n0), channel_id=1, source_target_pairs={{0,32},{32,0},{64,96},{96,64},{1,33},{33,1},{65,97},{97,65},{2,34}... | collective-permute-start | bytes 393224 | tf_op jit(solution)/shard_map/ppermute | solution.py:458
  (4 other events, 29.0 us)

commit v10 on v9

--- a/solution.py
+++ b/solution.py
@@ -97,18 +97,20 @@
 CUTS = 5
 
 
-def cut_kernel(start, source, out, sems):
+def cut_kernel(start, source, out, held, sems):
     size = out.shape[1] // CUTS
-    copies = []
+    arrive, leave = [], []
     for k in range(CUTS):
-        at = k * size
-        copies.append(
-            pltpu.make_async_copy(
-                source.at[:, start + at : start + at + size], out.at[:, at : at + size], sems.at[k]
-            )
-        )
-        copies[-1].start()
-    for copy in copies:
+        here = held.at[:, k * size : (k + 1) * size]
+        at = start + k * size
+        arrive.append(pltpu.make_async_copy(source.at[:, at : at + size], here, sems.at[0, k]))
+        leave.append(pltpu.make_async_copy(here, out.at[:, k * size : (k + 1) * size], sems.at[1, k]))
+    for copy in arrive:
+        copy.start()
+    for k in range(CUTS):
+        arrive[k].wait()
+        leave[k].start()
+    for copy in leave:
         copy.wait()
 
 
@@ -116,9 +118,12 @@
     return pl.pallas_call(
         functools.partial(cut_kernel, start),
         in_specs=[pl.BlockSpec(memory_space=pltpu.HBM)],
-        out_specs=pl.BlockSpec(memory_space=pltpu.VMEM),
+        out_specs=pl.BlockSpec(memory_space=pl.ANY),
         out_shape=jax.ShapeDtypeStruct((32, stop - start), source.dtype),
-        scratch_shapes=[pltpu.SemaphoreType.DMA((CUTS,))],
+        scratch_shapes=[
+            pltpu.VMEM((32, stop - start), source.dtype),
+            pltpu.SemaphoreType.DMA((2, CUTS)),
+        ],
         compiler_params=pltpu.CompilerParams(vmem_limit_bytes=VMEM_LIMIT),
     )(source)
 

time: 70.9 us -> 70.8 us (level)
  no operation moved by 1% of the time
where the time goes in v10:
time: 70.8 us; the launch traced here: 69.8 us
  Pallas kernels  28.7 us (41%)
  starting transfers between devices  27.5 us (39%)
  waiting for transfers between devices  12.4 us (18%)
    ppermute x12, starting transfers between devices, body(): swap = lambda value, pairs: lax.ppermute(value, 'band', pairs)  17.1 us
    pallas_call x2, Pallas kernels, run_rows(): pl.pallas_call(functools.partial(rows_kernel, first, groups, carried), gr...  16.2 us
    ppermute x12, waiting for transfers between devices, body(): swap = lambda value, pairs: lax.ppermute(value, 'band', pairs)  6.23 us
    pallas_call x1, Pallas kernels, run_tables(): pl.pallas_call(tables_kernel, grid_spec=pltpu.PrefetchScalarGridSpec(num_...  6.11 us
    ppermute x2, starting transfers between devices, body(): lax.ppermute(value, 'wide', [(i, (i + 2 * k) % n_wide) for i in range(n_w...  4.12 us
    ppermute x1, waiting for transfers between devices, body(): lax.ppermute(jnp.where(second == 0, odd[1], even[0]), 'wide', [(i, j) for...  4.04 us
    pallas_call x2, Pallas kernels, run_cut(): pl.pallas_call(functools.partial(cut_kernel, start), in_specs=[pl.BlockSp...  3.81 us
    ppermute x3, starting transfers between devices, body(): lax.ppermute(half, ('band', 'wide'), [(at(d ^ db, k ^ dw), at(d, k)) for...  3.35 us
  transfers between devices with their start and end apart: 18, of which 8 were waited for; matrix products, arithmetic and copies ran while one was open for 1% of the time, Pallas kernels for 36%

profile of v10, /device:TPU:25, one launch (start us, length us, event | category | flops | bytes accessed | tf_op | source)
XLA Modules:
  0.0 69.8 jit_solution(3915867429841502093)
XLA Ops:
  0.0 2.0 %shard_map.119 = bf16[32,8320]{1,0:T(8,128)(2,1)} custom-call(bf16[32,16512]{1,0:T(8,128)(2,1)} %refs_6_.3), custom_call_target="tpu_custom_call" | custom-call | tf_op jit(solution)/shard_map/pallas_call | solution.py:118
  2.0 2.8 %collective-permute-start.2 = (bf16[32,8320]{1,0:T(8,128)(2,1)}, bf16[32,8320]{1,0:T(8,128)(2,1)}, u32[]{:S(2)}, u32[]{:S(2)}) collective-permute-start(bf16[32,8320]{1,0:T(8,128)(2,1)} %shard_map.119), channel_id=1, source_target_pairs={{0,64},{32,96},{64,0},{96,32},{1,65},{33,97},{65,1},{97,33},{2,66}... | collective-permute-start | bytes 1597448 | tf_op jit(solution)/shard_map/ppermute | solution.py:463
  4.8 1.0 %collective-permute-start = (bf16[32,16512]{1,0:T(8,128)(2,1)}, bf16[32,16512]{1,0:T(8,128)(2,1)S(1)}, u32[]{:S(2)}, u32[]{:S(2)}) collective-permute-start(bf16[32,16512]{1,0:T(8,128)(2,1)} %refs_6_.3), channel_id=1, source_target_pairs={{0,32},{32,0},{64,96},{96,64},{1,33},{33,1},{65,97},{97,65},{2,34}... | collective-permute-start | bytes 3170312 | tf_op jit(solution)/shard_map/ppermute | solution.py:463
  5.8 1.8 %shard_map.120 = bf16[32,8320]{1,0:T(8,128)(2,1)} custom-call(bf16[32,16512]{1,0:T(8,128)(2,1)} %refs_6_.3), custom_call_target="tpu_custom_call" | custom-call | tf_op jit(solution)/shard_map/pallas_call | solution.py:118
  8.6 6.1 %shard_map.118 = (bf16[128,256,128]{2,1,0:T(8,128)(2,1)S(1)}, bf16[64,128]{1,0:T(8,128)(2,1)S(1)}, f32[32,128]{1,0:T(8,128)S(1)}, bf16[16,32]{1,0:T(8,128)(2,1)S(1)}, f32[32,128]{1,0:T(8,128)S(1)}) custom-call(s32[2]{0:T(128)S(1)} %pad_add_fusion.here_ref, s32[128]{0:T(128)S(1)} %copy-done.4, f32[4,128]{1,0:T(4,128)S(1)} %maximum_reduce-precision_fusion.tap_ref, ...), custom_call_target="tpu_custom_call" | custom-call | tf_op jit(solution)/shard_map/pallas_call | solution.py:134
  14.8 2.1 %collective-permute-done.2.refs_4_.refs_8_ = bf16[32,8320]{1,0:T(8,128)(2,1)} collective-permute-done((bf16[32,8320]{1,0:T(8,128)(2,1)}, bf16[32,8320]{1,0:T(8,128)(2,1)}, u32[]{:S(2)}, u32[]{:S(2)}) %collective-permute-start.2) | collective-permute-done | bytes 532512 | tf_op jit(solution)/shard_map/ppermute | solution.py:463
  16.9 2.7 %collective-permute-start.3 = (bf16[32,8320]{1,0:T(8,128)(2,1)}, bf16[32,8320]{1,0:T(8,128)(2,1)S(1)}, u32[]{:S(2)}, u32[]{:S(2)}) collective-permute-start(bf16[32,8320]{1,0:T(8,128)(2,1)} %collective-permute-done.2.refs_4_.refs_8_), channel_id=1, source_target_pairs={{0,32},{32,0},{64,96},{96,64},{1,33},{33,1},{65,97},{97,65},{2,34}... | collective-permute-start | bytes 1597448 | tf_op jit(solution)/shard_map/ppermute | solution.py:463
  19.7 1.6 %collective-permute-done.3.refs_5_.refs_9_ = bf16[32,8320]{1,0:T(8,128)(2,1)S(1)} collective-permute-done((bf16[32,8320]{1,0:T(8,128)(2,1)}, bf16[32,8320]{1,0:T(8,128)(2,1)S(1)}, u32[]{:S(2)}, u32[]{:S(2)}) %collective-permute-start.3) | collective-permute-done | bytes 532512 | tf_op jit(solution)/shard_map/ppermute | solution.py:463
  21.4 7.7 %shard_map.121 = (bf16[32,7168]{1,0:T(8,128)(2,1)S(1)}, f32[2,56,128]{2,1,0:T(8,128)S(1)}, f32[8,32,128]{2,1,0:T(8,128)S(1)}, f32[40,128]{1,0:T(8,128)S(1)}, f32...) custom-call(s32[128]{0:T(128)S(1)} %fusion.7.refs_0_, f32[2,128]{1,0:T(2,128)S(1)} %copy-done.3, ...), custom_call_target="tpu_custom_call" | custom-call | tf_op jit(solution)/shard_map/pallas_call | solution.py:337
  29.9 2.7 %collective-permute-start.7 = (bf16[32,7168]{1,0:T(8,128)(2,1)S(1)}, bf16[32,7168]{1,0:T(8,128)(2,1)S(1)}, u32[]{:S(2)}, u32[]{:S(2)}) collective-permute-start(bf16[32,7168]{1,0:T(8,128)(2,1)S(1)} %get-tuple-element.54.rest_0_), channel_id=1, source_target_pairs={{0,64},{32,96},{64,0},{96,32},{1,65},{33,97},{65,1},{97,33},{2,66}... | collective-permute-start | bytes 1376264 | tf_op jit(solution)/shard_map/ppermute | solution.py:463
  32.6 8.6 %shard_map.122 = (bf16[32,9216]{1,0:T(8,128)(2,1)S(1)}, f32[2,72,128]{2,1,0:T(8,128)S(1)}, f32[8,32,128]{2,1,0:T(8,128)}, f32[40,128]{1,0:T(8,128)}, f32[40,128]{1,0:T(8,128)}, /*index=5*/bf16[16,1024]{1,0:T(8,128)(2,1)}) custom-call(s32[128]{0:T(128)S(1)} %fusion.7.refs_0_, f32[2,128]{1,0:T(2,128)S(1)} %copy-done.3, bf16[32,16512]{1,0:T(8,128)(2,1)} %refs_6_.3, ...), custom_call_target="tpu_custom_call" | custom-call | tf_op jit(solution)/shard_map/pallas_call | solution.py:337
  41.2 2.5 %collective-permute-start.6 = (bf16[2,128,128]{2,1,0:T(8,128)(2,1)S(1)}, bf16[2,128,128]{2,1,0:T(8,128)(2,1)S(1)}, u32[]{:S(2)}, u32[]{:S(2)}) collective-permute-start(bf16[2,128,128]{2,1,0:T(8,128)(2,1)S(1)} %convert_element_type.42), channel_id=1, source_target_pairs={{64,0},{65,1},{66,2},{67,3},{68,4},{69,5},{70,6},{71,7},{72,8},{73... | collective-permute-start | bytes 196616 | tf_op jit(solution)/shard_map/ppermute | solution.py:512
  44.6 1.6 %collective-permute-start.12 = (bf16[32,9216]{1,0:T(8,128)(2,1)S(1)}, bf16[32,9216]{1,0:T(8,128)(2,1)S(1)}, u32[]{:S(2)}, u32[]{:S(2)}) collective-permute-start(bf16[32,9216]{1,0:T(8,128)(2,1)S(1)} %get-tuple-element.57.rest_4_), channel_id=1, source_target_pairs={{0,32},{32,0},{64,96},{96,64},{1,33},{33,1},{65,97},{97,65},{2,34}... | collective-permute-start | bytes 1769480 | tf_op jit(solution)/shard_map/ppermute | solution.py:463
  46.2 1.3 %collective-permute-done.8 = bf16[2,128,128]{2,1,0:T(8,128)(2,1)S(1)} collective-permute-done((bf16[2,128,128]{2,1,0:T(8,128)(2,1)S(1)}, bf16[2,128,128]{2,1,0:T(8,128)(2,1)S(1)}, u32[]{:S(2)}, u32[]{:S(2)}) %collective-permute-start.8) | collective-permute-done | bytes 65568 | tf_op jit(solution)/shard_map/ppermute | solution.py:512
  47.5 0.8 %collective-permute-done.9 = bf16[2,128,128]{2,1,0:T(8,128)(2,1)S(1)} collective-permute-done((bf16[2,128,128]{2,1,0:T(8,128)(2,1)S(1)}, bf16[2,128,128]{2,1,0:T(8,128)(2,1)S(1)}, u32[]{:S(2)}, u32[]{:S(2)}) %collective-permute-start.9) | collective-permute-done | bytes 65568 | tf_op jit(solution)/shard_map/ppermute | solution.py:512
  48.4 1.6 %collective-permute-start.10 = (bf16[32,9216]{1,0:T(8,128)(2,1)S(1)}, bf16[32,9216]{1,0:T(8,128)(2,1)S(1)}, u32[]{:S(2)}, u32[]{:S(2)}) collective-permute-start(bf16[32,9216]{1,0:T(8,128)(2,1)S(1)} %get-tuple-element.57.rest_4_), channel_id=1, source_target_pairs={{0,64},{32,96},{64,0},{96,32},{1,65},{33,97},{65,1},{97,33},{2,66}... | collective-permute-start | bytes 1769480 | tf_op jit(solution)/shard_map/ppermute | solution.py:463
  50.1 1.7 %collective-permute-start.11 = (bf16[3,128,128]{2,1,0:T(8,128)(2,1)S(1)}, bf16[3,128,128]{2,1,0:T(8,128)(2,1)S(1)}, u32[]{:S(2)}, u32[]{:S(2)}) collective-permute-start(bf16[3,128,128]{2,1,0:T(8,128)(2,1)S(1)} %pad_maximum_fusion.1), channel_id=1, source_target_pairs={{0,2},{1,3},{2,4},{3,5},{4,6},{5,7},{6,8},{7,9},{8,10},{9,11},{10,... | collective-permute-start | bytes 294920 | tf_op jit(solution)/shard_map/ppermute | solution.py:526
  51.8 2.4 %collective-permute-start.13 = (bf16[3,128,128]{2,1,0:T(8,128)(2,1)S(1)}, bf16[3,128,128]{2,1,0:T(8,128)(2,1)S(1)}, u32[]{:S(2)}, u32[]{:S(2)}) collective-permute-start(bf16[3,128,128]{2,1,0:T(8,128)(2,1)S(1)} %pad_maximum_fusion.2), channel_id=1, source_target_pairs={{0,30},{1,31},{2,0},{3,1},{4,2},{5,3},{6,4},{7,5},{8,6},{9,7},{10,... | collective-permute-start | bytes 294920 | tf_op jit(solution)/shard_map/ppermute | solution.py:526
  54.2 3.0 %collective-permute-start.14 = (bf16[128,128]{1,0:T(8,128)(2,1)S(1)}, bf16[128,128]{1,0:T(8,128)(2,1)S(1)}, u32[]{:S(2)}, u32[]{:S(2)}) collective-permute-start(bf16[128,128]{1,0:T(8,128)(2,1)S(1)} %get-tuple-element.69), channel_id=1, source_target_pairs={{0,4},{2,6},{4,8},{5,1},{6,10},{7,3},{8,12},{9,5},{10,14},{11,7},{... | collective-permute-start | bytes 98312 | tf_op jit(solution)/shard_map/ppermute | solution.py:531
  57.2 4.0 %collective-permute-done.14.distant = bf16[128,128]{1,0:T(8,128)(2,1)S(1)} collective-permute-done((bf16[128,128]{1,0:T(8,128)(2,1)S(1)}, bf16[128,128]{1,0:T(8,128)(2,1)S(1)}, u32[]{:S(2)}, u32[]{:S(2)}) %collective-permute-start.14) | collective-permute-done | bytes 32800 | tf_op jit(solution)/shard_map/ppermute | solution.py:531
  61.3 0.9 %shard_map.123.n0 = f32[2,128,128]{2,1,0:T(8,128)S(1)} custom-call(s32[1]{0:T(128)} %bitcast.block_ref, f32[32,128]{1,0:T(8,128)S(1)} %get-tuple-element.58.corner_ref, f32[2,128,128]{2,1,0:T(8,128)S(1)} %convert_add_fusion.1.own, f32[2,128,128]{2,1,0:T(8,128)S(1)} %convert_add_fusion.other, bf16[3,128,128]{2,1,0:T(8,128)(2,1)S(1)} %collective-permute-done.11.below, ...), custom_call_target="tpu_custom_call" | custom-call | tf_op jit(solution)/shard_map/pallas_call | solution.py:378
  62.7 3.0 %collective-permute-start.17 = (bf16[32,9216]{1,0:T(8,128)(2,1)S(1)}, bf16[32,9216]{1,0:T(8,128)(2,1)S(1)}, u32[]{:S(2)}, u32[]{:S(2)}) collective-permute-start(bf16[32,9216]{1,0:T(8,128)(2,1)S(1)} %collective-permute-done.10.rest_6_), channel_id=1, source_target_pairs={{0,32},{32,0},{64,96},{96,64},{1,33},{33,1},{65,97},{97,65},{2,34}... | collective-permute-start | bytes 1769480 | tf_op jit(solution)/shard_map/ppermute | solution.py:463
  66.2 1.8 %collective-permute-done.16.rest_3_ = bf16[32,7168]{1,0:T(8,128)(2,1)S(1)} collective-permute-done((bf16[32,7168]{1,0:T(8,128)(2,1)S(1)}, bf16[32,7168]{1,0:T(8,128)(2,1)S(1)}, u32[]{:S(2)}, u32[]{:S(2)}) %collective-permute-start.16) | collective-permute-done | bytes 458784 | tf_op jit(solution)/shard_map/ppermute | solution.py:463
  68.2 1.6 %shard_map.124 = f32[32,16384]{1,0:T(8,128)} custom-call(bf16[64,128]{1,0:T(8,128)(2,1)S(1)} %get-tuple-element.36.w_ref, f32[32,128]{1,0:T(8,128)S(1)} %get-tuple-element.37.ends_ref, f32[2,128,128]{2,1,0:T(8,128)S(1)} %shard_map.123.n0, f32[2,128,128]{2,1,0:T(8,128)S(1)} %collective-permute-done.15.n1, bf16[32,7168]{1,0:T(8,128)(2,1)S(1)} %get-tuple-element.54.rest_0_, ...), custom_call_target="tpu_custom_call" | custom-call | tf_op jit(solution)/shard_map/pallas_call | solution.py:427
  (63 shorter events, 4.1 us)
Async XLA Ops:
  0.0 8.2 %copy-start.8 = (f32[128]{0:T(128)S(1)}, f32[128]{0:T(128)}, u32[]{:S(2)}) copy-start(f32[128]{0:T(128)} %param.19) | copy-start | bytes 1540
  0.0 8.5 %copy-start.7 = (f32[2,32]{1,0:T(2,128)S(1)}, f32[2,32]{1,0:T(2,128)}, u32[]{:S(2)}) copy-start(f32[2,32]{1,0:T(2,128)} %param.23) | copy-start | bytes 772
  0.0 8.5 %copy-start.4 = (s32[128]{0:T(128)S(1)}, s32[128]{0:T(128)}, u32[]{:S(2)}) copy-start(s32[128]{0:T(128)} %shift_ref.1) | copy-start | bytes 1540
  0.0 8.5 %copy-start = (f32[32,128,128]{2,1,0:T(8,128)S(1)}, f32[32,128,128]{2,1,0:T(8,128)}, u32[]{:S(2)}) copy-start(f32[32,128,128]{2,1,0:T(8,128)} %last_ref.1) | copy-start | bytes 6291460
  2.0 14.9 %collective-permute-start.2 = (bf16[32,8320]{1,0:T(8,128)(2,1)}, bf16[32,8320]{1,0:T(8,128)(2,1)}, u32[]{:S(2)}, u32[]{:S(2)}) collective-permute-start(bf16[32,8320]{1,0:T(8,128)(2,1)} %shard_map.119), channel_id=1, source_target_pairs={{0,64},{32,96},{64,0},{96,32},{1,65},{33,97},{65,1},{97,33},{2,66}... | collective-permute-start | bytes 1597448 | tf_op jit(solution)/shard_map/ppermute | solution.py:463
  4.8 14.9 %collective-permute-start = (bf16[32,16512]{1,0:T(8,128)(2,1)}, bf16[32,16512]{1,0:T(8,128)(2,1)S(1)}, u32[]{:S(2)}, u32[]{:S(2)}) collective-permute-start(bf16[32,16512]{1,0:T(8,128)(2,1)} %refs_6_.3), channel_id=1, source_target_pairs={{0,32},{32,0},{64,96},{96,64},{1,33},{33,1},{65,97},{97,65},{2,34}... | collective-permute-start | bytes 3170312 | tf_op jit(solution)/shard_map/ppermute | solution.py:463
  7.6 21.4 %collective-permute-start.1 = (bf16[32,8320]{1,0:T(8,128)(2,1)}, bf16[32,8320]{1,0:T(8,128)(2,1)}, u32[]{:S(2)}, u32[]{:S(2)}) collective-permute-start(bf16[32,8320]{1,0:T(8,128)(2,1)} %shard_map.120), channel_id=1, source_target_pairs={{0,64},{32,96},{64,0},{96,32},{1,65},{33,97},{65,1},{97,33},{2,66}... | collective-permute-start | bytes 1597448 | tf_op jit(solution)/shard_map/ppermute | solution.py:463
  8.6 12.8 %copy-start.1 = (s32[32,16384]{1,0:T(8,128)S(1)}, s32[32,16384]{1,0:T(8,128)}, u32[]{:S(2)}) copy-start(s32[32,16384]{1,0:T(8,128)} %refs_12_.3) | copy-start | bytes 6291460
  8.6 12.8 %copy-start.2 = (f32[32,16384]{1,0:T(8,128)S(1)}, f32[32,16384]{1,0:T(8,128)}, u32[]{:S(2)}) copy-start(f32[32,16384]{1,0:T(8,128)} %refs_13_.3) | copy-start | bytes 6291460
  16.9 4.5 %collective-permute-start.3 = (bf16[32,8320]{1,0:T(8,128)(2,1)}, bf16[32,8320]{1,0:T(8,128)(2,1)S(1)}, u32[]{:S(2)}, u32[]{:S(2)}) collective-permute-start(bf16[32,8320]{1,0:T(8,128)(2,1)} %collective-permute-done.2.refs_4_.refs_8_), channel_id=1, source_target_pairs={{0,32},{32,0},{64,96},{96,64},{1,33},{33,1},{65,97},{97,65},{2,34}... | collective-permute-start | bytes 1597448 | tf_op jit(solution)/shard_map/ppermute | solution.py:463
  29.1 3.6 %collective-permute-start.4 = (bf16[32,8320]{1,0:T(8,128)(2,1)}, bf16[32,8320]{1,0:T(8,128)(2,1)S(1)}, u32[]{:S(2)}, u32[]{:S(2)}) collective-permute-start(bf16[32,8320]{1,0:T(8,128)(2,1)} %collective-permute-done.1.refs_4_.refs_8_), channel_id=1, source_target_pairs={{0,32},{32,0},{64,96},{96,64},{1,33},{33,1},{65,97},{97,65},{2,34}... | collective-permute-start | bytes 1597448 | tf_op jit(solution)/shard_map/ppermute | solution.py:463
  29.9 11.3 %collective-permute-start.5 = (bf16[32,7168]{1,0:T(8,128)(2,1)S(1)}, bf16[32,7168]{1,0:T(8,128)(2,1)S(1)}, u32[]{:S(2)}, u32[]{:S(2)}) collective-permute-start(bf16[32,7168]{1,0:T(8,128)(2,1)S(1)} %get-tuple-element.54.rest_0_), channel_id=1, source_target_pairs={{0,32},{32,0},{64,96},{96,64},{1,33},{33,1},{65,97},{97,65},{2,34}... | collective-permute-start | bytes 1376264 | tf_op jit(solution)/shard_map/ppermute | solution.py:463
  29.9 16.3 %collective-permute-start.7 = (bf16[32,7168]{1,0:T(8,128)(2,1)S(1)}, bf16[32,7168]{1,0:T(8,128)(2,1)S(1)}, u32[]{:S(2)}, u32[]{:S(2)}) collective-permute-start(bf16[32,7168]{1,0:T(8,128)(2,1)S(1)} %get-tuple-element.54.rest_0_), channel_id=1, source_target_pairs={{0,64},{32,96},{64,0},{96,32},{1,65},{33,97},{65,1},{97,33},{2,66}... | collective-permute-start | bytes 1376264 | tf_op jit(solution)/shard_map/ppermute | solution.py:463
  41.2 5.0 %collective-permute-start.6 = (bf16[2,128,128]{2,1,0:T(8,128)(2,1)S(1)}, bf16[2,128,128]{2,1,0:T(8,128)(2,1)S(1)}, u32[]{:S(2)}, u32[]{:S(2)}) collective-permute-start(bf16[2,128,128]{2,1,0:T(8,128)(2,1)S(1)} %convert_element_type.42), channel_id=1, source_target_pairs={{64,0},{65,1},{66,2},{67,3},{68,4},{69,5},{70,6},{71,7},{72,8},{73... | collective-permute-start | bytes 196616 | tf_op jit(solution)/shard_map/ppermute | solution.py:512
  43.7 3.8 %collective-permute-start.8 = (bf16[2,128,128]{2,1,0:T(8,128)(2,1)S(1)}, bf16[2,128,128]{2,1,0:T(8,128)(2,1)S(1)}, u32[]{:S(2)}, u32[]{:S(2)}) collective-permute-start(bf16[2,128,128]{2,1,0:T(8,128)(2,1)S(1)} %convert_element_type.42), channel_id=1, source_target_pairs={{1,0},{0,1},{3,2},{2,3},{5,4},{4,5},{7,6},{6,7},{9,8},{8,9},{11,10... | collective-permute-start | bytes 196616 | tf_op jit(solution)/shard_map/ppermute | solution.py:512
  44.0 4.3 %collective-permute-start.9 = (bf16[2,128,128]{2,1,0:T(8,128)(2,1)S(1)}, bf16[2,128,128]{2,1,0:T(8,128)(2,1)S(1)}, u32[]{:S(2)}, u32[]{:S(2)}) collective-permute-start(bf16[2,128,128]{2,1,0:T(8,128)(2,1)S(1)} %convert_element_type.42), channel_id=1, source_target_pairs={{65,0},{64,1},{67,2},{66,3},{69,4},{68,5},{71,6},{70,7},{73,8},{72... | collective-permute-start | bytes 196616 | tf_op jit(solution)/shard_map/ppermute | solution.py:512
  44.6 12.6 %collective-permute-start.12 = (bf16[32,9216]{1,0:T(8,128)(2,1)S(1)}, bf16[32,9216]{1,0:T(8,128)(2,1)S(1)}, u32[]{:S(2)}, u32[]{:S(2)}) collective-permute-start(bf16[32,9216]{1,0:T(8,128)(2,1)S(1)} %get-tuple-element.57.rest_4_), channel_id=1, source_target_pairs={{0,32},{32,0},{64,96},{96,64},{1,33},{33,1},{65,97},{97,65},{2,34}... | collective-permute-start | bytes 1769480 | tf_op jit(solution)/shard_map/ppermute | solution.py:463
  48.4 14.3 %collective-permute-start.10 = (bf16[32,9216]{1,0:T(8,128)(2,1)S(1)}, bf16[32,9216]{1,0:T(8,128)(2,1)S(1)}, u32[]{:S(2)}, u32[]{:S(2)}) collective-permute-start(bf16[32,9216]{1,0:T(8,128)(2,1)S(1)} %get-tuple-element.57.rest_4_), channel_id=1, source_target_pairs={{0,64},{32,96},{64,0},{96,32},{1,65},{33,97},{65,1},{97,33},{2,66}... | collective-permute-start | bytes 1769480 | tf_op jit(solution)/shard_map/ppermute | solution.py:463
  50.1 7.1 %collective-permute-start.11 = (bf16[3,128,128]{2,1,0:T(8,128)(2,1)S(1)}, bf16[3,128,128]{2,1,0:T(8,128)(2,1)S(1)}, u32[]{:S(2)}, u32[]{:S(2)}) collective-permute-start(bf16[3,128,128]{2,1,0:T(8,128)(2,1)S(1)} %pad_maximum_fusion.1), channel_id=1, source_target_pairs={{0,2},{1,3},{2,4},{3,5},{4,6},{5,7},{6,8},{7,9},{8,10},{9,11},{10,... | collective-permute-start | bytes 294920 | tf_op jit(solution)/shard_map/ppermute | solution.py:526
  51.8 9.5 %collective-permute-start.13 = (bf16[3,128,128]{2,1,0:T(8,128)(2,1)S(1)}, bf16[3,128,128]{2,1,0:T(8,128)(2,1)S(1)}, u32[]{:S(2)}, u32[]{:S(2)}) collective-permute-start(bf16[3,128,128]{2,1,0:T(8,128)(2,1)S(1)} %pad_maximum_fusion.2), channel_id=1, source_target_pairs={{0,30},{1,31},{2,0},{3,1},{4,2},{5,3},{6,4},{7,5},{8,6},{9,7},{10,... | collective-permute-start | bytes 294920 | tf_op jit(solution)/shard_map/ppermute | solution.py:526
  54.2 7.0 %collective-permute-start.14 = (bf16[128,128]{1,0:T(8,128)(2,1)S(1)}, bf16[128,128]{1,0:T(8,128)(2,1)S(1)}, u32[]{:S(2)}, u32[]{:S(2)}) collective-permute-start(bf16[128,128]{1,0:T(8,128)(2,1)S(1)} %get-tuple-element.69), channel_id=1, source_target_pairs={{0,4},{2,6},{4,8},{5,1},{6,10},{7,3},{8,12},{9,5},{10,14},{11,7},{... | collective-permute-start | bytes 98312 | tf_op jit(solution)/shard_map/ppermute | solution.py:531
  62.7 5.5 %collective-permute-start.17 = (bf16[32,9216]{1,0:T(8,128)(2,1)S(1)}, bf16[32,9216]{1,0:T(8,128)(2,1)S(1)}, u32[]{:S(2)}, u32[]{:S(2)}) collective-permute-start(bf16[32,9216]{1,0:T(8,128)(2,1)S(1)} %collective-permute-done.10.rest_6_), channel_id=1, source_target_pairs={{0,32},{32,0},{64,96},{96,64},{1,33},{33,1},{65,97},{97,65},{2,34}... | collective-permute-start | bytes 1769480 | tf_op jit(solution)/shard_map/ppermute | solution.py:463
  65.7 2.3 %collective-permute-start.16 = (bf16[32,7168]{1,0:T(8,128)(2,1)S(1)}, bf16[32,7168]{1,0:T(8,128)(2,1)S(1)}, u32[]{:S(2)}, u32[]{:S(2)}) collective-permute-start(bf16[32,7168]{1,0:T(8,128)(2,1)S(1)} %collective-permute-done.7.rest_2_), channel_id=1, source_target_pairs={{0,32},{32,0},{64,96},{96,64},{1,33},{33,1},{65,97},{97,65},{2,34}... | collective-permute-start | bytes 1376264 | tf_op jit(solution)/shard_map/ppermute | solution.py:463
  65.7 2.5 %collective-permute-start.15 = (f32[2,128,128]{2,1,0:T(8,128)S(1)}, f32[2,128,128]{2,1,0:T(8,128)S(1)}, u32[]{:S(2)}, u32[]{:S(2)}) collective-permute-start(f32[2,128,128]{2,1,0:T(8,128)S(1)} %shard_map.123.n0), channel_id=1, source_target_pairs={{0,32},{32,0},{64,96},{96,64},{1,33},{33,1},{65,97},{97,65},{2,34}... | collective-permute-start | bytes 393224 | tf_op jit(solution)/shard_map/ppermute | solution.py:463
  (4 other events, 28.6 us)
